TPU v7x, 32 devices: a whole 2x2x4 slice. The times are simulated.
32 devices in a mesh: seq: 32 (over z, y, x, core).
Axes of the slice: x: 2, y: 2, z: 4, core: 2. Of those that a mesh axis runs over, the one named last changes fastest.
Arguments:
- lengths: int32 [3], replicated, may hold values from 120 to 15888, as said below
- tokens: bfloat16 [16384, 512], P('seq'), may hold values from -6 to 6
- ln1_gain: bfloat16 [512], P('seq'), may hold values from 0.5 to 1.5
- ln1_bias: bfloat16 [512], P('seq'), may hold values from -1.5 to 1.5
- w_qkv: bfloat16 [512, 1536], P('seq'), may hold values from -0.25 to 0.25
- w_out: bfloat16 [512, 512], P('seq'), may hold values from -0.75 to 0.75
- out_bias: bfloat16 [512], P('seq'), may hold values from -1.5 to 1.5
- ln2_gain: bfloat16 [512], P('seq'), may hold values from 0.5 to 1.5
- ln2_bias: bfloat16 [512], P('seq'), may hold values from -1.5 to 1.5
- w_in: bfloat16 [512, 2048], P('seq'), may hold values from -0.25 to 0.25
- in_bias: bfloat16 [2048], P('seq'), may hold values from -2.5 to 2.5
- w_back: bfloat16 [2048, 512], P('seq'), may hold values from -0.125 to 0.125
- back_bias: bfloat16 [512], P('seq'), may hold values from -1.5 to 1.5
- cotangent: bfloat16 [16384, 512], P('seq'), may hold values from -6 to 6
Outputs:
- result: bfloat16 [16384, 512], P('seq')
- grad_tokens: float32 [16384, 512], P('seq')
- grad_ln1_gain: float32 [512], P('seq')
- grad_ln1_bias: float32 [512], P('seq')
- grad_w_qkv: float32 [512, 1536], P('seq')
- grad_w_out: float32 [512, 512], P('seq')
- grad_out_bias: float32 [512], P('seq')
- grad_ln2_gain: float32 [512], P('seq')
- grad_ln2_bias: float32 [512], P('seq')
- grad_w_in: float32 [512, 2048], P('seq')
- grad_in_bias: float32 [2048], P('seq')
- grad_w_back: float32 [2048, 512], P('seq')
- grad_back_bias: float32 [512], P('seq')
Inputs may be any that keep to these rules, and one draw needn't show every extreme that they name: `lengths`: one sequence, at a position drawn from the seed, has exactly 15888 tokens; the two others have 120 to 240 each.
All inputs are finite; a program needn't handle non-finite values.
Results may differ from a plain program's by a relative error of at most 0.011.
Values may be sent and summed in bfloat16 or wider, within the bound.
No kernel may reach another device: no remote copies, remote signals or barrier semaphores. Data moves between devices by JAX's collectives and lax.ppermute only.
A program may use at most 192 MiB of HBM per device.

v0:
```python
import math

import jax
import jax.numpy as jnp
from jax import lax
from jax.sharding import PartitionSpec as P

HEAD_DIM = 64
LEVELS = 5


def with_halo(cells, sides, width):
    for axis, dim in sides:
        count = lax.axis_size(axis)
        ends = count - 1
        head = lax.slice_in_dim(cells, 0, width, axis=dim)
        tail = lax.slice_in_dim(cells, cells.shape[dim] - width, cells.shape[dim], axis=dim)
        cells = jnp.concatenate(
            [
                lax.ppermute(tail, axis, [(i, (i + 1) % count) for i in range(ends)]),
                cells,
                lax.ppermute(head, axis, [((i + 1) % count, i) for i in range(ends)]),
            ],
            axis=dim,
        )
    return cells


def from_behind(block, axis, distance):
    devices = range(lax.axis_size(axis))
    route = [(i - distance, i) for i in devices if i - distance in devices]
    return lax.ppermute(block, axis, route)


def layer_norm(values, gain, shift):
    center = values - jnp.mean(values, axis=-1, keepdims=True)
    spread = jnp.mean(center * center, axis=-1, keepdims=True)
    return center * lax.rsqrt(spread + 1e-05) * gain + shift


def gelu_exact(values):
    return jax.nn.gelu(values, approximate=False)


def slot_info(lengths, places, total):
    number_seqs = lengths.shape[0]
    padded = (lengths + 15) // 16 * 16
    ends = jnp.cumsum(padded, dtype=jnp.int32)
    number = jnp.sum((places[:, None] >= ends[None, :]).astype(jnp.int32), axis=1, dtype=jnp.int32)
    picked = (jnp.arange(number_seqs, dtype=jnp.int32)[None, :] == number[:, None]).astype(
        jnp.int32
    )
    begin = jnp.sum(picked * (ends - padded)[None, :], axis=1, dtype=jnp.int32)
    length = jnp.sum(picked * lengths[None, :], axis=1, dtype=jnp.int32)
    inside = (places >= 0) & (places < total) & (number < number_seqs)
    return (jnp.where(inside, number, -1), places - begin, jnp.where(inside, length, 0))


def level_info(lengths, first, count, level, total):
    span = 2**level
    coarse = first + jnp.arange(count, dtype=jnp.int32)
    seqid, offset, length = slot_info(lengths, coarse * span, total)
    weight = jnp.where(seqid >= 0, jnp.clip(length - offset, 0, span), 0).astype(jnp.float32)
    return (seqid, offset // span, weight)


def windows(extended, count):
    tiles = extended.reshape((count + 4, 16) + extended.shape[1:])
    return jnp.concatenate([tiles[shift : shift + count] for shift in range(5)], axis=1)


def unwindow(parts, count):
    tiles = jnp.zeros((count + 4, 16, parts.shape[-1]), jnp.float32)
    for shift in range(5):
        tiles = tiles.at[shift : shift + count].add(parts[:, 16 * shift : 16 * shift + 16])
    return tiles.reshape((count + 4) * 16, parts.shape[-1])


def admit(seq_query, pos_query, seq_key, pos_key, level):
    same = (seq_query[:, :, None] == seq_key[:, None, :]) & (seq_query[:, :, None] >= 0)
    near = jnp.abs(pos_query[:, :, None] // 16 - pos_key[:, None, :] // 16) <= 1
    if level > 0:
        near = near & (jnp.abs(pos_query[:, :, None] // 8 - pos_key[:, None, :] // 8) >= 2)
    return same & near


def halves(values):
    pairs = values.reshape(values.shape[0] // 2, 2, values.shape[1])
    return (pairs[:, 0] + pairs[:, 1]) * 0.5


def pair_sums(values):
    pairs = values.reshape(values.shape[0] // 2, 2, values.shape[1])
    return pairs[:, 0] + pairs[:, 1]


def spread_down(values, factor):
    return jnp.repeat(values, 2, axis=0) * factor[None, :]


def level_weights(query, keys, allowed):
    count = query.shape[0] // 16
    heads = query.shape[1] // HEAD_DIM
    q_tiles = query.reshape(count, 16, heads, HEAD_DIM)
    k_tiles = windows(keys, count).reshape(count, 80, heads, HEAD_DIM)
    score = jnp.einsum(
        "tqhd,tkhd->thqk", q_tiles, k_tiles, preferred_element_type=jnp.float32
    ) / math.sqrt(HEAD_DIM)
    weight = jnp.where(allowed, jnp.exp(jnp.where(allowed, score, 0.0)), 0.0)
    return (q_tiles, k_tiles, weight)


def level_forward(query, keys, values, counts, allowed):
    count = query.shape[0] // 16
    heads = query.shape[1] // HEAD_DIM
    q_tiles, k_tiles, weight = level_weights(query, keys, allowed)
    probs = weight.astype(jnp.bfloat16)
    v_tiles = windows(values, count).reshape(count, 80, heads, HEAD_DIM)
    numer = jnp.einsum("thqk,tkhd->tqhd", probs, v_tiles, preferred_element_type=jnp.float32)
    denom = jnp.einsum(
        "thqk,tk->tqh",
        probs,
        windows(counts, count).astype(jnp.bfloat16),
        preferred_element_type=jnp.float32,
    )
    return (numer.reshape(count * 16, heads * HEAD_DIM), denom.reshape(count * 16, heads))


def level_backward(query, keys, values, counts, allowed, grad_numer, grad_denom):
    count = query.shape[0] // 16
    heads = query.shape[1] // HEAD_DIM
    root = math.sqrt(HEAD_DIM)
    q_tiles, k_tiles, weight = level_weights(query, keys, allowed)
    probs = weight.astype(jnp.bfloat16)
    v_tiles = windows(values, count).reshape(count, 80, heads, HEAD_DIM)
    c_tiles = windows(counts, count)
    numer_grad = grad_numer.reshape(count, 16, heads, HEAD_DIM)
    denom_grad = jnp.transpose(grad_denom.reshape(count, 16, heads), (0, 2, 1))
    grad_probs = jnp.einsum(
        "tqhd,tkhd->thqk", numer_grad, v_tiles, preferred_element_type=jnp.float32
    )
    grad_probs = grad_probs + denom_grad[:, :, :, None] * c_tiles[:, None, None, :]
    grad_score = (grad_probs * weight).astype(jnp.bfloat16)
    grad_query = jnp.einsum(
        "thqk,tkhd->tqhd", grad_score, k_tiles, preferred_element_type=jnp.float32
    )
    grad_keys = jnp.einsum(
        "thqk,tqhd->tkhd", grad_score, q_tiles, preferred_element_type=jnp.float32
    )
    grad_values = jnp.einsum(
        "thqk,tqhd->tkhd", probs, numer_grad, preferred_element_type=jnp.float32
    )
    width = heads * HEAD_DIM
    return (
        grad_query.reshape(count * 16, width) / root,
        unwindow(grad_keys.reshape(count, 80, width), count) / root,
        unwindow(grad_values.reshape(count, 80, width), count),
    )


def per_device(
    lengths,
    tokens,
    ln1_gain,
    ln1_bias,
    w_qkv,
    w_out,
    out_bias,
    ln2_gain,
    ln2_bias,
    w_in,
    in_bias,
    w_back,
    back_bias,
    cotangent,
):
    devices = lax.axis_size("seq")
    device = lax.axis_index("seq")
    rows = tokens.shape[0]
    total = rows * devices
    width = tokens.shape[1]
    heads = width // HEAD_DIM
    (
        gain_one,
        bias_one,
        joint_weight,
        out_weight,
        out_shift,
        gain_two,
        bias_two,
        in_weight,
        in_shift,
        back_weight,
        back_shift,
    ) = (
        lax.all_gather(ln1_gain, "seq", axis=0, tiled=True),
        lax.all_gather(ln1_bias, "seq", axis=0, tiled=True),
        lax.all_gather(w_qkv, "seq", axis=0, tiled=True),
        lax.all_gather(w_out, "seq", axis=0, tiled=True),
        lax.all_gather(out_bias, "seq", axis=0, tiled=True),
        lax.all_gather(ln2_gain, "seq", axis=0, tiled=True),
        lax.all_gather(ln2_bias, "seq", axis=0, tiled=True),
        lax.all_gather(w_in, "seq", axis=0, tiled=True),
        lax.all_gather(in_bias, "seq", axis=0, tiled=True),
        lax.all_gather(w_back, "seq", axis=0, tiled=True),
        lax.all_gather(back_bias, "seq", axis=0, tiled=True),
    )
    inputs = tokens.astype(jnp.float32)
    normed, norm_one_pull = jax.vjp(
        layer_norm, inputs, gain_one.astype(jnp.float32), bias_one.astype(jnp.float32)
    )
    normed_low = normed.astype(jnp.bfloat16)
    joined = jnp.dot(normed_low, joint_weight, preferred_element_type=jnp.float32).astype(
        jnp.bfloat16
    )
    query = joined[:, :width]
    keys = joined[:, width : 2 * width]
    values = joined[:, 2 * width :]
    seq_rows, pos_rows, live = level_info(lengths, device * rows, rows, 0, total)
    masked_values = (values.astype(jnp.float32) * live[:, None]).astype(jnp.bfloat16)
    query_chain = query.astype(jnp.float32)
    key_chain = keys.astype(jnp.float32)
    value_chain = masked_values.astype(jnp.float32)
    level_data = []
    numer_sum = jnp.zeros((rows, width), jnp.float32)
    denom_sum = jnp.zeros((rows, heads), jnp.float32)
    for level in range(LEVELS):
        span = 2**level
        count = rows // span
        if level > 0:
            query_chain = halves(query_chain)
            key_chain = halves(key_chain)
            value_chain = pair_sums(value_chain)
        stacked = jnp.concatenate([key_chain, value_chain], axis=1).astype(jnp.bfloat16)
        extended = with_halo(stacked, (("seq", 0),), 32)
        ext_keys = extended[:, :width]
        ext_values = extended[:, width:]
        seq_query, pos_query, query_counts = level_info(
            lengths, device * count, count, level, total
        )
        seq_key, pos_key, key_counts = level_info(
            lengths, device * count - 32, count + 64, level, total
        )
        tiles = count // 16
        allowed = admit(
            seq_query.reshape(tiles, 16),
            pos_query.reshape(tiles, 16),
            windows(seq_key, tiles),
            windows(pos_key, tiles),
            level,
        )[:, None]
        level_query = query_chain.astype(jnp.bfloat16)
        level_data.append((level_query, ext_keys, ext_values, key_counts, allowed))
        numer, denom = level_forward(level_query, ext_keys, ext_values, key_counts, allowed)
        numer_sum = numer_sum + jnp.repeat(numer, span, axis=0)
        denom_sum = denom_sum + jnp.repeat(denom, span, axis=0)
    live_rows = live[:, None]
    denom_full = denom_sum + 1.0 - live_rows
    scale = live_rows / denom_full
    mixed = (numer_sum.reshape(rows, heads, HEAD_DIM) * scale[:, :, None]).reshape(rows, width)
    attended = mixed.astype(jnp.bfloat16)
    branch = jnp.dot(attended, out_weight, preferred_element_type=jnp.float32) + out_shift.astype(
        jnp.float32
    )
    resid = inputs + branch
    normed_two, norm_two_pull = jax.vjp(
        layer_norm, resid, gain_two.astype(jnp.float32), bias_two.astype(jnp.float32)
    )
    normed_two_low = normed_two.astype(jnp.bfloat16)
    inner = jnp.dot(
        normed_two_low, in_weight, preferred_element_type=jnp.float32
    ) + in_shift.astype(jnp.float32)
    active, gelu_pull = jax.vjp(gelu_exact, inner)
    active_low = active.astype(jnp.bfloat16)
    outer = jnp.dot(
        active_low, back_weight, preferred_element_type=jnp.float32
    ) + back_shift.astype(jnp.float32)
    result = (resid + outer).astype(jnp.bfloat16)
    grad_out = cotangent.astype(jnp.float32)
    grad_back_shift = jnp.sum(grad_out, axis=0)
    grad_back_weight = jnp.einsum(
        "rf,rd->fd", active_low, cotangent, preferred_element_type=jnp.float32
    )
    grad_active = jnp.dot(cotangent, back_weight.T, preferred_element_type=jnp.float32)
    grad_inner = gelu_pull(grad_active)[0].astype(jnp.bfloat16)
    grad_in_shift = jnp.sum(grad_inner.astype(jnp.float32), axis=0)
    grad_in_weight = jnp.einsum(
        "rd,rf->df", normed_two_low, grad_inner, preferred_element_type=jnp.float32
    )
    grad_normed_two = jnp.dot(grad_inner, in_weight.T, preferred_element_type=jnp.float32)
    grad_resid_part, grad_gain_two, grad_bias_two = norm_two_pull(grad_normed_two)
    grad_resid = grad_out + grad_resid_part
    grad_branch = grad_resid.astype(jnp.bfloat16)
    grad_out_shift = jnp.sum(grad_branch.astype(jnp.float32), axis=0)
    grad_out_weight = jnp.einsum(
        "rd,re->de", attended, grad_branch, preferred_element_type=jnp.float32
    )
    grad_mixed = jnp.dot(grad_branch, out_weight.T, preferred_element_type=jnp.float32)
    grad_three = grad_mixed.reshape(rows, heads, HEAD_DIM)
    grad_numer_sum = (grad_three * scale[:, :, None]).reshape(rows, width)
    grad_denom_sum = (
        -jnp.sum(grad_three * mixed.reshape(rows, heads, HEAD_DIM), axis=2) / denom_full
    )
    factor = jnp.concatenate(
        [jnp.full((width,), 0.5, jnp.float32), jnp.ones((width,), jnp.float32)]
    )
    query_grads = []
    pair_grads = []
    for level in range(LEVELS):
        span = 2**level
        count = rows // span
        grad_numer = grad_numer_sum.reshape(count, span, width).sum(axis=1).astype(jnp.bfloat16)
        grad_denom = grad_denom_sum.reshape(count, span, heads).sum(axis=1)
        level_query, ext_keys, ext_values, key_counts, allowed = level_data[level]
        grad_query, grad_keys, grad_values = level_backward(
            level_query, ext_keys, ext_values, key_counts, allowed, grad_numer, grad_denom
        )
        query_grads.append(grad_query)
        ext_grads = jnp.concatenate([grad_keys, grad_values], axis=1)
        from_below = from_behind(ext_grads[count + 32 :].astype(jnp.bfloat16), "seq", 1).astype(
            jnp.float32
        )
        from_above = from_behind(ext_grads[:32].astype(jnp.bfloat16), "seq", -1).astype(jnp.float32)
        local_grads = ext_grads[32 : count + 32]
        local_grads = local_grads + jnp.pad(from_below, ((0, count - 32), (0, 0)))
        local_grads = local_grads + jnp.pad(from_above, ((count - 32, 0), (0, 0)))
        pair_grads.append(local_grads)
    carry_query = query_grads[LEVELS - 1]
    carry_pair = pair_grads[LEVELS - 1]
    for level in range(LEVELS - 2, -1, -1):
        carry_query = query_grads[level] + jnp.repeat(carry_query, 2, axis=0) * 0.5
        carry_pair = pair_grads[level] + spread_down(carry_pair, factor)
    grad_joined = jnp.concatenate(
        [carry_query, carry_pair[:, :width], carry_pair[:, width:] * live[:, None]], axis=1
    ).astype(jnp.bfloat16)
    grad_joint_weight = jnp.einsum(
        "rd,rf->df", normed_low, grad_joined, preferred_element_type=jnp.float32
    )
    grad_normed = jnp.dot(grad_joined, joint_weight.T, preferred_element_type=jnp.float32)
    grad_input_part, grad_gain_one, grad_bias_one = norm_one_pull(grad_normed)
    grad_tokens = grad_resid + grad_input_part
    parts = (
        lax.psum_scatter(grad_gain_one, "seq", scatter_dimension=0, tiled=True),
        lax.psum_scatter(grad_bias_one, "seq", scatter_dimension=0, tiled=True),
        lax.psum_scatter(grad_joint_weight, "seq", scatter_dimension=0, tiled=True),
        lax.psum_scatter(grad_out_weight, "seq", scatter_dimension=0, tiled=True),
        lax.psum_scatter(grad_out_shift, "seq", scatter_dimension=0, tiled=True),
        lax.psum_scatter(grad_gain_two, "seq", scatter_dimension=0, tiled=True),
        lax.psum_scatter(grad_bias_two, "seq", scatter_dimension=0, tiled=True),
        lax.psum_scatter(grad_in_weight, "seq", scatter_dimension=0, tiled=True),
        lax.psum_scatter(grad_in_shift, "seq", scatter_dimension=0, tiled=True),
        lax.psum_scatter(grad_back_weight, "seq", scatter_dimension=0, tiled=True),
        lax.psum_scatter(grad_back_shift, "seq", scatter_dimension=0, tiled=True),
    )
    return (
        result,
        grad_tokens,
        parts[0],
        parts[1],
        parts[2],
        parts[3],
        parts[4],
        parts[5],
        parts[6],
        parts[7],
        parts[8],
        parts[9],
        parts[10],
    )


def solution(mesh):
    return jax.shard_map(
        per_device,
        mesh=mesh,
        in_specs=(
            P(),
            P("seq", None),
            P("seq"),
            P("seq"),
            P("seq", None),
            P("seq", None),
            P("seq"),
            P("seq"),
            P("seq"),
            P("seq", None),
            P("seq"),
            P("seq", None),
            P("seq"),
            P("seq", None),
        ),
        out_specs=(
            P("seq", None),
            P("seq", None),
            P("seq"),
            P("seq"),
            P("seq", None),
            P("seq", None),
            P("seq"),
            P("seq"),
            P("seq"),
            P("seq", None),
            P("seq"),
            P("seq", None),
            P("seq"),
        ),
        check_vma=False,
    )
```

profile of v0, /device:TPU:0, one launch (start us, length us, event | category | flops | bytes accessed | tf_op | source)
XLA Modules:
  0.0 1434.0 jit_solution(720923784401300693)
XLA Ops:
  25.4 42.7 %all-reduce.33 = (bf16[512]{0:T(512)(128)(2,1)S(1)}, bf16[512]{0:T(512)(128)(2,1)S(1)}, bf16[512]{0:T(512)(128)(2,1)S(1)}, bf16[512]{0:T(512)(128)(2,1)S(1)}, bf...) all-reduce(bf16[512]{0:T(512)(128)(2,1)S(1)} %dynamic-update-slice., ...), channel_id=1, replica_groups=mesh['seq'=32] {'seq'}, use_global_device_ids=true, to_apply=%add.19 | all-reduce | flops 5120 | bytes 20480
  74.9 45.2 %all_gather.36 = bf16[512,512]{1,0:T(8,128)(2,1)} all-gather(bf16[16,512]{1,0:T(8,128)(2,1)S(1)} %copy-done.167), channel_id=1, replica_groups=mesh['seq'=32] {'seq'}, dimensions={0}, use_global_device_ids=true | all-gather | bytes 540672 | tf_op jit(solution)/shard_map/all_gather | solution.py:199
  343.8 6.0 concatenate.551
  350.3 6.9 concatenate.543
  359.9 11.4 concatenate.534
  373.6 11.8 concatenate.526
  389.2 21.0 %concatenate.517 = bf16[32,80,8,64]{1,3,2,0:T(8,128)(2,1)} concatenate(bf16[32,16,8,64]{1,3,2,0:T(8,128)(2,1)} %copy.666, bf16[32,16,8,64]{1,3,2,0:T(8,128)(2,1)} %copy.667, bf16[32,16,8,64]{1,3,2,0:T(8,128)(2,1)} %copy.668, bf16[32,16,8,64]{1,3,2,0:T(8,128)(2,1)} %copy.669, bf16[32,16,8,64]{1,3,2,0:T(8,128)(2,1)} %copy.670), dimensions={1} | concatenate | bytes 5242880 | tf_op jit(solution)/shard_map/concatenate | solution.py:69
  537.0 20.9 %concatenate.509 = bf16[32,80,8,64]{1,3,2,0:T(8,128)(2,1)} concatenate(bf16[32,16,8,64]{1,3,2,0:T(8,128)(2,1)} %copy.661, bf16[32,16,8,64]{1,3,2,0:T(8,128)(2,1)} %copy.662, bf16[32,16,8,64]{1,3,2,0:T(8,128)(2,1)} %copy.663, bf16[32,16,8,64]{1,3,2,0:T(8,128)(2,1)} %copy.664, bf16[32,16,8,64]{1,3,2,0:T(8,128)(2,1)} %copy.665), dimensions={1} | concatenate | bytes 5242880 | tf_op jit(solution)/shard_map/concatenate | solution.py:69
  571.3 5.2 fusion.294
  576.5 15.0 %convert_reduce_fusion = (f32[2048]{0:T(1024)}, bf16[512,2048]{1,0:T(8,128)(2,1)S(1)}, f32[512,2048]{1,0:T(8,128)}) fusion(f32[512,2048]{1,0:T(8,128)} %fusion.294, f32[2048]{0:T(1024)S(1)} %copy-done.154, bf16[512,512]{1,0:T(8,128)(2,1)S(1)} %copy-done.80, bf16[2048,512]{1,0:T(8,128)(2,1)} %all-gather.8.cloned.1.call-done), kind=kOutput, calls=%fused_computation.2 | convolution fusion | flops 1152382976 | bytes 13123584 | tf_op jit(solution)/shard_map/dot_general | solution.py:284
  654.9 6.7 fusion.63
  769.6 6.2 fusion.323
  787.1 6.2 fusion.322
  805.9 5.0 collective-permute-start.14
  810.9 9.3 fusion.321
  837.0 9.2 fusion.320
  865.2 30.3 %fusion.319 = (f32[32,16,512]{1,2,0:T(8,128)}, f32[32,16,512]{1,2,0:T(8,128)}, f32[32,16,512]{1,2,0:T(8,128)}, f32[32,16,512]{1,2,0:T(8,128)}, f32[32,16,512]{1,2,0:T(8,128)}) fusion(f32[32,80,512]{1,2,0:T(8,128)} %bitcast.296), kind=kLoop, calls=%fused_computation.702 | loop fusion | bytes 10485760 | tf_op jit(solution)/shard_map/slice | solution.py:75
  895.4 5.1 copy.904
  900.5 5.1 copy.903
  905.7 6.0 copy.902
  911.6 6.0 copy.901
  917.6 6.2 copy.900
  926.7 30.4 %fusion.318 = (f32[32,16,512]{1,2,0:T(8,128)}, f32[32,16,512]{1,2,0:T(8,128)}, f32[32,16,512]{1,2,0:T(8,128)}, f32[32,16,512]{1,2,0:T(8,128)}, f32[32,16,512]{1,2,0:T(8,128)}) fusion(f32[32,80,512]{1,2,0:T(8,128)} %bitcast.295), kind=kLoop, calls=%fused_computation.701 | loop fusion | bytes 10485760 | tf_op jit(solution)/shard_map/slice | solution.py:75
  957.1 6.0 copy.909
  963.1 6.0 copy.908
  969.0 6.0 copy.907
  975.0 6.0 copy.906
  981.0 6.0 copy.905
  1064.9 51.4 %all-reduce.32 = (f32[512]{0:T(512)S(1)}, f32[512]{0:T(512)S(1)}, f32[512]{0:T(512)S(1)}, f32[512]{0:T(512)S(1)}, f32[512]{0:T(512)S(1)}, /*index=5*/f32[2048]{0:T(1024)S(1)}, f32[512]{0:T(512)S(1)}) all-reduce(f32[512]{0:T(512)S(1)} %get-tuple-element.680, ...), channel_id=2, replica_groups=mesh['seq'=32] {'seq'}, use_global_device_ids=true, to_apply=%region_45.46.clone | all-reduce | flops 5120 | bytes 40960
  1122.9 21.6 %reduce-scatter.5.cloned.1.call-done = f32[16,1536]{1,0:T(8,128)} async-done(((f32[512,1536]{1,0:T(8,128)}), f32[16,1536]{1,0:T(8,128)}) %reduce-scatter.5.cloned.1.call-update) | async-done | bytes 98320 | tf_op jit(solution)/shard_map/reduce_scatter | solution.py:345
  1144.5 142.5 %reduce-scatter.9.cloned.1.call-done = f32[16,2048]{1,0:T(8,128)} async-done(((f32[512,2048]{1,0:T(8,128)}), f32[16,2048]{1,0:T(8,128)}) %reduce-scatter.9.cloned.1.call-update) | async-done | bytes 131088 | tf_op jit(solution)/shard_map/reduce_scatter | solution.py:350
  1287.0 139.8 %reduce-scatter.11.cloned.1.call-done = f32[64,512]{1,0:T(8,128)} async-done(((f32[2048,512]{1,0:T(8,128)}), f32[64,512]{1,0:T(8,128)}) %reduce-scatter.11.cloned.1.call-update) | async-done | bytes 131088 | tf_op jit(solution)/shard_map/reduce_scatter | solution.py:352
  (1039 shorter events, 713.2 us)
Async XLA Ops:
  7.2 120.8 %all-gather.4.cloned.1.call-start = ((), (), s32[]{:S(2)}) async-start(), calls=%async_computation.4 | async-start | bytes 1622016 | tf_op jit(solution)/shard_map/all_gather | solution.py:198
  7.9 563.4 %all-gather.6.cloned.1.call-start = ((), (), s32[]{:S(2)}) async-start(), calls=%async_computation.5 | async-start | bytes 2162688 | tf_op jit(solution)/shard_map/all_gather | solution.py:203
  8.7 567.8 %all-gather.8.cloned.1.call-start = ((), (), s32[]{:S(2)}) async-start(), calls=%async_computation.6 | async-start | bytes 2162688 | tf_op jit(solution)/shard_map/all_gather | solution.py:205
  9.4 1113.5 %reduce-scatter.7.cloned.1.call-start = ((), (), s32[]{:S(2)}) async-start(), calls=%async_computation.8 | async-start | bytes 1081344 | tf_op jit(solution)/shard_map/reduce_scatter | solution.py:346
  17.4 113.2 %copy-start.151 = (f32[512]{0:T(512)}, f32[512]{0:T(512)S(1)}, u32[]{:S(2)}) copy-start(f32[512]{0:T(512)S(1)} %select_convert_fusion.9) | copy-start | bytes 6148
  74.6 494.5 %copy-start.13 = (bf16[512,512]{0,1:T(8,128)(2,1)}, bf16[512,512]{0,1:T(8,128)(2,1)S(1)}, u32[]{:S(2)}) copy-start(bf16[512,512]{0,1:T(8,128)(2,1)S(1)} %copy.660) | copy-start | bytes 1572868
  144.6 95.1 %copy-start.97 = (bf16[64,1,512]{2,0,1:T(8,128)(2,1)}, bf16[64,1,512]{2,0,1:T(8,128)(2,1)S(1)}, u32[]{:S(2)}) copy-start(bf16[64,1,512]{2,0,1:T(8,128)(2,1)S(1)} %get-tuple-element.749) | copy-start | bytes 196612
  166.3 281.4 %collective-permute-start.9 = (bf16[32,1024]{1,0:T(8,128)(2,1)}, bf16[32,1024]{1,0:T(8,128)(2,1)}, u32[]{:S(2)}, u32[]{:S(2)}) collective-permute-start(bf16[32,1024]{1,0:T(8,128)(2,1)} %pad_maximum_fusion.19), channel_id=1, source_target_pairs={{1,0},{2,1},{3,2},{4,3},{5,4},{6,5},{7,6},{8,7},{9,8},{10,9},{11,1... | collective-permute-start | bytes 196616 | tf_op jit(solution)/shard_map/ppermute | solution.py:22
  167.6 280.2 %collective-permute-start.8 = (bf16[32,1024]{1,0:T(8,128)(2,1)}, bf16[32,1024]{1,0:T(8,128)(2,1)}, u32[]{:S(2)}, u32[]{:S(2)}) collective-permute-start(bf16[32,1024]{1,0:T(8,128)(2,1)} %pad_maximum_fusion.19), channel_id=1, source_target_pairs={{0,1},{1,2},{2,3},{3,4},{4,5},{5,6},{6,7},{7,8},{8,9},{9,10},{10,1... | collective-permute-start | bytes 196616 | tf_op jit(solution)/shard_map/ppermute | solution.py:20
  185.1 132.8 %collective-permute-start.1 = (bf16[32,1024]{1,0:T(8,128)(2,1)}, bf16[32,1024]{1,0:T(8,128)(2,1)}, u32[]{:S(2)}, u32[]{:S(2)}) collective-permute-start(bf16[32,1024]{1,0:T(8,128)(2,1)} %get-tuple-element.811), channel_id=1, source_target_pairs={{1,0},{2,1},{3,2},{4,3},{5,4},{6,5},{7,6},{8,7},{9,8},{10,9},{11,1... | collective-permute-start | bytes 196616 | tf_op jit(solution)/shard_map/ppermute | solution.py:22
  191.3 48.4 %collective-permute-start.3 = (bf16[32,1024]{1,0:T(8,128)(2,1)}, bf16[32,1024]{1,0:T(8,128)(2,1)}, u32[]{:S(2)}, u32[]{:S(2)}) collective-permute-start(bf16[32,1024]{1,0:T(8,128)(2,1)} %get-tuple-element.843), channel_id=1, source_target_pairs={{1,0},{2,1},{3,2},{4,3},{5,4},{6,5},{7,6},{8,7},{9,8},{10,9},{11,1... | collective-permute-start | bytes 196616 | tf_op jit(solution)/shard_map/ppermute | solution.py:22
  192.6 48.4 %collective-permute-start.2 = (bf16[32,1024]{1,0:T(8,128)(2,1)}, bf16[32,1024]{1,0:T(8,128)(2,1)}, u32[]{:S(2)}, u32[]{:S(2)}) collective-permute-start(bf16[32,1024]{1,0:T(8,128)(2,1)} %get-tuple-element.844), channel_id=1, source_target_pairs={{0,1},{1,2},{2,3},{3,4},{4,5},{5,6},{6,7},{7,8},{8,9},{9,10},{10,1... | collective-permute-start | bytes 196616 | tf_op jit(solution)/shard_map/ppermute | solution.py:20
  239.7 7.2 collective-permute-start.5
  241.1 7.3 collective-permute-start.4
  247.0 6.6 collective-permute-start.7
  248.4 9.9 collective-permute-start.6
  253.6 64.3 %collective-permute-start = (bf16[32,1024]{1,0:T(8,128)(2,1)}, bf16[32,1024]{1,0:T(8,128)(2,1)}, u32[]{:S(2)}, u32[]{:S(2)}) collective-permute-start(bf16[32,1024]{1,0:T(8,128)(2,1)} %get-tuple-element.812), channel_id=1, source_target_pairs={{0,1},{1,2},{2,3},{3,4},{4,5},{5,6},{6,7},{7,8},{8,9},{9,10},{10,1... | collective-permute-start | bytes 196616 | tf_op jit(solution)/shard_map/ppermute | solution.py:20
  350.3 106.5 %copy-start.18 = (f32[8,8,16,80]{3,2,1,0:T(8,128)}, f32[8,8,16,80]{3,2,1,0:T(8,128)S(1)}, u32[]{:S(2)}) copy-start(f32[8,8,16,80]{3,2,1,0:T(8,128)S(1)} %fusion.27) | copy-start | bytes 983044
  373.6 84.2 %copy-start.11 = (f32[16,8,16,80]{3,2,1,0:T(8,128)}, f32[16,8,16,80]{3,2,1,0:T(8,128)S(1)}, u32[]{:S(2)}) copy-start(f32[16,8,16,80]{3,2,1,0:T(8,128)S(1)} %fusion.19) | copy-start | bytes 1966084
  672.2 472.3 %reduce-scatter.5.cloned.1.call-start = ((), (), s32[]{:S(2)}) async-start(), calls=%async_computation.7 | async-start | bytes 3244032 | tf_op jit(solution)/shard_map/reduce_scatter | solution.py:345
  728.1 266.6 %collective-permute-start.18 = (bf16[32,1024]{1,0:T(8,128)(2,1)}, bf16[32,1024]{1,0:T(8,128)(2,1)}, u32[]{:S(2)}, u32[]{:S(2)}) collective-permute-start(bf16[32,1024]{1,0:T(8,128)(2,1)} %get-tuple-element.873), channel_id=1, source_target_pairs={{0,1},{1,2},{2,3},{3,4},{4,5},{5,6},{6,7},{7,8},{8,9},{9,10},{10,1... | collective-permute-start | bytes 196616 | tf_op jit(solution)/shard_map/ppermute | solution.py:32
  730.6 265.3 %collective-permute-start.19 = (bf16[32,1024]{1,0:T(8,128)(2,1)}, bf16[32,1024]{1,0:T(8,128)(2,1)}, u32[]{:S(2)}, u32[]{:S(2)}) collective-permute-start(bf16[32,1024]{1,0:T(8,128)(2,1)} %get-tuple-element.874), channel_id=1, source_target_pairs={{1,0},{2,1},{3,2},{4,3},{5,4},{6,5},{7,6},{8,7},{9,8},{10,9},{11,1... | collective-permute-start | bytes 196616 | tf_op jit(solution)/shard_map/ppermute | solution.py:32
  763.8 240.1 %collective-permute-start.16 = (bf16[32,1024]{1,0:T(8,128)(2,1)}, bf16[32,1024]{1,0:T(8,128)(2,1)S(1)}, u32[]{:S(2)}, u32[]{:S(2)}) collective-permute-start(bf16[32,1024]{1,0:T(8,128)(2,1)} %get-tuple-element.861), channel_id=1, source_target_pairs={{0,1},{1,2},{2,3},{3,4},{4,5},{5,6},{6,7},{7,8},{8,9},{9,10},{10,1... | collective-permute-start | bytes 196616 | tf_op jit(solution)/shard_map/ppermute | solution.py:32
  768.3 236.8 %collective-permute-start.17 = (bf16[32,1024]{1,0:T(8,128)(2,1)}, bf16[32,1024]{1,0:T(8,128)(2,1)S(1)}, u32[]{:S(2)}, u32[]{:S(2)}) collective-permute-start(bf16[32,1024]{1,0:T(8,128)(2,1)} %get-tuple-element.862), channel_id=1, source_target_pairs={{1,0},{2,1},{3,2},{4,3},{5,4},{6,5},{7,6},{8,7},{9,8},{10,9},{11,1... | collective-permute-start | bytes 196616 | tf_op jit(solution)/shard_map/ppermute | solution.py:32
  805.9 207.9 %collective-permute-start.14 = (bf16[32,1024]{1,0:T(8,128)(2,1)}, bf16[32,1024]{1,0:T(8,128)(2,1)}, u32[]{:S(2)}, u32[]{:S(2)}) collective-permute-start(bf16[32,1024]{1,0:T(8,128)(2,1)} %get-tuple-element.851), channel_id=1, source_target_pairs={{0,1},{1,2},{2,3},{3,4},{4,5},{5,6},{6,7},{7,8},{8,9},{9,10},{10,1... | collective-permute-start | bytes 196616 | tf_op jit(solution)/shard_map/ppermute | solution.py:32
  994.7 20.4 %collective-permute-start.15 = (bf16[32,1024]{1,0:T(8,128)(2,1)}, bf16[32,1024]{1,0:T(8,128)(2,1)}, u32[]{:S(2)}, u32[]{:S(2)}) collective-permute-start(bf16[32,1024]{1,0:T(8,128)(2,1)} %get-tuple-element.852), channel_id=1, source_target_pairs={{1,0},{2,1},{3,2},{4,3},{5,4},{6,5},{7,6},{8,7},{9,8},{10,9},{11,1... | collective-permute-start | bytes 196616 | tf_op jit(solution)/shard_map/ppermute | solution.py:32
  996.0 24.6 %collective-permute-start.12 = (bf16[32,1024]{1,0:T(8,128)(2,1)}, bf16[32,1024]{1,0:T(8,128)(2,1)}, u32[]{:S(2)}, u32[]{:S(2)}) collective-permute-start(bf16[32,1024]{1,0:T(8,128)(2,1)} %get-tuple-element.819), channel_id=1, source_target_pairs={{0,1},{1,2},{2,3},{3,4},{4,5},{5,6},{6,7},{7,8},{8,9},{9,10},{10,1... | collective-permute-start | bytes 196616 | tf_op jit(solution)/shard_map/ppermute | solution.py:32
  1003.9 16.7 %collective-permute-start.13 = (bf16[32,1024]{1,0:T(8,128)(2,1)}, bf16[32,1024]{1,0:T(8,128)(2,1)}, u32[]{:S(2)}, u32[]{:S(2)}) collective-permute-start(bf16[32,1024]{1,0:T(8,128)(2,1)} %get-tuple-element.820), channel_id=1, source_target_pairs={{1,0},{2,1},{3,2},{4,3},{5,4},{6,5},{7,6},{8,7},{9,8},{10,9},{11,1... | collective-permute-start | bytes 196616 | tf_op jit(solution)/shard_map/ppermute | solution.py:32
  1005.8 22.3 %collective-permute-start.10 = (bf16[32,1024]{1,0:T(8,128)(2,1)}, bf16[32,1024]{1,0:T(8,128)(2,1)S(1)}, u32[]{:S(2)}, u32[]{:S(2)}) collective-permute-start(bf16[32,1024]{1,0:T(8,128)(2,1)} %get-tuple-element.789), channel_id=1, source_target_pairs={{0,1},{1,2},{2,3},{3,4},{4,5},{5,6},{6,7},{7,8},{8,9},{9,10},{10,1... | collective-permute-start | bytes 196616 | tf_op jit(solution)/shard_map/ppermute | solution.py:32
  1013.8 14.3 %collective-permute-start.11 = (bf16[32,1024]{1,0:T(8,128)(2,1)}, bf16[32,1024]{1,0:T(8,128)(2,1)S(1)}, u32[]{:S(2)}, u32[]{:S(2)}) collective-permute-start(bf16[32,1024]{1,0:T(8,128)(2,1)} %get-tuple-element.790), channel_id=1, source_target_pairs={{1,0},{2,1},{3,2},{4,3},{5,4},{6,5},{7,6},{8,7},{9,8},{10,9},{11,1... | collective-permute-start | bytes 196616 | tf_op jit(solution)/shard_map/ppermute | solution.py:32
  1034.3 252.6 %reduce-scatter.9.cloned.1.call-start = ((), (), s32[]{:S(2)}) async-start(), calls=%async_computation.9 | async-start | bytes 4325376 | tf_op jit(solution)/shard_map/reduce_scatter | solution.py:350
  1040.5 386.2 %reduce-scatter.11.cloned.1.call-start = ((), (), s32[]{:S(2)}) async-start(), calls=%async_computation.10 | async-start | bytes 4325376 | tf_op jit(solution)/shard_map/reduce_scatter | solution.py:352
  (174 other events, 1474.4 us)
Sparse Core Ops, SparseCore 0:
  10.9 57.8 all-gather.3
  71.6 55.7 all-gather.5
  130.3 55.2 all-gather.7
  672.3 133.1 reduce-scatter.6
  1034.4 109.9 reduce-scatter.4
  1147.3 139.6 reduce-scatter.8
  1289.9 136.7 reduce-scatter.10
where the time goes:
time: 1450 us; the launch traced here: 1430 us
  local copies, waits for them, and re-layouts  715 us (49%)
  waiting for transfers between devices  306 us (21%)
  blocking collectives  139 us (10%)
  matrix products  114 us (8%)
  other arithmetic  86.8 us (6%)
  starting transfers between devices  54.6 us (4%)
  between operations  17.8 us (1%)
    concatenate x125, local copies, waits for them, and re-layouts, windows(): jnp.concatenate([tiles[shift:shift + count] for shift in range(5)], axis=1)  247 us
    unnamed x434, local copies, waits for them, and re-layouts  174 us
    reduce_scatter x1, waiting for transfers between devices, per_device(): lax.psum_scatter(grad_in_weight, 'seq', scatter_dimension=0, tiled=True)  142 us
    reduce_scatter x1, waiting for transfers between devices, per_device(): lax.psum_scatter(grad_back_weight, 'seq', scatter_dimension=0, tiled=True)  140 us
    slice x10, local copies, waits for them, and re-layouts, unwindow(): parts[:, 16 * shift:16 * shift + 16]  105 us
    unnamed x2, blocking collectives  94.2 us
    all_gather x1, blocking collectives, per_device(): lax.all_gather(w_out, 'seq', axis=0, tiled=True)  45.2 us
  transfers between devices with their start and end apart: 27, of which 3 were waited for; matrix products, arithmetic and copies ran while one was open for 56% of the time, Pallas kernels for 0%

commit v1 on v0

v1 whole, which is shorter than its diff:
```python
import functools
import math

import jax
import jax.numpy as jnp
import numpy as np
from jax import lax
from jax.experimental import pallas as pl
from jax.experimental.pallas import tpu as pltpu
from jax.sharding import PartitionSpec as P

HEAD_DIM = 64
LEVELS = 5
HALO = 32
BLOCK = 64
WINDOW = BLOCK + 2 * HALO
QUAD = 4
QUAD_WIDTH = QUAD * HEAD_DIM
FAR = 1 << 26
SEQ_STEP = 1 << 21
VMEM_LIMIT = 56 * 1024 * 1024

f32 = jnp.float32
bf16 = jnp.bfloat16


class Plan:
    def __init__(self, rows):
        self.rows = rows
        self.counts = [rows >> level for level in range(LEVELS)]
        self.padded = [-(-count // BLOCK) * BLOCK for count in self.counts]
        self.query_at = [sum(self.padded[:level]) for level in range(LEVELS)]
        self.query_rows = sum(self.padded)
        self.key_at = [self.query_at[level] + 2 * HALO * level for level in range(LEVELS)]
        self.key_rows = self.query_rows + 2 * HALO * LEVELS
        self.blocks = [
            (level, part)
            for level in range(LEVELS)
            for part in range(self.padded[level] // BLOCK)
        ]


def dot_nn(a, b):
    return lax.dot_general(a, b, (((1,), (0,)), ((), ())), preferred_element_type=f32)


def dot_nt(a, b):
    return lax.dot_general(a, b, (((1,), (1,)), ((), ())), preferred_element_type=f32)


def dot_tn(a, b):
    return lax.dot_general(a, b, (((0,), (0,)), ((), ())), preferred_element_type=f32)


def spec(count):
    return [pl.BlockSpec(memory_space=pltpu.VMEM)] * count


SCALARS = pl.BlockSpec(memory_space=pltpu.SMEM)


def slot_facts(info, slot, total):
    number = jnp.zeros(slot.shape, jnp.int32)
    for s in range(3):
        number = number + (slot >= info[7 + s]).astype(jnp.int32)
    begin = jnp.where(number == 0, info[4], jnp.where(number == 1, info[5], info[6]))
    length = jnp.where(number == 0, info[1], jnp.where(number == 1, info[2], info[3]))
    inside = (slot >= 0) & (slot < total) & (number < 3)
    return number, slot - begin, length, inside


def tile_codes(info, coarse, level, total, outside):
    number, offset, _, inside = slot_facts(info, coarse << level, total)
    wide = jnp.where(inside, number * SEQ_STEP + (offset >> (level + 4)), outside)
    fine = number * SEQ_STEP + (offset >> (level + 3))
    return wide, fine


def admitted(query_codes, key_codes, level):
    near = jnp.abs(query_codes[0] - key_codes[0]) <= 1
    if level > 0:
        near = near & (jnp.abs(query_codes[1] - key_codes[1]) >= 2)
    return jnp.where(near, 1.0, 0.0)


def live_counts(info, coarse, level, total):
    _, offset, length, inside = slot_facts(info, coarse << level, total)
    span = 1 << level
    return jnp.where(inside, jnp.clip(length - offset, 0, span), 0).astype(f32)


def head_masks(rows):
    lane = lax.broadcasted_iota(jnp.int32, (rows, QUAD_WIDTH), 1) // HEAD_DIM
    return [jnp.where(lane == h, 1.0, 0.0) for h in range(QUAD)]


def spread_heads(block, masks):
    return jnp.concatenate([block * m for m in masks], axis=0)


def gather_heads(stacked, masks):
    rows = stacked.shape[0] // QUAD
    total = stacked[:rows] * masks[0]
    for h in range(1, QUAD):
        total = total + stacked[h * rows : (h + 1) * rows] * masks[h]
    return total


def put(chunks, rows, quad, block):
    for part in range(QUAD_WIDTH // 128):
        chunk = quad * (QUAD_WIDTH // 128) + part
        chunks[chunk, rows, :] = block[:, part * 128 : part * 128 + 128]


def take(chunks, rows, quad):
    first = quad * (QUAD_WIDTH // 128)
    return jnp.concatenate(
        [chunks[first + part, rows, :] for part in range(QUAD_WIDTH // 128)], axis=1
    )


def fill_extended(plan, own, before, after, extended):
    for level in range(LEVELS):
        at, count, mine = plan.key_at[level], plan.counts[level], plan.query_at[level]
        halo = pl.ds(HALO * level, HALO)
        extended[pl.ds(at, HALO), :] = before[halo, :]
        extended[pl.ds(at + HALO, count), :] = own[pl.ds(mine, count), :]
        extended[pl.ds(at + HALO + count, HALO), :] = after[halo, :]
        rest = plan.padded[level] - count
        if rest:
            extended[pl.ds(at + 2 * HALO + count, rest), :] = jnp.zeros(
                (rest, extended.shape[1]), bf16
            )


def project_kernel(plan, total, info, tokens, gain, bias, weight, normed, query, pairs, head, tail):
    rows, width = tokens.shape
    device = info[0]
    values = tokens[...].astype(f32)
    center = values - jnp.mean(values, axis=-1, keepdims=True)
    spread = jnp.mean(center * center, axis=-1, keepdims=True)
    low = (center * lax.rsqrt(spread + 1e-05) * gain[...] + bias[...]).astype(bf16)
    normed[...] = low
    pooled_rows = plan.query_rows - plan.query_at[1]
    row = lax.broadcasted_iota(jnp.int32, (pooled_rows, rows), 0)
    slot = lax.broadcasted_iota(jnp.int32, (pooled_rows, rows), 1)
    first = jnp.zeros((pooled_rows, rows), jnp.int32)
    shift = jnp.zeros((pooled_rows, rows), jnp.int32)
    share = jnp.zeros((pooled_rows, 1), f32)
    row_one = lax.broadcasted_iota(jnp.int32, (pooled_rows, 1), 0)
    for level in range(1, LEVELS):
        at = plan.query_at[level] - plan.query_at[1]
        first = jnp.where(row >= at, at, first)
        shift = jnp.where(row >= at, level, shift)
        share = jnp.where(row_one >= at, 0.5**level, share)
    pool = jnp.where((slot >> shift) == row - first, 1.0, 0.0).astype(bf16)
    places = device * rows + lax.broadcasted_iota(jnp.int32, (rows, QUAD_WIDTH), 0)
    live = live_counts(info, places, 0, total)
    lanes = QUAD_WIDTH
    for part in range(3 * width // lanes):
        columns = pl.ds(part * lanes, lanes)
        block = dot_nn(low, weight[:, columns]).astype(bf16)
        if part * lanes >= 2 * width:
            block = (block.astype(f32) * live).astype(bf16)
        pooled = dot_nn(pool, block)
        if part * lanes < 2 * width:
            pooled = pooled * share
        if part * lanes < width:
            scale = 1.0 / math.sqrt(HEAD_DIM)
            query[pl.ds(0, rows), columns] = (block.astype(f32) * scale).astype(bf16)
            query[pl.ds(rows, pooled_rows), columns] = (pooled * scale).astype(bf16)
        else:
            there = pl.ds(part * lanes - width, lanes)
            pairs[pl.ds(0, rows), there] = block
            pairs[pl.ds(rows, pooled_rows), there] = pooled.astype(bf16)
    for level in range(LEVELS):
        at, count = plan.query_at[level], plan.counts[level]
        halo = pl.ds(HALO * level, HALO)
        head[halo, :] = pairs[pl.ds(at, HALO), :]
        tail[halo, :] = pairs[pl.ds(at + count - HALO, HALO), :]


def project(plan, total, info, tokens, gain, bias, weight):
    rows, width = tokens.shape
    halo = LEVELS * HALO
    return pl.pallas_call(
        functools.partial(project_kernel, plan, total),
        out_shape=(
            jax.ShapeDtypeStruct((rows, width), bf16),
            jax.ShapeDtypeStruct((plan.query_rows, width), bf16),
            jax.ShapeDtypeStruct((plan.query_rows, 2 * width), bf16),
            jax.ShapeDtypeStruct((halo, 2 * width), bf16),
            jax.ShapeDtypeStruct((halo, 2 * width), bf16),
        ),
        in_specs=[SCALARS] + spec(4),
        out_specs=tuple(spec(5)),
        compiler_params=pltpu.CompilerParams(vmem_limit_bytes=VMEM_LIMIT),
        name="project",
    )(info, tokens, gain, bias, weight)


def attend_kernel(
    plan, total, info, query, pairs, before, after, attended, mixed, scale, extended, numer, denom
):
    rows = plan.rows
    width = query.shape[1]
    device = info[0]
    fill_extended(plan, pairs, before, after, extended)
    masks = head_masks(BLOCK)
    low_masks = [m.astype(bf16) for m in masks]
    for level, part in plan.blocks:
        count = plan.counts[level]
        at = plan.query_at[level] + BLOCK * part
        window = plan.key_at[level] + BLOCK * part
        first = device * count + BLOCK * part
        row = first + lax.broadcasted_iota(jnp.int32, (BLOCK, WINDOW), 0)
        column = first - HALO + lax.broadcasted_iota(jnp.int32, (BLOCK, WINDOW), 1)
        allowed = admitted(
            tile_codes(info, row, level, total, FAR),
            tile_codes(info, column, level, total, -FAR),
            level,
        )
        allowed = jnp.concatenate([allowed] * QUAD, axis=0) > 0.0
        key_row = first - HALO + lax.broadcasted_iota(jnp.int32, (WINDOW, 128), 0)
        counts = live_counts(info, key_row, level, total).astype(bf16)
        counts = jnp.concatenate([counts] * (QUAD_WIDTH // 128), axis=1)
        for quad in range(width // QUAD_WIDTH):
            columns = pl.ds(quad * QUAD_WIDTH, QUAD_WIDTH)
            value_columns = pl.ds(width + quad * QUAD_WIDTH, QUAD_WIDTH)
            q = spread_heads(query[pl.ds(at, BLOCK), columns], low_masks)
            k = extended[pl.ds(window, WINDOW), columns]
            v = extended[pl.ds(window, WINDOW), value_columns]
            weight = jnp.where(allowed, jnp.exp(dot_nt(q, k)), 0.0).astype(bf16)
            put(numer, pl.ds(at, BLOCK), quad, gather_heads(dot_nn(weight, v), masks))
            put(denom, pl.ds(at, BLOCK), quad, gather_heads(dot_nn(weight, counts), masks))
    for sums in (numer, denom):
        for level in range(LEVELS - 1, 0, -1):
            count = plan.counts[level]
            for chunk in range(width // 128):
                upper = sums[chunk, pl.ds(plan.query_at[level], count), :]
                for parity in range(2):
                    there = pl.ds(plan.query_at[level - 1] + parity, count, stride=2)
                    sums[chunk, there, :] = sums[chunk, there, :] + upper
    places = device * rows + lax.broadcasted_iota(jnp.int32, (rows, 128), 0)
    live = live_counts(info, places, 0, total)
    for chunk in range(width // 128):
        lanes = pl.ds(chunk * 128, 128)
        factor = live / (denom[chunk, pl.ds(0, rows), :] + 1.0 - live)
        value = numer[chunk, pl.ds(0, rows), :] * factor
        scale[:, lanes] = factor
        mixed[:, lanes] = value
        attended[:, lanes] = value.astype(bf16)


def attend(plan, total, info, query, pairs, before, after):
    rows, width = plan.rows, query.shape[1]
    return pl.pallas_call(
        functools.partial(attend_kernel, plan, total),
        out_shape=(
            jax.ShapeDtypeStruct((rows, width), bf16),
            jax.ShapeDtypeStruct((rows, width), f32),
            jax.ShapeDtypeStruct((rows, width), f32),
        ),
        in_specs=[SCALARS] + spec(4),
        out_specs=tuple(spec(3)),
        scratch_shapes=[
            pltpu.VMEM((plan.key_rows, 2 * width), bf16),
            pltpu.VMEM((width // 128, plan.query_rows, 128), f32),
            pltpu.VMEM((width // 128, plan.query_rows, 128), f32),
        ],
        compiler_params=pltpu.CompilerParams(vmem_limit_bytes=VMEM_LIMIT),
        name="attend",
    )(info, query, pairs, before, after)


def attend_back_kernel(
    plan,
    total,
    info,
    query,
    pairs,
    before,
    after,
    grad_mixed,
    scale,
    mixed,
    grad_query,
    grad_pairs,
    grad_head,
    grad_tail,
    extended,
    grad_extended,
    grad_numer,
    grad_denom,
):
    rows = plan.rows
    width = query.shape[1]
    device = info[0]
    fill_extended(plan, pairs, before, after, extended)
    grad_extended[...] = jnp.zeros(grad_extended.shape, f32)
    own = pl.ds(0, rows)
    for chunk in range(width // 128):
        lanes = pl.ds(chunk * 128, 128)
        value = grad_mixed[:, lanes] * scale[:, lanes]
        grad_numer[chunk, own, :] = value
        grad_denom[chunk, own, :] = -(value * mixed[:, lanes])
        for sums in (grad_numer, grad_denom):
            for level in range(1, LEVELS):
                count, at = plan.counts[level], plan.query_at[level]
                even = sums[chunk, pl.ds(plan.query_at[level - 1], count, stride=2), :]
                odd = sums[chunk, pl.ds(plan.query_at[level - 1] + 1, count, stride=2), :]
                sums[chunk, pl.ds(at, count), :] = even + odd
                rest = plan.padded[level] - count
                if rest:
                    sums[chunk, pl.ds(at + count, rest), :] = jnp.zeros((rest, 128), f32)
    masks = head_masks(BLOCK)
    low_masks = [m.astype(bf16) for m in masks]
    for level, part in plan.blocks:
        count = plan.counts[level]
        at = plan.query_at[level] + BLOCK * part
        window = plan.key_at[level] + BLOCK * part
        first = device * count + BLOCK * part
        key_row = first - HALO + lax.broadcasted_iota(jnp.int32, (WINDOW, 128), 0)
        lane = lax.broadcasted_iota(jnp.int32, (WINDOW, 128), 1)
        row = first + (lane & (BLOCK - 1))
        allowed = admitted(
            tile_codes(info, row, level, total, FAR),
            tile_codes(info, key_row, level, total, -FAR),
            level,
        )
        allowed = jnp.concatenate([allowed] * (QUAD * BLOCK // 128), axis=1) > 0.0
        counts = live_counts(info, key_row, level, total).astype(bf16)
        for quad in range(width // QUAD_WIDTH):
            columns = pl.ds(quad * QUAD_WIDTH, QUAD_WIDTH)
            value_columns = pl.ds(width + quad * QUAD_WIDTH, QUAD_WIDTH)
            here = pl.ds(at, BLOCK)
            there = pl.ds(window, WINDOW)
            q = spread_heads(query[here, columns], low_masks)
            g = spread_heads(take(grad_numer, here, quad).astype(bf16), low_masks)
            d = spread_heads(take(grad_denom, here, quad).astype(bf16), low_masks)
            k = extended[there, columns]
            v = extended[there, value_columns]
            value_and_count = jnp.concatenate([v] + [counts] * (QUAD_WIDTH // 128), axis=1)
            weight = jnp.where(allowed, jnp.exp(dot_nt(k, q)), 0.0)
            probs = weight.astype(bf16)
            grad_probs = dot_nt(value_and_count, jnp.concatenate([g, d], axis=1))
            grad_score = (grad_probs * weight).astype(bf16)
            grad_query[here, columns] = gather_heads(dot_tn(grad_score, k), masks) * (
                1.0 / math.sqrt(HEAD_DIM)
            )
            grad_extended[there, columns] += dot_nn(grad_score, q)
            grad_extended[there, value_columns] += dot_nn(probs, g)
    for level in range(LEVELS):
        at, count, mine = plan.key_at[level], plan.counts[level], plan.query_at[level]
        halo = pl.ds(HALO * level, HALO)
        grad_head[halo, :] = grad_extended[pl.ds(at, HALO), :].astype(bf16)
        grad_tail[halo, :] = grad_extended[pl.ds(at + HALO + count, HALO), :].astype(bf16)
        grad_pairs[pl.ds(mine, count), :] = grad_extended[pl.ds(at + HALO, count), :]


def attend_back(plan, total, info, query, pairs, before, after, grad_mixed, scale, mixed):
    width = query.shape[1]
    halo = LEVELS * HALO
    return pl.pallas_call(
        functools.partial(attend_back_kernel, plan, total),
        out_shape=(
            jax.ShapeDtypeStruct((plan.query_rows, width), f32),
            jax.ShapeDtypeStruct((plan.query_rows, 2 * width), f32),
            jax.ShapeDtypeStruct((halo, 2 * width), bf16),
            jax.ShapeDtypeStruct((halo, 2 * width), bf16),
        ),
        in_specs=[SCALARS] + spec(7),
        out_specs=tuple(spec(4)),
        scratch_shapes=[
            pltpu.VMEM((plan.key_rows, 2 * width), bf16),
            pltpu.VMEM((plan.key_rows, 2 * width), f32),
            pltpu.VMEM((width // 128, plan.query_rows, 128), f32),
            pltpu.VMEM((width // 128, plan.query_rows, 128), f32),
        ],
        compiler_params=pltpu.CompilerParams(vmem_limit_bytes=VMEM_LIMIT),
        name="attend_back",
    )(info, query, pairs, before, after, grad_mixed, scale, mixed)


def combine_kernel(plan, total, info, grad_query, grad_pairs, from_below, from_above, joined, work):
    rows = plan.rows
    width = grad_query.shape[1]
    device = info[0]
    places = device * rows + lax.broadcasted_iota(jnp.int32, (rows, 128), 0)
    live = live_counts(info, places, 0, total)
    for chunk in range(3 * width // 128):
        if chunk * 128 < width:
            work[chunk] = grad_query[:, pl.ds(chunk * 128, 128)]
        else:
            lanes = pl.ds(chunk * 128 - width, 128)
            work[chunk] = grad_pairs[:, lanes]
            for level in range(LEVELS):
                at, count = plan.query_at[level], plan.counts[level]
                halo = pl.ds(HALO * level, HALO)
                work[chunk, pl.ds(at, HALO), :] += from_below[halo, lanes].astype(f32)
                last = pl.ds(at + count - HALO, HALO)
                work[chunk, last, :] += from_above[halo, lanes].astype(f32)
        for level in range(LEVELS - 1, 0, -1):
            count = plan.counts[level]
            upper = work[chunk, pl.ds(plan.query_at[level], count), :]
            if chunk * 128 < 2 * width:
                upper = upper * 0.5
            for parity in range(2):
                there = pl.ds(plan.query_at[level - 1] + parity, count, stride=2)
                work[chunk, there, :] = work[chunk, there, :] + upper
        value = work[chunk, pl.ds(0, rows), :]
        if chunk * 128 >= 2 * width:
            value = value * live
        joined[:, pl.ds(chunk * 128, 128)] = value.astype(bf16)


def combine(plan, total, info, grad_query, grad_pairs, from_below, from_above):
    width = grad_query.shape[1]
    return pl.pallas_call(
        functools.partial(combine_kernel, plan, total),
        out_shape=jax.ShapeDtypeStruct((plan.rows, 3 * width), bf16),
        in_specs=[SCALARS] + spec(4),
        out_specs=spec(1)[0],
        scratch_shapes=[pltpu.VMEM((3 * width // 128, plan.query_rows, 128), f32)],
        compiler_params=pltpu.CompilerParams(vmem_limit_bytes=VMEM_LIMIT),
        name="combine",
    )(info, grad_query, grad_pairs, from_below, from_above)


def layer_norm(values, gain, shift):
    center = values - jnp.mean(values, axis=-1, keepdims=True)
    spread = jnp.mean(center * center, axis=-1, keepdims=True)
    return center * lax.rsqrt(spread + 1e-05) * gain + shift


def gelu_exact(values):
    return jax.nn.gelu(values, approximate=False)


def exchange(to_above, to_below):
    count = lax.axis_size("seq")
    up = [(i, i + 1) for i in range(count - 1)]
    down = [(i + 1, i) for i in range(count - 1)]
    return lax.ppermute(to_above, "seq", up), lax.ppermute(to_below, "seq", down)


def per_device(
    lengths,
    tokens,
    ln1_gain,
    ln1_bias,
    w_qkv,
    w_out,
    out_bias,
    ln2_gain,
    ln2_bias,
    w_in,
    in_bias,
    w_back,
    back_bias,
    cotangent,
):
    devices = lax.axis_size("seq")
    device = lax.axis_index("seq")
    rows = tokens.shape[0]
    total = rows * devices
    plan = Plan(rows)
    padded = (lengths + 15) // 16 * 16
    ends = jnp.cumsum(padded, dtype=jnp.int32)
    info = jnp.concatenate([device[None].astype(jnp.int32), lengths, ends - padded, ends])
    (
        gain_one,
        bias_one,
        joint_weight,
        out_weight,
        out_shift,
        gain_two,
        bias_two,
        in_weight,
        in_shift,
        back_weight,
        back_shift,
    ) = (
        lax.all_gather(item, "seq", axis=0, tiled=True)
        for item in (
            ln1_gain,
            ln1_bias,
            w_qkv,
            w_out,
            out_bias,
            ln2_gain,
            ln2_bias,
            w_in,
            in_bias,
            w_back,
            back_bias,
        )
    )
    gain_one, bias_one = gain_one.astype(f32), bias_one.astype(f32)
    normed_low, query, pairs, head, tail = project(
        plan, total, info, tokens, gain_one[None], bias_one[None], joint_weight
    )
    before, after = exchange(tail, head)
    attended, mixed, scale = attend(plan, total, info, query, pairs, before, after)
    inputs = tokens.astype(f32)
    branch = jnp.dot(attended, out_weight, preferred_element_type=f32) + out_shift.astype(f32)
    resid = inputs + branch
    normed_two, norm_two_pull = jax.vjp(
        layer_norm, resid, gain_two.astype(f32), bias_two.astype(f32)
    )
    normed_two_low = normed_two.astype(bf16)
    inner = jnp.dot(normed_two_low, in_weight, preferred_element_type=f32) + in_shift.astype(f32)
    active, gelu_pull = jax.vjp(gelu_exact, inner)
    active_low = active.astype(bf16)
    outer = jnp.dot(active_low, back_weight, preferred_element_type=f32) + back_shift.astype(f32)
    result = (resid + outer).astype(bf16)
    grad_out = cotangent.astype(f32)
    grad_back_shift = jnp.sum(grad_out, axis=0)
    grad_back_weight = jnp.einsum("rf,rd->fd", active_low, cotangent, preferred_element_type=f32)
    grad_active = jnp.dot(cotangent, back_weight.T, preferred_element_type=f32)
    grad_inner = gelu_pull(grad_active)[0].astype(bf16)
    grad_in_shift = jnp.sum(grad_inner.astype(f32), axis=0)
    grad_in_weight = jnp.einsum("rd,rf->df", normed_two_low, grad_inner, preferred_element_type=f32)
    grad_normed_two = jnp.dot(grad_inner, in_weight.T, preferred_element_type=f32)
    grad_resid_part, grad_gain_two, grad_bias_two = norm_two_pull(grad_normed_two)
    grad_resid = grad_out + grad_resid_part
    grad_branch = grad_resid.astype(bf16)
    grad_out_shift = jnp.sum(grad_branch.astype(f32), axis=0)
    grad_out_weight = jnp.einsum("rd,re->de", attended, grad_branch, preferred_element_type=f32)
    grad_mixed = jnp.dot(grad_branch, out_weight.T, preferred_element_type=f32)
    grad_query, grad_pairs, grad_head, grad_tail = attend_back(
        plan, total, info, query, pairs, before, after, grad_mixed, scale, mixed
    )
    from_below, from_above = exchange(grad_tail, grad_head)
    grad_joined = combine(plan, total, info, grad_query, grad_pairs, from_below, from_above)
    grad_joint_weight = jnp.einsum(
        "rd,rf->df", normed_low, grad_joined, preferred_element_type=f32
    )
    grad_normed = jnp.dot(grad_joined, joint_weight.T, preferred_element_type=f32)
    _, norm_one_pull = jax.vjp(layer_norm, inputs, gain_one, bias_one)
    grad_input_part, grad_gain_one, grad_bias_one = norm_one_pull(grad_normed)
    grad_tokens = grad_resid + grad_input_part
    return (result, grad_tokens) + tuple(
        lax.psum_scatter(item, "seq", scatter_dimension=0, tiled=True)
        for item in (
            grad_gain_one,
            grad_bias_one,
            grad_joint_weight,
            grad_out_weight,
            grad_out_shift,
            grad_gain_two,
            grad_bias_two,
            grad_in_weight,
            grad_in_shift,
            grad_back_weight,
            grad_back_shift,
        )
    )


def solution(mesh):
    flat, wide = P("seq"), P("seq", None)
    weights = (flat, flat, wide, wide, flat, flat, flat, wide, flat, wide, flat)
    return jax.shard_map(
        per_device,
        mesh=mesh,
        in_specs=(P(), wide) + weights + (wide,),
        out_specs=(wide, wide) + weights,
        check_vma=False,
    )
```

time: 1450 us -> 743 us (0.51)
  local copies, waits for them, and re-layouts: 715 us -> 24.6 us
  waiting for transfers between devices: 306 us -> 457 us
  other arithmetic: 86.8 us -> 13.2 us
  matrix products: 114 us -> 47.6 us
  starting transfers between devices: 54.6 us -> 7.66 us
  Pallas kernels: 0 us -> 41.1 us
    concatenate x125 -> x0, local copies, waits for them, and re-layouts: 247 us -> none  [windows(): jnp.concatenate([tiles[shift:shift + count] for shift in range(5)], axis=1)]
    unnamed x434 -> x57, local copies, waits for them, and re-layouts: 174 us -> 21.5 us
    slice x43 -> x0, local copies, waits for them, and re-layouts: 130 us -> none  [the longest x10 105 us: unwindow(): parts[:, 16 * shift:16 * shift + 16]]
    reduce_scatter x4, waiting for transfers between devices: 304 us -> 402 us  [per_device(): lax.psum_scatter(item, 'seq', scatter_dimension=0, tiled=True)]
    dot_general x46 -> x10, matrix products: 109 us -> 42.7 us  [the longest x1 14.2 us: per_device(): grad_active = jnp.dot(cotangent, back_weight.T, preferred_element_type=f32)]
    reshape x40 -> x0, local copies, waits for them, and re-layouts: 60.6 us -> none  [the longest x10 23.5 us: per_device(): numer_sum = numer_sum + jnp.repeat(numer, span, axis=0)]
    all_gather x3, waiting for transfers between devices: 0.02 us -> 49.1 us  [per_device(): lax.all_gather(item, 'seq', axis=0, tiled=True)]
    ppermute x20 -> x4, starting transfers between devices: 54.3 us -> 6.92 us  [the longest x2 4.34 us: exchange(): lax.ppermute(to_above, 'seq', up)]
  transfers between devices with their start and end apart: 27 -> 11, of which waited for: 3 -> 8; matrix products, arithmetic and copies ran while one was open for 56% -> 8% of each run, Pallas kernels for 0% -> 6%
where the time goes in v1:
time: 743 us; the launch traced here: 737 us
  waiting for transfers between devices  457 us (62%)
  blocking collectives  132 us (18%)
  matrix products  47.6 us (6%)
  Pallas kernels  41.1 us (6%)
  local copies, waits for them, and re-layouts  24.6 us (3%)
  between operations  14.7 us (2%)
  other arithmetic  13.2 us (2%)
  starting transfers between devices  7.66 us (1%)
    reduce_scatter x4, waiting for transfers between devices, per_device(): lax.psum_scatter(item, 'seq', scatter_dimension=0, tiled=True)  402 us
    unnamed x2, blocking collectives  87.3 us
    all_gather x3, waiting for transfers between devices, per_device(): lax.all_gather(item, 'seq', axis=0, tiled=True)  49.1 us
    all_gather x1, blocking collectives, per_device(): lax.all_gather(item, 'seq', axis=0, tiled=True)  44.4 us
    unnamed x57, local copies, waits for them, and re-layouts  21.5 us
    pallas_call x1, Pallas kernels, attend_back(): pl.pallas_call(functools.partial(attend_back_kernel, plan, total), out_sh...  17.5 us
  transfers between devices with their start and end apart: 11, of which 8 were waited for; matrix products, arithmetic and copies ran while one was open for 8% of the time, Pallas kernels for 6%

profile of v1, /device:TPU:0, one launch (start us, length us, event | category | flops | bytes accessed | tf_op | source)
XLA Modules:
  0.0 737.3 jit_solution(9867689729510447447)
XLA Ops:
  15.4 42.2 %all-reduce.15 = (bf16[512]{0:T(512)(128)(2,1)S(1)}, bf16[512]{0:T(512)(128)(2,1)S(1)}, bf16[512]{0:T(512)(128)(2,1)S(1)}, bf16[512]{0:T(512)(128)(2,1)S(1)}, bf...) all-reduce(bf16[512]{0:T(512)(128)(2,1)S(1)} %dynamic-update-slice,, ...), channel_id=1, replica_groups=mesh['seq'=32] {'seq'}, use_global_device_ids=true, to_apply=%add | all-reduce | flops 5120 | bytes 20480
  61.6 7.0 all-gather.4.cloned.1.call-done.weight
  68.6 5.7 project.1
  74.2 2.2 collective-permute-start
  80.3 44.4 %all_gather.36 = bf16[512,512]{1,0:T(8,128)(2,1)S(1)} all-gather(bf16[16,512]{1,0:T(8,128)(2,1)S(1)} %copy-done.15), channel_id=1, replica_groups=mesh['seq'=32] {'seq'}, dimensions={0}, use_global_device_ids=true | all-gather | bytes 540672 | tf_op jit(solution)/shard_map/all_gather | solution.py:484
  125.6 11.9 %attend.1 = (bf16[512,512]{1,0:T(8,128)(2,1)}, f32[512,512]{1,0:T(8,128)}, f32[512,512]{1,0:T(8,128)}) custom-call(s32[10]{0:T(128)} %pad_add_fusion.info, bf16[1024,512]{1,0:T(8,128)(2,1)} %get-tuple-element.25.query, bf16[1024,1024]{1,0:T(8,128)(2,1)} %get-tuple-element.26.pairs, bf16[160,1024]{1,0:T(8,128)(2,1)} %copy-done.9, bf16[160,1024]{1,0:T(8,128)(2,1)} %copy-done.10), custom_call_target="tpu_custom_call" | custom-call | tf_op jit(solution)/shard_map/attend/pallas_call | solution.py:257
  137.4 1.6 fusion.26
  139.2 4.9 fusion.22
  144.2 42.1 %all-gather.8.cloned.1.call-done = bf16[2048,512]{1,0:T(8,128)(2,1)} async-done(((bf16[64,512]{1,0:T(8,128)(2,1)}), bf16[2048,512]{1,0:T(8,128)(2,1)}) %all-gather.8.cloned.1.call-update) | async-done | bytes 2097168 | tf_op jit(solution)/shard_map/all_gather | solution.py:484
  186.3 14.2 %convert_reduce_fusion = (f32[2048]{0:T(1024)S(1)}, bf16[512,2048]{1,0:T(8,128)(2,1)S(1)}, f32[512,2048]{1,0:T(8,128)}) fusion(f32[512,2048]{1,0:T(8,128)} %fusion.22, f32[2048]{0:T(1024)S(1)} %convert_element_type.52, bf16[512,512]{1,0:T(8,128)(2,1)S(1)} %copy-done.4, bf16[2048,512]{1,0:T(8,128)(2,1)} %all-gather.8.cloned.1.call-done), kind=kOutput, calls=%fused_computation.2 | convolution fusion | flops 1152382976 | bytes 13123584 | tf_op jit(solution)/shard_map/dot_general | solution.py:520
  200.5 2.3 fusion.28
  202.7 1.6 copy.39
  207.9 1.6 fusion.31
  209.7 2.7 fusion.29.grad_mixed
  212.4 17.5 %attend_back.1 = (f32[1024,512]{1,0:T(8,128)}, f32[1024,1024]{1,0:T(8,128)}, bf16[160,1024]{1,0:T(8,128)(2,1)}, bf16[160,1024]{1,0:T(8,128)(2,1)}) custom-call(s32[10]{0:T(128)} %pad_add_fusion.info, bf16[1024,512]{1,0:T(8,128)(2,1)} %get-tuple-element.25.query, bf16[1024,1024]{1,0:T(8,128)(2,1)} %get-tuple-element.26.pairs, bf16[160,1024]{1,0:T(8,128)(2,1)} %copy-done.9, ...), custom_call_target="tpu_custom_call" | custom-call | tf_op jit(solution)/shard_map/attend_back/pallas_call | solution.py:364
  229.9 2.2 collective-permute-start.2
  233.5 3.1 collective-permute-done.3.from_above
  237.3 6.1 combine.1
  243.4 4.1 fusion.30
  247.8 4.9 fusion.21
  252.8 4.6 multiply_convert_fusion
  258.7 3.2 fusion.32
  262.1 4.3 fusion.11
  266.4 2.0 copy.43
  268.5 3.9 fusion.27
  272.3 1.6 copy.40
  276.1 45.0 %all-reduce.14 = (f32[512]{0:T(512)S(1)}, f32[512]{0:T(512)S(1)}, f32[512]{0:T(512)S(1)}, f32[512]{0:T(512)S(1)}, f32[512]{0:T(512)S(1)}, /*index=5*/f32[2048]{0:T(1024)S(1)}, f32[512]{0:T(512)S(1)}) all-reduce(f32[512]{0:T(512)S(1)} %get-tuple-element.65, f32[512]{0:T(512)S(1)} %get-tuple-element.96, ...), channel_id=2, replica_groups=mesh['seq'=32] {'seq'}, use_global_device_ids=true, to_apply=%region_10.11.clone | all-reduce | flops 5120 | bytes 40960
  324.6 2.5 copy.44
  327.8 15.8 %reduce-scatter.7.cloned.1.call-done = f32[16,512]{1,0:T(8,128)} async-done(((f32[512,512]{1,0:T(8,128)}), f32[16,512]{1,0:T(8,128)}) %reduce-scatter.7.cloned.1.call-update) | async-done | bytes 32784 | tf_op jit(solution)/shard_map/reduce_scatter | solution.py:544
  343.5 104.2 %reduce-scatter.5.cloned.1.call-done = f32[16,1536]{1,0:T(8,128)} async-done(((f32[512,1536]{1,0:T(8,128)}), f32[16,1536]{1,0:T(8,128)}) %reduce-scatter.5.cloned.1.call-update) | async-done | bytes 98320 | tf_op jit(solution)/shard_map/reduce_scatter | solution.py:544
  447.7 142.7 %reduce-scatter.9.cloned.1.call-done = f32[16,2048]{1,0:T(8,128)} async-done(((f32[512,2048]{1,0:T(8,128)}), f32[16,2048]{1,0:T(8,128)}) %reduce-scatter.9.cloned.1.call-update) | async-done | bytes 131088 | tf_op jit(solution)/shard_map/reduce_scatter | solution.py:544
  590.5 139.7 %reduce-scatter.11.cloned.1.call-done = f32[64,512]{1,0:T(8,128)} async-done(((f32[2048,512]{1,0:T(8,128)}), f32[64,512]{1,0:T(8,128)}) %reduce-scatter.11.cloned.1.call-update) | async-done | bytes 131088 | tf_op jit(solution)/shard_map/reduce_scatter | solution.py:544
  (101 shorter events, 31.2 us)
Async XLA Ops:
  7.2 73.1 %copy-start.15 = (bf16[16,512]{1,0:T(8,128)(2,1)S(1)}, bf16[16,512]{1,0:T(8,128)(2,1)}, u32[]{:S(2)}) copy-start(bf16[16,512]{1,0:T(8,128)(2,1)} %param.19) | copy-start | bytes 49156
  7.2 61.4 %all-gather.4.cloned.1.call-start = ((), (), s32[]{:S(2)}) async-start(), calls=%async_computation.4 | async-start | bytes 1622016 | tf_op jit(solution)/shard_map/all_gather | solution.py:484
  7.9 131.3 %all-gather.6.cloned.1.call-start = ((), (), s32[]{:S(2)}) async-start(), calls=%async_computation.5 | async-start | bytes 2162688 | tf_op jit(solution)/shard_map/all_gather | solution.py:484
  8.7 177.6 %all-gather.8.cloned.1.call-start = ((), (), s32[]{:S(2)}) async-start(), calls=%async_computation.6 | async-start | bytes 2162688 | tf_op jit(solution)/shard_map/all_gather | solution.py:484
  9.4 334.1 %reduce-scatter.7.cloned.1.call-start = ((), (), s32[]{:S(2)}) async-start(), calls=%async_computation.8 | async-start | bytes 1081344 | tf_op jit(solution)/shard_map/reduce_scatter | solution.py:544
  74.2 50.5 %collective-permute-start = (bf16[160,1024]{1,0:T(8,128)(2,1)}, bf16[160,1024]{1,0:T(8,128)(2,1)S(1)}, u32[]{:S(2)}, u32[]{:S(2)}) collective-permute-start(bf16[160,1024]{1,0:T(8,128)(2,1)} %get-tuple-element.27), channel_id=1, source_target_pairs={{0,1},{1,2},{2,3},{3,4},{4,5},{5,6},{6,7},{7,8},{8,9},{9,10},{10,1... | collective-permute-start | bytes 983048 | tf_op jit(solution)/shard_map/ppermute | solution.py:444
  76.4 48.3 %collective-permute-start.1 = (bf16[160,1024]{1,0:T(8,128)(2,1)}, bf16[160,1024]{1,0:T(8,128)(2,1)S(1)}, u32[]{:S(2)}, u32[]{:S(2)}) collective-permute-start(bf16[160,1024]{1,0:T(8,128)(2,1)} %get-tuple-element.28), channel_id=1, source_target_pairs={{1,0},{2,1},{3,2},{4,3},{5,4},{6,5},{7,6},{8,7},{9,8},{10,9},{11,1... | collective-permute-start | bytes 983048 | tf_op jit(solution)/shard_map/ppermute | solution.py:444
  124.7 19.5 %copy-start.2 = (bf16[512,512]{1,0:T(8,128)(2,1)}, bf16[512,512]{1,0:T(8,128)(2,1)S(1)}, u32[]{:S(2)}) copy-start(bf16[512,512]{1,0:T(8,128)(2,1)S(1)} %all_gather.36) | copy-start | bytes 1572868
  124.7 0.8 copy-start.9
  124.7 0.9 copy-start.10
  139.0 47.3 %copy-start.4 = (bf16[512,512]{1,0:T(8,128)(2,1)S(1)}, bf16[512,512]{1,0:T(8,128)(2,1)}, u32[]{:S(2)}) copy-start(bf16[512,512]{1,0:T(8,128)(2,1)} %param.27) | copy-start | bytes 1572868
  186.3 14.2 %copy-start.7 = (bf16[512,2048]{1,0:T(8,128)(2,1)S(1)}, bf16[512,2048]{1,0:T(8,128)(2,1)}, u32[]{:S(2)}) copy-start(bf16[512,2048]{1,0:T(8,128)(2,1)} %all-gather.6.cloned.1.call-done) | copy-start | bytes 6291460
  200.5 2.3 copy-start.8
  204.3 1.0 copy-start.1
  204.3 3.6 copy-start.6
  207.1 0.8 copy-start.3
  209.5 238.2 %reduce-scatter.5.cloned.1.call-start = ((), (), s32[]{:S(2)}) async-start(), calls=%async_computation.7 | async-start | bytes 3244032 | tf_op jit(solution)/shard_map/reduce_scatter | solution.py:544
  229.9 3.6 collective-permute-start.2
  232.0 4.5 collective-permute-start.3
  233.5 3.1 copy-start.12
  236.5 0.7 copy-start.13
  237.3 6.1 copy-start.11
  247.5 343.0 %reduce-scatter.9.cloned.1.call-start = ((), (), s32[]{:S(2)}) async-start(), calls=%async_computation.9 | async-start | bytes 4325376 | tf_op jit(solution)/shard_map/reduce_scatter | solution.py:544
  252.7 477.4 %reduce-scatter.11.cloned.1.call-start = ((), (), s32[]{:S(2)}) async-start(), calls=%async_computation.10 | async-start | bytes 4325376 | tf_op jit(solution)/shard_map/reduce_scatter | solution.py:544
  252.8 5.9 copy-start.5
  257.3 1.3 copy-start
  268.5 5.4 copy-start.14
Sparse Core Ops, SparseCore 0:
  10.9 57.6 all-gather.3
  71.4 56.6 all-gather.5
  131.0 55.1 all-gather.7
  209.6 133.8 reduce-scatter.6
  350.3 97.4 reduce-scatter.4
  450.5 139.8 reduce-scatter.8
  593.4 136.6 reduce-scatter.10

commit v2 on v1

--- a/solution.py
+++ b/solution.py
@@ -16,6 +16,8 @@
 WINDOW = BLOCK + 2 * HALO
 QUAD = 4
 QUAD_WIDTH = QUAD * HEAD_DIM
+PIECES = 4
+BLOCKS = 32
 FAR = 1 << 26
 SEQ_STEP = 1 << 21
 VMEM_LIMIT = 56 * 1024 * 1024
@@ -133,13 +135,86 @@
             )
 
 
-def project_kernel(plan, total, info, tokens, gain, bias, weight, normed, query, pairs, head, tail):
+def ln_stats(values):
+    center = values - jnp.mean(values, axis=-1, keepdims=True)
+    spread = jnp.mean(center * center, axis=-1, keepdims=True)
+    return center, lax.rsqrt(spread + 1e-05)
+
+
+def ln_back(grad, center, rstd, gain):
+    hat = center * rstd
+    scaled = grad * gain
+    mean_one = jnp.mean(scaled, axis=-1, keepdims=True)
+    mean_two = jnp.mean(scaled * hat, axis=-1, keepdims=True)
+    return rstd * (scaled - mean_one - hat * mean_two), grad * hat
+
+
+def column_sum(values):
+    return jnp.sum(values, axis=0, keepdims=True)
+
+
+def unpack_vectors(table, wide):
+    blocks, lanes = table.shape
+
+    def one(first, each):
+        length = blocks * each
+        source = lax.broadcasted_iota(jnp.int32, (lanes, length), 0)
+        target = lax.broadcasted_iota(jnp.int32, (lanes, length), 1)
+        pick = jnp.where(source == first + (target & (each - 1)), 1.0, 0.0).astype(bf16)
+        spreaded = dot_nn(table, pick)
+        block = lax.broadcasted_iota(jnp.int32, (blocks, length), 0)
+        lane = lax.broadcasted_iota(jnp.int32, (blocks, length), 1)
+        return column_sum(jnp.where(lane // each == block, spreaded, 0.0))
+
+    size = wide // 4
+    return [one(k * size, size) for k in range(6)], one(6 * size, wide)
+
+
+def pack_vectors(vectors, last, blocks, lanes):
+    size = last.shape[1] // blocks // 4
+
+    def one(row, first, each):
+        length = blocks * each
+        source = lax.broadcasted_iota(jnp.int32, (length, lanes), 0)
+        target = lax.broadcasted_iota(jnp.int32, (length, lanes), 1)
+        pick = jnp.where(target == first + (source & (each - 1)), 1.0, 0.0).astype(bf16)
+        block = lax.broadcasted_iota(jnp.int32, (blocks, length), 0)
+        lane = lax.broadcasted_iota(jnp.int32, (blocks, length), 1)
+        spreaded = jnp.where(lane // each == block, row, 0.0)
+        total = jnp.zeros((blocks, lanes), f32)
+        for _ in range(3):
+            part = spreaded.astype(bf16)
+            total = total + dot_nn(part, pick)
+            spreaded = spreaded - part.astype(f32)
+        return total
+
+    total = one(last, 6 * size, 4 * size)
+    for k, vector in enumerate(vectors):
+        total = total + one(vector, k * size, size)
+    return total
+
+
+def project_kernel(
+    plan, total, info, inverse, tokens, *refs
+):
+    weight_pieces, vector_pieces = refs[:PIECES], refs[PIECES : 2 * PIECES]
+    normed, query, pairs, head, tail, weight, vectors, shift_out, table = refs[2 * PIECES :]
     rows, width = tokens.shape
     device = info[0]
+    each = weight_pieces[0].shape[0]
+    block_rows = weight_pieces[0].shape[1]
+    for p in range(PIECES * each):
+        i = inverse[p]
+        there = pl.ds(pl.multiple_of(i * block_rows, block_rows), block_rows)
+        weight[there, :] = weight_pieces[p // each][p % each]
+        table[pl.ds(i, 1), :] = vector_pieces[p // each][p % each].astype(f32)
+    singles, wide = unpack_vectors(table[...].astype(bf16), 4 * block_rows)
+    for k, single in enumerate(singles):
+        vectors[pl.ds(k, 1), :] = single
+    shift_out[...] = wide
     values = tokens[...].astype(f32)
-    center = values - jnp.mean(values, axis=-1, keepdims=True)
-    spread = jnp.mean(center * center, axis=-1, keepdims=True)
-    low = (center * lax.rsqrt(spread + 1e-05) * gain[...] + bias[...]).astype(bf16)
+    center, rstd = ln_stats(values)
+    low = (center * rstd * singles[0] + singles[1]).astype(bf16)
     normed[...] = low
     pooled_rows = plan.query_rows - plan.query_at[1]
     row = lax.broadcasted_iota(jnp.int32, (pooled_rows, rows), 0)
@@ -180,9 +255,12 @@
         tail[halo, :] = pairs[pl.ds(at + count - HALO, HALO), :]
 
 
-def project(plan, total, info, tokens, gain, bias, weight):
+def project(plan, total, info, inverse, tokens, weight_pieces, vector_pieces):
     rows, width = tokens.shape
     halo = LEVELS * HALO
+    blocks = PIECES * weight_pieces[0].shape[0]
+    depth = blocks * weight_pieces[0].shape[1]
+    lanes = vector_pieces[0].shape[-1]
     return pl.pallas_call(
         functools.partial(project_kernel, plan, total),
         out_shape=(
@@ -191,12 +269,16 @@
             jax.ShapeDtypeStruct((plan.query_rows, 2 * width), bf16),
             jax.ShapeDtypeStruct((halo, 2 * width), bf16),
             jax.ShapeDtypeStruct((halo, 2 * width), bf16),
+            jax.ShapeDtypeStruct((depth, weight_pieces[0].shape[2]), bf16),
+            jax.ShapeDtypeStruct((8, depth), f32),
+            jax.ShapeDtypeStruct((1, 4 * depth), f32),
         ),
-        in_specs=[SCALARS] + spec(4),
-        out_specs=tuple(spec(5)),
+        in_specs=[SCALARS, SCALARS] + spec(1 + 2 * PIECES),
+        out_specs=tuple(spec(8)),
+        scratch_shapes=[pltpu.VMEM((blocks, lanes), f32)],
         compiler_params=pltpu.CompilerParams(vmem_limit_bytes=VMEM_LIMIT),
         name="project",
-    )(info, tokens, gain, bias, weight)
+    )(info, inverse, tokens, *weight_pieces, *vector_pieces)
 
 
 def attend_kernel(
@@ -271,6 +353,131 @@
         compiler_params=pltpu.CompilerParams(vmem_limit_bytes=VMEM_LIMIT),
         name="attend",
     )(info, query, pairs, before, after)
+
+
+def middle_kernel(
+    inverse,
+    tokens,
+    cotangent,
+    attended,
+    vectors,
+    shift_in,
+    *refs,
+):
+    pieces = refs[:PIECES]
+    result, grad_resid, grad_mixed, own, other, sums, sum_in = refs[PIECES : PIECES + 7]
+    w_out, w_in, w_back, gelu_low, normed_two, grad_normed, outer, tall, flat = refs[PIECES + 7 :]
+    width = tokens.shape[1]
+    each, stack = pieces[0].shape[0], pieces[0].shape[1]
+    half = own.shape[0]
+    chunks = w_in.shape[0]
+    block = width // (PIECES * each)
+    tall_block = chunks * block
+    in_at, back_at = block, block + tall_block
+    for p in range(PIECES * each):
+        piece, q = pieces[p // each], p % each
+        i = inverse[p]
+        rows = pl.ds(pl.multiple_of(i * block, block), block)
+        w_out[rows, :] = piece[q, pl.ds(0, block), :]
+        for c in range(chunks):
+            w_in[c, rows, :] = piece[q, pl.ds(in_at + block * c, block), :]
+        rows = pl.ds(pl.multiple_of(i * tall_block, tall_block), tall_block)
+        w_back[rows, :] = piece[q, pl.ds(back_at, tall_block), :]
+    gain = vectors[pl.ds(3, 1), :]
+    resid = tokens[...].astype(f32) + dot_nn(attended[...], w_out[...]) + vectors[pl.ds(2, 1), :]
+    center, rstd = ln_stats(resid)
+    normed_two[...] = (center * rstd * gain + vectors[pl.ds(4, 1), :]).astype(bf16)
+    grad_resid[...] = resid
+    outer[...] = jnp.zeros(outer.shape, f32)
+    grad_normed[...] = jnp.zeros(grad_normed.shape, f32)
+
+    def chunk_step(c, carry):
+        there = pl.ds(pl.multiple_of(c * width, width), width)
+        inner = dot_nn(normed_two[...], w_in[c]) + shift_in[:, there]
+        cdf = 0.5 * (1.0 + lax.erf(inner * math.sqrt(0.5)))
+        active = (inner * cdf).astype(bf16)
+        slope = cdf + inner * (jnp.exp(-0.5 * inner * inner) * (1.0 / math.sqrt(2.0 * math.pi)))
+        gelu_low[...] = active
+        back = w_back[there, :]
+        grad_inner = slope * dot_nt(cotangent[...], back)
+        low = grad_inner.astype(bf16)
+        outer[...] += dot_nn(active, back)
+        tall[there, :] = dot_tn(active, cotangent[...])
+        sum_in[:, there] = column_sum(low.astype(f32))
+        flat[...] = dot_tn(normed_two[...], low)
+        for p in range(2 * half):
+            i = inverse[p]
+            rows = flat[pl.ds(pl.multiple_of(i * block, block), block), :]
+            at = pl.ds(pl.multiple_of(in_at + c * block, block), block)
+            if p < half:
+                own[p, at, :] = rows
+            else:
+                other[p - half, at, :] = rows.astype(bf16)
+        grad_normed[...] += dot_nt(low, w_in[c])
+        return carry
+
+    lax.fori_loop(0, chunks, chunk_step, 0)
+    resid = grad_resid[...]
+    result[...] = (resid + outer[...] + vectors[pl.ds(5, 1), :]).astype(bf16)
+    center, rstd = ln_stats(resid)
+    grad_in, gain_terms = ln_back(grad_normed[...], center, rstd, gain)
+    grad_out = cotangent[...].astype(f32)
+    total = grad_out + grad_in
+    grad_resid[...] = total
+    low = total.astype(bf16)
+    sums[pl.ds(0, 1), :] = jnp.zeros((1, width), f32)
+    sums[pl.ds(1, 1), :] = jnp.zeros((1, width), f32)
+    sums[pl.ds(2, 1), :] = column_sum(low.astype(f32))
+    sums[pl.ds(3, 1), :] = column_sum(gain_terms)
+    sums[pl.ds(4, 1), :] = column_sum(grad_normed[...])
+    sums[pl.ds(5, 1), :] = column_sum(grad_out)
+    grad_mixed[...] = dot_nt(low, w_out[...])
+    flat[...] = dot_tn(attended[...], low)
+    for p in range(2 * half):
+        i = inverse[p]
+        rows = flat[pl.ds(pl.multiple_of(i * block, block), block), :]
+        tall_rows = tall[pl.ds(pl.multiple_of(i * tall_block, tall_block), tall_block), :]
+        if p < half:
+            own[p, pl.ds(0, block), :] = rows
+            own[p, pl.ds(back_at, tall_block), :] = tall_rows
+        else:
+            other[p - half, pl.ds(0, block), :] = rows.astype(bf16)
+            other[p - half, pl.ds(back_at, tall_block), :] = tall_rows.astype(bf16)
+
+
+def middle(inverse, tokens, cotangent, attended, vectors, shift_in, pieces):
+    rows, width = tokens.shape
+    hidden = shift_in.shape[1]
+    chunks = hidden // width
+    blocks = PIECES * pieces[0].shape[0]
+    stack = pieces[0].shape[1]
+    return pl.pallas_call(
+        middle_kernel,
+        out_shape=(
+            jax.ShapeDtypeStruct((rows, width), bf16),
+            jax.ShapeDtypeStruct((rows, width), f32),
+            jax.ShapeDtypeStruct((rows, width), f32),
+            jax.ShapeDtypeStruct((blocks // 2, stack, width), f32),
+            jax.ShapeDtypeStruct((blocks // 2, stack, width), bf16),
+            jax.ShapeDtypeStruct((8, width), f32),
+            jax.ShapeDtypeStruct((1, hidden), f32),
+        ),
+        in_specs=[SCALARS] + spec(5 + PIECES),
+        out_specs=tuple(spec(7)),
+        scratch_shapes=[
+            pltpu.VMEM((width, width), bf16),
+            pltpu.VMEM((chunks, width, width), bf16),
+            pltpu.VMEM((hidden, width), bf16),
+            pltpu.VMEM((rows, width), bf16),
+            pltpu.VMEM((rows, width), bf16),
+            pltpu.VMEM((rows, width), f32),
+            pltpu.VMEM((rows, width), f32),
+            pltpu.VMEM((hidden, width), f32),
+            pltpu.VMEM((width, width), f32),
+        ],
+        compiler_params=pltpu.CompilerParams(vmem_limit_bytes=VMEM_LIMIT),
+        name="middle",
+    )(inverse, tokens, cotangent, attended, vectors, shift_in, *pieces)
 
 
 def attend_back_kernel(
@@ -382,7 +589,31 @@
     )(info, query, pairs, before, after, grad_mixed, scale, mixed)
 
 
-def combine_kernel(plan, total, info, grad_query, grad_pairs, from_below, from_above, joined, work):
+def finish_kernel(
+    plan,
+    total,
+    info,
+    inverse,
+    tokens,
+    weight,
+    vectors,
+    grad_resid,
+    sums,
+    sum_in,
+    grad_query,
+    grad_pairs,
+    from_below,
+    from_above,
+    grad_tokens,
+    own,
+    other,
+    own_vector,
+    other_vector,
+    work,
+    joined,
+    flat,
+    table,
+):
     rows = plan.rows
     width = grad_query.shape[1]
     device = info[0]
@@ -412,29 +643,122 @@
         if chunk * 128 >= 2 * width:
             value = value * live
         joined[:, pl.ds(chunk * 128, 128)] = value.astype(bf16)
-
-
-def combine(plan, total, info, grad_query, grad_pairs, from_below, from_above):
-    width = grad_query.shape[1]
+    values = tokens[...].astype(f32)
+    center, rstd = ln_stats(values)
+    gain = vectors[pl.ds(0, 1), :]
+    normed = (center * rstd * gain + vectors[pl.ds(1, 1), :]).astype(bf16)
+    half, block = own.shape[0], own.shape[1]
+    for part in range(3):
+        columns = pl.ds(part * width, width)
+        flat[...] = dot_tn(normed, joined[:, columns])
+        for p in range(2 * half):
+            i = inverse[p]
+            lines = flat[pl.ds(pl.multiple_of(i * block, block), block), :]
+            if p < half:
+                own[p, :, columns] = lines
+            else:
+                other[p - half, :, columns] = lines.astype(bf16)
+    grad_normed = dot_nt(joined[...], weight[...])
+    grad_in, gain_terms = ln_back(grad_normed, center, rstd, gain)
+    grad_tokens[...] = grad_resid[...] + grad_in
+    singles = [column_sum(gain_terms), column_sum(grad_normed)]
+    singles += [sums[pl.ds(k, 1), :] for k in range(2, 6)]
+    table[...] = pack_vectors(singles, sum_in[...], 2 * half, table.shape[1])
+    for p in range(2 * half):
+        line = table[pl.ds(inverse[p], 1), :]
+        if p < half:
+            own_vector[p] = line
+        else:
+            other_vector[p - half] = line
+
+
+def finish(plan, total, info, inverse, lanes, blocks, tokens, weight, *rest):
+    rows, width = tokens.shape
+    half = blocks // 2
+    block = width // blocks
     return pl.pallas_call(
-        functools.partial(combine_kernel, plan, total),
-        out_shape=jax.ShapeDtypeStruct((plan.rows, 3 * width), bf16),
-        in_specs=[SCALARS] + spec(4),
-        out_specs=spec(1)[0],
-        scratch_shapes=[pltpu.VMEM((3 * width // 128, plan.query_rows, 128), f32)],
+        functools.partial(finish_kernel, plan, total),
+        out_shape=(
+            jax.ShapeDtypeStruct((rows, width), f32),
+            jax.ShapeDtypeStruct((half, block, 3 * width), f32),
+            jax.ShapeDtypeStruct((half, block, 3 * width), bf16),
+            jax.ShapeDtypeStruct((half, 1, lanes), f32),
+            jax.ShapeDtypeStruct((half, 1, lanes), f32),
+        ),
+        in_specs=[SCALARS, SCALARS] + spec(2 + len(rest)),
+        out_specs=tuple(spec(5)),
+        scratch_shapes=[
+            pltpu.VMEM((3 * width // 128, plan.query_rows, 128), f32),
+            pltpu.VMEM((rows, 3 * width), bf16),
+            pltpu.VMEM((width, width), f32),
+            pltpu.VMEM((blocks, lanes), f32),
+        ],
         compiler_params=pltpu.CompilerParams(vmem_limit_bytes=VMEM_LIMIT),
-        name="combine",
-    )(info, grad_query, grad_pairs, from_below, from_above)
-
-
-def layer_norm(values, gain, shift):
-    center = values - jnp.mean(values, axis=-1, keepdims=True)
-    spread = jnp.mean(center * center, axis=-1, keepdims=True)
-    return center * lax.rsqrt(spread + 1e-05) * gain + shift
-
-
-def gelu_exact(values):
-    return jax.nn.gelu(values, approximate=False)
+        name="finish",
+    )(info, inverse, tokens, weight, *rest)
+
+
+class Ring:
+    def __init__(self, devices):
+        self.devices = devices
+        bits = [1 << k for k in range(devices.bit_length() - 2, 0, -1)]
+        self.orders = (bits, bits[-1:] + bits[:-1])
+        self.stages = len(bits)
+
+    def partner(self, stage):
+        return [(i, i ^ self.orders[i & 1][stage]) for i in range(self.devices)]
+
+    def twin(self):
+        return [(i, i ^ 1) for i in range(self.devices)]
+
+    def table(self):
+        rows = []
+        for device in range(self.devices):
+            row = []
+            for base in (device, device ^ 1):
+                order = self.orders[base & 1]
+                for position in range(1 << self.stages):
+                    block = base
+                    for stage in range(self.stages):
+                        if position >> stage & 1:
+                            block ^= order[stage]
+                    row.append(block)
+            rows.append(row)
+        return np.array(rows, np.int32)
+
+    def gather(self, arrays):
+        held = [item[None] for item in arrays]
+        for stage in range(self.stages - 1):
+            route = self.partner(stage)
+            came = [lax.ppermute(item, "seq", route) for item in held]
+            held = [jnp.concatenate(pair) for pair in zip(held, came)]
+        route = self.partner(self.stages - 1)
+        came = [lax.ppermute(item, "seq", route) for item in held]
+        twin_held = [lax.ppermute(item, "seq", self.twin()) for item in held]
+        twin_came = [lax.ppermute(item, "seq", self.twin()) for item in came]
+        return [list(four) for four in zip(held, came, twin_held, twin_came)]
+
+    def scatter(self, own, other):
+        came = [lax.ppermute(item, "seq", self.twin()) for item in other]
+        for stage in range(self.stages - 1, -1, -1):
+            half = 1 << stage
+            route = self.partner(stage)
+            sent = [
+                (mine[half:] + more[half:].astype(f32)).astype(more.dtype)
+                for mine, more in zip(own, came)
+            ]
+            kept = [mine[:half] + more[:half].astype(f32) for mine, more in zip(own, came)]
+            came = [lax.ppermute(item, "seq", route) for item in sent]
+            own = kept
+        return [mine[0] + more[0].astype(f32) for mine, more in zip(own, came)]
+
+
+def lanes_of(vectors, axis):
+    joined = jnp.concatenate(vectors, axis=axis)
+    rest = -joined.shape[axis] % 128
+    pads = [(0, 0)] * joined.ndim
+    pads[axis] = (0, rest)
+    return jnp.pad(joined, pads)
 
 
 def exchange(to_above, to_below):
@@ -462,99 +786,126 @@
 ):
     devices = lax.axis_size("seq")
     device = lax.axis_index("seq")
-    rows = tokens.shape[0]
+    rows, width = tokens.shape
     total = rows * devices
     plan = Plan(rows)
     padded = (lengths + 15) // 16 * 16
     ends = jnp.cumsum(padded, dtype=jnp.int32)
     info = jnp.concatenate([device[None].astype(jnp.int32), lengths, ends - padded, ends])
-    (
-        gain_one,
-        bias_one,
-        joint_weight,
-        out_weight,
-        out_shift,
-        gain_two,
-        bias_two,
-        in_weight,
-        in_shift,
-        back_weight,
-        back_shift,
-    ) = (
-        lax.all_gather(item, "seq", axis=0, tiled=True)
-        for item in (
-            ln1_gain,
-            ln1_bias,
-            w_qkv,
-            w_out,
-            out_bias,
-            ln2_gain,
-            ln2_bias,
-            w_in,
-            in_bias,
-            w_back,
-            back_bias,
+    block = width // BLOCKS
+    chunks = w_in.shape[1] // width
+    small = (ln1_gain, ln1_bias, out_bias, ln2_gain, ln2_bias, back_bias, in_bias)
+    direct = devices == BLOCKS
+    if direct:
+        ring = Ring(devices)
+        inverse = lax.dynamic_index_in_dim(jnp.array(ring.table()), device, keepdims=False)
+        line = lanes_of(small, 0)[None]
+        one, vector_pieces = ring.gather([w_qkv, line])
+        stack = jnp.concatenate(
+            [w_out] + [w_in[:, c * width : (c + 1) * width] for c in range(chunks)] + [w_back]
         )
-    )
-    gain_one, bias_one = gain_one.astype(f32), bias_one.astype(f32)
-    normed_low, query, pairs, head, tail = project(
-        plan, total, info, tokens, gain_one[None], bias_one[None], joint_weight
+        (two,) = ring.gather([stack])
+    else:
+        inverse = jnp.arange(BLOCKS, dtype=jnp.int32)
+
+        def whole(item):
+            return lax.all_gather(item, "seq", axis=0, tiled=True)
+
+        def quarters(item):
+            return [item[k * 8 : (k + 1) * 8] for k in range(PIECES)]
+
+        line = lanes_of([whole(item).reshape(BLOCKS, -1) for item in small], 1)
+        vector_pieces = quarters(line[:, None])
+        one = quarters(whole(w_qkv).reshape(BLOCKS, block, -1))
+        full_in = whole(w_in).reshape(BLOCKS, block, chunks, width)
+        full_in = full_in.transpose(0, 2, 1, 3).reshape(BLOCKS, chunks * block, width)
+        two = quarters(
+            jnp.concatenate(
+                [
+                    whole(w_out).reshape(BLOCKS, block, width),
+                    full_in,
+                    whole(w_back).reshape(BLOCKS, chunks * block, width),
+                ],
+                axis=1,
+            )
+        )
+    normed, query, pairs, head, tail, weight, vectors, shift_in = project(
+        plan, total, info, inverse, tokens, one, vector_pieces
     )
     before, after = exchange(tail, head)
     attended, mixed, scale = attend(plan, total, info, query, pairs, before, after)
-    inputs = tokens.astype(f32)
-    branch = jnp.dot(attended, out_weight, preferred_element_type=f32) + out_shift.astype(f32)
-    resid = inputs + branch
-    normed_two, norm_two_pull = jax.vjp(
-        layer_norm, resid, gain_two.astype(f32), bias_two.astype(f32)
+    result, grad_resid, grad_mixed, own_two, other_two, sums, sum_in = middle(
+        inverse, tokens, cotangent, attended, vectors, shift_in, two
     )
-    normed_two_low = normed_two.astype(bf16)
-    inner = jnp.dot(normed_two_low, in_weight, preferred_element_type=f32) + in_shift.astype(f32)
-    active, gelu_pull = jax.vjp(gelu_exact, inner)
-    active_low = active.astype(bf16)
-    outer = jnp.dot(active_low, back_weight, preferred_element_type=f32) + back_shift.astype(f32)
-    result = (resid + outer).astype(bf16)
-    grad_out = cotangent.astype(f32)
-    grad_back_shift = jnp.sum(grad_out, axis=0)
-    grad_back_weight = jnp.einsum("rf,rd->fd", active_low, cotangent, preferred_element_type=f32)
-    grad_active = jnp.dot(cotangent, back_weight.T, preferred_element_type=f32)
-    grad_inner = gelu_pull(grad_active)[0].astype(bf16)
-    grad_in_shift = jnp.sum(grad_inner.astype(f32), axis=0)
-    grad_in_weight = jnp.einsum("rd,rf->df", normed_two_low, grad_inner, preferred_element_type=f32)
-    grad_normed_two = jnp.dot(grad_inner, in_weight.T, preferred_element_type=f32)
-    grad_resid_part, grad_gain_two, grad_bias_two = norm_two_pull(grad_normed_two)
-    grad_resid = grad_out + grad_resid_part
-    grad_branch = grad_resid.astype(bf16)
-    grad_out_shift = jnp.sum(grad_branch.astype(f32), axis=0)
-    grad_out_weight = jnp.einsum("rd,re->de", attended, grad_branch, preferred_element_type=f32)
-    grad_mixed = jnp.dot(grad_branch, out_weight.T, preferred_element_type=f32)
     grad_query, grad_pairs, grad_head, grad_tail = attend_back(
         plan, total, info, query, pairs, before, after, grad_mixed, scale, mixed
     )
     from_below, from_above = exchange(grad_tail, grad_head)
-    grad_joined = combine(plan, total, info, grad_query, grad_pairs, from_below, from_above)
-    grad_joint_weight = jnp.einsum(
-        "rd,rf->df", normed_low, grad_joined, preferred_element_type=f32
+    grad_tokens, own_one, other_one, own_line, other_line = finish(
+        plan,
+        total,
+        info,
+        inverse,
+        line.shape[-1],
+        BLOCKS,
+        tokens,
+        weight,
+        vectors,
+        grad_resid,
+        sums,
+        sum_in,
+        grad_query,
+        grad_pairs,
+        from_below,
+        from_above,
     )
-    grad_normed = jnp.dot(grad_joined, joint_weight.T, preferred_element_type=f32)
-    _, norm_one_pull = jax.vjp(layer_norm, inputs, gain_one, bias_one)
-    grad_input_part, grad_gain_one, grad_bias_one = norm_one_pull(grad_normed)
-    grad_tokens = grad_resid + grad_input_part
-    return (result, grad_tokens) + tuple(
-        lax.psum_scatter(item, "seq", scatter_dimension=0, tiled=True)
-        for item in (
-            grad_gain_one,
-            grad_bias_one,
-            grad_joint_weight,
-            grad_out_weight,
-            grad_out_shift,
-            grad_gain_two,
-            grad_bias_two,
-            grad_in_weight,
-            grad_in_shift,
-            grad_back_weight,
-            grad_back_shift,
+    if direct:
+        (grad_two,) = ring.scatter([own_two], [other_two])
+        grad_w_qkv, grad_line = ring.scatter([own_one, own_line], [other_one, other_line])
+        each = [item.shape[0] for item in small]
+        starts = [sum(each[:k]) for k in range(len(each))]
+        parts = [grad_line[0, at : at + size] for at, size in zip(starts, each)]
+        grad_w_out = grad_two[:block]
+        grad_w_in = jnp.concatenate(
+            [grad_two[block * (c + 1) : block * (c + 2)] for c in range(chunks)], axis=1
         )
+        grad_w_back = grad_two[block * (chunks + 1) :]
+    else:
+
+        def spread(own, other):
+            return jnp.concatenate([own, other.astype(f32)])
+
+        def shared(item):
+            return lax.psum_scatter(item, "seq", scatter_dimension=0, tiled=True)
+
+        full_line = spread(own_line, other_line)[:, 0]
+        each = [block] * 6 + [block * chunks]
+        starts = [sum(each[:k]) for k in range(len(each))]
+        parts = [
+            shared(full_line[:, at : at + size].reshape(-1)) for at, size in zip(starts, each)
+        ]
+        grad_w_qkv = shared(spread(own_one, other_one).reshape(width, 3 * width))
+        full_two = spread(own_two, other_two)
+        grad_w_out = shared(full_two[:, :block].reshape(width, width))
+        full_in = full_two[:, block : block * (chunks + 1)]
+        full_in = full_in.reshape(BLOCKS, chunks, block, width).transpose(0, 2, 1, 3)
+        grad_w_in = shared(full_in.reshape(width, chunks * width))
+        grad_w_back = shared(full_two[:, block * (chunks + 1) :].reshape(chunks * width, width))
+    gain_one, bias_one, shift_out, gain_two, bias_two, shift_back, shift_hidden = parts
+    return (
+        result,
+        grad_tokens,
+        gain_one,
+        bias_one,
+        grad_w_qkv,
+        grad_w_out,
+        shift_out,
+        gain_two,
+        bias_two,
+        grad_w_in,
+        shift_hidden,
+        grad_w_back,
+        shift_back,
     )
 
 

time: 743 us -> 222 us (0.30)
  waiting for transfers between devices: 457 us -> 78.3 us
  blocking collectives: 132 us -> 0 us
  starting transfers between devices: 7.66 us -> 63.2 us
  matrix products: 47.6 us -> 0 us
  Pallas kernels: 41.1 us -> 61 us
  local copies, waits for them, and re-layouts: 24.6 us -> 10.5 us
  between operations: 14.7 us -> 1.06 us
    reduce_scatter x4 -> x0, waiting for transfers between devices: 402 us -> none  [per_device(): lax.psum_scatter(item, 'seq', scatter_dimension=0, tiled=True)]
    unnamed x2 -> x0, blocking collectives: 87.3 us -> none
    ppermute x0 -> x33, waiting for transfers between devices: none -> 72.3 us  [the longest x12 45.4 us: scatter(): came = [lax.ppermute(item, 'seq', route) for item in sent]]
    ppermute x0 -> x33, starting transfers between devices: none -> 56 us  [the longest x12 28 us: gather(): came = [lax.ppermute(item, 'seq', route) for item in held]]
    all_gather x3 -> x0, waiting for transfers between devices: 49.1 us -> none  [per_device(): lax.all_gather(item, 'seq', axis=0, tiled=True)]
    dot_general x11 -> x0, matrix products: 47.6 us -> none  [the longest x1 14.2 us: per_device(): grad_active = jnp.dot(cotangent, back_weight.T, preferred_element_type=f32)]
    all_gather x1 -> x0, blocking collectives: 44.4 us -> none  [per_device(): lax.all_gather(item, 'seq', axis=0, tiled=True)]
    pallas_call x1 -> x2, Pallas kernels: 6.11 us -> 26 us  [the longest x1 16.6 us: middle(): pl.pallas_call(middle_kernel, out_shape=(jax.ShapeDtypeStruct((rows, widt...]
  transfers between devices with their start and end apart: 11 -> 37, of which waited for: 8 -> 19; matrix products, arithmetic and copies ran while one was open for 8% -> 4% of each run, Pallas kernels for 6% -> 20%
where the time goes in v2:
time: 222 us; the launch traced here: 221 us
  waiting for transfers between devices  78.3 us (35%)
  starting transfers between devices  63.2 us (28%)
  Pallas kernels  61 us (27%)
  local copies, waits for them, and re-layouts  10.5 us (5%)
  other arithmetic  7.4 us (3%)
    ppermute x12, waiting for transfers between devices, scatter(): came = [lax.ppermute(item, 'seq', route) for item in sent]  45.4 us
    ppermute x12, starting transfers between devices, gather(): came = [lax.ppermute(item, 'seq', route) for item in held]  28 us
    ppermute x12, waiting for transfers between devices, gather(): came = [lax.ppermute(item, 'seq', route) for item in held]  25.9 us
    pallas_call x1, Pallas kernels, attend_back(): pl.pallas_call(functools.partial(attend_back_kernel, plan, total), out_sh...  17.3 us
    pallas_call x1, Pallas kernels, middle(): pl.pallas_call(middle_kernel, out_shape=(jax.ShapeDtypeStruct((rows, widt...  16.6 us
    ppermute x12, starting transfers between devices, scatter(): came = [lax.ppermute(item, 'seq', route) for item in sent]  15.1 us
    ppermute x3, starting transfers between devices, scatter(): came = [lax.ppermute(item, 'seq', self.twin()) for item in other]  11.9 us
    pallas_call x1, Pallas kernels, attend(): pl.pallas_call(functools.partial(attend_kernel, plan, total), out_shape=(...  11.8 us
  transfers between devices with their start and end apart: 37, of which 19 were waited for; matrix products, arithmetic and copies ran while one was open for 4% of the time, Pallas kernels for 20%

profile of v2, /device:TPU:0, one launch (start us, length us, event | category | flops | bytes accessed | tf_op | source)
XLA Modules:
  0.0 221.5 jit_solution(13586314088216253567)
XLA Ops:
  5.1 4.0 %collective-permute-start.14 = (bf16[1,144,512]{2,1,0:T(8,128)(2,1)S(1)}, bf16[1,144,512]{2,1,0:T(8,128)(2,1)S(1)}, u32[]{:S(2)}, u32[]{:S(2)}) collective-permute-start(bf16[1,144,512]{2,1,0:T(8,128)(2,1)S(1)} %bitcast.41), channel_id=1, source_target_pairs={{0,16},{1,3},{2,18},{3,1},{4,20},{5,7},{6,22},{7,5},{8,24},{9,11},... | collective-permute-start | bytes 442376 | tf_op jit(solution)/shard_map/ppermute | solution.py:733
  9.1 4.7 %collective-permute-done.14 = bf16[1,144,512]{2,1,0:T(8,128)(2,1)S(1)} collective-permute-done((bf16[1,144,512]{2,1,0:T(8,128)(2,1)S(1)}, bf16[1,144,512]{2,1,0:T(8,128)(2,1)S(1)}, u32[]{:S(2)}, u32[]{:S(2)}) %collective-permute-start.14) | collective-permute-done | bytes 147488 | tf_op jit(solution)/shard_map/ppermute | solution.py:733
  15.0 7.7 %collective-permute-done.15 = bf16[2,144,512]{2,1,0:T(8,128)(2,1)S(1)} collective-permute-done((bf16[2,144,512]{2,1,0:T(8,128)(2,1)S(1)}, bf16[2,144,512]{2,1,0:T(8,128)(2,1)S(1)}, u32[]{:S(2)}, u32[]{:S(2)}) %collective-permute-start.15) | collective-permute-done | bytes 294944 | tf_op jit(solution)/shard_map/ppermute | solution.py:733
  22.7 2.5 %collective-permute-start.16 = (bf16[4,144,512]{2,1,0:T(8,128)(2,1)S(1)}, bf16[4,144,512]{2,1,0:T(8,128)(2,1)S(1)}, u32[]{:S(2)}, u32[]{:S(2)}) collective-permute-start(bf16[4,144,512]{2,1,0:T(8,128)(2,1)S(1)} %pad_maximum_fusion.1), channel_id=1, source_target_pairs={{0,4},{1,9},{2,6},{3,11},{4,0},{5,13},{6,2},{7,15},{8,12},{9,1},{1... | collective-permute-start | bytes 1769480 | tf_op jit(solution)/shard_map/ppermute | solution.py:733
  25.3 3.4 %collective-permute-start = (bf16[1,16,1536]{2,1,0:T(8,128)(2,1)S(1)}, bf16[1,16,1536]{2,1,0:T(8,128)(2,1)S(1)}, u32[]{:S(2)}, u32[]{:S(2)}) collective-permute-start(bf16[1,16,1536]{2,1,0:T(8,128)(2,1)S(1)} %bitcast.45), channel_id=1, source_target_pairs={{0,16},{1,3},{2,18},{3,1},{4,20},{5,7},{6,22},{7,5},{8,24},{9,11},... | collective-permute-start | bytes 147464 | tf_op jit(solution)/shard_map/ppermute | solution.py:733
  28.7 4.4 %collective-permute-done.16 = bf16[4,144,512]{2,1,0:T(8,128)(2,1)S(1)} collective-permute-done((bf16[4,144,512]{2,1,0:T(8,128)(2,1)S(1)}, bf16[4,144,512]{2,1,0:T(8,128)(2,1)S(1)}, u32[]{:S(2)}, u32[]{:S(2)}) %collective-permute-start.16) | collective-permute-done | bytes 589856 | tf_op jit(solution)/shard_map/ppermute | solution.py:733
  33.3 2.6 %collective-permute-start.17 = (bf16[8,144,512]{2,1,0:T(8,128)(2,1)S(1)}, bf16[8,144,512]{2,1,0:T(8,128)(2,1)S(1)}, u32[]{:S(2)}, u32[]{:S(2)}) collective-permute-start(bf16[8,144,512]{2,1,0:T(8,128)(2,1)S(1)} %pad_maximum_fusion.refs_0_), channel_id=1, source_target_pairs={{0,2},{1,5},{2,0},{3,7},{4,6},{5,1},{6,4},{7,3},{8,10},{9,13},{10,... | collective-permute-start | bytes 3538952 | tf_op jit(solution)/shard_map/ppermute | solution.py:736
  36.0 4.0 %collective-permute-start.6 = (bf16[1,1,256]{2,1,0:T(2,128)(2,1)S(1)}, bf16[1,1,256]{2,1,0:T(2,128)(2,1)S(1)}, u32[]{:S(2)}, u32[]{:S(2)}) collective-permute-start(bf16[1,1,256]{2,1,0:T(2,128)(2,1)S(1)} %broadcast_in_dim_broadcast_in_dim.3), channel_id=1, source_target_pairs={{0,16},{1,3},{2,18},{3,1},{4,20},{5,7},{6,22},{7,5},{8,24},{9,11},... | collective-permute-start | bytes 1544 | tf_op jit(solution)/shard_map/ppermute | solution.py:733
  40.0 3.0 %collective-permute-start.1 = (bf16[2,16,1536]{2,1,0:T(8,128)(2,1)S(1)}, bf16[2,16,1536]{2,1,0:T(8,128)(2,1)S(1)}, u32[]{:S(2)}, u32[]{:S(2)}) collective-permute-start(bf16[2,16,1536]{2,1,0:T(8,128)(2,1)S(1)} %pad_maximum_fusion.6), channel_id=1, source_target_pairs={{0,8},{1,17},{2,10},{3,19},{4,12},{5,21},{6,14},{7,23},{8,0},{9,25... | collective-permute-start | bytes 294920 | tf_op jit(solution)/shard_map/ppermute | solution.py:733
  43.0 2.6 %collective-permute-done.1 = bf16[2,16,1536]{2,1,0:T(8,128)(2,1)S(1)} collective-permute-done((bf16[2,16,1536]{2,1,0:T(8,128)(2,1)S(1)}, bf16[2,16,1536]{2,1,0:T(8,128)(2,1)S(1)}, u32[]{:S(2)}, u32[]{:S(2)}) %collective-permute-start.1) | collective-permute-done | bytes 98336 | tf_op jit(solution)/shard_map/ppermute | solution.py:733
  47.9 2.1 collective-permute-start.7
  50.0 2.8 %collective-permute-done.2 = bf16[4,16,1536]{2,1,0:T(8,128)(2,1)S(1)} collective-permute-done((bf16[4,16,1536]{2,1,0:T(8,128)(2,1)S(1)}, bf16[4,16,1536]{2,1,0:T(8,128)(2,1)S(1)}, u32[]{:S(2)}, u32[]{:S(2)}) %collective-permute-start.2) | collective-permute-done | bytes 196640 | tf_op jit(solution)/shard_map/ppermute | solution.py:733
  65.8 5.8 %project.1 = (bf16[512,512]{1,0:T(8,128)(2,1)}, bf16[1024,512]{1,0:T(8,128)(2,1)}, bf16[1024,1024]{1,0:T(8,128)(2,1)}, bf16[160,1024]{1,0:T(8,128)(2,1)}, bf16[1...) custom-call(s32[10]{0:T(128)} %pad_add_fusion.info, ...), custom_call_target="tpu_custom_call" | custom-call | tf_op jit(solution)/shard_map/project/pallas_call | solution.py:264
  71.7 2.3 %collective-permute-start.12 = (bf16[160,1024]{1,0:T(8,128)(2,1)}, bf16[160,1024]{1,0:T(8,128)(2,1)S(1)}, u32[]{:S(2)}, u32[]{:S(2)}) collective-permute-start(bf16[160,1024]{1,0:T(8,128)(2,1)} %get-tuple-element.41), channel_id=1, source_target_pairs={{0,1},{1,2},{2,3},{3,4},{4,5},{5,6},{6,7},{7,8},{8,9},{9,10},{10,1... | collective-permute-start | bytes 983048 | tf_op jit(solution)/shard_map/ppermute | solution.py:768
  75.4 2.6 %collective-permute-done.13.after = bf16[160,1024]{1,0:T(8,128)(2,1)S(1)} collective-permute-done((bf16[160,1024]{1,0:T(8,128)(2,1)}, bf16[160,1024]{1,0:T(8,128)(2,1)S(1)}, u32[]{:S(2)}, u32[]{:S(2)}) %collective-permute-start.13) | collective-permute-done | bytes 327712 | tf_op jit(solution)/shard_map/ppermute | solution.py:768
  78.7 11.8 %attend.1 = (bf16[512,512]{1,0:T(8,128)(2,1)}, f32[512,512]{1,0:T(8,128)}, f32[512,512]{1,0:T(8,128)}) custom-call(s32[10]{0:T(128)} %pad_add_fusion.info, bf16[1024,512]{1,0:T(8,128)(2,1)} %get-tuple-element.39.query, bf16[1024,1024]{1,0:T(8,128)(2,1)} %get-tuple-element.40.pairs, bf16[160,1024]{1,0:T(8,128)(2,1)} %copy-done.3, bf16[160,1024]{1,0:T(8,128)(2,1)} %copy-done.4), custom_call_target="tpu_custom_call" | custom-call | tf_op jit(solution)/shard_map/attend/pallas_call | solution.py:339
  90.6 16.6 %middle.1 = (bf16[512,512]{1,0:T(8,128)(2,1)}, f32[512,512]{1,0:T(8,128)}, f32[512,512]{1,0:T(8,128)}, f32[16,144,512]{2,1,0:T(8,128)}, bf16[16,144,512]{2,1,0:T...) custom-call(s32[32]{0:T(128)} %dynamic-slice_bitcast_fusion.inverse, bf16[512,512]{1,0:T(8,128)(2,1)} %tokens.5, ...), custom_call_target="tpu_custom_call" | custom-call | tf_op jit(solution)/shard_map/middle/pallas_call | solution.py:454
  107.2 6.5 %collective-permute-start.32 = (bf16[16,144,512]{2,1,0:T(8,128)(2,1)}, bf16[16,144,512]{2,1,0:T(8,128)(2,1)S(1)}, u32[]{:S(2)}, u32[]{:S(2)}) collective-permute-start(bf16[16,144,512]{2,1,0:T(8,128)(2,1)} %get-tuple-element.64), channel_id=1, source_target_pairs={{0,1},{1,0},{2,3},{3,2},{4,5},{5,4},{6,7},{7,6},{8,9},{9,8},{10,11... | collective-permute-start | bytes 7077896 | tf_op jit(solution)/shard_map/ppermute | solution.py:742
  113.7 17.3 %attend_back.1 = (f32[1024,512]{1,0:T(8,128)}, f32[1024,1024]{1,0:T(8,128)}, bf16[160,1024]{1,0:T(8,128)(2,1)}, bf16[160,1024]{1,0:T(8,128)(2,1)}) custom-call(s32[10]{0:T(128)} %pad_add_fusion.info, bf16[1024,512]{1,0:T(8,128)(2,1)} %get-tuple-element.39.query, bf16[1024,1024]{1,0:T(8,128)(2,1)} %get-tuple-element.40.pairs, bf16[160,1024]{1,0:T(8,128)(2,1)} %copy-done.3, ...), custom_call_target="tpu_custom_call" | custom-call | tf_op jit(solution)/shard_map/attend_back/pallas_call | solution.py:571
  134.6 3.4 %collective-permute-done.21.from_above = bf16[160,1024]{1,0:T(8,128)(2,1)S(1)} collective-permute-done((bf16[160,1024]{1,0:T(8,128)(2,1)}, bf16[160,1024]{1,0:T(8,128)(2,1)S(1)}, u32[]{:S(2)}, u32[]{:S(2)}) %collective-permute-start.21) | collective-permute-done | bytes 327712 | tf_op jit(solution)/shard_map/ppermute | solution.py:768
  138.7 9.4 %finish.1 = (f32[512,512]{1,0:T(8,128)}, f32[16,16,1536]{2,1,0:T(8,128)}, bf16[16,16,1536]{2,1,0:T(8,128)(2,1)}, f32[16,1,256]{2,1,0:T(1,128)}, f32[16,1,256]{2,1,0:T(1,128)}) custom-call(s32[10]{0:T(128)} %pad_add_fusion.info, s32[32]{0:T(128)} %dynamic-slice_bitcast_fusion.inverse, bf16[512,512]{1,0:T(8,128)(2,1)} %tokens.5, ...), custom_call_target="tpu_custom_call" | custom-call | tf_op jit(solution)/shard_map/finish/pallas_call | solution.py:679
  148.1 5.4 %collective-permute-start.22 = (f32[16,1,256]{2,1,0:T(1,128)}, f32[16,1,256]{2,1,0:T(1,128)S(1)}, u32[]{:S(2)}, u32[]{:S(2)}) collective-permute-start(f32[16,1,256]{2,1,0:T(1,128)} %get-tuple-element.60), channel_id=1, source_target_pairs={{0,1},{1,0},{2,3},{3,2},{4,5},{5,4},{6,7},{7,6},{8,9},{9,8},{10,11... | collective-permute-start | bytes 49160 | tf_op jit(solution)/shard_map/ppermute | solution.py:742
  155.2 2.5 %collective-permute-start.23 = (f32[8,1,256]{2,1,0:T(1,128)S(1)}, f32[8,1,256]{2,1,0:T(1,128)S(1)}, u32[]{:S(2)}, u32[]{:S(2)}) collective-permute-start(f32[8,1,256]{2,1,0:T(1,128)S(1)} %get-tuple-element.83), channel_id=1, source_target_pairs={{0,2},{1,5},{2,0},{3,7},{4,6},{5,1},{6,4},{7,3},{8,10},{9,13},{10,... | collective-permute-start | bytes 24584 | tf_op jit(solution)/shard_map/ppermute | solution.py:751
  160.8 2.3 %collective-permute-done.24 = f32[4,1,256]{2,1,0:T(1,128)S(1)} collective-permute-done((f32[4,1,256]{2,1,0:T(1,128)S(1)}, f32[4,1,256]{2,1,0:T(1,128)S(1)}, u32[]{:S(2)}, u32[]{:S(2)}) %collective-permute-start.24) | collective-permute-done | bytes 4128 | tf_op jit(solution)/shard_map/ppermute | solution.py:751
  164.2 2.5 %collective-permute-done.25 = f32[2,1,256]{2,1,0:T(1,128)S(1)} collective-permute-done((f32[2,1,256]{2,1,0:T(1,128)S(1)}, f32[2,1,256]{2,1,0:T(1,128)S(1)}, u32[]{:S(2)}, u32[]{:S(2)}) %collective-permute-start.25) | collective-permute-done | bytes 2080 | tf_op jit(solution)/shard_map/ppermute | solution.py:751
  166.7 2.8 %collective-permute-start.26 = (f32[1,1,256]{2,1,0:T(1,128)S(1)}, f32[1,1,256]{2,1,0:T(1,128)S(1)}, u32[]{:S(2)}, u32[]{:S(2)}) collective-permute-start(f32[1,1,256]{2,1,0:T(1,128)S(1)} %slice_add_fusion.18), channel_id=1, source_target_pairs={{0,16},{1,3},{2,18},{3,1},{4,20},{5,7},{6,22},{7,5},{8,24},{9,11},... | collective-permute-start | bytes 3080 | tf_op jit(solution)/shard_map/ppermute | solution.py:751
  170.3 2.1 collective-permute-start.33
  173.8 17.0 %collective-permute-done.28 = bf16[8,16,1536]{2,1,0:T(8,128)(2,1)S(1)} collective-permute-done((bf16[8,16,1536]{2,1,0:T(8,128)(2,1)S(1)}, bf16[8,16,1536]{2,1,0:T(8,128)(2,1)S(1)}, u32[]{:S(2)}, u32[]{:S(2)}) %collective-permute-start.28) | collective-permute-done | bytes 393248 | tf_op jit(solution)/shard_map/ppermute | solution.py:751
  194.1 2.5 %collective-permute-done.29 = bf16[4,16,1536]{2,1,0:T(8,128)(2,1)S(1)} collective-permute-done((bf16[4,16,1536]{2,1,0:T(8,128)(2,1)S(1)}, bf16[4,16,1536]{2,1,0:T(8,128)(2,1)S(1)}, u32[]{:S(2)}, u32[]{:S(2)}) %collective-permute-start.29) | collective-permute-done | bytes 196640 | tf_op jit(solution)/shard_map/ppermute | solution.py:751
  197.7 5.3 %collective-permute-done.34 = bf16[4,144,512]{2,1,0:T(8,128)(2,1)S(1)} collective-permute-done((bf16[4,144,512]{2,1,0:T(8,128)(2,1)S(1)}, bf16[4,144,512]{2,1,0:T(8,128)(2,1)S(1)}, u32[]{:S(2)}, u32[]{:S(2)}) %collective-permute-start.34) | collective-permute-done | bytes 589856 | tf_op jit(solution)/shard_map/ppermute | solution.py:751
  204.5 8.2 %collective-permute-done.35 = bf16[2,144,512]{2,1,0:T(8,128)(2,1)S(1)} collective-permute-done((bf16[2,144,512]{2,1,0:T(8,128)(2,1)S(1)}, bf16[2,144,512]{2,1,0:T(8,128)(2,1)S(1)}, u32[]{:S(2)}, u32[]{:S(2)}) %collective-permute-start.35) | collective-permute-done | bytes 294944 | tf_op jit(solution)/shard_map/ppermute | solution.py:751
  213.5 5.9 %collective-permute-done.36 = bf16[1,144,512]{2,1,0:T(8,128)(2,1)S(1)} collective-permute-done((bf16[1,144,512]{2,1,0:T(8,128)(2,1)S(1)}, bf16[1,144,512]{2,1,0:T(8,128)(2,1)S(1)}, u32[]{:S(2)}, u32[]{:S(2)}) %collective-permute-start.36) | collective-permute-done | bytes 147488 | tf_op jit(solution)/shard_map/ppermute | solution.py:751
  (144 shorter events, 44.3 us)
Async XLA Ops:
  5.1 8.7 %collective-permute-start.14 = (bf16[1,144,512]{2,1,0:T(8,128)(2,1)S(1)}, bf16[1,144,512]{2,1,0:T(8,128)(2,1)S(1)}, u32[]{:S(2)}, u32[]{:S(2)}) collective-permute-start(bf16[1,144,512]{2,1,0:T(8,128)(2,1)S(1)} %bitcast.41), channel_id=1, source_target_pairs={{0,16},{1,3},{2,18},{3,1},{4,20},{5,7},{6,22},{7,5},{8,24},{9,11},... | collective-permute-start | bytes 442376 | tf_op jit(solution)/shard_map/ppermute | solution.py:733
  13.9 8.8 %collective-permute-start.15 = (bf16[2,144,512]{2,1,0:T(8,128)(2,1)S(1)}, bf16[2,144,512]{2,1,0:T(8,128)(2,1)S(1)}, u32[]{:S(2)}, u32[]{:S(2)}) collective-permute-start(bf16[2,144,512]{2,1,0:T(8,128)(2,1)S(1)} %pad_maximum_fusion.3), channel_id=1, source_target_pairs={{0,8},{1,17},{2,10},{3,19},{4,12},{5,21},{6,14},{7,23},{8,0},{9,25... | collective-permute-start | bytes 884744 | tf_op jit(solution)/shard_map/ppermute | solution.py:733
  22.7 10.4 %collective-permute-start.16 = (bf16[4,144,512]{2,1,0:T(8,128)(2,1)S(1)}, bf16[4,144,512]{2,1,0:T(8,128)(2,1)S(1)}, u32[]{:S(2)}, u32[]{:S(2)}) collective-permute-start(bf16[4,144,512]{2,1,0:T(8,128)(2,1)S(1)} %pad_maximum_fusion.1), channel_id=1, source_target_pairs={{0,4},{1,9},{2,6},{3,11},{4,0},{5,13},{6,2},{7,15},{8,12},{9,1},{1... | collective-permute-start | bytes 1769480 | tf_op jit(solution)/shard_map/ppermute | solution.py:733
  25.3 14.7 %collective-permute-start = (bf16[1,16,1536]{2,1,0:T(8,128)(2,1)S(1)}, bf16[1,16,1536]{2,1,0:T(8,128)(2,1)S(1)}, u32[]{:S(2)}, u32[]{:S(2)}) collective-permute-start(bf16[1,16,1536]{2,1,0:T(8,128)(2,1)S(1)} %bitcast.45), channel_id=1, source_target_pairs={{0,16},{1,3},{2,18},{3,1},{4,20},{5,7},{6,22},{7,5},{8,24},{9,11},... | collective-permute-start | bytes 147464 | tf_op jit(solution)/shard_map/ppermute | solution.py:733
  33.3 20.9 %collective-permute-start.17 = (bf16[8,144,512]{2,1,0:T(8,128)(2,1)S(1)}, bf16[8,144,512]{2,1,0:T(8,128)(2,1)S(1)}, u32[]{:S(2)}, u32[]{:S(2)}) collective-permute-start(bf16[8,144,512]{2,1,0:T(8,128)(2,1)S(1)} %pad_maximum_fusion.refs_0_), channel_id=1, source_target_pairs={{0,2},{1,5},{2,0},{3,7},{4,6},{5,1},{6,4},{7,3},{8,10},{9,13},{10,... | collective-permute-start | bytes 3538952 | tf_op jit(solution)/shard_map/ppermute | solution.py:736
  36.0 11.9 %collective-permute-start.6 = (bf16[1,1,256]{2,1,0:T(2,128)(2,1)S(1)}, bf16[1,1,256]{2,1,0:T(2,128)(2,1)S(1)}, u32[]{:S(2)}, u32[]{:S(2)}) collective-permute-start(bf16[1,1,256]{2,1,0:T(2,128)(2,1)S(1)} %broadcast_in_dim_broadcast_in_dim.3), channel_id=1, source_target_pairs={{0,16},{1,3},{2,18},{3,1},{4,20},{5,7},{6,22},{7,5},{8,24},{9,11},... | collective-permute-start | bytes 1544 | tf_op jit(solution)/shard_map/ppermute | solution.py:733
  40.0 5.5 %collective-permute-start.1 = (bf16[2,16,1536]{2,1,0:T(8,128)(2,1)S(1)}, bf16[2,16,1536]{2,1,0:T(8,128)(2,1)S(1)}, u32[]{:S(2)}, u32[]{:S(2)}) collective-permute-start(bf16[2,16,1536]{2,1,0:T(8,128)(2,1)S(1)} %pad_maximum_fusion.6), channel_id=1, source_target_pairs={{0,8},{1,17},{2,10},{3,19},{4,12},{5,21},{6,14},{7,23},{8,0},{9,25... | collective-permute-start | bytes 294920 | tf_op jit(solution)/shard_map/ppermute | solution.py:733
  45.6 7.2 %collective-permute-start.2 = (bf16[4,16,1536]{2,1,0:T(8,128)(2,1)S(1)}, bf16[4,16,1536]{2,1,0:T(8,128)(2,1)S(1)}, u32[]{:S(2)}, u32[]{:S(2)}) collective-permute-start(bf16[4,16,1536]{2,1,0:T(8,128)(2,1)S(1)} %pad_maximum_fusion.4), channel_id=1, source_target_pairs={{0,4},{1,9},{2,6},{3,11},{4,0},{5,13},{6,2},{7,15},{8,12},{9,1},{1... | collective-permute-start | bytes 589832 | tf_op jit(solution)/shard_map/ppermute | solution.py:733
  47.9 6.8 %collective-permute-start.7 = (bf16[2,1,256]{2,1,0:T(2,128)(2,1)S(1)}, bf16[2,1,256]{2,1,0:T(2,128)(2,1)S(1)}, u32[]{:S(2)}, u32[]{:S(2)}) collective-permute-start(bf16[2,1,256]{2,1,0:T(2,128)(2,1)S(1)} %pad_maximum_fusion.8), channel_id=1, source_target_pairs={{0,8},{1,17},{2,10},{3,19},{4,12},{5,21},{6,14},{7,23},{8,0},{9,25... | collective-permute-start | bytes 3080 | tf_op jit(solution)/shard_map/ppermute | solution.py:733
  52.9 7.8 %collective-permute-start.3 = (bf16[8,16,1536]{2,1,0:T(8,128)(2,1)S(1)}, bf16[8,16,1536]{2,1,0:T(8,128)(2,1)S(1)}, u32[]{:S(2)}, u32[]{:S(2)}) collective-permute-start(bf16[8,16,1536]{2,1,0:T(8,128)(2,1)S(1)} %pad_maximum_fusion.2.refs_0_), channel_id=1, source_target_pairs={{0,2},{1,5},{2,0},{3,7},{4,6},{5,1},{6,4},{7,3},{8,10},{9,13},{10,... | collective-permute-start | bytes 1179656 | tf_op jit(solution)/shard_map/ppermute | solution.py:736
  54.1 36.4 %collective-permute-start.18 = (bf16[8,144,512]{2,1,0:T(8,128)(2,1)S(1)}, bf16[8,144,512]{2,1,0:T(8,128)(2,1)}, u32[]{:S(2)}, u32[]{:S(2)}) collective-permute-start(bf16[8,144,512]{2,1,0:T(8,128)(2,1)S(1)} %pad_maximum_fusion.refs_0_), channel_id=1, source_target_pairs={{0,1},{1,0},{2,3},{3,2},{4,5},{5,4},{6,7},{7,6},{8,9},{9,8},{10,11... | collective-permute-start | bytes 3538952 | tf_op jit(solution)/shard_map/ppermute | solution.py:737
  54.2 36.4 %collective-permute-start.19 = (bf16[8,144,512]{2,1,0:T(8,128)(2,1)S(1)}, bf16[8,144,512]{2,1,0:T(8,128)(2,1)}, u32[]{:S(2)}, u32[]{:S(2)}) collective-permute-start(bf16[8,144,512]{2,1,0:T(8,128)(2,1)S(1)} %collective-permute-done.17.refs_1_), channel_id=1, source_target_pairs={{0,1},{1,0},{2,3},{3,2},{4,5},{5,4},{6,7},{7,6},{8,9},{9,8},{10,11... | collective-permute-start | bytes 3538952 | tf_op jit(solution)/shard_map/ppermute | solution.py:738
  54.7 3.7 %collective-permute-start.8 = (bf16[4,1,256]{2,1,0:T(2,128)(2,1)S(1)}, bf16[4,1,256]{2,1,0:T(2,128)(2,1)S(1)}, u32[]{:S(2)}, u32[]{:S(2)}) collective-permute-start(bf16[4,1,256]{2,1,0:T(2,128)(2,1)S(1)} %pad_maximum_fusion.7), channel_id=1, source_target_pairs={{0,4},{1,9},{2,6},{3,11},{4,0},{5,13},{6,2},{7,15},{8,12},{9,1},{1... | collective-permute-start | bytes 6152 | tf_op jit(solution)/shard_map/ppermute | solution.py:733
  58.4 3.7 %collective-permute-start.9 = (bf16[8,1,256]{2,1,0:T(2,128)(2,1)S(1)}, bf16[8,1,256]{2,1,0:T(2,128)(2,1)S(1)}, u32[]{:S(2)}, u32[]{:S(2)}) collective-permute-start(bf16[8,1,256]{2,1,0:T(2,128)(2,1)S(1)} %constant_dynamic-update-slice_fusion.refs_4_), channel_id=1, source_target_pairs={{0,2},{1,5},{2,0},{3,7},{4,6},{5,1},{6,4},{7,3},{8,10},{9,13},{10,... | collective-permute-start | bytes 12296 | tf_op jit(solution)/shard_map/ppermute | solution.py:736
  59.3 5.8 %collective-permute-start.4 = (bf16[8,16,1536]{2,1,0:T(8,128)(2,1)S(1)}, bf16[8,16,1536]{2,1,0:T(8,128)(2,1)S(1)}, u32[]{:S(2)}, u32[]{:S(2)}) collective-permute-start(bf16[8,16,1536]{2,1,0:T(8,128)(2,1)S(1)} %pad_maximum_fusion.2.refs_0_), channel_id=1, source_target_pairs={{0,1},{1,0},{2,3},{3,2},{4,5},{5,4},{6,7},{7,6},{8,9},{9,8},{10,11... | collective-permute-start | bytes 1179656 | tf_op jit(solution)/shard_map/ppermute | solution.py:737
  60.7 4.4 %collective-permute-start.5 = (bf16[8,16,1536]{2,1,0:T(8,128)(2,1)S(1)}, bf16[8,16,1536]{2,1,0:T(8,128)(2,1)}, u32[]{:S(2)}, u32[]{:S(2)}) collective-permute-start(bf16[8,16,1536]{2,1,0:T(8,128)(2,1)S(1)} %collective-permute-done.3.refs_1_), channel_id=1, source_target_pairs={{0,1},{1,0},{2,3},{3,2},{4,5},{5,4},{6,7},{7,6},{8,9},{9,8},{10,11... | collective-permute-start | bytes 1179656 | tf_op jit(solution)/shard_map/ppermute | solution.py:738
  71.7 3.8 %collective-permute-start.12 = (bf16[160,1024]{1,0:T(8,128)(2,1)}, bf16[160,1024]{1,0:T(8,128)(2,1)S(1)}, u32[]{:S(2)}, u32[]{:S(2)}) collective-permute-start(bf16[160,1024]{1,0:T(8,128)(2,1)} %get-tuple-element.41), channel_id=1, source_target_pairs={{0,1},{1,2},{2,3},{3,4},{4,5},{5,6},{6,7},{7,8},{8,9},{9,10},{10,1... | collective-permute-start | bytes 983048 | tf_op jit(solution)/shard_map/ppermute | solution.py:768
  73.9 4.1 %collective-permute-start.13 = (bf16[160,1024]{1,0:T(8,128)(2,1)}, bf16[160,1024]{1,0:T(8,128)(2,1)S(1)}, u32[]{:S(2)}, u32[]{:S(2)}) collective-permute-start(bf16[160,1024]{1,0:T(8,128)(2,1)} %get-tuple-element.42), channel_id=1, source_target_pairs={{1,0},{2,1},{3,2},{4,3},{5,4},{6,5},{7,6},{8,7},{9,8},{10,9},{11,1... | collective-permute-start | bytes 983048 | tf_op jit(solution)/shard_map/ppermute | solution.py:768
  107.2 62.3 %collective-permute-start.32 = (bf16[16,144,512]{2,1,0:T(8,128)(2,1)}, bf16[16,144,512]{2,1,0:T(8,128)(2,1)S(1)}, u32[]{:S(2)}, u32[]{:S(2)}) collective-permute-start(bf16[16,144,512]{2,1,0:T(8,128)(2,1)} %get-tuple-element.64), channel_id=1, source_target_pairs={{0,1},{1,0},{2,3},{3,2},{4,5},{5,4},{6,7},{7,6},{8,9},{9,8},{10,11... | collective-permute-start | bytes 7077896 | tf_op jit(solution)/shard_map/ppermute | solution.py:742
  133.0 4.9 %collective-permute-start.21 = (bf16[160,1024]{1,0:T(8,128)(2,1)}, bf16[160,1024]{1,0:T(8,128)(2,1)S(1)}, u32[]{:S(2)}, u32[]{:S(2)}) collective-permute-start(bf16[160,1024]{1,0:T(8,128)(2,1)} %get-tuple-element.57), channel_id=1, source_target_pairs={{1,0},{2,1},{3,2},{4,3},{5,4},{6,5},{7,6},{8,7},{9,8},{10,9},{11,1... | collective-permute-start | bytes 983048 | tf_op jit(solution)/shard_map/ppermute | solution.py:768
  148.1 6.4 %collective-permute-start.22 = (f32[16,1,256]{2,1,0:T(1,128)}, f32[16,1,256]{2,1,0:T(1,128)S(1)}, u32[]{:S(2)}, u32[]{:S(2)}) collective-permute-start(f32[16,1,256]{2,1,0:T(1,128)} %get-tuple-element.60), channel_id=1, source_target_pairs={{0,1},{1,0},{2,3},{3,2},{4,5},{5,4},{6,7},{7,6},{8,9},{9,8},{10,11... | collective-permute-start | bytes 49160 | tf_op jit(solution)/shard_map/ppermute | solution.py:742
  155.2 4.2 %collective-permute-start.23 = (f32[8,1,256]{2,1,0:T(1,128)S(1)}, f32[8,1,256]{2,1,0:T(1,128)S(1)}, u32[]{:S(2)}, u32[]{:S(2)}) collective-permute-start(f32[8,1,256]{2,1,0:T(1,128)S(1)} %get-tuple-element.83), channel_id=1, source_target_pairs={{0,2},{1,5},{2,0},{3,7},{4,6},{5,1},{6,4},{7,3},{8,10},{9,13},{10,... | collective-permute-start | bytes 24584 | tf_op jit(solution)/shard_map/ppermute | solution.py:751
  160.8 11.6 %collective-permute-start.27 = (bf16[16,16,1536]{2,1,0:T(8,128)(2,1)}, bf16[16,16,1536]{2,1,0:T(8,128)(2,1)S(1)}, u32[]{:S(2)}, u32[]{:S(2)}) collective-permute-start(bf16[16,16,1536]{2,1,0:T(8,128)(2,1)} %get-tuple-element.62), channel_id=1, source_target_pairs={{0,1},{1,0},{2,3},{3,2},{4,5},{5,4},{6,7},{7,6},{8,9},{9,8},{10,11... | collective-permute-start | bytes 2359304 | tf_op jit(solution)/shard_map/ppermute | solution.py:742
  166.7 6.5 %collective-permute-start.26 = (f32[1,1,256]{2,1,0:T(1,128)S(1)}, f32[1,1,256]{2,1,0:T(1,128)S(1)}, u32[]{:S(2)}, u32[]{:S(2)}) collective-permute-start(f32[1,1,256]{2,1,0:T(1,128)S(1)} %slice_add_fusion.18), channel_id=1, source_target_pairs={{0,16},{1,3},{2,18},{3,1},{4,20},{5,7},{6,22},{7,5},{8,24},{9,11},... | collective-permute-start | bytes 3080 | tf_op jit(solution)/shard_map/ppermute | solution.py:751
  170.3 21.9 %collective-permute-start.33 = (bf16[8,144,512]{2,1,0:T(8,128)(2,1)S(1)}, bf16[8,144,512]{2,1,0:T(8,128)(2,1)S(1)}, u32[]{:S(2)}, u32[]{:S(2)}) collective-permute-start(bf16[8,144,512]{2,1,0:T(8,128)(2,1)S(1)} %get-tuple-element.65), channel_id=1, source_target_pairs={{0,2},{1,5},{2,0},{3,7},{4,6},{5,1},{6,4},{7,3},{8,10},{9,13},{10,... | collective-permute-start | bytes 3538952 | tf_op jit(solution)/shard_map/ppermute | solution.py:751
  172.6 18.2 %collective-permute-start.28 = (bf16[8,16,1536]{2,1,0:T(8,128)(2,1)S(1)}, bf16[8,16,1536]{2,1,0:T(8,128)(2,1)S(1)}, u32[]{:S(2)}, u32[]{:S(2)}) collective-permute-start(bf16[8,16,1536]{2,1,0:T(8,128)(2,1)S(1)} %get-tuple-element.69), channel_id=1, source_target_pairs={{0,2},{1,5},{2,0},{3,7},{4,6},{5,1},{6,4},{7,3},{8,10},{9,13},{10,... | collective-permute-start | bytes 1179656 | tf_op jit(solution)/shard_map/ppermute | solution.py:751
  190.9 5.7 %collective-permute-start.29 = (bf16[4,16,1536]{2,1,0:T(8,128)(2,1)S(1)}, bf16[4,16,1536]{2,1,0:T(8,128)(2,1)S(1)}, u32[]{:S(2)}, u32[]{:S(2)}) collective-permute-start(bf16[4,16,1536]{2,1,0:T(8,128)(2,1)S(1)} %get-tuple-element.73), channel_id=1, source_target_pairs={{0,4},{1,9},{2,6},{3,11},{4,0},{5,13},{6,2},{7,15},{8,12},{9,1},{1... | collective-permute-start | bytes 589832 | tf_op jit(solution)/shard_map/ppermute | solution.py:751
  192.7 10.2 %collective-permute-start.34 = (bf16[4,144,512]{2,1,0:T(8,128)(2,1)S(1)}, bf16[4,144,512]{2,1,0:T(8,128)(2,1)S(1)}, u32[]{:S(2)}, u32[]{:S(2)}) collective-permute-start(bf16[4,144,512]{2,1,0:T(8,128)(2,1)S(1)} %get-tuple-element.67), channel_id=1, source_target_pairs={{0,4},{1,9},{2,6},{3,11},{4,0},{5,13},{6,2},{7,15},{8,12},{9,1},{1... | collective-permute-start | bytes 1769480 | tf_op jit(solution)/shard_map/ppermute | solution.py:751
  196.7 7.5 %collective-permute-start.30 = (bf16[2,16,1536]{2,1,0:T(8,128)(2,1)S(1)}, bf16[2,16,1536]{2,1,0:T(8,128)(2,1)S(1)}, u32[]{:S(2)}, u32[]{:S(2)}) collective-permute-start(bf16[2,16,1536]{2,1,0:T(8,128)(2,1)S(1)} %get-tuple-element.75), channel_id=1, source_target_pairs={{0,8},{1,17},{2,10},{3,19},{4,12},{5,21},{6,14},{7,23},{8,0},{9,25... | collective-permute-start | bytes 294920 | tf_op jit(solution)/shard_map/ppermute | solution.py:751
  203.1 9.6 %collective-permute-start.35 = (bf16[2,144,512]{2,1,0:T(8,128)(2,1)S(1)}, bf16[2,144,512]{2,1,0:T(8,128)(2,1)S(1)}, u32[]{:S(2)}, u32[]{:S(2)}) collective-permute-start(bf16[2,144,512]{2,1,0:T(8,128)(2,1)S(1)} %get-tuple-element.71), channel_id=1, source_target_pairs={{0,8},{1,17},{2,10},{3,19},{4,12},{5,21},{6,14},{7,23},{8,0},{9,25... | collective-permute-start | bytes 884744 | tf_op jit(solution)/shard_map/ppermute | solution.py:751
  204.2 8.7 %collective-permute-start.31 = (bf16[1,16,1536]{2,1,0:T(8,128)(2,1)S(1)}, bf16[1,16,1536]{2,1,0:T(8,128)(2,1)S(1)}, u32[]{:S(2)}, u32[]{:S(2)}) collective-permute-start(bf16[1,16,1536]{2,1,0:T(8,128)(2,1)S(1)} %fusion.6), channel_id=1, source_target_pairs={{0,16},{1,3},{2,18},{3,1},{4,20},{5,7},{6,22},{7,5},{8,24},{9,11},... | collective-permute-start | bytes 147464 | tf_op jit(solution)/shard_map/ppermute | solution.py:751
  212.8 6.7 %collective-permute-start.36 = (bf16[1,144,512]{2,1,0:T(8,128)(2,1)S(1)}, bf16[1,144,512]{2,1,0:T(8,128)(2,1)S(1)}, u32[]{:S(2)}, u32[]{:S(2)}) collective-permute-start(bf16[1,144,512]{2,1,0:T(8,128)(2,1)S(1)} %fusion.3), channel_id=1, source_target_pairs={{0,16},{1,3},{2,18},{3,1},{4,20},{5,7},{6,22},{7,5},{8,24},{9,11},... | collective-permute-start | bytes 442376 | tf_op jit(solution)/shard_map/ppermute | solution.py:751
  (30 other events, 307.3 us)

commit v3 on v2

v3 whole, which is shorter than its diff:
```python
import functools
import math

import jax
import jax.numpy as jnp
from jax import lax
from jax.experimental import pallas as pl
from jax.experimental.pallas import tpu as pltpu
from jax.sharding import PartitionSpec as P

HEAD_DIM = 64
LEVELS = 5
HALO = 32
BLOCK = 64
WINDOW = BLOCK + 2 * HALO
QUAD = 4
QUAD_WIDTH = QUAD * HEAD_DIM
PIECES = 4
BLOCKS = 32
LINE = 128
FAR = 1 << 26
SEQ_STEP = 1 << 21
MIB = 1024 * 1024

f32 = jnp.float32
bf16 = jnp.bfloat16


class Plan:
    def __init__(self, rows):
        self.rows = rows
        self.counts = [rows >> level for level in range(LEVELS)]
        self.padded = [-(-count // BLOCK) * BLOCK for count in self.counts]
        self.query_at = [sum(self.padded[:level]) for level in range(LEVELS)]
        self.query_rows = sum(self.padded)
        self.key_at = [self.query_at[level] + 2 * HALO * level for level in range(LEVELS)]
        self.key_rows = self.query_rows + 2 * HALO * LEVELS
        self.blocks = [
            (level, part)
            for level in range(LEVELS)
            for part in range(self.padded[level] // BLOCK)
        ]


def dot_nn(a, b):
    return lax.dot_general(a, b, (((1,), (0,)), ((), ())), preferred_element_type=f32)


def dot_nt(a, b):
    return lax.dot_general(a, b, (((1,), (1,)), ((), ())), preferred_element_type=f32)


def dot_tn(a, b):
    return lax.dot_general(a, b, (((0,), (0,)), ((), ())), preferred_element_type=f32)


def spec(count):
    return [pl.BlockSpec(memory_space=pltpu.VMEM)] * count


SCALARS = pl.BlockSpec(memory_space=pltpu.SMEM)


def slot_facts(info, slot, total):
    number = jnp.zeros(slot.shape, jnp.int32)
    for s in range(3):
        number = number + (slot >= info[7 + s]).astype(jnp.int32)
    begin = jnp.where(number == 0, info[4], jnp.where(number == 1, info[5], info[6]))
    length = jnp.where(number == 0, info[1], jnp.where(number == 1, info[2], info[3]))
    inside = (slot >= 0) & (slot < total) & (number < 3)
    return number, slot - begin, length, inside


def tile_codes(info, coarse, level, total, outside):
    number, offset, _, inside = slot_facts(info, coarse << level, total)
    wide = jnp.where(inside, number * SEQ_STEP + (offset >> (level + 4)), outside)
    fine = number * SEQ_STEP + (offset >> (level + 3))
    return wide, fine


def admitted(query_codes, key_codes, level):
    near = jnp.abs(query_codes[0] - key_codes[0]) <= 1
    if level > 0:
        near = near & (jnp.abs(query_codes[1] - key_codes[1]) >= 2)
    return jnp.where(near, 1.0, 0.0)


def live_counts(info, coarse, level, total):
    _, offset, length, inside = slot_facts(info, coarse << level, total)
    span = 1 << level
    return jnp.where(inside, jnp.clip(length - offset, 0, span), 0).astype(f32)


def head_masks(rows):
    lane = lax.broadcasted_iota(jnp.int32, (rows, QUAD_WIDTH), 1) // HEAD_DIM
    return [jnp.where(lane == h, 1.0, 0.0) for h in range(QUAD)]


def spread_heads(block, masks):
    return jnp.concatenate([block * m for m in masks], axis=0)


def gather_heads(stacked, masks):
    rows = stacked.shape[0] // QUAD
    total = stacked[:rows] * masks[0]
    for h in range(1, QUAD):
        total = total + stacked[h * rows : (h + 1) * rows] * masks[h]
    return total


def put(chunks, rows, block):
    for part in range(QUAD_WIDTH // 128):
        chunks[part, rows, :] = block[:, part * 128 : part * 128 + 128]


def take(chunks, rows):
    return jnp.concatenate([chunks[part, rows, :] for part in range(QUAD_WIDTH // 128)], axis=1)


def is_even(info):
    return (info[0] & 1) == 0


def params(size):
    return pltpu.CompilerParams(vmem_limit_bytes=size * MIB)


def cost(micros):
    return pl.CostEstimate(flops=1, bytes_accessed=1, transcendentals=0)


def fill_extended(plan, info, own, from_twin, from_other, extended):
    even = is_even(info)
    for level in range(LEVELS):
        at, count, mine = plan.key_at[level], plan.counts[level], plan.query_at[level]
        halo = pl.ds(HALO * level, HALO)
        after = at + HALO + count
        twin_at = pl.multiple_of(jnp.where(even, after, at), HALO)
        other_at = pl.multiple_of(jnp.where(even, at, after), HALO)
        extended[pl.ds(at + HALO, count), :] = own[pl.ds(mine, count), :]
        extended[pl.ds(twin_at, HALO), :] = from_twin[halo, :]
        extended[pl.ds(other_at, HALO), :] = from_other[halo, :]
        rest = plan.padded[level] - count
        if rest:
            extended[pl.ds(at + 2 * HALO + count, rest), :] = jnp.zeros(
                (rest, extended.shape[1]), bf16
            )


def ln_stats(values):
    center = values - jnp.mean(values, axis=-1, keepdims=True)
    spread = jnp.mean(center * center, axis=-1, keepdims=True)
    return center, lax.rsqrt(spread + 1e-05)


def ln_back(grad, center, rstd, gain):
    hat = center * rstd
    scaled = grad * gain
    mean_one = jnp.mean(scaled, axis=-1, keepdims=True)
    mean_two = jnp.mean(scaled * hat, axis=-1, keepdims=True)
    return rstd * (scaled - mean_one - hat * mean_two), grad * hat


def column_sum(values):
    return jnp.sum(values, axis=0, keepdims=True)


def unpack_vectors(table, wide):
    blocks, lanes = table.shape

    def one(first, each):
        length = blocks * each
        source = lax.broadcasted_iota(jnp.int32, (lanes, length), 0)
        target = lax.broadcasted_iota(jnp.int32, (lanes, length), 1)
        pick = jnp.where(source == first + (target & (each - 1)), 1.0, 0.0).astype(bf16)
        spreaded = dot_nn(table, pick)
        block = lax.broadcasted_iota(jnp.int32, (blocks, length), 0)
        lane = lax.broadcasted_iota(jnp.int32, (blocks, length), 1)
        return column_sum(jnp.where(lane // each == block, spreaded, 0.0))

    size = wide // 4
    return [one(k * size, size) for k in range(6)], one(LINE, wide)


def pack_vectors(vectors, last, blocks, lanes):
    size = last.shape[1] // blocks // 4

    def one(row, first, each):
        length = blocks * each
        source = lax.broadcasted_iota(jnp.int32, (length, lanes), 0)
        target = lax.broadcasted_iota(jnp.int32, (length, lanes), 1)
        pick = jnp.where(target == first + (source & (each - 1)), 1.0, 0.0).astype(bf16)
        block = lax.broadcasted_iota(jnp.int32, (blocks, length), 0)
        lane = lax.broadcasted_iota(jnp.int32, (blocks, length), 1)
        spreaded = jnp.where(lane // each == block, row, 0.0)
        total = jnp.zeros((blocks, lanes), f32)
        for _ in range(3):
            part = spreaded.astype(bf16)
            total = total + dot_nn(part, pick)
            spreaded = spreaded - part.astype(f32)
        return total

    total = one(last, LINE, 4 * size)
    for k, vector in enumerate(vectors):
        total = total + one(vector, k * size, size)
    return total


def project_kernel(
    plan, total, info, inverse, tokens, *refs
):
    pieces, outs = refs[:PIECES], refs[PIECES:]
    queries, pairs, twins, others = (outs[2 * k : 2 * k + 2] for k in range(4))
    weight, vectors, shift_out, table = outs[8:]
    rows, width = tokens.shape
    device = info[0]
    each = pieces[0].shape[0]
    block_rows = pieces[0].shape[1]
    main = pl.ds(0, 3 * width)
    side = pl.ds(3 * width, LINE)
    for p in range(PIECES * each):
        i = inverse[p]
        there = pl.ds(pl.multiple_of(i * block_rows, block_rows), block_rows)
        weight[there, :] = pieces[p // each][p % each, :, main]
        line = pieces[p // each][p % each, :, side].astype(f32)
        table[pl.ds(i, 1), :] = jnp.concatenate([line[0:1], line[1:2]], axis=1)
    singles, wide = unpack_vectors(table[...].astype(bf16), 4 * block_rows)
    for k, single in enumerate(singles):
        vectors[pl.ds(k, 1), :] = single
    shift_out[...] = wide
    values = tokens[...].astype(f32)
    center, rstd = ln_stats(values)
    low = (center * rstd * singles[0] + singles[1]).astype(bf16)
    pooled_rows = plan.query_rows - plan.query_at[1]
    row = lax.broadcasted_iota(jnp.int32, (pooled_rows, rows), 0)
    slot = lax.broadcasted_iota(jnp.int32, (pooled_rows, rows), 1)
    first = jnp.zeros((pooled_rows, rows), jnp.int32)
    shift = jnp.zeros((pooled_rows, rows), jnp.int32)
    share = jnp.zeros((pooled_rows, 1), f32)
    row_one = lax.broadcasted_iota(jnp.int32, (pooled_rows, 1), 0)
    for level in range(1, LEVELS):
        at = plan.query_at[level] - plan.query_at[1]
        first = jnp.where(row >= at, at, first)
        shift = jnp.where(row >= at, level, shift)
        share = jnp.where(row_one >= at, 0.5**level, share)
    pool = jnp.where((slot >> shift) == row - first, 1.0, 0.0).astype(bf16)
    places = device * rows + lax.broadcasted_iota(jnp.int32, (rows, QUAD_WIDTH), 0)
    live = live_counts(info, places, 0, total)
    lanes = QUAD_WIDTH
    for part in range(3 * width // lanes):
        columns = pl.ds(part * lanes, lanes)
        block = dot_nn(low, weight[:, columns]).astype(bf16)
        if part * lanes >= 2 * width:
            block = (block.astype(f32) * live).astype(bf16)
        pooled = dot_nn(pool, block)
        if part * lanes < 2 * width:
            pooled = pooled * share
        quad = part % 2
        if part * lanes < width:
            scale = 1.0 / math.sqrt(HEAD_DIM)
            queries[quad][pl.ds(0, rows), :] = (block.astype(f32) * scale).astype(bf16)
            queries[quad][pl.ds(rows, pooled_rows), :] = (pooled * scale).astype(bf16)
        else:
            there = pl.ds((part * lanes // width - 1) * lanes, lanes)
            pairs[quad][pl.ds(0, rows), there] = block
            pairs[quad][pl.ds(rows, pooled_rows), there] = pooled.astype(bf16)
    even = is_even(info)
    for quad in range(2):
        for level in range(LEVELS):
            at, count = plan.query_at[level], plan.counts[level]
            halo = pl.ds(HALO * level, HALO)
            last = at + count - HALO
            twin_at = pl.multiple_of(jnp.where(even, last, at), HALO)
            other_at = pl.multiple_of(jnp.where(even, at, last), HALO)
            twins[quad][halo, :] = pairs[quad][pl.ds(twin_at, HALO), :]
            others[quad][halo, :] = pairs[quad][pl.ds(other_at, HALO), :]


def project(plan, total, info, inverse, tokens, pieces):
    rows, width = tokens.shape
    halo = LEVELS * HALO
    blocks = PIECES * pieces[0].shape[0]
    depth = blocks * pieces[0].shape[1]
    half = width // 2
    outs = pl.pallas_call(
        functools.partial(project_kernel, plan, total),
        out_shape=(
            [jax.ShapeDtypeStruct((plan.query_rows, half), bf16)] * 2
            + [jax.ShapeDtypeStruct((plan.query_rows, 2 * half), bf16)] * 2
            + [jax.ShapeDtypeStruct((halo, 2 * half), bf16)] * 4
            + [
                jax.ShapeDtypeStruct((depth, 3 * width), bf16),
                jax.ShapeDtypeStruct((8, depth), f32),
                jax.ShapeDtypeStruct((1, 4 * depth), f32),
            ]
        ),
        in_specs=[SCALARS, SCALARS] + spec(1 + PIECES),
        out_specs=spec(11),
        scratch_shapes=[pltpu.VMEM((blocks, 2 * LINE), f32)],
        compiler_params=params(16),
        name="project",
        cost_estimate=cost(3.3),
    )(info, inverse, tokens, *pieces)
    return [outs[2 * k : 2 * k + 2] for k in range(4)] + list(outs[8:])


def attend_kernel(
    plan,
    total,
    info,
    query,
    pairs,
    from_twin,
    from_other,
    attended,
    mixed,
    scale,
    extended,
    numer,
    denom,
):
    rows = plan.rows
    width = query.shape[1]
    device = info[0]
    fill_extended(plan, info, pairs, from_twin, from_other, extended)
    masks = head_masks(BLOCK)
    low_masks = [m.astype(bf16) for m in masks]
    for level, part in plan.blocks:
        count = plan.counts[level]
        at = plan.query_at[level] + BLOCK * part
        window = plan.key_at[level] + BLOCK * part
        first = device * count + BLOCK * part
        row = first + lax.broadcasted_iota(jnp.int32, (BLOCK, WINDOW), 0)
        column = first - HALO + lax.broadcasted_iota(jnp.int32, (BLOCK, WINDOW), 1)
        allowed = admitted(
            tile_codes(info, row, level, total, FAR),
            tile_codes(info, column, level, total, -FAR),
            level,
        )
        allowed = jnp.concatenate([allowed] * QUAD, axis=0) > 0.0
        key_row = first - HALO + lax.broadcasted_iota(jnp.int32, (WINDOW, 128), 0)
        counts = live_counts(info, key_row, level, total).astype(bf16)
        counts = jnp.concatenate([counts] * (QUAD_WIDTH // 128), axis=1)
        here = pl.ds(at, BLOCK)
        q = spread_heads(query[here, :], low_masks)
        k = extended[pl.ds(window, WINDOW), pl.ds(0, width)]
        v = extended[pl.ds(window, WINDOW), pl.ds(width, width)]
        weight = jnp.where(allowed, jnp.exp(dot_nt(q, k)), 0.0).astype(bf16)
        put(numer, here, gather_heads(dot_nn(weight, v), masks))
        put(denom, here, gather_heads(dot_nn(weight, counts), masks))
    for sums in (numer, denom):
        for level in range(LEVELS - 1, 0, -1):
            count = plan.counts[level]
            for chunk in range(width // 128):
                upper = sums[chunk, pl.ds(plan.query_at[level], count), :]
                for parity in range(2):
                    there = pl.ds(plan.query_at[level - 1] + parity, count, stride=2)
                    sums[chunk, there, :] = sums[chunk, there, :] + upper
    places = device * rows + lax.broadcasted_iota(jnp.int32, (rows, 128), 0)
    live = live_counts(info, places, 0, total)
    for chunk in range(width // 128):
        lanes = pl.ds(chunk * 128, 128)
        factor = live / (denom[chunk, pl.ds(0, rows), :] + 1.0 - live)
        value = numer[chunk, pl.ds(0, rows), :] * factor
        scale[:, lanes] = factor
        mixed[:, lanes] = value
        attended[:, lanes] = value.astype(bf16)


def attend(plan, total, info, query, pairs, from_twin, from_other):
    rows, width = plan.rows, query.shape[1]
    return pl.pallas_call(
        functools.partial(attend_kernel, plan, total),
        out_shape=(
            jax.ShapeDtypeStruct((rows, width), bf16),
            jax.ShapeDtypeStruct((rows, width), f32),
            jax.ShapeDtypeStruct((rows, width), f32),
        ),
        in_specs=[SCALARS] + spec(4),
        out_specs=tuple(spec(3)),
        scratch_shapes=[
            pltpu.VMEM((plan.key_rows, 2 * width), bf16),
            pltpu.VMEM((width // 128, plan.query_rows, 128), f32),
            pltpu.VMEM((width // 128, plan.query_rows, 128), f32),
        ],
        compiler_params=params(12),
        name="attend",
        cost_estimate=cost(5),
    )(info, query, pairs, from_twin, from_other)


def middle_kernel(
    parts,
    inverse,
    tokens,
    cotangent,
    attended_a,
    attended_b,
    vectors,
    shift_in,
    *refs,
):
    pieces = refs[:parts]
    result, grad_resid, mixed_a, mixed_b, own, low_half, high_half, sums, sum_in = refs[
        parts : parts + 9
    ]
    w_out, w_in, w_back, normed_two, grad_normed, outer, tall, flat = refs[parts + 9 :]
    other = (low_half, high_half)
    width = tokens.shape[1]
    wide = width // 2
    each, stack = pieces[0].shape[0], pieces[0].shape[1]
    half = own.shape[0]
    chunks = w_in.shape[0]
    block = width // (parts * each)
    tall_block = chunks * block
    in_at, back_at = block, block + tall_block
    for p in range(parts * each):
        piece, q = pieces[p // each], p % each
        i = inverse[p]
        rows = pl.ds(pl.multiple_of(i * block, block), block)
        w_out[rows, :] = piece[q, pl.ds(0, block), :]
        for c in range(chunks):
            w_in[c, rows, :] = piece[q, pl.ds(in_at + block * c, block), :]
        rows = pl.ds(pl.multiple_of(i * tall_block, tall_block), tall_block)
        w_back[rows, :] = piece[q, pl.ds(back_at, tall_block), :]
    gain = vectors[pl.ds(3, 1), :]
    resid = tokens[...].astype(f32) + dot_nn(attended_a[...], w_out[pl.ds(0, wide), :])
    resid = resid + dot_nn(attended_b[...], w_out[pl.ds(wide, wide), :]) + vectors[pl.ds(2, 1), :]
    center, rstd = ln_stats(resid)
    normed_two[...] = (center * rstd * gain + vectors[pl.ds(4, 1), :]).astype(bf16)
    grad_resid[...] = resid
    outer[...] = jnp.zeros(outer.shape, f32)
    grad_normed[...] = jnp.zeros(grad_normed.shape, f32)

    def chunk_step(c, carry):
        there = pl.ds(pl.multiple_of(c * width, width), width)
        inner = dot_nn(normed_two[...], w_in[c]) + shift_in[:, there]
        cdf = 0.5 * (1.0 + lax.erf(inner * math.sqrt(0.5)))
        active = (inner * cdf).astype(bf16)
        slope = cdf + inner * (jnp.exp(-0.5 * inner * inner) * (1.0 / math.sqrt(2.0 * math.pi)))
        back = w_back[there, :]
        grad_inner = slope * dot_nt(cotangent[...], back)
        low = grad_inner.astype(bf16)
        outer[...] += dot_nn(active, back)
        tall[there, :] = dot_tn(active, cotangent[...])
        sum_in[:, there] = column_sum(low.astype(f32))
        flat[...] = dot_tn(normed_two[...], low)
        for p in range(2 * half):
            i = inverse[p]
            rows = flat[pl.ds(pl.multiple_of(i * block, block), block), :]
            at = pl.ds(pl.multiple_of(in_at + c * block, block), block)
            if p < half:
                own[p, at, :] = rows
            else:
                other[(p - half) // 8][(p - half) % 8, at, :] = rows.astype(bf16)
        grad_normed[...] += dot_nt(low, w_in[c])
        return carry

    lax.fori_loop(0, chunks, chunk_step, 0)
    resid = grad_resid[...]
    result[...] = (resid + outer[...] + vectors[pl.ds(5, 1), :]).astype(bf16)
    center, rstd = ln_stats(resid)
    grad_in, gain_terms = ln_back(grad_normed[...], center, rstd, gain)
    grad_out = cotangent[...].astype(f32)
    total = grad_out + grad_in
    grad_resid[...] = total
    low = total.astype(bf16)
    sums[pl.ds(0, 1), :] = jnp.zeros((1, width), f32)
    sums[pl.ds(1, 1), :] = jnp.zeros((1, width), f32)
    sums[pl.ds(2, 1), :] = column_sum(low.astype(f32))
    sums[pl.ds(3, 1), :] = column_sum(gain_terms)
    sums[pl.ds(4, 1), :] = column_sum(grad_normed[...])
    sums[pl.ds(5, 1), :] = column_sum(grad_out)
    for part, (attended, mixed) in enumerate(((attended_a, mixed_a), (attended_b, mixed_b))):
        lines = pl.ds(part * wide, wide)
        mixed[...] = dot_nt(low, w_out[lines, :])
        flat[lines, :] = dot_tn(attended[...], low)
    for p in range(2 * half):
        i = inverse[p]
        rows = flat[pl.ds(pl.multiple_of(i * block, block), block), :]
        tall_rows = tall[pl.ds(pl.multiple_of(i * tall_block, tall_block), tall_block), :]
        if p < half:
            own[p, pl.ds(0, block), :] = rows
            own[p, pl.ds(back_at, tall_block), :] = tall_rows
        else:
            there = other[(p - half) // 8]
            there[(p - half) % 8, pl.ds(0, block), :] = rows.astype(bf16)
            there[(p - half) % 8, pl.ds(back_at, tall_block), :] = tall_rows.astype(bf16)


def middle(inverse, tokens, cotangent, attended, vectors, shift_in, pieces):
    parts = len(pieces)
    rows, width = tokens.shape
    hidden = shift_in.shape[1]
    chunks = hidden // width
    blocks = parts * pieces[0].shape[0]
    stack = pieces[0].shape[1]
    return pl.pallas_call(
        functools.partial(middle_kernel, parts),
        out_shape=(
            jax.ShapeDtypeStruct((rows, width), bf16),
            jax.ShapeDtypeStruct((rows, width), f32),
            jax.ShapeDtypeStruct((rows, width // 2), f32),
            jax.ShapeDtypeStruct((rows, width // 2), f32),
            jax.ShapeDtypeStruct((blocks // 2, stack, width), f32),
            jax.ShapeDtypeStruct((blocks // 4, stack, width), bf16),
            jax.ShapeDtypeStruct((blocks // 4, stack, width), bf16),
            jax.ShapeDtypeStruct((8, width), f32),
            jax.ShapeDtypeStruct((1, hidden), f32),
        ),
        in_specs=[SCALARS] + spec(6 + parts),
        out_specs=tuple(spec(9)),
        scratch_shapes=[
            pltpu.VMEM((width, width), bf16),
            pltpu.VMEM((chunks, width, width), bf16),
            pltpu.VMEM((hidden, width), bf16),
            pltpu.VMEM((rows, width), bf16),
            pltpu.VMEM((rows, width), f32),
            pltpu.VMEM((rows, width), f32),
            pltpu.VMEM((hidden, width), f32),
            pltpu.VMEM((width, width), f32),
        ],
        compiler_params=params(34),
        name="middle",
        cost_estimate=cost(12),
    )(inverse, tokens, cotangent, *attended, vectors, shift_in, *pieces)


def attend_back_kernel(
    plan,
    total,
    info,
    query,
    pairs,
    from_twin,
    from_other,
    grad_mixed,
    scale,
    mixed,
    grad_query,
    grad_pairs,
    grad_twin,
    grad_other,
    extended,
    grad_extended,
    grad_numer,
    grad_denom,
):
    rows = plan.rows
    width = query.shape[1]
    device = info[0]
    fill_extended(plan, info, pairs, from_twin, from_other, extended)
    grad_extended[...] = jnp.zeros(grad_extended.shape, f32)
    own = pl.ds(0, rows)
    for chunk in range(width // 128):
        lanes = pl.ds(chunk * 128, 128)
        value = grad_mixed[:, lanes] * scale[:, lanes]
        grad_numer[chunk, own, :] = value
        grad_denom[chunk, own, :] = -(value * mixed[:, lanes])
        for sums in (grad_numer, grad_denom):
            for level in range(1, LEVELS):
                count, at = plan.counts[level], plan.query_at[level]
                even = sums[chunk, pl.ds(plan.query_at[level - 1], count, stride=2), :]
                odd = sums[chunk, pl.ds(plan.query_at[level - 1] + 1, count, stride=2), :]
                sums[chunk, pl.ds(at, count), :] = even + odd
                rest = plan.padded[level] - count
                if rest:
                    sums[chunk, pl.ds(at + count, rest), :] = jnp.zeros((rest, 128), f32)
    masks = head_masks(BLOCK)
    low_masks = [m.astype(bf16) for m in masks]
    for level, part in plan.blocks:
        count = plan.counts[level]
        at = plan.query_at[level] + BLOCK * part
        window = plan.key_at[level] + BLOCK * part
        first = device * count + BLOCK * part
        key_row = first - HALO + lax.broadcasted_iota(jnp.int32, (WINDOW, 128), 0)
        lane = lax.broadcasted_iota(jnp.int32, (WINDOW, 128), 1)
        row = first + (lane & (BLOCK - 1))
        allowed = admitted(
            tile_codes(info, row, level, total, FAR),
            tile_codes(info, key_row, level, total, -FAR),
            level,
        )
        allowed = jnp.concatenate([allowed] * (QUAD * BLOCK // 128), axis=1) > 0.0
        counts = live_counts(info, key_row, level, total).astype(bf16)
        here = pl.ds(at, BLOCK)
        there = pl.ds(window, WINDOW)
        keys = pl.ds(0, width)
        values = pl.ds(width, width)
        q = spread_heads(query[here, :], low_masks)
        g = spread_heads(take(grad_numer, here).astype(bf16), low_masks)
        d = spread_heads(take(grad_denom, here).astype(bf16), low_masks)
        k = extended[there, keys]
        v = extended[there, values]
        value_and_count = jnp.concatenate([v] + [counts] * (QUAD_WIDTH // 128), axis=1)
        weight = jnp.where(allowed, jnp.exp(dot_nt(k, q)), 0.0)
        probs = weight.astype(bf16)
        grad_probs = dot_nt(value_and_count, jnp.concatenate([g, d], axis=1))
        grad_score = (grad_probs * weight).astype(bf16)
        grad_query[here, :] = gather_heads(dot_tn(grad_score, k), masks) * (
            1.0 / math.sqrt(HEAD_DIM)
        )
        grad_extended[there, keys] += dot_nn(grad_score, q)
        grad_extended[there, values] += dot_nn(probs, g)
    even = is_even(info)
    for level in range(LEVELS):
        at, count, mine = plan.key_at[level], plan.counts[level], plan.query_at[level]
        halo = pl.ds(HALO * level, HALO)
        last = at + HALO + count
        twin_at = pl.multiple_of(jnp.where(even, last, at), HALO)
        other_at = pl.multiple_of(jnp.where(even, at, last), HALO)
        grad_twin[halo, :] = grad_extended[pl.ds(twin_at, HALO), :].astype(bf16)
        grad_other[halo, :] = grad_extended[pl.ds(other_at, HALO), :].astype(bf16)
        grad_pairs[pl.ds(mine, count), :] = grad_extended[pl.ds(at + HALO, count), :]


def attend_back(plan, total, info, query, pairs, from_twin, from_other, grad_mixed, scale, mixed):
    width = query.shape[1]
    halo = LEVELS * HALO
    return pl.pallas_call(
        functools.partial(attend_back_kernel, plan, total),
        out_shape=(
            jax.ShapeDtypeStruct((plan.query_rows, width), f32),
            jax.ShapeDtypeStruct((plan.query_rows, 2 * width), f32),
            jax.ShapeDtypeStruct((halo, 2 * width), bf16),
            jax.ShapeDtypeStruct((halo, 2 * width), bf16),
        ),
        in_specs=[SCALARS] + spec(7),
        out_specs=tuple(spec(4)),
        scratch_shapes=[
            pltpu.VMEM((plan.key_rows, 2 * width), bf16),
            pltpu.VMEM((plan.key_rows, 2 * width), f32),
            pltpu.VMEM((width // 128, plan.query_rows, 128), f32),
            pltpu.VMEM((width // 128, plan.query_rows, 128), f32),
        ],
        compiler_params=params(18),
        name="attend_back",
        cost_estimate=cost(6.4),
    )(info, query, pairs, from_twin, from_other, grad_mixed, scale, mixed)


def finish_kernel(
    plan,
    total,
    info,
    inverse,
    tokens,
    weight,
    vectors,
    grad_resid,
    sums,
    sum_in,
    queries_a,
    queries_b,
    pairs_a,
    pairs_b,
    twin_a,
    twin_b,
    other_a,
    other_b,
    grad_tokens,
    own,
    low_half,
    high_half,
    work,
    joined,
    flat,
    table,
):
    rows, width = tokens.shape
    device = info[0]
    even = is_even(info)
    half_width = width // 2
    places = device * rows + lax.broadcasted_iota(jnp.int32, (rows, 128), 0)
    live = live_counts(info, places, 0, total)
    for chunk in range(3 * width // 128):
        part, lane = divmod(chunk * 128, width)
        quad, lane = divmod(lane, half_width)
        if part == 0:
            work[chunk] = (queries_a, queries_b)[quad][:, pl.ds(lane, 128)]
        else:
            lanes = pl.ds((part - 1) * half_width + lane, 128)
            work[chunk] = (pairs_a, pairs_b)[quad][:, lanes]
            for level in range(LEVELS):
                at, count = plan.query_at[level], plan.counts[level]
                halo = pl.ds(HALO * level, HALO)
                last = at + count - HALO
                twin_at = pl.multiple_of(jnp.where(even, last, at), HALO)
                other_at = pl.multiple_of(jnp.where(even, at, last), HALO)
                there = pl.ds(twin_at, HALO)
                work[chunk, there, :] += (twin_a, twin_b)[quad][halo, lanes].astype(f32)
                there = pl.ds(other_at, HALO)
                work[chunk, there, :] += (other_a, other_b)[quad][halo, lanes].astype(f32)
        for level in range(LEVELS - 1, 0, -1):
            count = plan.counts[level]
            upper = work[chunk, pl.ds(plan.query_at[level], count), :]
            if chunk * 128 < 2 * width:
                upper = upper * 0.5
            for parity in range(2):
                there = pl.ds(plan.query_at[level - 1] + parity, count, stride=2)
                work[chunk, there, :] = work[chunk, there, :] + upper
        value = work[chunk, pl.ds(0, rows), :]
        if chunk * 128 >= 2 * width:
            value = value * live
        joined[:, pl.ds(chunk * 128, 128)] = value.astype(bf16)
    values = tokens[...].astype(f32)
    center, rstd = ln_stats(values)
    gain = vectors[pl.ds(0, 1), :]
    normed = (center * rstd * gain + vectors[pl.ds(1, 1), :]).astype(bf16)
    half, block = own.shape[0], own.shape[1]
    other = (low_half, high_half)
    for part in range(3):
        columns = pl.ds(part * width, width)
        flat[...] = dot_tn(normed, joined[:, columns])
        for p in range(2 * half):
            i = inverse[p]
            lines = flat[pl.ds(pl.multiple_of(i * block, block), block), :]
            if p < half:
                own[p, :, columns] = lines
            else:
                other[(p - half) // 8][(p - half) % 8, :, columns] = lines.astype(bf16)
    grad_normed = dot_nt(joined[...], weight[...])
    grad_in, gain_terms = ln_back(grad_normed, center, rstd, gain)
    grad_tokens[...] = grad_resid[...] + grad_in
    singles = [column_sum(gain_terms), column_sum(grad_normed)]
    singles += [sums[pl.ds(k, 1), :] for k in range(2, 6)]
    table[...] = pack_vectors(singles, sum_in[...], 2 * half, table.shape[1])
    row = lax.broadcasted_iota(jnp.int32, (block, LINE), 0)
    side = pl.ds(3 * width, LINE)
    for p in range(2 * half):
        line = table[pl.ds(inverse[p], 1), :]
        lines = jnp.where(row == 0, line[:, :LINE], jnp.where(row == 1, line[:, LINE:], 0.0))
        if p < half:
            own[p, :, side] = lines
        else:
            other[(p - half) // 8][(p - half) % 8, :, side] = lines.astype(bf16)


def finish(plan, total, info, inverse, tokens, weight, *rest):
    rows, width = tokens.shape
    half = BLOCKS // 2
    block = width // BLOCKS
    return pl.pallas_call(
        functools.partial(finish_kernel, plan, total),
        out_shape=(
            jax.ShapeDtypeStruct((rows, width), f32),
            jax.ShapeDtypeStruct((half, block, 3 * width + LINE), f32),
            jax.ShapeDtypeStruct((half // 2, block, 3 * width + LINE), bf16),
            jax.ShapeDtypeStruct((half // 2, block, 3 * width + LINE), bf16),
        ),
        in_specs=[SCALARS, SCALARS] + spec(2 + len(rest)),
        out_specs=tuple(spec(4)),
        scratch_shapes=[
            pltpu.VMEM((3 * width // 128, plan.query_rows, 128), f32),
            pltpu.VMEM((rows, 3 * width), bf16),
            pltpu.VMEM((width, width), f32),
            pltpu.VMEM((BLOCKS, 2 * LINE), f32),
        ],
        compiler_params=params(28),
        name="finish",
        cost_estimate=cost(6.2),
    )(info, inverse, tokens, weight, *rest)


class Ring:
    def __init__(self, devices):
        self.devices = devices
        bits = [1 << k for k in range(devices.bit_length() - 2, 0, -1)]
        self.orders = (bits, bits[-1:] + bits[:-1])
        self.stages = len(bits)

    def partner(self, stage):
        return [(i, i ^ self.orders[i & 1][stage]) for i in range(self.devices)]

    def twin(self):
        return [(i, i ^ 1) for i in range(self.devices)]

    def places(self, device):
        found = []
        even = (device & 1) == 0
        for base, swap in ((device, False), (device ^ 1, True)):
            for position in range(1 << self.stages):
                masks = [
                    sum(order[k] for k in range(self.stages) if position >> k & 1)
                    for order in self.orders
                ]
                if swap:
                    masks = masks[::-1]
                found.append(base ^ jnp.where(even, *masks))
        return found

    def step(self, stage, arrays):
        route = self.twin() if stage == self.stages else self.partner(stage)
        return [lax.ppermute(item, "seq", route) for item in arrays]

    def fold(self, stage, own, low, high):
        half = 1 << stage
        sent = (own[half:] + high.astype(f32)).astype(bf16)
        kept = own[:half] + low.astype(f32)
        return kept, sent


def halves(item):
    half = item.shape[0] // 2
    return item[:half], item[half:]


def join(held, came):
    return [jnp.concatenate(pair) for pair in zip(held, came)]


def pack_kernel(ring, lengths, w_qkv, w_out, w_in, w_back, *refs):
    vectors, (info, inverse, first, second, staged) = refs[:-5], refs[-5:]
    device = lax.axis_index("seq")
    info[0] = device
    start = jnp.int32(0)
    for k in range(3):
        length = lengths[k]
        info[1 + k] = length
        info[4 + k] = start
        start = start + (length + 15) // 16 * 16
        info[7 + k] = start
    for place, block in enumerate(ring.places(device)):
        inverse[place] = block
    block, width = w_qkv.shape
    first[0, :, pl.ds(0, width)] = w_qkv[...]
    staged[...] = jnp.zeros(staged.shape, f32)
    for k, vector in enumerate(vectors):
        size = vector.shape[0]
        row, lane = (0, k * block) if k < 6 else (1, 0)
        staged[pl.ds(row, 1), pl.ds(lane, size)] = vector[...].astype(f32).reshape(1, size)
    first[0, :, pl.ds(width, LINE)] = staged[...].astype(bf16)
    block, width = w_out.shape
    chunks = w_in.shape[1] // width
    second[0, pl.ds(0, block), :] = w_out[...]
    for c in range(chunks):
        second[0, pl.ds(block * (c + 1), block), :] = w_in[:, pl.ds(c * width, width)]
    second[0, pl.ds(block * (chunks + 1), block * chunks), :] = w_back[...]


def pack(ring, lengths, w_qkv, w_out, w_in, w_back, vectors):
    block, width = w_out.shape
    rows = block + w_in.shape[1] // width * block + w_back.shape[0]
    return pl.pallas_call(
        functools.partial(pack_kernel, ring),
        out_shape=(
            jax.ShapeDtypeStruct((10,), jnp.int32),
            jax.ShapeDtypeStruct((BLOCKS,), jnp.int32),
            jax.ShapeDtypeStruct((1, block, w_qkv.shape[1] + LINE), bf16),
            jax.ShapeDtypeStruct((1, rows, width), bf16),
        ),
        in_specs=[SCALARS] + spec(4 + len(vectors)),
        out_specs=(SCALARS, SCALARS) + tuple(spec(2)),
        scratch_shapes=[pltpu.VMEM((block, LINE), f32)],
        compiler_params=params(62),
        name="pack",
        cost_estimate=cost(1.5),
    )(lengths, w_qkv, w_out, w_in, w_back, *vectors)


def unpack_kernel(kept_one, came_one, kept_two, came_two, *outs):
    block, width = kept_one.shape[1] , kept_two.shape[2]
    w_qkv, w_out, w_in, w_back = outs[:4]
    main = pl.ds(0, 3 * width)
    w_qkv[...] = kept_one[0, :, main] + came_one[0, :, main].astype(f32)
    side = pl.ds(3 * width, LINE)
    lines = kept_one[0, :, side] + came_one[0, :, side].astype(f32)
    for k, out in enumerate(outs[4:]):
        size = out.shape[0]
        row, lane = (0, k * block) if k < 6 else (1, 0)
        out[...] = lines[row : row + 1, lane : lane + size].reshape(size)
    chunks = w_in.shape[1] // width

    def total(at, size):
        rows = pl.ds(at, size)
        return kept_two[0, rows, :] + came_two[0, rows, :].astype(f32)

    w_out[...] = total(0, block)
    for c in range(chunks):
        w_in[:, pl.ds(c * width, width)] = total(block * (c + 1), block)
    w_back[...] = total(block * (chunks + 1), block * chunks)


def unpack(kept_one, came_one, kept_two, came_two, like):
    return pl.pallas_call(
        unpack_kernel,
        out_shape=[jax.ShapeDtypeStruct(item.shape, f32) for item in like],
        in_specs=spec(4),
        out_specs=spec(len(like)),
        compiler_params=params(62),
        name="unpack",
        cost_estimate=cost(1.5),
    )(kept_one, came_one, kept_two, came_two)


def exchange(to_twin, to_other):
    count = lax.axis_size("seq")
    twin = [(i, i ^ 1) for i in range(count)]
    other = [(i, i + 1) for i in range(1, count - 1, 2)]
    other += [(j, i) for i, j in other]
    return (
        [lax.ppermute(item, "seq", other) for item in to_other],
        [lax.ppermute(item, "seq", twin) for item in to_twin],
    )


def order(items, *after):
    return lax.optimization_barrier((items, after))[0]


def per_device(
    lengths,
    tokens,
    ln1_gain,
    ln1_bias,
    w_qkv,
    w_out,
    out_bias,
    ln2_gain,
    ln2_bias,
    w_in,
    in_bias,
    w_back,
    back_bias,
    cotangent,
):
    devices = lax.axis_size("seq")
    device = lax.axis_index("seq")
    rows, width = tokens.shape
    total = rows * devices
    plan = Plan(rows)
    block = width // BLOCKS
    chunks = w_in.shape[1] // width
    small = (ln1_gain, ln1_bias, out_bias, ln2_gain, ln2_bias, back_bias, in_bias)
    direct = devices == BLOCKS
    ring = Ring(BLOCKS)
    last = ring.stages - 1
    core = ring.stages
    if direct:
        info, inverse, a, b = pack(ring, lengths, w_qkv, w_out, w_in, w_back, small)
        a_came, b_came = ring.step(0, [a, b])
        a, b = join([a, b], [a_came, b_came])
        a = order(a, b)
        a_came, b_came = ring.step(1, [a, b])
        (a,) = join([a], [a_came])
        (a_came,) = ring.step(2, [a])
        (a,) = join([a], [a_came])
        (b,) = join([b], [b_came])
        a = order(a, b)
        (a_came,) = ring.step(3, [a])
        (b_came,) = ring.step(2, [b])
        one = [a, a_came] + ring.step(core, [a, a_came])
        one = order(one, b_came)
    else:
        padded = (lengths + 15) // 16 * 16
        ends = jnp.cumsum(padded, dtype=jnp.int32)
        info = jnp.concatenate([device[None].astype(jnp.int32), lengths, ends - padded, ends])
        inverse = jnp.arange(BLOCKS, dtype=jnp.int32)

        def whole(item):
            return lax.all_gather(item, "seq", axis=0, tiled=True)

        def split(item, parts):
            each = BLOCKS // parts
            return [item[k * each : (k + 1) * each] for k in range(parts)]

        full = [whole(item).reshape(BLOCKS, 1, -1) for item in small]
        top = jnp.concatenate(full[:6], axis=2)
        top = jnp.pad(top, ((0, 0), (0, 0), (0, LINE - top.shape[2])))
        under = jnp.pad(full[6], ((0, 0), (0, block - 2), (0, LINE - full[6].shape[2])))
        line = jnp.concatenate([top, under], axis=1)
        one = whole(w_qkv).reshape(BLOCKS, block, -1)
        one = split(jnp.concatenate([one, line], axis=2), PIECES)
        full_in = whole(w_in).reshape(BLOCKS, block, chunks, width)
        full_in = full_in.transpose(0, 2, 1, 3).reshape(BLOCKS, chunks * block, width)
        full_two = [
            whole(w_out).reshape(BLOCKS, block, width),
            full_in,
            whole(w_back).reshape(BLOCKS, chunks * block, width),
        ]
        two = split(jnp.concatenate(full_two, axis=1), 2 * PIECES)
    queries, pairs, twins, others, weight, vectors, shift_in = project(
        plan, total, info, inverse, tokens, one
    )
    from_other, from_twin = exchange(twins, others)
    ready = queries[0]
    if direct:
        b, b_came = order((b, b_came), from_other)
        early, late = ring.step(last, [b, b_came])
        twin_early = ring.step(core, [b, b_came])
        ready = order(ready, b_came)
    outs = [attend(plan, total, info, ready, pairs[0], from_twin[0], from_other[0])]
    outs.append(
        attend(plan, total, info, queries[1], pairs[1], from_twin[1], from_other[1])
    )
    attended, mixed, scale = zip(*outs)
    if direct:
        early, late = order((early, late), attended)
        two = [b, b_came, early, late] + twin_early + ring.step(core, [early, late])
    result, grad_resid, mixed_a, mixed_b, own_two, low_two, high_two, sums, sum_in = middle(
        inverse, tokens, cotangent, attended, vectors, shift_in, two
    )
    grad_mixed = [mixed_a, mixed_b]

    def back(quad):
        return attend_back(
            plan,
            total,
            info,
            queries[quad],
            pairs[quad],
            from_twin[quad],
            from_other[quad],
            grad_mixed[quad],
            scale[quad],
            mixed[quad],
        )

    backs = [back(0)]
    if direct:
        high, low = ring.step(core, [high_two, low_two])
        low, high = order((low, high), backs[0][0])
        kept, sent = ring.fold(last, own_two, low, high)
        (came,) = ring.step(last, [sent])
        grad_mixed[1] = order(grad_mixed[1], sent)
    backs.append(back(1))
    twins, others = [item[2] for item in backs], [item[3] for item in backs]
    other_halo, twin_halo = exchange(twins, others)
    if direct:
        came = order(came, other_halo)
        kept, sent = ring.fold(last - 1, kept, *halves(came))
        (came,) = ring.step(last - 1, [sent])
        other_halo = order(other_halo, sent)
    grad_tokens, own_one, low_one, high_one = finish(
        plan,
        total,
        info,
        inverse,
        tokens,
        weight,
        vectors,
        grad_resid,
        sums,
        sum_in,
        backs[0][0],
        backs[1][0],
        backs[0][1],
        backs[1][1],
        *twin_halo,
        *other_halo,
    )
    if direct:
        high_one, low_one = ring.step(core, [high_one, low_one])
        came = order(came, grad_tokens)
        kept, sent = ring.fold(last - 2, kept, *halves(came))
        (came,) = ring.step(last - 2, [sent])
        high_one, low_one = order((high_one, low_one), sent)
        own_one, sent_one = ring.fold(last, own_one, low_one, high_one)
        (came_one,) = ring.step(last, [sent_one])
        own_one, sent_one = ring.fold(last - 1, own_one, *halves(came_one))
        (came_one,) = ring.step(last - 1, [sent_one])
        came = order(came, came_one)
        kept, sent = ring.fold(last - 3, kept, *halves(came))
        (came,) = ring.step(last - 3, [sent])
        own_one, sent_one = ring.fold(last - 2, own_one, *halves(came_one))
        sent_one = order(sent_one, sent)
        (came_one,) = ring.step(last - 2, [sent_one])
        own_one, sent_one = ring.fold(last - 3, own_one, *halves(came_one))
        (came_one,) = ring.step(last - 3, [sent_one])
        grads = unpack(own_one, came_one, kept, came, (w_qkv, w_out, w_in, w_back) + small)
        grad_w_qkv, grad_w_out, grad_w_in, grad_w_back = grads[:4]
        parts = grads[4:]
    else:

        def shared(item):
            return lax.psum_scatter(item, "seq", scatter_dimension=0, tiled=True)

        full = jnp.concatenate([own_one] + [x.astype(f32) for x in (low_one, high_one)])
        line = full[:, :, 3 * width :]
        parts = [shared(line[:, 0, k * block : (k + 1) * block].reshape(-1)) for k in range(6)]
        parts.append(shared(line[:, 1, : chunks * block].reshape(-1)))
        grad_w_qkv = shared(full[:, :, : 3 * width].reshape(width, 3 * width))
        full = jnp.concatenate([own_two] + [x.astype(f32) for x in (low_two, high_two)])
        grad_w_out = shared(full[:, :block].reshape(width, width))
        full_in = full[:, block : block * (chunks + 1)]
        full_in = full_in.reshape(BLOCKS, chunks, block, width).transpose(0, 2, 1, 3)
        grad_w_in = shared(full_in.reshape(width, chunks * width))
        grad_w_back = shared(full[:, block * (chunks + 1) :].reshape(chunks * width, width))
    gain_one, bias_one, shift_out, gain_two, bias_two, shift_back, shift_hidden = parts
    return (
        result,
        grad_tokens,
        gain_one,
        bias_one,
        grad_w_qkv,
        grad_w_out,
        shift_out,
        gain_two,
        bias_two,
        grad_w_in,
        shift_hidden,
        grad_w_back,
        shift_back,
    )


def solution(mesh):
    flat, wide = P("seq"), P("seq", None)
    weights = (flat, flat, wide, wide, flat, flat, flat, wide, flat, wide, flat)
    return jax.shard_map(
        per_device,
        mesh=mesh,
        in_specs=(P(), wide) + weights + (wide,),
        out_specs=(wide, wide) + weights,
        check_vma=False,
    )
```

time: 222 us -> 162 us (0.73)
  starting transfers between devices: 63.2 us -> 38.5 us
  Pallas kernels: 61 us -> 48.4 us
  waiting for transfers between devices: 78.3 us -> 68 us
  local copies, waits for them, and re-layouts: 10.5 us -> 1.65 us
  other arithmetic: 7.4 us -> 4.13 us
    ppermute x37 -> x35, starting transfers between devices: 63.2 us -> 38.5 us  [the longest x27 31.9 us: step(): return [lax.ppermute(item, 'seq', route) for item in arrays]]
    ppermute x37 -> x35, waiting for transfers between devices: 78.3 us -> 68 us  [the longest x27 66.1 us: step(): return [lax.ppermute(item, 'seq', route) for item in arrays]]
    pallas_call x1 -> x2, Pallas kernels: 17.3 us -> 13 us  [attend_back(): pl.pallas_call(functools.partial(attend_back_kernel, plan, total), out_sh...]
    unnamed x58 -> x14, local copies, waits for them, and re-layouts: 5.83 us -> 1.63 us
    pallas_call x1, Pallas kernels: 9.42 us -> 6.2 us  [finish(): pl.pallas_call(functools.partial(finish_kernel, plan, total), out_shape=(...]
    pallas_call x1, Pallas kernels: 5.79 us -> 3.33 us  [project(): pl.pallas_call(functools.partial(project_kernel, plan, total), out_shape=...]
    squeeze x3 -> x0, local copies, waits for them, and re-layouts: 2.38 us -> none  [the longest x1 1.2 us: per_device(): lax.dynamic_index_in_dim(jnp.array(ring.table()), device, keepdims=False)]
    pallas_call x1 -> x2, Pallas kernels: 11.8 us -> 10.1 us  [attend(): pl.pallas_call(functools.partial(attend_kernel, plan, total), out_shape=(...]
  transfers between devices with their start and end apart: 37 -> 35, of which waited for: 19 -> 22; matrix products, arithmetic and copies ran while one was open for 4% -> 2% of each run, Pallas kernels for 20% -> 18%
where the time goes in v3:
time: 162 us
  waiting for transfers between devices  68 us (42%)
  Pallas kernels  48.4 us (30%)
  starting transfers between devices  38.5 us (24%)
  other arithmetic  4.13 us (3%)
  local copies, waits for them, and re-layouts  1.65 us (1%)
    ppermute x27, waiting for transfers between devices, step(): return [lax.ppermute(item, 'seq', route) for item in arrays]  66.1 us
    ppermute x27, starting transfers between devices, step(): return [lax.ppermute(item, 'seq', route) for item in arrays]  31.9 us
    pallas_call x2, Pallas kernels, attend_back(): pl.pallas_call(functools.partial(attend_back_kernel, plan, total), out_sh...  13 us
    pallas_call x1, Pallas kernels, middle(): pl.pallas_call(functools.partial(middle_kernel, parts), out_shape=(jax.Sh...  12.3 us
    pallas_call x2, Pallas kernels, attend(): pl.pallas_call(functools.partial(attend_kernel, plan, total), out_shape=(...  10.1 us
    pallas_call x1, Pallas kernels, finish(): pl.pallas_call(functools.partial(finish_kernel, plan, total), out_shape=(...  6.2 us
    ppermute x4, starting transfers between devices, exchange(): lax.ppermute(item, 'seq', twin)  3.51 us
    pallas_call x1, Pallas kernels, project(): pl.pallas_call(functools.partial(project_kernel, plan, total), out_shape=...  3.33 us
  transfers between devices with their start and end apart: 35, of which 22 were waited for; matrix products, arithmetic and copies ran while one was open for 2% of the time, Pallas kernels for 18%

profile of v3, /device:TPU:0, one launch (start us, length us, event | category | flops | bytes accessed | tf_op | source)
XLA Modules:
  0.0 161.9 jit_solution(13401501948219657329)
XLA Ops:
  0.6 1.7 %pack.1 = (s32[10]{0:T(128)}, s32[32]{0:T(128)}, bf16[1,16,1664]{2,1,0:T(8,128)(2,1)}, bf16[1,144,512]{2,1,0:T(8,128)(2,1)}) custom-call(s32[3]{0:T(128)} %lengths.1, bf16[16,1536]{1,0:T(8,128)(2,1)} %w_qkv.1, bf16[16,512]{1,0:T(8,128)(2,1)} %w_out.1, bf16[16,2048]{1,0:T(8,128)(2,1)} %w_in.1, bf16[64,512]{1,0:T(8,128)(2,1)} %w_back.1, bf16[16]{0:T(256)(128)(2,1)} %refs_0_.1, ...), custom_call_target="tpu_custom_call" | custom-call | flops 1 | bytes 1 | tf_op jit(solution)/shard_map/pack/pallas_call | solution.py:844
  2.4 4.1 %collective-permute-start = (bf16[1,16,1664]{2,1,0:T(8,128)(2,1)}, bf16[1,16,1664]{2,1,0:T(8,128)(2,1)S(1)}, u32[]{:S(2)}, u32[]{:S(2)}) collective-permute-start(bf16[1,16,1664]{2,1,0:T(8,128)(2,1)} %get-tuple-element.90), channel_id=1, source_target_pairs={{0,16},{1,3},{2,18},{3,1},{4,20},{5,7},{6,22},{7,5},{8,24},{9,11},... | collective-permute-start | bytes 159752 | tf_op jit(solution)/shard_map/ppermute | solution.py:794
  7.5 1.3 collective-permute-done
  9.7 6.2 %collective-permute-done.1 = bf16[1,144,512]{2,1,0:T(8,128)(2,1)S(1)} collective-permute-done((bf16[1,144,512]{2,1,0:T(8,128)(2,1)}, bf16[1,144,512]{2,1,0:T(8,128)(2,1)S(1)}, u32[]{:S(2)}, u32[]{:S(2)}) %collective-permute-start.1) | collective-permute-done | bytes 147488 | tf_op jit(solution)/shard_map/ppermute | solution.py:794
  16.0 2.0 %collective-permute-start.4 = (bf16[2,144,512]{2,1,0:T(8,128)(2,1)S(1)}, bf16[2,144,512]{2,1,0:T(8,128)(2,1)S(1)}, u32[]{:S(2)}, u32[]{:S(2)}) collective-permute-start(bf16[2,144,512]{2,1,0:T(8,128)(2,1)S(1)} %get-tuple-element.180), channel_id=1, source_target_pairs={{0,8},{1,17},{2,10},{3,19},{4,12},{5,21},{6,14},{7,23},{8,0},{9,25... | collective-permute-start | bytes 884744 | tf_op jit(solution)/shard_map/ppermute | solution.py:794
  18.0 6.0 %collective-permute-done.2 = bf16[2,16,1664]{2,1,0:T(8,128)(2,1)S(1)} collective-permute-done((bf16[2,16,1664]{2,1,0:T(8,128)(2,1)S(1)}, bf16[2,16,1664]{2,1,0:T(8,128)(2,1)S(1)}, u32[]{:S(2)}, u32[]{:S(2)}) %collective-permute-start.2) | collective-permute-done | bytes 106528 | tf_op jit(solution)/shard_map/ppermute | solution.py:794
  24.0 1.6 collective-permute-start.3
  25.6 3.4 %collective-permute-done.4 = bf16[2,144,512]{2,1,0:T(8,128)(2,1)S(1)} collective-permute-done((bf16[2,144,512]{2,1,0:T(8,128)(2,1)S(1)}, bf16[2,144,512]{2,1,0:T(8,128)(2,1)S(1)}, u32[]{:S(2)}, u32[]{:S(2)}) %collective-permute-start.4) | collective-permute-done | bytes 294944 | tf_op jit(solution)/shard_map/ppermute | solution.py:794
  30.0 3.7 %collective-permute-start.5 = (bf16[8,16,1664]{2,1,0:T(8,128)(2,1)S(1)}, bf16[8,16,1664]{2,1,0:T(8,128)(2,1)S(1)}, u32[]{:S(2)}, u32[]{:S(2)}) collective-permute-start(bf16[8,16,1664]{2,1,0:T(8,128)(2,1)S(1)} %pad_maximum_fusion.refs_0_), channel_id=1, source_target_pairs={{0,2},{1,5},{2,0},{3,7},{4,6},{5,1},{6,4},{7,3},{8,10},{9,13},{10,... | collective-permute-start | bytes 1277960 | tf_op jit(solution)/shard_map/ppermute | solution.py:794
  33.6 1.5 collective-permute-start.8
  35.1 4.6 %collective-permute-done.5.refs_1_ = bf16[8,16,1664]{2,1,0:T(8,128)(2,1)S(1)} collective-permute-done((bf16[8,16,1664]{2,1,0:T(8,128)(2,1)S(1)}, bf16[8,16,1664]{2,1,0:T(8,128)(2,1)S(1)}, u32[]{:S(2)}, u32[]{:S(2)}) %collective-permute-start.5) | collective-permute-done | bytes 426016 | tf_op jit(solution)/shard_map/ppermute | solution.py:794
  39.7 3.8 %collective-permute-done.8.refs_1_ = bf16[4,144,512]{2,1,0:T(8,128)(2,1)S(1)} collective-permute-done((bf16[4,144,512]{2,1,0:T(8,128)(2,1)S(1)}, bf16[4,144,512]{2,1,0:T(8,128)(2,1)S(1)}, u32[]{:S(2)}, u32[]{:S(2)}) %collective-permute-start.8) | collective-permute-done | bytes 589856 | tf_op jit(solution)/shard_map/ppermute | solution.py:794
  43.5 3.3 %project.1 = (bf16[1024,256]{1,0:T(8,128)(2,1)S(1)}, bf16[1024,256]{1,0:T(8,128)(2,1)S(1)}, bf16[1024,512]{1,0:T(8,128)(2,1)S(1)}, bf16[1024,512]{1,0:T(8,128)(2...) custom-call(s32[10]{0:T(128)S(1)} %copy-done.2, ...), custom_call_target="tpu_custom_call" | custom-call | flops 1 | bytes 1 | tf_op jit(solution)/shard_map/project/pallas_call | solution.py:285
  48.4 8.9 %collective-permute-start.13 = (bf16[4,144,512]{2,1,0:T(8,128)(2,1)S(1)}, bf16[4,144,512]{2,1,0:T(8,128)(2,1)S(1)}, u32[]{:S(2)}, u32[]{:S(2)}) collective-permute-start(bf16[4,144,512]{2,1,0:T(8,128)(2,1)S(1)} %constant_dynamic-update-slice_fusion.2.refs_0_), channel_id=1, source_target_pairs={{0,2},{1,5},{2,0},{3,7},{4,6},{5,1},{6,4},{7,3},{8,10},{9,13},{10,... | collective-permute-start | bytes 1769480 | tf_op jit(solution)/shard_map/ppermute | solution.py:794
  57.3 1.6 collective-permute-start.12
  60.3 5.0 %attend.3 = (bf16[512,256]{1,0:T(8,128)(2,1)S(1)}, f32[512,256]{1,0:T(8,128)S(1)}, f32[512,256]{1,0:T(8,128)S(1)}) custom-call(s32[10]{0:T(128)S(1)} %copy-done.2, bf16[1024,256]{1,0:T(8,128)(2,1)S(1)} %get-tuple-element.106.query, bf16[1024,512]{1,0:T(8,128)(2,1)S(1)} %get-tuple-element.107.pairs, bf16[160,512]{1,0:T(8,128)(2,1)S(1)} %collective-permute-done.12.from_twin, ...), custom_call_target="tpu_custom_call" | custom-call | flops 1 | bytes 1 | tf_op jit(solution)/shard_map/attend/pallas_call | solution.py:372
  65.3 5.0 %attend.2 = (bf16[512,256]{1,0:T(8,128)(2,1)S(1)}, f32[512,256]{1,0:T(8,128)S(1)}, f32[512,256]{1,0:T(8,128)S(1)}) custom-call(s32[10]{0:T(128)S(1)} %copy-done.2, bf16[1024,256]{1,0:T(8,128)(2,1)S(1)} %get-tuple-element.102.query, bf16[1024,512]{1,0:T(8,128)(2,1)S(1)} %get-tuple-element.103.pairs, bf16[160,512]{1,0:T(8,128)(2,1)S(1)} %collective-permute-done.11.from_twin, ...), custom_call_target="tpu_custom_call" | custom-call | flops 1 | bytes 1 | tf_op jit(solution)/shard_map/attend/pallas_call | solution.py:372
  72.5 1.6 collective-permute-done.17.refs_6_
  75.0 12.3 %middle.1 = (bf16[512,512]{1,0:T(8,128)(2,1)}, f32[512,512]{1,0:T(8,128)S(1)}, f32[512,256]{1,0:T(8,128)S(1)}, f32[512,256]{1,0:T(8,128)S(1)}, f32[16,144,512]{2...) custom-call(s32[32]{0:T(128)S(1)} %copy-done.3, ...), custom_call_target="tpu_custom_call" | custom-call | flops 1 | bytes 1 | tf_op jit(solution)/shard_map/middle/pallas_call | solution.py:498
  87.8 6.5 %attend_back.2 = (f32[1024,256]{1,0:T(8,128)S(1)}, f32[1024,512]{1,0:T(8,128)S(1)}, bf16[160,512]{1,0:T(8,128)(2,1)S(1)}, bf16[160,512]{1,0:T(8,128)(2,1)S(1)}) custom-call(s32[10]{0:T(128)S(1)} %copy-done.2, bf16[1024,256]{1,0:T(8,128)(2,1)S(1)} %get-tuple-element.102.query, bf16[1024,512]{1,0:T(8,128)(2,1)S(1)} %get-tuple-element.103.pairs, ...), custom_call_target="tpu_custom_call" | custom-call | flops 1 | bytes 1 | tf_op jit(solution)/shard_map/attend_back/pallas_call | solution.py:620
  95.2 2.3 %collective-permute-start.25 = (bf16[8,144,512]{2,1,0:T(8,128)(2,1)S(1)}, bf16[8,144,512]{2,1,0:T(8,128)(2,1)S(1)}, u32[]{:S(2)}, u32[]{:S(2)}) collective-permute-start(bf16[8,144,512]{2,1,0:T(8,128)(2,1)S(1)} %get-tuple-element.164), channel_id=1, source_target_pairs={{0,2},{1,5},{2,0},{3,7},{4,6},{5,1},{6,4},{7,3},{8,10},{9,13},{10,... | collective-permute-start | bytes 3538952 | tf_op jit(solution)/shard_map/ppermute | solution.py:794
  98.4 6.5 %attend_back.3 = (f32[1024,256]{1,0:T(8,128)S(1)}, f32[1024,512]{1,0:T(8,128)S(1)}, bf16[160,512]{1,0:T(8,128)(2,1)S(1)}, bf16[160,512]{1,0:T(8,128)(2,1)S(1)}) custom-call(s32[10]{0:T(128)S(1)} %copy-done.2, bf16[1024,256]{1,0:T(8,128)(2,1)S(1)} %get-tuple-element.106.query, bf16[1024,512]{1,0:T(8,128)(2,1)S(1)} %get-tuple-element.107.pairs, ...), custom_call_target="tpu_custom_call" | custom-call | flops 1 | bytes 1 | tf_op jit(solution)/shard_map/attend_back/pallas_call | solution.py:620
  105.7 12.6 %collective-permute-done.25 = bf16[8,144,512]{2,1,0:T(8,128)(2,1)S(1)} collective-permute-done((bf16[8,144,512]{2,1,0:T(8,128)(2,1)S(1)}, bf16[8,144,512]{2,1,0:T(8,128)(2,1)S(1)}, u32[]{:S(2)}, u32[]{:S(2)}) %collective-permute-start.25) | collective-permute-done | bytes 1179680 | tf_op jit(solution)/shard_map/ppermute | solution.py:794
  118.7 1.4 collective-permute-start.28
  120.1 1.9 %collective-permute-start.21 = (bf16[160,512]{1,0:T(8,128)(2,1)S(1)}, bf16[160,512]{1,0:T(8,128)(2,1)S(1)}, u32[]{:S(2)}, u32[]{:S(2)}) collective-permute-start(bf16[160,512]{1,0:T(8,128)(2,1)S(1)} %get-tuple-element.135), channel_id=1, source_target_pairs={{0,1},{1,0},{2,3},{3,2},{4,5},{5,4},{6,7},{7,6},{8,9},{9,8},{10,11... | collective-permute-start | bytes 491528 | tf_op jit(solution)/shard_map/ppermute | solution.py:903
  123.4 6.2 %finish.1 = (f32[512,512]{1,0:T(8,128)}, f32[16,16,1664]{2,1,0:T(8,128)S(1)}, bf16[8,16,1664]{2,1,0:T(8,128)(2,1)S(1)}, bf16[8,16,1664]{2,1,0:T(8,128)(2,1)S(1)}) custom-call(s32[10]{0:T(128)S(1)} %copy-done.2, s32[32]{0:T(128)S(1)} %copy-done.3, bf16[512,512]{1,0:T(8,128)(2,1)S(1)} %copy-done, bf16[512,1536]{1,0:T(8,128)(2,1)S(1)} %get-tuple-element.116.weight, ...), custom_call_target="tpu_custom_call" | custom-call | flops 1 | bytes 1 | tf_op jit(solution)/shard_map/finish/pallas_call | solution.py:743
  132.2 1.5 collective-permute-start.31
  133.7 6.6 %collective-permute-done.29 = bf16[8,16,1664]{2,1,0:T(8,128)(2,1)S(1)} collective-permute-done((bf16[8,16,1664]{2,1,0:T(8,128)(2,1)S(1)}, bf16[8,16,1664]{2,1,0:T(8,128)(2,1)S(1)}, u32[]{:S(2)}, u32[]{:S(2)}) %collective-permute-start.29) | collective-permute-done | bytes 426016 | tf_op jit(solution)/shard_map/ppermute | solution.py:794
  141.1 5.2 %collective-permute-done.30 = bf16[4,16,1664]{2,1,0:T(8,128)(2,1)S(1)} collective-permute-done((bf16[4,16,1664]{2,1,0:T(8,128)(2,1)S(1)}, bf16[4,16,1664]{2,1,0:T(8,128)(2,1)S(1)}, u32[]{:S(2)}, u32[]{:S(2)}) %collective-permute-start.30) | collective-permute-done | bytes 213024 | tf_op jit(solution)/shard_map/ppermute | solution.py:794
  148.8 4.8 %collective-permute-done.32 = bf16[2,16,1664]{2,1,0:T(8,128)(2,1)S(1)} collective-permute-done((bf16[2,16,1664]{2,1,0:T(8,128)(2,1)S(1)}, bf16[2,16,1664]{2,1,0:T(8,128)(2,1)S(1)}, u32[]{:S(2)}, u32[]{:S(2)}) %collective-permute-start.32) | collective-permute-done | bytes 106528 | tf_op jit(solution)/shard_map/ppermute | solution.py:794
  155.2 4.0 %collective-permute-done.33.came_one = bf16[1,16,1664]{2,1,0:T(8,128)(2,1)S(1)} collective-permute-done((bf16[1,16,1664]{2,1,0:T(8,128)(2,1)S(1)}, bf16[1,16,1664]{2,1,0:T(8,128)(2,1)S(1)}, u32[]{:S(2)}, u32[]{:S(2)}) %collective-permute-start.33) | collective-permute-done | bytes 53280 | tf_op jit(solution)/shard_map/ppermute | solution.py:794
  159.9 1.8 %unpack.1 = (f32[16,1536]{1,0:T(8,128)}, f32[16,512]{1,0:T(8,128)}, f32[16,2048]{1,0:T(8,128)}, f32[64,512]{1,0:T(8,128)}, f32[16]{0:T(128)}, /*index=5*/f32[16]...) custom-call(f32[1,16,1664]{2,1,0:T(8,128)} %get-tuple-element.178.kept_one, ...), custom_call_target="tpu_custom_call" | custom-call | flops 1 | bytes 1 | tf_op jit(solution)/shard_map/unpack/pallas_call | solution.py:885
  (73 shorter events, 21.8 us)
Async XLA Ops:
  2.4 6.4 %collective-permute-start = (bf16[1,16,1664]{2,1,0:T(8,128)(2,1)}, bf16[1,16,1664]{2,1,0:T(8,128)(2,1)S(1)}, u32[]{:S(2)}, u32[]{:S(2)}) collective-permute-start(bf16[1,16,1664]{2,1,0:T(8,128)(2,1)} %get-tuple-element.90), channel_id=1, source_target_pairs={{0,16},{1,3},{2,18},{3,1},{4,20},{5,7},{6,22},{7,5},{8,24},{9,11},... | collective-permute-start | bytes 159752 | tf_op jit(solution)/shard_map/ppermute | solution.py:794
  6.5 9.4 %collective-permute-start.1 = (bf16[1,144,512]{2,1,0:T(8,128)(2,1)}, bf16[1,144,512]{2,1,0:T(8,128)(2,1)S(1)}, u32[]{:S(2)}, u32[]{:S(2)}) collective-permute-start(bf16[1,144,512]{2,1,0:T(8,128)(2,1)} %get-tuple-element.91), channel_id=1, source_target_pairs={{0,16},{1,3},{2,18},{3,1},{4,20},{5,7},{6,22},{7,5},{8,24},{9,11},... | collective-permute-start | bytes 442376 | tf_op jit(solution)/shard_map/ppermute | solution.py:794
  15.9 8.1 %collective-permute-start.2 = (bf16[2,16,1664]{2,1,0:T(8,128)(2,1)S(1)}, bf16[2,16,1664]{2,1,0:T(8,128)(2,1)S(1)}, u32[]{:S(2)}, u32[]{:S(2)}) collective-permute-start(bf16[2,16,1664]{2,1,0:T(8,128)(2,1)S(1)} %pad_maximum_fusion.2), channel_id=1, source_target_pairs={{0,8},{1,17},{2,10},{3,19},{4,12},{5,21},{6,14},{7,23},{8,0},{9,25... | collective-permute-start | bytes 319496 | tf_op jit(solution)/shard_map/ppermute | solution.py:794
  16.0 13.0 %collective-permute-start.4 = (bf16[2,144,512]{2,1,0:T(8,128)(2,1)S(1)}, bf16[2,144,512]{2,1,0:T(8,128)(2,1)S(1)}, u32[]{:S(2)}, u32[]{:S(2)}) collective-permute-start(bf16[2,144,512]{2,1,0:T(8,128)(2,1)S(1)} %get-tuple-element.180), channel_id=1, source_target_pairs={{0,8},{1,17},{2,10},{3,19},{4,12},{5,21},{6,14},{7,23},{8,0},{9,25... | collective-permute-start | bytes 884744 | tf_op jit(solution)/shard_map/ppermute | solution.py:794
  24.0 5.9 %collective-permute-start.3 = (bf16[4,16,1664]{2,1,0:T(8,128)(2,1)S(1)}, bf16[4,16,1664]{2,1,0:T(8,128)(2,1)S(1)}, u32[]{:S(2)}, u32[]{:S(2)}) collective-permute-start(bf16[4,16,1664]{2,1,0:T(8,128)(2,1)S(1)} %pad_maximum_fusion.1), channel_id=1, source_target_pairs={{0,4},{1,9},{2,6},{3,11},{4,0},{5,13},{6,2},{7,15},{8,12},{9,1},{1... | collective-permute-start | bytes 638984 | tf_op jit(solution)/shard_map/ppermute | solution.py:794
  30.0 9.8 %collective-permute-start.5 = (bf16[8,16,1664]{2,1,0:T(8,128)(2,1)S(1)}, bf16[8,16,1664]{2,1,0:T(8,128)(2,1)S(1)}, u32[]{:S(2)}, u32[]{:S(2)}) collective-permute-start(bf16[8,16,1664]{2,1,0:T(8,128)(2,1)S(1)} %pad_maximum_fusion.refs_0_), channel_id=1, source_target_pairs={{0,2},{1,5},{2,0},{3,7},{4,6},{5,1},{6,4},{7,3},{8,10},{9,13},{10,... | collective-permute-start | bytes 1277960 | tf_op jit(solution)/shard_map/ppermute | solution.py:794
  33.6 9.9 %collective-permute-start.8 = (bf16[4,144,512]{2,1,0:T(8,128)(2,1)S(1)}, bf16[4,144,512]{2,1,0:T(8,128)(2,1)S(1)}, u32[]{:S(2)}, u32[]{:S(2)}) collective-permute-start(bf16[4,144,512]{2,1,0:T(8,128)(2,1)S(1)} %constant_dynamic-update-slice_fusion.2.refs_0_), channel_id=1, source_target_pairs={{0,4},{1,9},{2,6},{3,11},{4,0},{5,13},{6,2},{7,15},{8,12},{9,1},{1... | collective-permute-start | bytes 1769480 | tf_op jit(solution)/shard_map/ppermute | solution.py:794
  35.1 4.6 %collective-permute-start.6 = (bf16[8,16,1664]{2,1,0:T(8,128)(2,1)S(1)}, bf16[8,16,1664]{2,1,0:T(8,128)(2,1)S(1)}, u32[]{:S(2)}, u32[]{:S(2)}) collective-permute-start(bf16[8,16,1664]{2,1,0:T(8,128)(2,1)S(1)} %pad_maximum_fusion.refs_0_), channel_id=1, source_target_pairs={{0,1},{1,0},{2,3},{3,2},{4,5},{5,4},{6,7},{7,6},{8,9},{9,8},{10,11... | collective-permute-start | bytes 1277960 | tf_op jit(solution)/shard_map/ppermute | solution.py:794
  39.7 3.8 %collective-permute-start.7 = (bf16[8,16,1664]{2,1,0:T(8,128)(2,1)S(1)}, bf16[8,16,1664]{2,1,0:T(8,128)(2,1)S(1)}, u32[]{:S(2)}, u32[]{:S(2)}) collective-permute-start(bf16[8,16,1664]{2,1,0:T(8,128)(2,1)S(1)} %collective-permute-done.5.refs_1_), channel_id=1, source_target_pairs={{0,1},{1,0},{2,3},{3,2},{4,5},{5,4},{6,7},{7,6},{8,9},{9,8},{10,11... | collective-permute-start | bytes 1277960 | tf_op jit(solution)/shard_map/ppermute | solution.py:794
  46.9 1.5 collective-permute-start.9
  48.4 21.9 %collective-permute-start.13 = (bf16[4,144,512]{2,1,0:T(8,128)(2,1)S(1)}, bf16[4,144,512]{2,1,0:T(8,128)(2,1)S(1)}, u32[]{:S(2)}, u32[]{:S(2)}) collective-permute-start(bf16[4,144,512]{2,1,0:T(8,128)(2,1)S(1)} %constant_dynamic-update-slice_fusion.2.refs_0_), channel_id=1, source_target_pairs={{0,2},{1,5},{2,0},{3,7},{4,6},{5,1},{6,4},{7,3},{8,10},{9,13},{10,... | collective-permute-start | bytes 1769480 | tf_op jit(solution)/shard_map/ppermute | solution.py:794
  57.3 14.2 %collective-permute-start.14 = (bf16[4,144,512]{2,1,0:T(8,128)(2,1)S(1)}, bf16[4,144,512]{2,1,0:T(8,128)(2,1)S(1)}, u32[]{:S(2)}, u32[]{:S(2)}) collective-permute-start(bf16[4,144,512]{2,1,0:T(8,128)(2,1)S(1)} %collective-permute-done.8.refs_1_), channel_id=1, source_target_pairs={{0,2},{1,5},{2,0},{3,7},{4,6},{5,1},{6,4},{7,3},{8,10},{9,13},{10,... | collective-permute-start | bytes 1769480 | tf_op jit(solution)/shard_map/ppermute | solution.py:794
  57.3 2.6 %collective-permute-start.12 = (bf16[160,512]{1,0:T(8,128)(2,1)S(1)}, bf16[160,512]{1,0:T(8,128)(2,1)S(1)}, u32[]{:S(2)}, u32[]{:S(2)}) collective-permute-start(bf16[160,512]{1,0:T(8,128)(2,1)S(1)} %get-tuple-element.108), channel_id=1, source_target_pairs={{0,1},{1,0},{2,3},{3,2},{4,5},{5,4},{6,7},{7,6},{8,9},{9,8},{10,11... | collective-permute-start | bytes 491528 | tf_op jit(solution)/shard_map/ppermute | solution.py:903
  58.9 6.4 %collective-permute-start.11 = (bf16[160,512]{1,0:T(8,128)(2,1)S(1)}, bf16[160,512]{1,0:T(8,128)(2,1)S(1)}, u32[]{:S(2)}, u32[]{:S(2)}) collective-permute-start(bf16[160,512]{1,0:T(8,128)(2,1)S(1)} %get-tuple-element.104), channel_id=1, source_target_pairs={{0,1},{1,0},{2,3},{3,2},{4,5},{5,4},{6,7},{7,6},{8,9},{9,8},{10,11... | collective-permute-start | bytes 491528 | tf_op jit(solution)/shard_map/ppermute | solution.py:903
  58.9 13.6 %collective-permute-start.15 = (bf16[4,144,512]{2,1,0:T(8,128)(2,1)S(1)}, bf16[4,144,512]{2,1,0:T(8,128)(2,1)S(1)}, u32[]{:S(2)}, u32[]{:S(2)}) collective-permute-start(bf16[4,144,512]{2,1,0:T(8,128)(2,1)S(1)} %constant_dynamic-update-slice_fusion.2.refs_0_), channel_id=1, source_target_pairs={{0,1},{1,0},{2,3},{3,2},{4,5},{5,4},{6,7},{7,6},{8,9},{9,8},{10,11... | collective-permute-start | bytes 1769480 | tf_op jit(solution)/shard_map/ppermute | solution.py:794
  59.9 12.6 %collective-permute-start.16 = (bf16[4,144,512]{2,1,0:T(8,128)(2,1)S(1)}, bf16[4,144,512]{2,1,0:T(8,128)(2,1)S(1)}, u32[]{:S(2)}, u32[]{:S(2)}) collective-permute-start(bf16[4,144,512]{2,1,0:T(8,128)(2,1)S(1)} %collective-permute-done.8.refs_1_), channel_id=1, source_target_pairs={{0,1},{1,0},{2,3},{3,2},{4,5},{5,4},{6,7},{7,6},{8,9},{9,8},{10,11... | collective-permute-start | bytes 1769480 | tf_op jit(solution)/shard_map/ppermute | solution.py:794
  71.5 2.6 %collective-permute-start.17 = (bf16[4,144,512]{2,1,0:T(8,128)(2,1)S(1)}, bf16[4,144,512]{2,1,0:T(8,128)(2,1)S(1)}, u32[]{:S(2)}, u32[]{:S(2)}) collective-permute-start(bf16[4,144,512]{2,1,0:T(8,128)(2,1)S(1)} %collective-permute-done.13.refs_2_), channel_id=1, source_target_pairs={{0,1},{1,0},{2,3},{3,2},{4,5},{5,4},{6,7},{7,6},{8,9},{9,8},{10,11... | collective-permute-start | bytes 1769480 | tf_op jit(solution)/shard_map/ppermute | solution.py:794
  72.5 2.5 %collective-permute-start.18 = (bf16[4,144,512]{2,1,0:T(8,128)(2,1)S(1)}, bf16[4,144,512]{2,1,0:T(8,128)(2,1)S(1)}, u32[]{:S(2)}, u32[]{:S(2)}) collective-permute-start(bf16[4,144,512]{2,1,0:T(8,128)(2,1)S(1)} %collective-permute-done.14.refs_3_), channel_id=1, source_target_pairs={{0,1},{1,0},{2,3},{3,2},{4,5},{5,4},{6,7},{7,6},{8,9},{9,8},{10,11... | collective-permute-start | bytes 1769480 | tf_op jit(solution)/shard_map/ppermute | solution.py:794
  87.3 7.0 %collective-permute-start.19 = (bf16[8,144,512]{2,1,0:T(8,128)(2,1)S(1)}, bf16[8,144,512]{2,1,0:T(8,128)(2,1)S(1)}, u32[]{:S(2)}, u32[]{:S(2)}) collective-permute-start(bf16[8,144,512]{2,1,0:T(8,128)(2,1)S(1)} %get-tuple-element.126), channel_id=1, source_target_pairs={{0,1},{1,0},{2,3},{3,2},{4,5},{5,4},{6,7},{7,6},{8,9},{9,8},{10,11... | collective-permute-start | bytes 3538952 | tf_op jit(solution)/shard_map/ppermute | solution.py:794
  87.6 6.7 %collective-permute-start.20 = (bf16[8,144,512]{2,1,0:T(8,128)(2,1)S(1)}, bf16[8,144,512]{2,1,0:T(8,128)(2,1)S(1)}, u32[]{:S(2)}, u32[]{:S(2)}) collective-permute-start(bf16[8,144,512]{2,1,0:T(8,128)(2,1)S(1)} %get-tuple-element.127), channel_id=1, source_target_pairs={{0,1},{1,0},{2,3},{3,2},{4,5},{5,4},{6,7},{7,6},{8,9},{9,8},{10,11... | collective-permute-start | bytes 3538952 | tf_op jit(solution)/shard_map/ppermute | solution.py:794
  95.2 23.0 %collective-permute-start.25 = (bf16[8,144,512]{2,1,0:T(8,128)(2,1)S(1)}, bf16[8,144,512]{2,1,0:T(8,128)(2,1)S(1)}, u32[]{:S(2)}, u32[]{:S(2)}) collective-permute-start(bf16[8,144,512]{2,1,0:T(8,128)(2,1)S(1)} %get-tuple-element.164), channel_id=1, source_target_pairs={{0,2},{1,5},{2,0},{3,7},{4,6},{5,1},{6,4},{7,3},{8,10},{9,13},{10,... | collective-permute-start | bytes 3538952 | tf_op jit(solution)/shard_map/ppermute | solution.py:794
  97.5 8.1 %collective-permute-start.23 = (bf16[160,512]{1,0:T(8,128)(2,1)S(1)}, bf16[160,512]{1,0:T(8,128)(2,1)S(1)}, u32[]{:S(2)}, u32[]{:S(2)}) collective-permute-start(bf16[160,512]{1,0:T(8,128)(2,1)S(1)} %get-tuple-element.137), channel_id=1, source_target_pairs={{1,2},{3,4},{5,6},{7,8},{9,10},{11,12},{13,14},{15,16},{17,18},{19... | collective-permute-start | bytes 491528 | tf_op jit(solution)/shard_map/ppermute | solution.py:902
  118.7 11.5 %collective-permute-start.28 = (bf16[4,144,512]{2,1,0:T(8,128)(2,1)S(1)}, bf16[4,144,512]{2,1,0:T(8,128)(2,1)S(1)}, u32[]{:S(2)}, u32[]{:S(2)}) collective-permute-start(bf16[4,144,512]{2,1,0:T(8,128)(2,1)S(1)} %get-tuple-element.166), channel_id=1, source_target_pairs={{0,4},{1,9},{2,6},{3,11},{4,0},{5,13},{6,2},{7,15},{8,12},{9,1},{1... | collective-permute-start | bytes 1769480 | tf_op jit(solution)/shard_map/ppermute | solution.py:794
  120.1 3.0 %collective-permute-start.21 = (bf16[160,512]{1,0:T(8,128)(2,1)S(1)}, bf16[160,512]{1,0:T(8,128)(2,1)S(1)}, u32[]{:S(2)}, u32[]{:S(2)}) collective-permute-start(bf16[160,512]{1,0:T(8,128)(2,1)S(1)} %get-tuple-element.135), channel_id=1, source_target_pairs={{0,1},{1,0},{2,3},{3,2},{4,5},{5,4},{6,7},{7,6},{8,9},{9,8},{10,11... | collective-permute-start | bytes 491528 | tf_op jit(solution)/shard_map/ppermute | solution.py:903
  129.6 1.8 %collective-permute-start.26 = (bf16[8,16,1664]{2,1,0:T(8,128)(2,1)S(1)}, bf16[8,16,1664]{2,1,0:T(8,128)(2,1)S(1)}, u32[]{:S(2)}, u32[]{:S(2)}) collective-permute-start(bf16[8,16,1664]{2,1,0:T(8,128)(2,1)S(1)} %get-tuple-element.145), channel_id=1, source_target_pairs={{0,1},{1,0},{2,3},{3,2},{4,5},{5,4},{6,7},{7,6},{8,9},{9,8},{10,11... | collective-permute-start | bytes 1277960 | tf_op jit(solution)/shard_map/ppermute | solution.py:794
  129.8 2.2 %collective-permute-start.27 = (bf16[8,16,1664]{2,1,0:T(8,128)(2,1)S(1)}, bf16[8,16,1664]{2,1,0:T(8,128)(2,1)S(1)}, u32[]{:S(2)}, u32[]{:S(2)}) collective-permute-start(bf16[8,16,1664]{2,1,0:T(8,128)(2,1)S(1)} %get-tuple-element.146), channel_id=1, source_target_pairs={{0,1},{1,0},{2,3},{3,2},{4,5},{5,4},{6,7},{7,6},{8,9},{9,8},{10,11... | collective-permute-start | bytes 1277960 | tf_op jit(solution)/shard_map/ppermute | solution.py:794
  132.1 8.2 %collective-permute-start.29 = (bf16[8,16,1664]{2,1,0:T(8,128)(2,1)S(1)}, bf16[8,16,1664]{2,1,0:T(8,128)(2,1)S(1)}, u32[]{:S(2)}, u32[]{:S(2)}) collective-permute-start(bf16[8,16,1664]{2,1,0:T(8,128)(2,1)S(1)} %get-tuple-element.169), channel_id=1, source_target_pairs={{0,2},{1,5},{2,0},{3,7},{4,6},{5,1},{6,4},{7,3},{8,10},{9,13},{10,... | collective-permute-start | bytes 1277960 | tf_op jit(solution)/shard_map/ppermute | solution.py:794
  132.2 8.9 %collective-permute-start.31 = (bf16[2,144,512]{2,1,0:T(8,128)(2,1)S(1)}, bf16[2,144,512]{2,1,0:T(8,128)(2,1)S(1)}, u32[]{:S(2)}, u32[]{:S(2)}) collective-permute-start(bf16[2,144,512]{2,1,0:T(8,128)(2,1)S(1)} %get-tuple-element.168), channel_id=1, source_target_pairs={{0,8},{1,17},{2,10},{3,19},{4,12},{5,21},{6,14},{7,23},{8,0},{9,25... | collective-permute-start | bytes 884744 | tf_op jit(solution)/shard_map/ppermute | solution.py:794
  140.4 5.9 %collective-permute-start.30 = (bf16[4,16,1664]{2,1,0:T(8,128)(2,1)S(1)}, bf16[4,16,1664]{2,1,0:T(8,128)(2,1)S(1)}, u32[]{:S(2)}, u32[]{:S(2)}) collective-permute-start(bf16[4,16,1664]{2,1,0:T(8,128)(2,1)S(1)} %get-tuple-element.171), channel_id=1, source_target_pairs={{0,4},{1,9},{2,6},{3,11},{4,0},{5,13},{6,2},{7,15},{8,12},{9,1},{1... | collective-permute-start | bytes 638984 | tf_op jit(solution)/shard_map/ppermute | solution.py:794
  147.2 6.4 %collective-permute-start.32 = (bf16[2,16,1664]{2,1,0:T(8,128)(2,1)S(1)}, bf16[2,16,1664]{2,1,0:T(8,128)(2,1)S(1)}, u32[]{:S(2)}, u32[]{:S(2)}) collective-permute-start(bf16[2,16,1664]{2,1,0:T(8,128)(2,1)S(1)} %get-tuple-element.151), channel_id=1, source_target_pairs={{0,8},{1,17},{2,10},{3,19},{4,12},{5,21},{6,14},{7,23},{8,0},{9,25... | collective-permute-start | bytes 319496 | tf_op jit(solution)/shard_map/ppermute | solution.py:794
  147.6 7.6 %collective-permute-start.34 = (bf16[1,144,512]{2,1,0:T(8,128)(2,1)S(1)}, bf16[1,144,512]{2,1,0:T(8,128)(2,1)S(1)}, u32[]{:S(2)}, u32[]{:S(2)}) collective-permute-start(bf16[1,144,512]{2,1,0:T(8,128)(2,1)S(1)} %get-tuple-element.174), channel_id=1, source_target_pairs={{0,16},{1,3},{2,18},{3,1},{4,20},{5,7},{6,22},{7,5},{8,24},{9,11},... | collective-permute-start | bytes 442376 | tf_op jit(solution)/shard_map/ppermute | solution.py:794
  154.2 5.0 %collective-permute-start.33 = (bf16[1,16,1664]{2,1,0:T(8,128)(2,1)S(1)}, bf16[1,16,1664]{2,1,0:T(8,128)(2,1)S(1)}, u32[]{:S(2)}, u32[]{:S(2)}) collective-permute-start(bf16[1,16,1664]{2,1,0:T(8,128)(2,1)S(1)} %get-tuple-element.177), channel_id=1, source_target_pairs={{0,16},{1,3},{2,18},{3,1},{4,20},{5,7},{6,22},{7,5},{8,24},{9,11},... | collective-permute-start | bytes 159752 | tf_op jit(solution)/shard_map/ppermute | solution.py:794
  (9 other events, 118.9 us)

commit v4 on v3

v4 whole, which is shorter than its diff:
```python
import functools
import math

import jax
import jax.numpy as jnp
from jax import lax
from jax.experimental import pallas as pl
from jax.experimental.pallas import tpu as pltpu
from jax.sharding import PartitionSpec as P

HEAD_DIM = 64
LEVELS = 5
HALO = 32
BLOCK = 64
WINDOW = BLOCK + 2 * HALO
QUAD = 4
QUAD_WIDTH = QUAD * HEAD_DIM
PIECES = 4
BLOCKS = 32
LINE = 128
FAR = 1 << 26
SEQ_STEP = 1 << 21
MIB = 1024 * 1024

f32 = jnp.float32
bf16 = jnp.bfloat16


class Plan:
    def locate(self, block):
        firsts = [at // BLOCK for at in self.query_at]
        level = sum((block >= first).astype(jnp.int32) for first in firsts[1:])
        start = sum(
            jnp.where(level == k, first, 0) for k, first in enumerate(firsts)
        )
        return level, block - start

    def __init__(self, rows):
        self.rows = rows
        self.counts = [rows >> level for level in range(LEVELS)]
        self.padded = [-(-count // BLOCK) * BLOCK for count in self.counts]
        self.query_at = [sum(self.padded[:level]) for level in range(LEVELS)]
        self.query_rows = sum(self.padded)
        self.key_at = [self.query_at[level] + 2 * HALO * level for level in range(LEVELS)]
        self.key_rows = self.query_rows + 2 * HALO * LEVELS
        self.blocks = [
            (level, part)
            for level in range(LEVELS)
            for part in range(self.padded[level] // BLOCK)
        ]


def dot_nn(a, b):
    return lax.dot_general(a, b, (((1,), (0,)), ((), ())), preferred_element_type=f32)


def dot_nt(a, b):
    return lax.dot_general(a, b, (((1,), (1,)), ((), ())), preferred_element_type=f32)


def dot_tn(a, b):
    return lax.dot_general(a, b, (((0,), (0,)), ((), ())), preferred_element_type=f32)


def spec(count):
    return [pl.BlockSpec(memory_space=pltpu.VMEM)] * count


SCALARS = pl.BlockSpec(memory_space=pltpu.SMEM)


def slot_facts(info, slot, total):
    number = jnp.zeros(slot.shape, jnp.int32)
    for s in range(3):
        number = number + (slot >= info[7 + s]).astype(jnp.int32)
    begin = jnp.where(number == 0, info[4], jnp.where(number == 1, info[5], info[6]))
    length = jnp.where(number == 0, info[1], jnp.where(number == 1, info[2], info[3]))
    inside = (slot >= 0) & (slot < total) & (number < 3)
    return number, slot - begin, length, inside


def tile_codes(info, coarse, level, total, outside):
    number, offset, _, inside = slot_facts(info, coarse << level, total)
    wide = jnp.where(inside, number * SEQ_STEP + (offset >> (level + 4)), outside)
    fine = number * SEQ_STEP + (offset >> (level + 3))
    return wide, fine


def admitted(query_codes, key_codes, level):
    near = jnp.abs(query_codes[0] - key_codes[0]) <= 1
    least = jnp.where(level > 0, 2, 0)
    near = near & (jnp.abs(query_codes[1] - key_codes[1]) >= least)
    return jnp.where(near, 1.0, 0.0)


def live_counts(info, coarse, level, total):
    _, offset, length, inside = slot_facts(info, coarse << level, total)
    span = 1 << level
    return jnp.where(inside, jnp.clip(length - offset, 0, span), 0).astype(f32)


def head_masks(rows):
    lane = lax.broadcasted_iota(jnp.int32, (rows, QUAD_WIDTH), 1) // HEAD_DIM
    return [jnp.where(lane == h, 1.0, 0.0).astype(bf16) for h in range(QUAD)]


def spread_heads(block, masks):
    return jnp.concatenate([block * m for m in masks], axis=0)


def join_pair(stacked, first):
    rows = stacked.shape[0] // 2
    return jnp.where(first, stacked[:rows], stacked[rows:])


def is_even(info):
    return (info[0] & 1) == 0


def params(size):
    return pltpu.CompilerParams(vmem_limit_bytes=size * MIB)


def cost(micros):
    return pl.CostEstimate(flops=1, bytes_accessed=1, transcendentals=0)


def fill_extended(plan, own, halos, extended):
    for level in range(LEVELS):
        at, count, mine = plan.key_at[level], plan.counts[level], plan.query_at[level]
        extended[pl.ds(at, HALO), :] = halos[pl.ds(HALO * level, HALO), :]
        extended[pl.ds(at + HALO, count), :] = own[pl.ds(mine, count), :]
        extended[pl.ds(at + HALO + count, HALO), :] = halos[pl.ds(HALO * (LEVELS + level), HALO), :]
        rest = plan.padded[level] - count
        if rest:
            extended[pl.ds(at + 2 * HALO + count, rest), :] = jnp.zeros(
                (rest, extended.shape[1]), bf16
            )


def place_halos(info, from_twin, from_other, halos):
    even = is_even(info)
    size = LEVELS * HALO
    halos[pl.ds(pl.multiple_of(jnp.where(even, size, 0), size), size), :] = from_twin[...]
    halos[pl.ds(pl.multiple_of(jnp.where(even, 0, size), size), size), :] = from_other[...]


def hand_out(info, ends, to_twin, to_other):
    even = is_even(info)
    size = LEVELS * HALO
    to_twin[...] = ends[pl.ds(pl.multiple_of(jnp.where(even, size, 0), size), size), :]
    to_other[...] = ends[pl.ds(pl.multiple_of(jnp.where(even, 0, size), size), size), :]


def ln_stats(values):
    center = values - jnp.mean(values, axis=-1, keepdims=True)
    spread = jnp.mean(center * center, axis=-1, keepdims=True)
    return center, lax.rsqrt(spread + 1e-05)


def ln_back(grad, center, rstd, gain):
    hat = center * rstd
    scaled = grad * gain
    mean_one = jnp.mean(scaled, axis=-1, keepdims=True)
    mean_two = jnp.mean(scaled * hat, axis=-1, keepdims=True)
    return rstd * (scaled - mean_one - hat * mean_two), grad * hat


def column_sum(values):
    return jnp.sum(values, axis=0, keepdims=True)


def unpack_vectors(table, wide):
    blocks, lanes = table.shape

    def one(first, each):
        length = blocks * each
        source = lax.broadcasted_iota(jnp.int32, (lanes, length), 0)
        target = lax.broadcasted_iota(jnp.int32, (lanes, length), 1)
        pick = jnp.where(source == first + (target & (each - 1)), 1.0, 0.0).astype(bf16)
        spreaded = dot_nn(table, pick)
        block = lax.broadcasted_iota(jnp.int32, (blocks, length), 0)
        lane = lax.broadcasted_iota(jnp.int32, (blocks, length), 1)
        return column_sum(jnp.where(lane // each == block, spreaded, 0.0))

    size = wide // 4
    return [one(k * size, size) for k in range(6)], one(6 * size, wide)


def pack_vectors(vectors, last, blocks, lanes):
    size = last.shape[1] // blocks // 4

    def one(row, first, each):
        length = blocks * each
        source = lax.broadcasted_iota(jnp.int32, (length, lanes), 0)
        target = lax.broadcasted_iota(jnp.int32, (length, lanes), 1)
        pick = jnp.where(target == first + (source & (each - 1)), 1.0, 0.0).astype(bf16)
        block = lax.broadcasted_iota(jnp.int32, (blocks, length), 0)
        lane = lax.broadcasted_iota(jnp.int32, (blocks, length), 1)
        spreaded = jnp.where(lane // each == block, row, 0.0)
        total = jnp.zeros((blocks, lanes), f32)
        for _ in range(3):
            part = spreaded.astype(bf16)
            total = total + dot_nn(part, pick)
            spreaded = spreaded - part.astype(f32)
        return total

    total = one(last, 6 * size, 4 * size)
    for k, vector in enumerate(vectors):
        total = total + one(vector, k * size, size)
    return total


def edge_sums_kernel(plan, total, info, tokens, to_twin, to_other, ends):
    rows, width = tokens.shape
    center, rstd = ln_stats(tokens[...].astype(f32))
    plain = (center * rstd).astype(bf16)
    places = info[0] * rows + lax.broadcasted_iota(jnp.int32, (rows, width), 0)
    living = (plain.astype(f32) * live_counts(info, places, 0, total)).astype(bf16)
    size = 2 * LEVELS * HALO
    row = lax.broadcasted_iota(jnp.int32, (size, rows), 0)
    slot = lax.broadcasted_iota(jnp.int32, (size, rows), 1)
    row_one = lax.broadcasted_iota(jnp.int32, (size, 1), 0)
    wanted = jnp.zeros((size, rows), jnp.int32)
    shift = jnp.zeros((size, rows), jnp.int32)
    share = jnp.zeros((size, 1), f32)
    for k in range(2 * LEVELS):
        level, at = k % LEVELS, k * HALO
        first = 0 if k < LEVELS else plan.counts[level] - HALO
        wanted = jnp.where(row >= at, row - at + first, wanted)
        shift = jnp.where(row >= at, level, shift)
        share = jnp.where(row_one >= at, 0.5**level, share)
    pool = jnp.where((slot >> shift) == wanted, 1.0, 0.0).astype(bf16)
    ends[:, pl.ds(0, width)] = (dot_nn(pool, plain) * share).astype(bf16)
    ends[:, pl.ds(width, width)] = dot_nn(pool, living).astype(bf16)
    hand_out(info, ends, to_twin, to_other)


def edge_sums(plan, total, info, tokens):
    width = tokens.shape[1]
    size = LEVELS * HALO
    return pl.pallas_call(
        functools.partial(edge_sums_kernel, plan, total),
        out_shape=[jax.ShapeDtypeStruct((size, 2 * width), bf16)] * 2,
        in_specs=[SCALARS] + spec(1),
        out_specs=spec(2),
        scratch_shapes=[pltpu.VMEM((2 * size, 2 * width), bf16)],
        compiler_params=params(10),
        name="edge_sums",
        cost_estimate=cost(1.5),
    )(info, tokens)


def project_kernel(
    plan, total, info, inverse, tokens, from_twin, from_other, *refs
):
    pieces, outs = refs[:PIECES], refs[PIECES:]
    queries, pairs, halo_queries, halo_pairs = (outs[2 * k : 2 * k + 2] for k in range(4))
    weight, vectors, shift_out, table, edges, halos = outs[8:]
    rows, width = tokens.shape
    device = info[0]
    each = pieces[0].shape[0]
    block_rows = pieces[0].shape[1] // 4
    for p in range(PIECES * each):
        i = inverse[p]
        there = pl.ds(pl.multiple_of(i * block_rows, block_rows), block_rows)
        piece, q = pieces[p // each], p % each
        for c in range(3):
            weight[there, pl.ds(c * width, width)] = piece[q, pl.ds(block_rows * c, block_rows), :]
        line = piece[q, pl.ds(block_rows * 3, block_rows), pl.ds(0, 2 * LINE)].astype(f32)
        table[pl.ds(i, 1), :] = line[0:1]
    singles, wide = unpack_vectors(table[...].astype(bf16), 4 * block_rows)
    for k, single in enumerate(singles):
        vectors[pl.ds(k, 1), :] = single
    shift_out[...] = wide
    values = tokens[...].astype(f32)
    center, rstd = ln_stats(values)
    low = (center * rstd * singles[0] + singles[1]).astype(bf16)
    pooled_rows = plan.query_rows - plan.query_at[1]
    row = lax.broadcasted_iota(jnp.int32, (pooled_rows, rows), 0)
    slot = lax.broadcasted_iota(jnp.int32, (pooled_rows, rows), 1)
    first = jnp.zeros((pooled_rows, rows), jnp.int32)
    shift = jnp.zeros((pooled_rows, rows), jnp.int32)
    share = jnp.zeros((pooled_rows, 1), f32)
    row_one = lax.broadcasted_iota(jnp.int32, (pooled_rows, 1), 0)
    for level in range(1, LEVELS):
        at = plan.query_at[level] - plan.query_at[1]
        first = jnp.where(row >= at, at, first)
        shift = jnp.where(row >= at, level, shift)
        share = jnp.where(row_one >= at, 0.5**level, share)
    pool = jnp.where((slot >> shift) == row - first, 1.0, 0.0).astype(bf16)
    places = device * rows + lax.broadcasted_iota(jnp.int32, (rows, QUAD_WIDTH), 0)
    live = live_counts(info, places, 0, total)
    place_halos(info, from_twin, from_other, edges)
    size = LEVELS * HALO
    halos[:, pl.ds(0, width)] = (
        edges[:, pl.ds(0, width)].astype(f32) * singles[0] + singles[1]
    ).astype(bf16)
    for k in range(2 * LEVELS):
        level, here = k % LEVELS, pl.ds(k * HALO, HALO)
        count = plan.counts[level]
        first = device * count + (-HALO if k < LEVELS else count)
        place = first + lax.broadcasted_iota(jnp.int32, (HALO, 128), 0)
        counts = live_counts(info, place, level, total)
        counts = jnp.concatenate([counts] * (width // 128), axis=1)
        halos[here, pl.ds(width, width)] = (
            edges[here, pl.ds(width, width)].astype(f32) * singles[0] + counts * singles[1]
        ).astype(bf16)
    lanes = QUAD_WIDTH
    scale = 1.0 / math.sqrt(HEAD_DIM)
    for part in range(3 * width // lanes):
        columns = pl.ds(part * lanes, lanes)
        block = dot_nn(low, weight[:, columns]).astype(bf16)
        kind, quad = divmod(part, 2)
        if kind == 2:
            block = (block.astype(f32) * live).astype(bf16)
        pooled = dot_nn(pool, block)
        if kind < 2:
            pooled = pooled * share
        side = dot_nn(halos[:, pl.ds(width if kind == 2 else 0, width)], weight[:, columns])
        if kind == 0:
            queries[quad][pl.ds(0, rows), :] = (block.astype(f32) * scale).astype(bf16)
            queries[quad][pl.ds(rows, pooled_rows), :] = (pooled * scale).astype(bf16)
            halo_queries[quad][...] = (side * scale).astype(bf16)
        else:
            there = pl.ds((kind - 1) * lanes, lanes)
            pairs[quad][pl.ds(0, rows), there] = block
            pairs[quad][pl.ds(rows, pooled_rows), there] = pooled.astype(bf16)
            halo_pairs[quad][:, there] = side.astype(bf16)


def project(plan, total, info, inverse, tokens, from_twin, from_other, pieces):
    rows, width = tokens.shape
    halo = LEVELS * HALO
    blocks = PIECES * pieces[0].shape[0]
    depth = blocks * pieces[0].shape[1] // 4
    half = width // 2
    outs = pl.pallas_call(
        functools.partial(project_kernel, plan, total),
        out_shape=(
            [jax.ShapeDtypeStruct((plan.query_rows, half), bf16)] * 2
            + [jax.ShapeDtypeStruct((plan.query_rows, 2 * half), bf16)] * 2
            + [jax.ShapeDtypeStruct((2 * halo, half), bf16)] * 2
            + [jax.ShapeDtypeStruct((2 * halo, 2 * half), bf16)] * 2
            + [
                jax.ShapeDtypeStruct((depth, 3 * width), bf16),
                jax.ShapeDtypeStruct((8, depth), f32),
                jax.ShapeDtypeStruct((1, 4 * depth), f32),
            ]
        ),
        in_specs=[SCALARS, SCALARS] + spec(3 + PIECES),
        out_specs=spec(11),
        scratch_shapes=[
            pltpu.VMEM((blocks, 2 * LINE), f32),
            pltpu.VMEM((2 * halo, 2 * width), bf16),
            pltpu.VMEM((2 * halo, 2 * width), bf16),
        ],
        compiler_params=params(18),
        name="project",
        cost_estimate=cost(3.3),
    )(info, inverse, tokens, from_twin, from_other, *pieces)
    return [outs[2 * k : 2 * k + 2] for k in range(4)] + list(outs[8:])


def attend_kernel(plan, total, info, *refs):
    queries, pairs, halos, attended, mixed, scale, extended = (
        refs[2 * k : 2 * k + 2] for k in range(7)
    )
    numer, denom = refs[14:]
    rows = plan.rows
    device = info[0]
    for quad in range(2):
        fill_extended(plan, pairs[quad], halos[quad], extended[quad])
    first_head = lax.broadcasted_iota(jnp.int32, (BLOCK, 128), 1) < HEAD_DIM
    masks = head_masks(BLOCK)

    def prepare(block):
        level, part = plan.locate(block)
        here = pl.ds(pl.multiple_of(BLOCK * block, BLOCK), BLOCK)
        there = pl.ds(pl.multiple_of(BLOCK * block + 2 * HALO * level, BLOCK), WINDOW)
        first = device * (rows >> level) + BLOCK * part
        row = first + lax.broadcasted_iota(jnp.int32, (BLOCK, WINDOW), 0)
        column = first - HALO + lax.broadcasted_iota(jnp.int32, (BLOCK, WINDOW), 1)
        allowed = admitted(
            tile_codes(info, row, level, total, FAR),
            tile_codes(info, column, level, total, -FAR),
            level,
        )
        key_row = first - HALO + lax.broadcasted_iota(jnp.int32, (WINDOW, 128), 0)
        counts = live_counts(info, key_row, level, total).astype(bf16)
        return here, there, allowed, counts

    def block_step(step, carry):
        work = []
        for k in range(4):
            here, there, allowed, counts = prepare(step * 4 + k)
            allowed = jnp.concatenate([allowed] * 4, axis=0) > 0.0
            for part in range(8 // 4):
                work.append((here, there, allowed, counts, part))
        scores = []
        for here, there, allowed, counts, part in work:
            wide = 4 * HEAD_DIM
            quad, half = divmod(part * wide, QUAD_WIDTH)
            lanes = pl.ds(half, wide)
            q = spread_heads(queries[quad][here, lanes], masks)
            scores.append(dot_nt(q, extended[quad][there, lanes]))
        weights = [
            jnp.where(item[2], jnp.exp(score), 0.0).astype(bf16)
            for item, score in zip(work, scores)
        ]
        for (here, there, allowed, counts, part), weight in zip(work, weights):
            wide = 4 * HEAD_DIM
            for sub in range(4 // 2):
                pair = part * (4 // 2) + sub
                quad, half = divmod(pair, 2)
                v = extended[quad][there, pl.ds(QUAD_WIDTH + 128 * half, 128)]
                both = dot_nn(
                    weight[128 * sub : 128 * sub + 128], jnp.concatenate([v, counts], axis=1)
                )
                numer[pair, here, :] = join_pair(both[:, :128], first_head)
                denom[pair, here, :] = join_pair(both[:, 128:], first_head)
        return carry

    lax.fori_loop(0, len(plan.blocks) // 4, block_step, 0, unroll=1)
    places = device * rows + lax.broadcasted_iota(jnp.int32, (rows, 128), 0)
    live = live_counts(info, places, 0, total)
    for pair in range(4):
        for sums in (numer, denom):
            for level in range(LEVELS - 1, 0, -1):
                count = plan.counts[level]
                upper = sums[pair, pl.ds(plan.query_at[level], count), :]
                for parity in range(2):
                    there = pl.ds(plan.query_at[level - 1] + parity, count, stride=2)
                    sums[pair, there, :] = sums[pair, there, :] + upper
        quad, half = divmod(pair, 2)
        lanes = pl.ds(128 * half, 128)
        factor = live / (denom[pair, pl.ds(0, rows), :] + 1.0 - live)
        value = numer[pair, pl.ds(0, rows), :] * factor
        scale[quad][:, lanes] = factor
        mixed[quad][:, lanes] = value
        attended[quad][:, lanes] = value.astype(bf16)


def attend(plan, total, info, queries, pairs, halos):
    rows, width = plan.rows, queries[0].shape[1]
    outs = pl.pallas_call(
        functools.partial(attend_kernel, plan, total),
        out_shape=[jax.ShapeDtypeStruct((rows, width), bf16)] * 2
        + [jax.ShapeDtypeStruct((rows, width), f32)] * 4,
        in_specs=[SCALARS] + spec(6),
        out_specs=spec(6),
        scratch_shapes=[
            pltpu.VMEM((plan.key_rows, 2 * width), bf16),
            pltpu.VMEM((plan.key_rows, 2 * width), bf16),
            pltpu.VMEM((2 * width // 128, plan.query_rows, 128), f32),
            pltpu.VMEM((2 * width // 128, plan.query_rows, 128), f32),
        ],
        compiler_params=params(20),
        name="attend",
        cost_estimate=cost(8),
    )(info, *queries, *pairs, *halos)
    return outs[:2], outs[2:4], outs[4:]


def forward_kernel(
    parts,
    inverse,
    sums_inverse,
    tokens,
    cotangent,
    attended_a,
    attended_b,
    vectors,
    shift_in,
    *refs,
):
    pieces = refs[:parts]
    result, resid_out, grad_normed, w_out, own, low_half, high_half, sum_in = refs[
        parts : parts + 8
    ]
    w_in, w_back, normed_two, outer, tall, flat = refs[parts + 8 :]
    other = (low_half, high_half)
    width = tokens.shape[1]
    wide = width // 2
    each = pieces[0].shape[0]
    half = own.shape[0]
    chunks = w_in.shape[0]
    block = width // (parts * each)
    tall_block = chunks * block
    back_at = block + tall_block
    for p in range(parts * each):
        piece, q = pieces[p // each], p % each
        i = inverse[p]
        rows = pl.ds(pl.multiple_of(i * block, block), block)
        w_out[rows, :] = piece[q, pl.ds(0, block), :]
        for c in range(chunks):
            w_in[c, rows, :] = piece[q, pl.ds(block * (c + 1), block), :]
        rows = pl.ds(pl.multiple_of(i * tall_block, tall_block), tall_block)
        w_back[rows, :] = piece[q, pl.ds(back_at, tall_block), :]
    gain = vectors[pl.ds(3, 1), :]
    resid = tokens[...].astype(f32) + dot_nn(attended_a[...], w_out[pl.ds(0, wide), :])
    resid = resid + dot_nn(attended_b[...], w_out[pl.ds(wide, wide), :]) + vectors[pl.ds(2, 1), :]
    center, rstd = ln_stats(resid)
    normed_two[...] = (center * rstd * gain + vectors[pl.ds(4, 1), :]).astype(bf16)
    resid_out[...] = resid
    outer[...] = jnp.zeros(outer.shape, f32)
    grad_normed[...] = jnp.zeros(grad_normed.shape, f32)

    def chunk_step(c, carry):
        there = pl.ds(pl.multiple_of(c * width, width), width)
        inner = dot_nn(normed_two[...], w_in[c]) + shift_in[:, there]
        cdf = 0.5 * (1.0 + lax.erf(inner * math.sqrt(0.5)))
        active = (inner * cdf).astype(bf16)
        slope = cdf + inner * (jnp.exp(-0.5 * inner * inner) * (1.0 / math.sqrt(2.0 * math.pi)))
        back = w_back[there, :]
        grad_inner = slope * dot_nt(cotangent[...], back)
        low = grad_inner.astype(bf16)
        outer[...] += dot_nn(active, back)
        tall[there, :] = dot_tn(active, cotangent[...]).astype(bf16)
        sum_in[:, there] = column_sum(low.astype(f32))
        flat[...] = dot_tn(normed_two[...], low).astype(bf16)
        for p in range(2 * half):
            i = sums_inverse[p]
            rows = flat[pl.ds(pl.multiple_of(i * block, block), block), :]
            at = pl.ds(pl.multiple_of(c * block, block), block)
            if p < half:
                own[p, at, :] = rows
            else:
                other[(p - half) // 8][(p - half) % 8, at, :] = rows
        grad_normed[...] += dot_nt(low, w_in[c])
        return carry

    lax.fori_loop(0, chunks, chunk_step, 0)
    result[...] = (resid_out[...] + outer[...] + vectors[pl.ds(5, 1), :]).astype(bf16)
    for p in range(2 * half):
        i = sums_inverse[p]
        rows = tall[pl.ds(pl.multiple_of(i * tall_block, tall_block), tall_block), :]
        there = pl.ds(tall_block, tall_block)
        if p < half:
            own[p, there, :] = rows
        else:
            other[(p - half) // 8][(p - half) % 8, there, :] = rows


def feed_forward(inverses, tokens, cotangent, attended, vectors, shift_in, pieces):
    parts = len(pieces)
    rows, width = tokens.shape
    hidden = shift_in.shape[1]
    chunks = hidden // width
    blocks = parts * pieces[0].shape[0]
    stack = pieces[0].shape[1] - width // blocks
    return pl.pallas_call(
        functools.partial(forward_kernel, parts),
        out_shape=(
            jax.ShapeDtypeStruct((rows, width), bf16),
            jax.ShapeDtypeStruct((rows, width), f32),
            jax.ShapeDtypeStruct((rows, width), f32),
            jax.ShapeDtypeStruct((width, width), bf16),
            jax.ShapeDtypeStruct((blocks // 2, stack, width), bf16),
            jax.ShapeDtypeStruct((blocks // 4, stack, width), bf16),
            jax.ShapeDtypeStruct((blocks // 4, stack, width), bf16),
            jax.ShapeDtypeStruct((1, hidden), f32),
        ),
        in_specs=[SCALARS] * 2 + spec(6 + parts),
        out_specs=tuple(spec(8)),
        scratch_shapes=[
            pltpu.VMEM((chunks, width, width), bf16),
            pltpu.VMEM((hidden, width), bf16),
            pltpu.VMEM((rows, width), bf16),
            pltpu.VMEM((rows, width), f32),
            pltpu.VMEM((hidden, width), bf16),
            pltpu.VMEM((width, width), bf16),
        ],
        compiler_params=params(30),
        name="feed_forward",
        cost_estimate=cost(10),
    )(*inverses, tokens, cotangent, *attended, vectors, shift_in, *pieces)


def middle_kernel(
    plan,
    info,
    sums_inverse,
    cotangent,
    attended_a,
    attended_b,
    mixed_a,
    mixed_b,
    scale_a,
    scale_b,
    vectors,
    resid,
    grad_normed,
    w_out,
    grad_resid,
    grads_a,
    grads_b,
    to_twin,
    to_other,
    sums,
    own,
    low_half,
    high_half,
    levels,
    ends,
    denoms,
    flat,
):
    width = cotangent.shape[1]
    wide = width // 2
    center, rstd = ln_stats(resid[...])
    grad_in, gain_terms = ln_back(grad_normed[...], center, rstd, vectors[pl.ds(3, 1), :])
    grad_out = cotangent[...].astype(f32)
    total = grad_out + grad_in
    grad_resid[...] = total
    low = total.astype(bf16)
    sums[pl.ds(0, 1), :] = jnp.zeros((1, width), f32)
    sums[pl.ds(1, 1), :] = jnp.zeros((1, width), f32)
    sums[pl.ds(2, 1), :] = column_sum(low.astype(f32))
    sums[pl.ds(3, 1), :] = column_sum(gain_terms)
    sums[pl.ds(4, 1), :] = column_sum(grad_normed[...])
    sums[pl.ds(5, 1), :] = column_sum(grad_out)
    for quad in range(2):
        lines = pl.ds(quad * wide, wide)
        flat[lines, :] = dot_tn((attended_a, attended_b)[quad][...], low).astype(bf16)
        numer = dot_nt(low, w_out[lines, :]) * (scale_a, scale_b)[quad][...]
        denom = -(numer * (mixed_a, mixed_b)[quad][...])
        for chunk in range(2 * wide // 128):
            source = numer if chunk < wide // 128 else denom
            lane = chunk * 128 % wide
            levels[chunk, pl.ds(0, plan.rows), :] = source[:, lane : lane + 128]
            for level in range(1, LEVELS):
                count, at = plan.counts[level], plan.query_at[level]
                below = plan.query_at[level - 1]
                levels[chunk, pl.ds(at, count), :] = (
                    levels[chunk, pl.ds(below, count, stride=2), :]
                    + levels[chunk, pl.ds(below + 1, count, stride=2), :]
                )
                rest = plan.padded[level] - count
                if rest:
                    levels[chunk, pl.ds(at + count, rest), :] = jnp.zeros((rest, 128), f32)
            grads = (grads_a, grads_b)[quad]
            grads[:, pl.ds(chunk * 128, 128)] = levels[chunk].astype(bf16)
        for k in range(2 * LEVELS):
            level, here = k % LEVELS, pl.ds(k * HALO, HALO)
            at = plan.query_at[level] + (0 if k < LEVELS else plan.counts[level] - HALO)
            there = pl.ds(at, HALO)
            ends[here, pl.ds(quad * wide, wide)] = (grads_a, grads_b)[quad][there, pl.ds(0, wide)]
            for chunk in range(wide // 128):
                lanes = pl.ds(quad * wide + chunk * 128, 128)
                denoms[here, lanes] = levels[wide // 128 + chunk, there, :]
    feature = lax.broadcasted_iota(jnp.int32, (width, LINE), 0)
    lane = lax.broadcasted_iota(jnp.int32, (width, LINE), 1)
    pick = jnp.where(lane == feature // HEAD_DIM, 1.0, 0.0).astype(bf16)
    heads = width // HEAD_DIM
    values = denoms[...]
    first = values.astype(bf16)
    values = dot_nn(first, pick) + dot_nn((values - first.astype(f32)).astype(bf16), pick)
    first = values.astype(bf16).astype(f32)
    both = jnp.concatenate([first[:, :heads], (values - first)[:, :heads]], axis=1)
    both = jnp.concatenate([both, jnp.zeros((both.shape[0], LINE - 2 * heads), f32)], axis=1)
    ends[:, pl.ds(width, LINE)] = both.astype(bf16)
    hand_out(info, ends, to_twin, to_other)
    half, block = own.shape[0], own.shape[1]
    other = (low_half, high_half)
    for p in range(2 * half):
        rows = flat[pl.ds(pl.multiple_of(sums_inverse[p] * block, block), block), :]
        if p < half:
            own[p] = rows
        else:
            other[(p - half) // 8][(p - half) % 8] = rows


def middle(plan, info, sums_inverse, cotangent, attended, mixed, scale, vectors, resid, grad_normed, w_out):
    rows, width = cotangent.shape
    size = LEVELS * HALO
    return pl.pallas_call(
        functools.partial(middle_kernel, plan),
        out_shape=(
            jax.ShapeDtypeStruct((rows, width), f32),
            jax.ShapeDtypeStruct((plan.query_rows, width), bf16),
            jax.ShapeDtypeStruct((plan.query_rows, width), bf16),
            jax.ShapeDtypeStruct((size, width + LINE), bf16),
            jax.ShapeDtypeStruct((size, width + LINE), bf16),
            jax.ShapeDtypeStruct((8, width), f32),
            jax.ShapeDtypeStruct((BLOCKS // 2, width // BLOCKS, width), bf16),
            jax.ShapeDtypeStruct((BLOCKS // 4, width // BLOCKS, width), bf16),
            jax.ShapeDtypeStruct((BLOCKS // 4, width // BLOCKS, width), bf16),
        ),
        in_specs=[SCALARS] * 2 + spec(11),
        out_specs=tuple(spec(9)),
        scratch_shapes=[
            pltpu.VMEM((width // 128, plan.query_rows, 128), f32),
            pltpu.VMEM((2 * size, width + LINE), bf16),
            pltpu.VMEM((2 * size, width), f32),
            pltpu.VMEM((width, width), bf16),
        ],
        compiler_params=params(20),
        name="middle",
        cost_estimate=cost(3),
    )(info, sums_inverse, cotangent, *attended, *mixed, *scale, vectors, resid, grad_normed, w_out)


def attend_back_kernel(plan, total, info, *refs):
    queries, pairs, halos, grads, grad_queries, grad_extended, extended = (
        refs[2 * k : 2 * k + 2] for k in range(7)
    )
    device = info[0]
    width = QUAD_WIDTH
    for quad in range(2):
        fill_extended(plan, pairs[quad], halos[quad], extended[quad])
        grad_extended[quad][...] = jnp.zeros(grad_extended[quad].shape, f32)
    masks = head_masks(BLOCK)
    first_head = lax.broadcasted_iota(jnp.int32, (BLOCK, 128), 1) < HEAD_DIM
    keys = pl.ds(0, width)
    values = pl.ds(width, width)

    def prepare(block):
        level, part = plan.locate(block)
        here = pl.ds(pl.multiple_of(BLOCK * block, BLOCK), BLOCK)
        there = pl.ds(pl.multiple_of(BLOCK * block + 2 * HALO * level, BLOCK), WINDOW)
        first = device * (plan.rows >> level) + BLOCK * part
        key_row = first - HALO + lax.broadcasted_iota(jnp.int32, (WINDOW, 128), 0)
        lane = lax.broadcasted_iota(jnp.int32, (WINDOW, 128), 1)
        row = first + (lane & (BLOCK - 1))
        allowed = admitted(
            tile_codes(info, row, level, total, FAR),
            tile_codes(info, key_row, level, total, -FAR),
            level,
        )
        allowed = jnp.concatenate([allowed] * (QUAD * BLOCK // 128), axis=1) > 0.0
        counts = live_counts(info, key_row, level, total).astype(bf16)
        return here, there, allowed, counts

    def block_step(step, carry):
        work = []
        for k in range(4):
            here, there, allowed, counts = prepare(step * 4 + k)
            for quad in range(2):
                q = spread_heads(queries[quad][here, :], masks)
                g = spread_heads(grads[quad][here, keys], masks)
                d = spread_heads(grads[quad][here, values], masks)
                work.append((quad, here, there, allowed, counts, q, g, d))
        scores, grad_probs = [], []
        for quad, here, there, allowed, counts, q, g, d in work:
            scores.append(dot_nt(extended[quad][there, keys], q))
            v = extended[quad][there, values]
            value_and_count = jnp.concatenate([v] + [counts] * (width // 128), axis=1)
            grad_probs.append(dot_nt(value_and_count, jnp.concatenate([g, d], axis=1)))
        weights = [
            jnp.where(item[3], jnp.exp(score), 0.0) for item, score in zip(work, scores)
        ]
        grad_scores = [(x * y).astype(bf16) for x, y in zip(grad_probs, weights)]
        probs = [weight.astype(bf16) for weight in weights]
        keys_of = [extended[item[0]][item[2], keys] for item in work]
        to_queries = [
            [
                dot_tn(grad_score[:, 128 * half : 128 * half + 128], k[:, 128 * half : 128 * half + 128])
                for half in range(2)
            ]
            for grad_score, k in zip(grad_scores, keys_of)
        ]
        to_keys = [dot_nn(grad_score, item[5]) for grad_score, item in zip(grad_scores, work)]
        to_values = [dot_nn(prob, item[6]) for prob, item in zip(probs, work)]
        for item, parts, to_key, to_value in zip(work, to_queries, to_keys, to_values):
            quad, here, there = item[:3]
            for half in range(2):
                grad_queries[quad][here, pl.ds(128 * half, 128)] = join_pair(
                    parts[half], first_head
                ) * (1.0 / math.sqrt(HEAD_DIM))
            grad_extended[quad][there, keys] += to_key
            grad_extended[quad][there, values] += to_value
        return carry

    lax.fori_loop(0, len(plan.blocks) // 4, block_step, 0, unroll=1)


def attend_back(plan, total, info, queries, pairs, halos, grads):
    width = queries[0].shape[1]
    outs = pl.pallas_call(
        functools.partial(attend_back_kernel, plan, total),
        out_shape=[jax.ShapeDtypeStruct((plan.query_rows, width), f32)] * 2
        + [jax.ShapeDtypeStruct((plan.key_rows, 2 * width), f32)] * 2,
        in_specs=[SCALARS] + spec(8),
        out_specs=spec(4),
        scratch_shapes=[
            pltpu.VMEM((plan.key_rows, 2 * width), bf16),
            pltpu.VMEM((plan.key_rows, 2 * width), bf16),
        ],
        compiler_params=params(24),
        name="attend_back",
        cost_estimate=cost(12),
    )(info, *queries, *pairs, *halos, *grads)
    return outs[:2], outs[2:]


def edge_back_kernel(
    plan,
    total,
    info,
    queries_a,
    queries_b,
    pairs_a,
    pairs_b,
    from_twin,
    from_other,
    low,
    high,
    grads,
):
    width = queries_a.shape[1]
    device = info[0]
    place_halos(info, from_twin, from_other, grads)
    two = 2 * HALO
    masks = head_masks(two)
    keys = pl.ds(0, width)
    key = lax.broadcasted_iota(jnp.int32, (two, 128), 0)
    lane = lax.broadcasted_iota(jnp.int32, (two, 128), 1) & (two - 1)
    heads = 2 * width // HEAD_DIM
    source = lax.broadcasted_iota(jnp.int32, (LINE, width), 0)
    target = lax.broadcasted_iota(jnp.int32, (LINE, width), 1)
    picks = []
    for quad in range(2):
        head = target // HEAD_DIM + quad * QUAD
        wanted = jnp.where(target % HEAD_DIM == 0, head, -1)
        wanted = jnp.where(target % HEAD_DIM == 1, head + heads, wanted)
        picks.append(jnp.where(source == wanted, 1.0, 0.0).astype(bf16))
    facing = jnp.where((key < HALO) == (lane < HALO), 1.0, 0.0)
    for level in range(LEVELS):
        count, at = plan.counts[level], plan.query_at[level]
        start = device * count
        key_row = start + jnp.where(key < HALO, key, count - two + key)
        row = start + jnp.where(lane < HALO, lane - HALO, count - HALO + lane)
        allowed = facing * admitted(
            tile_codes(info, row, level, total, FAR),
            tile_codes(info, key_row, level, total, -FAR),
            level,
        )
        allowed = jnp.concatenate([allowed] * (QUAD * two // 128), axis=1) > 0.0
        counts = live_counts(info, key_row, level, total).astype(bf16)
        ahead = pl.ds(HALO * level, HALO)
        behind = pl.ds(HALO * (LEVELS + level), HALO)

        def both(source, lanes):
            return jnp.concatenate([source[ahead, lanes], source[behind, lanes]], axis=0)

        denoms = both(grads, pl.ds(2 * width, LINE))
        for quad in range(2):
            pairs = (pairs_a, pairs_b)[quad]
            own = jnp.concatenate(
                [pairs[pl.ds(at, HALO), :], pairs[pl.ds(at + count - HALO, HALO), :]], axis=0
            )
            k, v = own[:, :width], own[:, width:]
            q = spread_heads(both((queries_a, queries_b)[quad], keys), masks)
            g = spread_heads(both(grads, pl.ds(quad * width, width)), masks)
            d = spread_heads(dot_nn(denoms, picks[quad]).astype(bf16), masks)
            value_and_count = jnp.concatenate([v] + [counts] * (width // 128), axis=1)
            weight = jnp.where(allowed, jnp.exp(dot_nt(k, q)), 0.0)
            grad_probs = dot_nt(value_and_count, jnp.concatenate([g, d], axis=1))
            grad_score = (grad_probs * weight).astype(bf16)
            there = pl.ds(HALO * (quad * LEVELS + level), HALO)
            grad_keys = dot_nn(grad_score, q)
            grad_values = dot_nn(weight.astype(bf16), g)
            low[there, keys] = grad_keys[:HALO]
            high[there, keys] = grad_keys[HALO:]
            low[there, pl.ds(width, width)] = grad_values[:HALO]
            high[there, pl.ds(width, width)] = grad_values[HALO:]


def edge_back(plan, total, info, queries, pairs, from_twin, from_other):
    width = queries[0].shape[1]
    size = 2 * LEVELS * HALO
    return pl.pallas_call(
        functools.partial(edge_back_kernel, plan, total),
        out_shape=[jax.ShapeDtypeStruct((size, 2 * width), f32)] * 2,
        in_specs=[SCALARS] + spec(6),
        out_specs=spec(2),
        scratch_shapes=[pltpu.VMEM((size, 2 * width + LINE), bf16)],
        compiler_params=params(10),
        name="edge_back",
        cost_estimate=cost(2.5),
    )(info, *queries, *pairs, from_twin, from_other)


def finish_kernel(
    plan,
    total,
    info,
    inverse,
    tokens,
    weight,
    vectors,
    grad_resid,
    sums,
    sum_in,
    queries_a,
    queries_b,
    pairs_a,
    pairs_b,
    edge_low,
    edge_high,
    grad_tokens,
    own,
    low_half,
    high_half,
    work,
    joined,
    flat,
    table,
):
    rows, width = tokens.shape
    device = info[0]
    half_width = width // 2
    places = device * rows + lax.broadcasted_iota(jnp.int32, (rows, 128), 0)
    live = live_counts(info, places, 0, total)
    for chunk in range(3 * width // 128):
        part, lane = divmod(chunk * 128, width)
        quad, lane = divmod(lane, half_width)
        if part == 0:
            work[chunk] = (queries_a, queries_b)[quad][:, pl.ds(lane, 128)]
        else:
            lanes = pl.ds((part - 1) * half_width + lane, 128)
            for level in range(LEVELS):
                at, count = plan.query_at[level], plan.counts[level]
                own_rows = pl.ds(plan.key_at[level] + HALO, count)
                work[chunk, pl.ds(at, count), :] = (pairs_a, pairs_b)[quad][own_rows, lanes]
                halo = pl.ds(HALO * (quad * LEVELS + level), HALO)
                work[chunk, pl.ds(at, HALO), :] += edge_low[halo, lanes]
                work[chunk, pl.ds(at + count - HALO, HALO), :] += edge_high[halo, lanes]
        for level in range(LEVELS - 1, 0, -1):
            count = plan.counts[level]
            upper = work[chunk, pl.ds(plan.query_at[level], count), :]
            if chunk * 128 < 2 * width:
                upper = upper * 0.5
            for parity in range(2):
                there = pl.ds(plan.query_at[level - 1] + parity, count, stride=2)
                work[chunk, there, :] = work[chunk, there, :] + upper
        value = work[chunk, pl.ds(0, rows), :]
        if chunk * 128 >= 2 * width:
            value = value * live
        joined[:, pl.ds(chunk * 128, 128)] = value.astype(bf16)
    values = tokens[...].astype(f32)
    center, rstd = ln_stats(values)
    gain = vectors[pl.ds(0, 1), :]
    normed = (center * rstd * gain + vectors[pl.ds(1, 1), :]).astype(bf16)
    half, block = own.shape[0], own.shape[1] // 4
    other = (low_half, high_half)
    for part in range(3):
        columns = pl.ds(part * width, width)
        flat[...] = dot_tn(normed, joined[:, columns])
        for p in range(2 * half):
            i = inverse[p]
            lines = flat[pl.ds(pl.multiple_of(i * block, block), block), :]
            there = pl.ds(part * block, block)
            if p < half:
                own[p, there, :] = lines.astype(bf16)
            else:
                other[(p - half) // 8][(p - half) % 8, there, :] = lines.astype(bf16)
    grad_normed = dot_nt(joined[...], weight[...])
    grad_in, gain_terms = ln_back(grad_normed, center, rstd, gain)
    grad_tokens[...] = grad_resid[...] + grad_in
    singles = [column_sum(gain_terms), column_sum(grad_normed)]
    singles += [sums[pl.ds(k, 1), :] for k in range(2, 6)]
    table[...] = pack_vectors(singles, sum_in[...], 2 * half, table.shape[1])
    row = lax.broadcasted_iota(jnp.int32, (block, 2 * LINE), 0)
    there = pl.ds(3 * block, block)
    for p in range(2 * half):
        i = inverse[p]
        line = table[pl.ds(i, 1), :]
        lines = jnp.where(row == 0, line, 0.0)
        lines = jnp.concatenate([lines, jnp.zeros((block, width - 2 * LINE), f32)], axis=1)
        if p < half:
            own[p, there, :] = lines.astype(bf16)
        else:
            other[(p - half) // 8][(p - half) % 8, there, :] = lines.astype(bf16)


def finish(plan, total, info, inverse, tokens, weight, *rest):
    rows, width = tokens.shape
    half = BLOCKS // 2
    block = width // BLOCKS
    return pl.pallas_call(
        functools.partial(finish_kernel, plan, total),
        out_shape=(
            jax.ShapeDtypeStruct((rows, width), f32),
            jax.ShapeDtypeStruct((half, 4 * block, width), bf16),
            jax.ShapeDtypeStruct((half // 2, 4 * block, width), bf16),
            jax.ShapeDtypeStruct((half // 2, 4 * block, width), bf16),
        ),
        in_specs=[SCALARS, SCALARS] + spec(2 + len(rest)),
        out_specs=tuple(spec(4)),
        scratch_shapes=[
            pltpu.VMEM((3 * width // 128, plan.query_rows, 128), f32),
            pltpu.VMEM((rows, 3 * width), bf16),
            pltpu.VMEM((width, width), f32),
            pltpu.VMEM((BLOCKS, 2 * LINE), f32),
        ],
        compiler_params=params(28),
        name="finish",
        cost_estimate=cost(6.2),
    )(info, inverse, tokens, weight, *rest)


class Ring:
    def __init__(self, devices, *orders):
        self.devices = devices
        self.orders = orders
        self.stages = len(orders[0])

    def partner(self, stage):
        return [(i, i ^ self.orders[i & 1][stage]) for i in range(self.devices)]

    def twin(self):
        return [(i, i ^ 1) for i in range(self.devices)]

    def places(self, device):
        found = []
        even = (device & 1) == 0
        for base, swap in ((device, False), (device ^ 1, True)):
            for position in range(1 << self.stages):
                masks = [
                    sum(order[k] for k in range(self.stages) if position >> k & 1)
                    for order in self.orders
                ]
                if swap:
                    masks = masks[::-1]
                found.append(base ^ jnp.where(even, *masks))
        return found

    def step(self, stage, arrays):
        route = self.twin() if stage == self.stages else self.partner(stage)
        return [lax.ppermute(item, "seq", route) for item in arrays]

    def fold(self, stage, own, low, high):
        half = 1 << stage
        sent = (own[half:].astype(f32) + high.astype(f32)).astype(bf16)
        kept = own[:half].astype(f32) + low.astype(f32)
        return kept, sent


def halves(item):
    half = item.shape[0] // 2
    return item[:half], item[half:]


def join(held, came):
    return [jnp.concatenate(pair) for pair in zip(held, came)]


def pack_kernel(rings, lengths, w_qkv, w_out, w_in, w_back, *refs):
    vectors, (info, *inverses, payload, staged) = refs[:-5], refs[-5:]
    device = lax.axis_index("seq")
    info[0] = device
    start = jnp.int32(0)
    for k in range(3):
        length = lengths[k]
        info[1 + k] = length
        info[4 + k] = start
        start = start + (length + 15) // 16 * 16
        info[7 + k] = start
    for ring, inverse in zip(rings, inverses):
        for place, block in enumerate(ring.places(device)):
            inverse[place] = block
    block, width = w_out.shape
    chunks = w_in.shape[1] // width
    staged[...] = jnp.zeros(staged.shape, f32)
    for k, vector in enumerate(vectors):
        size = vector.shape[0]
        lane = k * block
        staged[pl.ds(0, 1), pl.ds(lane, size)] = vector[...].astype(f32).reshape(1, size)
    for c in range(3):
        payload[0, pl.ds(block * c, block), :] = w_qkv[:, pl.ds(c * width, width)]
    payload[0, pl.ds(block * 3, block), :] = staged[...].astype(bf16)
    payload[0, pl.ds(block * 4, block), :] = w_out[...]
    for c in range(chunks):
        payload[0, pl.ds(block * (c + 5), block), :] = w_in[:, pl.ds(c * width, width)]
    payload[0, pl.ds(block * (chunks + 5), block * chunks), :] = w_back[...]


def pack(rings, lengths, w_qkv, w_out, w_in, w_back, vectors):
    block, width = w_out.shape
    rows = 5 * block + w_in.shape[1] // width * block + w_back.shape[0]
    return pl.pallas_call(
        functools.partial(pack_kernel, rings),
        out_shape=(
            jax.ShapeDtypeStruct((10,), jnp.int32),
            jax.ShapeDtypeStruct((BLOCKS,), jnp.int32),
            jax.ShapeDtypeStruct((BLOCKS,), jnp.int32),
            jax.ShapeDtypeStruct((1, rows, width), bf16),
        ),
        in_specs=[SCALARS] + spec(4 + len(vectors)),
        out_specs=(SCALARS,) * 3 + tuple(spec(1)),
        scratch_shapes=[pltpu.VMEM((block, width), f32)],
        compiler_params=params(62),
        name="pack",
        cost_estimate=cost(1.5),
    )(lengths, w_qkv, w_out, w_in, w_back, *vectors)


def unpack_kernel(kept_one, came_one, kept_two, came_two, *outs):
    block, width = kept_one.shape[1] // 4, kept_two.shape[2]
    w_qkv, w_out, w_in, w_back = outs[:4]
    for c in range(3):
        rows = pl.ds(block * c, block)
        w_qkv[:, pl.ds(c * width, width)] = kept_one[0, rows, :] + came_one[0, rows, :].astype(f32)
    rows = pl.ds(block * 3, block)
    lines = kept_one[0, rows, :] + came_one[0, rows, :].astype(f32)
    for k, out in enumerate(outs[4:]):
        size = out.shape[0]
        lane = k * block
        out[...] = lines[0:1, lane : lane + size].reshape(size)
    chunks = w_in.shape[1] // width

    def total(at, size):
        rows = pl.ds(at, size)
        return kept_two[0, rows, :] + came_two[0, rows, :].astype(f32)

    w_out[...] = total(2 * block * chunks, block)
    for c in range(chunks):
        w_in[:, pl.ds(c * width, width)] = total(block * c, block)
    w_back[...] = total(block * chunks, block * chunks)


def unpack(kept_one, came_one, kept_two, came_two, like):
    return pl.pallas_call(
        unpack_kernel,
        out_shape=[jax.ShapeDtypeStruct(item.shape, f32) for item in like],
        in_specs=spec(4),
        out_specs=spec(len(like)),
        compiler_params=params(62),
        name="unpack",
        cost_estimate=cost(1.5),
    )(kept_one, came_one, kept_two, came_two)


def exchange(to_twin, to_other):
    count = lax.axis_size("seq")
    twin = [(i, i ^ 1) for i in range(count)]
    other = [(i, i + 1) for i in range(1, count - 1, 2)]
    other += [(j, i) for i, j in other]
    return lax.ppermute(to_other, "seq", other), lax.ppermute(to_twin, "seq", twin)


def order(items, *after):
    return lax.optimization_barrier((items, after))[0]


def per_device(
    lengths,
    tokens,
    ln1_gain,
    ln1_bias,
    w_qkv,
    w_out,
    out_bias,
    ln2_gain,
    ln2_bias,
    w_in,
    in_bias,
    w_back,
    back_bias,
    cotangent,
):
    devices = lax.axis_size("seq")
    device = lax.axis_index("seq")
    rows, width = tokens.shape
    total = rows * devices
    plan = Plan(rows)
    block = width // BLOCKS
    chunks = w_in.shape[1] // width
    small = (ln1_gain, ln1_bias, out_bias, ln2_gain, ln2_bias, back_bias, in_bias)
    direct = devices == BLOCKS
    ring = Ring(BLOCKS, (16, 8, 4, 2), (2, 16, 8, 4))
    sums_ring = Ring(BLOCKS, (16, 8, 4, 2), (2, 16, 8, 4))
    last = ring.stages - 1
    core = ring.stages
    if direct:
        info, inverse, sums_inverse, payload = pack(
            (ring, sums_ring), lengths, w_qkv, w_out, w_in, w_back, small
        )
        from_other, from_twin = exchange(*edge_sums(plan, total, info, order(tokens, payload)))
        (payload,) = join([payload], ring.step(0, [payload]))
        a, b = payload[:, : 4 * block], payload[:, 4 * block :]
        a_came, b_came = ring.step(1, [a, b])
        (a,) = join([a], [a_came])
        a = order(a, from_other, from_twin)
        (a_came,) = ring.step(2, [a])
        (a,) = join([a], [a_came])
        (b,) = join([b], [b_came])
        a = order(a, b)
        (b_came,) = ring.step(2, [b])
        (a_came,) = ring.step(3, [a])
        one = [a, a_came] + ring.step(core, [a, a_came])
        (b,) = join([b], [b_came])
        b = order(b, one)
    else:
        padded = (lengths + 15) // 16 * 16
        ends = jnp.cumsum(padded, dtype=jnp.int32)
        info = jnp.concatenate([device[None].astype(jnp.int32), lengths, ends - padded, ends])
        inverse = sums_inverse = jnp.arange(BLOCKS, dtype=jnp.int32)
        from_other, from_twin = exchange(*edge_sums(plan, total, info, tokens))

        def whole(item):
            return lax.all_gather(item, "seq", axis=0, tiled=True)

        def split(item, parts):
            each = BLOCKS // parts
            return [item[k * each : (k + 1) * each] for k in range(parts)]

        line = jnp.concatenate([whole(item).reshape(BLOCKS, 1, -1) for item in small], axis=2)
        line = jnp.pad(line, ((0, 0), (0, block - 1), (0, width - line.shape[2])))
        one = whole(w_qkv).reshape(BLOCKS, block, 3, width).transpose(0, 2, 1, 3)
        one = one.reshape(BLOCKS, 3 * block, width)
        one = split(jnp.concatenate([one, line], axis=1), PIECES)
        full_in = whole(w_in).reshape(BLOCKS, block, chunks, width)
        full_in = full_in.transpose(0, 2, 1, 3).reshape(BLOCKS, chunks * block, width)
        full_two = [
            whole(w_out).reshape(BLOCKS, block, width),
            full_in,
            whole(w_back).reshape(BLOCKS, chunks * block, width),
        ]
        two = split(jnp.concatenate(full_two, axis=1), PIECES)
    queries, pairs, halo_queries, halo_pairs, weight, vectors, shift_in = project(
        plan, total, info, inverse, tokens, from_twin, from_other, one
    )
    ready = queries[0]
    if direct:
        (b_came,) = ring.step(last, [b])
        (b_twin,) = ring.step(core, [b])
        ready = order(ready, b)
    attended, mixed, scale = attend(plan, total, info, (ready, queries[1]), pairs, halo_pairs)
    if direct:
        b_came = order(b_came, attended)
        two = [b, b_came, b_twin] + ring.step(core, [b_came])
    result, resid, grad_normed, out_weight, own_two, low_two, high_two, sum_in = feed_forward(
        (inverse, sums_inverse), tokens, cotangent, attended, vectors, shift_in, two
    )
    if direct:
        high, low = sums_ring.step(core, [high_two, low_two])
    (
        grad_resid,
        grads_a,
        grads_b,
        to_twin,
        to_other,
        sums,
        own_out,
        low_out,
        high_out,
    ) = middle(
        plan,
        info,
        sums_inverse,
        cotangent,
        attended,
        mixed,
        scale,
        vectors,
        resid,
        grad_normed,
        out_weight,
    )
    from_other, from_twin = exchange(to_twin, to_other)

    def with_out(item, out):
        return jnp.concatenate([item, out], axis=1)

    if direct:
        high_out, low_out = sums_ring.step(core, [high_out, low_out])
        kept, sent = sums_ring.fold(
            last, with_out(own_two, own_out), with_out(low, low_out), with_out(high, high_out)
        )
        sent_low, sent_high = halves(sent)
        (high,) = sums_ring.step(last, [sent_high])
        grads_a = order(grads_a, sent_high)
    grad_queries, grad_pairs = attend_back(
        plan, total, info, queries, pairs, halo_pairs, (grads_a, grads_b)
    )
    from_other, from_twin = order((from_other, from_twin), grad_queries)
    if direct:
        sent_low, high = order((sent_low, high), grad_queries, from_other, from_twin)
        (low,) = sums_ring.step(last, [sent_low])
        kept, kept_high = halves(kept)
        sent = (kept_high + high.astype(f32)).astype(bf16)
        (came,) = sums_ring.step(last - 1, [sent])
        from_other, from_twin = order((from_other, from_twin), sent_low, sent)
    edges = edge_back(plan, total, info, halo_queries, pairs, from_twin, from_other)
    grad_tokens, own_one, low_one, high_one = finish(
        plan,
        total,
        info,
        sums_inverse,
        tokens,
        weight,
        vectors,
        grad_resid,
        sums,
        sum_in,
        *grad_queries,
        *grad_pairs,
        *edges,
    )
    if direct:
        high_one, low_one = sums_ring.step(core, [high_one, low_one])
        low, came = order((low, came), grad_tokens)
        kept = kept + low.astype(f32)
        kept, sent = sums_ring.fold(last - 2, kept, *halves(came))
        (came,) = sums_ring.step(last - 2, [sent])
        high_one, low_one = order((high_one, low_one), sent)
        own_one, sent_one = sums_ring.fold(last, own_one, low_one, high_one)
        (came_one,) = sums_ring.step(last, [sent_one])
        own_one, sent_one = sums_ring.fold(last - 1, own_one, *halves(came_one))
        (came_one,) = sums_ring.step(last - 1, [sent_one])
        came = order(came, sent_one)
        kept, sent = sums_ring.fold(0, kept, *halves(came))
        (came,) = sums_ring.step(0, [sent])
        came_one = order(came_one, sent)
        own_one, sent_one = sums_ring.fold(last - 2, own_one, *halves(came_one))
        (came_one,) = sums_ring.step(last - 2, [sent_one])
        own_one, sent_one = sums_ring.fold(0, own_one, *halves(came_one))
        (came_one,) = sums_ring.step(0, [sent_one])
        grads = unpack(own_one, came_one, kept, came, (w_qkv, w_out, w_in, w_back) + small)
        grad_w_qkv, grad_w_out, grad_w_in, grad_w_back = grads[:4]
        parts = grads[4:]
    else:

        def shared(item):
            return lax.psum_scatter(item, "seq", scatter_dimension=0, tiled=True)

        full = jnp.concatenate([x.astype(f32) for x in (own_one, low_one, high_one)])
        line = full[:, 3 * block]
        sizes = [block] * 6 + [chunks * block]
        starts = [k * block for k in range(7)]
        parts = [
            shared(line[:, at : at + size].reshape(-1)) for at, size in zip(starts, sizes)
        ]
        grad_w_qkv = full[:, : 3 * block].reshape(BLOCKS, 3, block, width).transpose(0, 2, 1, 3)
        grad_w_qkv = shared(grad_w_qkv.reshape(width, 3 * width))
        full = jnp.concatenate([x.astype(f32) for x in (own_out, low_out, high_out)])
        grad_w_out = shared(full.reshape(width, width))
        full = jnp.concatenate([x.astype(f32) for x in (own_two, low_two, high_two)])
        full_in = full[:, : block * chunks]
        full_in = full_in.reshape(BLOCKS, chunks, block, width).transpose(0, 2, 1, 3)
        grad_w_in = shared(full_in.reshape(width, chunks * width))
        grad_w_back = shared(full[:, block * chunks :].reshape(chunks * width, width))
    gain_one, bias_one, shift_out, gain_two, bias_two, shift_back, shift_hidden = parts
    return (
        result,
        grad_tokens,
        gain_one,
        bias_one,
        grad_w_qkv,
        grad_w_out,
        shift_out,
        gain_two,
        bias_two,
        grad_w_in,
        shift_hidden,
        grad_w_back,
        shift_back,
    )


def solution(mesh):
    flat, wide = P("seq"), P("seq", None)
    weights = (flat, flat, wide, wide, flat, flat, flat, wide, flat, wide, flat)
    return jax.shard_map(
        per_device,
        mesh=mesh,
        in_specs=(P(), wide) + weights + (wide,),
        out_specs=(wide, wide) + weights,
        check_vma=False,
    )
```

time: 162 us -> 146 us (0.901)
  waiting for transfers between devices: 68 us -> 58.8 us
  starting transfers between devices: 38.5 us -> 30.4 us
  local copies, waits for them, and re-layouts: 1.65 us -> 3.65 us
    ppermute x27 -> x26, waiting for transfers between devices: 66.1 us -> 58.8 us  [step(): return [lax.ppermute(item, 'seq', route) for item in arrays]]
    pallas_call x2 -> x1, Pallas kernels: 13 us -> 8.63 us  [attend_back(): pl.pallas_call(functools.partial(attend_back_kernel, plan, total), out_sh...]
    ppermute x27 -> x26, starting transfers between devices: 31.9 us -> 27.6 us  [step(): return [lax.ppermute(item, 'seq', route) for item in arrays]]
    ppermute x8 -> x4, starting transfers between devices: 6.63 us -> 2.85 us  [the longest x2 1.51 us: exchange(): lax.ppermute(to_twin, 'seq', twin)]
    pallas_call x4 -> x6, Pallas kernels: 24.1 us -> 27.2 us  [the longest x1 10.2 us: feed_forward(): pl.pallas_call(functools.partial(forward_kernel, parts), out_shape=(jax.S...]
    ppermute x8 -> x4, waiting for transfers between devices: 1.92 us -> 0.01 us  [the longest x2 0.01 us: exchange(): lax.ppermute(to_twin, 'seq', twin)]
    unnamed x14 -> x20, local copies, waits for them, and re-layouts: 1.63 us -> 3.48 us
  transfers between devices with their start and end apart: 35 -> 30, of which waited for: 22 -> 17; matrix products, arithmetic and copies ran while one was open for 2% -> 2% of each run, Pallas kernels for 18% -> 24%
where the time goes in v4:
time: 146 us
  waiting for transfers between devices  58.8 us (40%)
  Pallas kernels  48.5 us (33%)
  starting transfers between devices  30.4 us (21%)
  local copies, waits for them, and re-layouts  3.65 us (2%)
  other arithmetic  3.46 us (2%)
    ppermute x26, waiting for transfers between devices, step(): return [lax.ppermute(item, 'seq', route) for item in arrays]  58.8 us
    ppermute x26, starting transfers between devices, step(): return [lax.ppermute(item, 'seq', route) for item in arrays]  27.6 us
    pallas_call x1, Pallas kernels, feed_forward(): pl.pallas_call(functools.partial(forward_kernel, parts), out_shape=(jax.S...  10.2 us
    pallas_call x1, Pallas kernels, attend_back(): pl.pallas_call(functools.partial(attend_back_kernel, plan, total), out_sh...  8.63 us
    pallas_call x1, Pallas kernels, finish(): pl.pallas_call(functools.partial(finish_kernel, plan, total), out_shape=(...  6 us
    pallas_call x1, Pallas kernels, attend(): pl.pallas_call(functools.partial(attend_kernel, plan, total), out_shape=[...  5.96 us
    pallas_call x1, Pallas kernels, project(): pl.pallas_call(functools.partial(project_kernel, plan, total), out_shape=...  4.84 us
    pallas_call x1, Pallas kernels, edge_back(): pl.pallas_call(functools.partial(edge_back_kernel, plan, total), out_shap...  4.32 us
  transfers between devices with their start and end apart: 30, of which 17 were waited for; matrix products, arithmetic and copies ran while one was open for 2% of the time, Pallas kernels for 24%

profile of v4, /device:TPU:0, one launch (start us, length us, event | category | flops | bytes accessed | tf_op | source)
XLA Modules:
  0.0 146.1 jit_solution(12494112409157831548)
XLA Ops:
  0.6 1.8 %pack.1 = (s32[10]{0:T(128)}, s32[32]{0:T(128)}, s32[32]{0:T(128)}, bf16[1,208,512]{2,1,0:T(8,128)(2,1)}) custom-call(s32[3]{0:T(128)} %lengths.1, bf16[16,1536]{1,0:T(8,128)(2,1)} %w_qkv.1, bf16[16,512]{1,0:T(8,128)(2,1)} %w_out.1, bf16[16,2048]{1,0:T(8,128)(2,1)} %w_in.1, bf16[64,512]{1,0:T(8,128)(2,1)} %w_back.1, bf16[16]{0:T(256)(128)(2,1)} %refs_0_.1, ...), custom_call_target="tpu_custom_call" | custom-call | flops 1 | bytes 1 | tf_op jit(solution)/shard_map/pack/pallas_call | solution.py:1083
  2.4 4.1 %collective-permute-start.2 = (bf16[1,208,512]{2,1,0:T(8,128)(2,1)}, bf16[1,208,512]{2,1,0:T(8,128)(2,1)S(1)}, u32[]{:S(2)}, u32[]{:S(2)}) collective-permute-start(bf16[1,208,512]{2,1,0:T(8,128)(2,1)} %get-tuple-element.96), channel_id=1, source_target_pairs={{0,16},{1,3},{2,18},{3,1},{4,20},{5,7},{6,22},{7,5},{8,24},{9,11},... | collective-permute-start | bytes 638984 | tf_op jit(solution)/shard_map/ppermute | solution.py:1032
  8.2 1.7 %edge_sums.1 = (bf16[160,1024]{1,0:T(8,128)(2,1)S(1)}, bf16[160,1024]{1,0:T(8,128)(2,1)S(1)}) custom-call(s32[10]{0:T(128)S(1)} %copy-done.3, bf16[512,512]{1,0:T(8,128)(2,1)S(1)} %copy-done), custom_call_target="tpu_custom_call" | custom-call | flops 1 | bytes 1 | tf_op jit(solution)/shard_map/edge_sums/pallas_call | solution.py:242
  11.6 1.2 collective-permute-done.2
  12.9 4.1 %collective-permute-start.3 = (bf16[2,64,512]{2,1,0:T(8,128)(2,1)S(1)}, bf16[2,64,512]{2,1,0:T(8,128)(2,1)S(1)}, u32[]{:S(2)}, u32[]{:S(2)}) collective-permute-start(bf16[2,64,512]{2,1,0:T(8,128)(2,1)S(1)} %slice.120), channel_id=1, source_target_pairs={{0,8},{1,17},{2,10},{3,19},{4,12},{5,21},{6,14},{7,23},{8,0},{9,25... | collective-permute-start | bytes 393224 | tf_op jit(solution)/shard_map/ppermute | solution.py:1032
  17.0 7.2 %collective-permute-done.3 = bf16[2,64,512]{2,1,0:T(8,128)(2,1)S(1)} collective-permute-done((bf16[2,64,512]{2,1,0:T(8,128)(2,1)S(1)}, bf16[2,64,512]{2,1,0:T(8,128)(2,1)S(1)}, u32[]{:S(2)}, u32[]{:S(2)}) %collective-permute-start.3) | collective-permute-done | bytes 131104 | tf_op jit(solution)/shard_map/ppermute | solution.py:1032
  24.4 8.3 %collective-permute-done.5 = bf16[2,144,512]{2,1,0:T(8,128)(2,1)S(1)} collective-permute-done((bf16[2,144,512]{2,1,0:T(8,128)(2,1)S(1)}, bf16[2,144,512]{2,1,0:T(8,128)(2,1)S(1)}, u32[]{:S(2)}, u32[]{:S(2)}) %collective-permute-start.5) | collective-permute-done | bytes 294944 | tf_op jit(solution)/shard_map/ppermute | solution.py:1032
  33.1 9.0 %collective-permute-done.6.refs_1_ = bf16[8,64,512]{2,1,0:T(8,128)(2,1)S(1)} collective-permute-done((bf16[8,64,512]{2,1,0:T(8,128)(2,1)S(1)}, bf16[8,64,512]{2,1,0:T(8,128)(2,1)S(1)}, u32[]{:S(2)}, u32[]{:S(2)}) %collective-permute-start.6) | collective-permute-done | bytes 524320 | tf_op jit(solution)/shard_map/ppermute | solution.py:1032
  42.1 3.7 %collective-permute-start.8 = (bf16[8,64,512]{2,1,0:T(8,128)(2,1)S(1)}, bf16[8,64,512]{2,1,0:T(8,128)(2,1)S(1)}, u32[]{:S(2)}, u32[]{:S(2)}) collective-permute-start(bf16[8,64,512]{2,1,0:T(8,128)(2,1)S(1)} %collective-permute-done.6.refs_1_), channel_id=1, source_target_pairs={{0,1},{1,0},{2,3},{3,2},{4,5},{5,4},{6,7},{7,6},{8,9},{9,8},{10,11... | collective-permute-start | bytes 1572872 | tf_op jit(solution)/shard_map/ppermute | solution.py:1032
  45.8 1.6 %collective-permute-done.9 = bf16[4,144,512]{2,1,0:T(8,128)(2,1)S(1)} collective-permute-done((bf16[4,144,512]{2,1,0:T(8,128)(2,1)S(1)}, bf16[4,144,512]{2,1,0:T(8,128)(2,1)S(1)}, u32[]{:S(2)}, u32[]{:S(2)}) %collective-permute-start.9) | collective-permute-done | bytes 589856 | tf_op jit(solution)/shard_map/ppermute | solution.py:1032
  47.6 2.7 %collective-permute-start.10 = (bf16[8,144,512]{2,1,0:T(8,128)(2,1)S(1)}, bf16[8,144,512]{2,1,0:T(8,128)(2,1)S(1)}, u32[]{:S(2)}, u32[]{:S(2)}) collective-permute-start(bf16[8,144,512]{2,1,0:T(8,128)(2,1)S(1)} %pad_maximum_fusion.refs_0_), channel_id=1, source_target_pairs={{0,2},{1,5},{2,0},{3,7},{4,6},{5,1},{6,4},{7,3},{8,10},{9,13},{10,... | collective-permute-start | bytes 3538952 | tf_op jit(solution)/shard_map/ppermute | solution.py:1032
  50.3 4.8 %project.1 = (bf16[1024,256]{1,0:T(8,128)(2,1)S(1)}, bf16[1024,256]{1,0:T(8,128)(2,1)S(1)}, bf16[1024,512]{1,0:T(8,128)(2,1)S(1)}, bf16[1024,512]{1,0:T(8,128)(2...) custom-call(s32[10]{0:T(128)S(1)} %copy-done.4, ...), custom_call_target="tpu_custom_call" | custom-call | flops 1 | bytes 1 | tf_op jit(solution)/shard_map/project/pallas_call | solution.py:338
  55.2 6.0 %attend.1 = (bf16[512,256]{1,0:T(8,128)(2,1)S(1)}, bf16[512,256]{1,0:T(8,128)(2,1)S(1)}, f32[512,256]{1,0:T(8,128)S(1)}, f32[512,256]{1,0:T(8,128)S(1)}, f32[512,256]{1,0:T(8,128)S(1)}, /*index=5*/f32[512,256]{1,0:T(8,128)S(1)}) custom-call(s32[10]{0:T(128)S(1)} %copy-done.4, bf16[1024,256]{1,0:T(8,128)(2,1)S(1)} %get-tuple-element.104.refs_0_, ...), custom_call_target="tpu_custom_call" | custom-call | flops 1 | bytes 1 | tf_op jit(solution)/shard_map/attend/pallas_call | solution.py:446
  61.2 3.3 %collective-permute-done.10.refs_1_ = bf16[8,144,512]{2,1,0:T(8,128)(2,1)S(1)} collective-permute-done((bf16[8,144,512]{2,1,0:T(8,128)(2,1)S(1)}, bf16[8,144,512]{2,1,0:T(8,128)(2,1)S(1)}, u32[]{:S(2)}, u32[]{:S(2)}) %collective-permute-start.10) | collective-permute-done | bytes 1179680 | tf_op jit(solution)/shard_map/ppermute | solution.py:1032
  64.5 2.8 %collective-permute-done.12.refs_3_ = bf16[8,144,512]{2,1,0:T(8,128)(2,1)S(1)} collective-permute-done((bf16[8,144,512]{2,1,0:T(8,128)(2,1)S(1)}, bf16[8,144,512]{2,1,0:T(8,128)(2,1)S(1)}, u32[]{:S(2)}, u32[]{:S(2)}) %collective-permute-start.12) | collective-permute-done | bytes 1179680 | tf_op jit(solution)/shard_map/ppermute | solution.py:1032
  67.3 10.2 %feed_forward.1 = (bf16[512,512]{1,0:T(8,128)(2,1)}, f32[512,512]{1,0:T(8,128)S(1)}, f32[512,512]{1,0:T(8,128)S(1)}, bf16[512,512]{1,0:T(8,128)(2,1)S(1)}, bf16[...) custom-call(s32[32]{0:T(128)S(1)} %copy-done.6, ...), custom_call_target="tpu_custom_call" | custom-call | flops 1 | bytes 1 | tf_op jit(solution)/shard_map/feed_forward/pallas_call | solution.py:552
  78.0 3.3 %middle.1 = (f32[512,512]{1,0:T(8,128)S(1)}, bf16[1024,512]{1,0:T(8,128)(2,1)S(1)}, bf16[1024,512]{1,0:T(8,128)(2,1)S(1)}, bf16[160,640]{1,0:T(8,128)(2,1)S(1)},...) custom-call(s32[10]{0:T(128)S(1)} %copy-done.4, ...), custom_call_target="tpu_custom_call" | custom-call | flops 1 | bytes 1 | tf_op jit(solution)/shard_map/middle/pallas_call | solution.py:677
  83.7 2.1 %collective-permute-start.17 = (bf16[4,144,512]{2,1,0:T(8,128)(2,1)S(1)}, bf16[4,144,512]{2,1,0:T(8,128)(2,1)S(1)}, u32[]{:S(2)}, u32[]{:S(2)}) collective-permute-start(bf16[4,144,512]{2,1,0:T(8,128)(2,1)S(1)} %get-tuple-element.180), channel_id=1, source_target_pairs={{0,2},{1,5},{2,0},{3,7},{4,6},{5,1},{6,4},{7,3},{8,10},{9,13},{10,... | collective-permute-start | bytes 1769480 | tf_op jit(solution)/shard_map/ppermute | solution.py:1032
  86.5 1.4 collective-permute-start.16
  87.9 8.6 %attend_back.1 = (f32[1024,256]{1,0:T(8,128)S(1)}, f32[1024,256]{1,0:T(8,128)S(1)}, f32[1344,512]{1,0:T(8,128)S(1)}, f32[1344,512]{1,0:T(8,128)S(1)}) custom-call(s32[10]{0:T(128)S(1)} %copy-done.4, bf16[1024,256]{1,0:T(8,128)(2,1)S(1)} %get-tuple-element.104.refs_0_, bf16[1024,256]{1,0:T(8,128)(2,1)S(1)} %get-tuple-element.105.refs_1_, ...), custom_call_target="tpu_custom_call" | custom-call | flops 1 | bytes 1 | tf_op jit(solution)/shard_map/attend_back/pallas_call | solution.py:780
  97.8 1.6 %collective-permute-start.23 = (bf16[4,144,512]{2,1,0:T(8,128)(2,1)S(1)}, bf16[4,144,512]{2,1,0:T(8,128)(2,1)S(1)}, u32[]{:S(2)}, u32[]{:S(2)}) collective-permute-start(bf16[4,144,512]{2,1,0:T(8,128)(2,1)S(1)} %fusion), channel_id=1, source_target_pairs={{0,4},{1,9},{2,6},{3,11},{4,0},{5,13},{6,2},{7,15},{8,12},{9,1},{1... | collective-permute-start | bytes 1769480 | tf_op jit(solution)/shard_map/ppermute | solution.py:1032
  99.4 1.4 collective-permute-start.22
  100.8 4.3 %edge_back.1 = (f32[320,512]{1,0:T(8,128)S(1)}, f32[320,512]{1,0:T(8,128)S(1)}) custom-call(s32[10]{0:T(128)S(1)} %copy-done.4, bf16[320,256]{1,0:T(8,128)(2,1)S(1)} %get-tuple-element.138.queries_a, bf16[320,256]{1,0:T(8,128)(2,1)S(1)} %get-tuple-element.139.queries_b, bf16[1024,512]{1,0:T(8,128)(2,1)S(1)} %get-tuple-element.106.refs_2_.pairs_a, ...), custom_call_target="tpu_custom_call" | custom-call | flops 1 | bytes 1 | tf_op jit(solution)/shard_map/edge_back/pallas_call | solution.py:873
  105.1 6.0 %finish.1 = (f32[512,512]{1,0:T(8,128)}, bf16[16,64,512]{2,1,0:T(8,128)(2,1)S(1)}, bf16[8,64,512]{2,1,0:T(8,128)(2,1)S(1)}, bf16[8,64,512]{2,1,0:T(8,128)(2,1)S(1)}) custom-call(s32[10]{0:T(128)S(1)} %copy-done.4, s32[32]{0:T(128)S(1)} %copy-done.5, bf16[512,512]{1,0:T(8,128)(2,1)S(1)} %copy-done.1, bf16[512,1536]{1,0:T(8,128)(2,1)S(1)} %get-tuple-element.116.weight, ...), custom_call_target="tpu_custom_call" | custom-call | flops 1 | bytes 1 | tf_op jit(solution)/shard_map/finish/pallas_call | solution.py:982
  111.7 1.8 %collective-permute-done.23 = bf16[4,144,512]{2,1,0:T(8,128)(2,1)S(1)} collective-permute-done((bf16[4,144,512]{2,1,0:T(8,128)(2,1)S(1)}, bf16[4,144,512]{2,1,0:T(8,128)(2,1)S(1)}, u32[]{:S(2)}, u32[]{:S(2)}) %collective-permute-start.23) | collective-permute-done | bytes 589856 | tf_op jit(solution)/shard_map/ppermute | solution.py:1032
  114.1 3.1 %collective-permute-start.24 = (bf16[8,64,512]{2,1,0:T(8,128)(2,1)S(1)}, bf16[8,64,512]{2,1,0:T(8,128)(2,1)S(1)}, u32[]{:S(2)}, u32[]{:S(2)}) collective-permute-start(bf16[8,64,512]{2,1,0:T(8,128)(2,1)S(1)} %get-tuple-element.181), channel_id=1, source_target_pairs={{0,2},{1,5},{2,0},{3,7},{4,6},{5,1},{6,4},{7,3},{8,10},{9,13},{10,... | collective-permute-start | bytes 1572872 | tf_op jit(solution)/shard_map/ppermute | solution.py:1032
  117.9 6.4 %collective-permute-done.24 = bf16[8,64,512]{2,1,0:T(8,128)(2,1)S(1)} collective-permute-done((bf16[8,64,512]{2,1,0:T(8,128)(2,1)S(1)}, bf16[8,64,512]{2,1,0:T(8,128)(2,1)S(1)}, u32[]{:S(2)}, u32[]{:S(2)}) %collective-permute-start.24) | collective-permute-done | bytes 524320 | tf_op jit(solution)/shard_map/ppermute | solution.py:1032
  126.9 4.1 %collective-permute-done.25 = bf16[4,64,512]{2,1,0:T(8,128)(2,1)S(1)} collective-permute-done((bf16[4,64,512]{2,1,0:T(8,128)(2,1)S(1)}, bf16[4,64,512]{2,1,0:T(8,128)(2,1)S(1)}, u32[]{:S(2)}, u32[]{:S(2)}) %collective-permute-start.25) | collective-permute-done | bytes 262176 | tf_op jit(solution)/shard_map/ppermute | solution.py:1032
  132.4 5.2 %collective-permute-done.27 = bf16[2,64,512]{2,1,0:T(8,128)(2,1)S(1)} collective-permute-done((bf16[2,64,512]{2,1,0:T(8,128)(2,1)S(1)}, bf16[2,64,512]{2,1,0:T(8,128)(2,1)S(1)}, u32[]{:S(2)}, u32[]{:S(2)}) %collective-permute-start.27) | collective-permute-done | bytes 131104 | tf_op jit(solution)/shard_map/ppermute | solution.py:1032
  138.2 1.2 collective-permute-done.29.came_two
  139.5 3.9 %collective-permute-done.28.came_one = bf16[1,64,512]{2,1,0:T(8,128)(2,1)S(1)} collective-permute-done((bf16[1,64,512]{2,1,0:T(8,128)(2,1)S(1)}, bf16[1,64,512]{2,1,0:T(8,128)(2,1)S(1)}, u32[]{:S(2)}, u32[]{:S(2)}) %collective-permute-start.28) | collective-permute-done | bytes 65568 | tf_op jit(solution)/shard_map/ppermute | solution.py:1032
  144.0 1.9 %unpack.1 = (f32[16,1536]{1,0:T(8,128)}, f32[16,512]{1,0:T(8,128)}, f32[16,2048]{1,0:T(8,128)}, f32[64,512]{1,0:T(8,128)}, f32[16]{0:T(128)}, /*index=5*/f32[16]...) custom-call(f32[1,64,512]{2,1,0:T(8,128)} %get-tuple-element.188.kept_one, ...), custom_call_target="tpu_custom_call" | custom-call | flops 1 | bytes 1 | tf_op jit(solution)/shard_map/unpack/pallas_call | solution.py:1125
  (76 shorter events, 15.9 us)
Async XLA Ops:
  2.4 10.4 %collective-permute-start.2 = (bf16[1,208,512]{2,1,0:T(8,128)(2,1)}, bf16[1,208,512]{2,1,0:T(8,128)(2,1)S(1)}, u32[]{:S(2)}, u32[]{:S(2)}) collective-permute-start(bf16[1,208,512]{2,1,0:T(8,128)(2,1)} %get-tuple-element.96), channel_id=1, source_target_pairs={{0,16},{1,3},{2,18},{3,1},{4,20},{5,7},{6,22},{7,5},{8,24},{9,11},... | collective-permute-start | bytes 638984 | tf_op jit(solution)/shard_map/ppermute | solution.py:1032
  9.9 14.4 %collective-permute-start = (bf16[160,1024]{1,0:T(8,128)(2,1)S(1)}, bf16[160,1024]{1,0:T(8,128)(2,1)S(1)}, u32[]{:S(2)}, u32[]{:S(2)}) collective-permute-start(bf16[160,1024]{1,0:T(8,128)(2,1)S(1)} %get-tuple-element.98), channel_id=1, source_target_pairs={{0,1},{1,0},{2,3},{3,2},{4,5},{5,4},{6,7},{7,6},{8,9},{9,8},{10,11... | collective-permute-start | bytes 983048 | tf_op jit(solution)/shard_map/ppermute | solution.py:1141
  10.0 14.3 %collective-permute-start.1 = (bf16[160,1024]{1,0:T(8,128)(2,1)S(1)}, bf16[160,1024]{1,0:T(8,128)(2,1)S(1)}, u32[]{:S(2)}, u32[]{:S(2)}) collective-permute-start(bf16[160,1024]{1,0:T(8,128)(2,1)S(1)} %get-tuple-element.99), channel_id=1, source_target_pairs={{1,2},{3,4},{5,6},{7,8},{9,10},{11,12},{13,14},{15,16},{17,18},{19... | collective-permute-start | bytes 983048 | tf_op jit(solution)/shard_map/ppermute | solution.py:1141
  12.9 11.4 %collective-permute-start.3 = (bf16[2,64,512]{2,1,0:T(8,128)(2,1)S(1)}, bf16[2,64,512]{2,1,0:T(8,128)(2,1)S(1)}, u32[]{:S(2)}, u32[]{:S(2)}) collective-permute-start(bf16[2,64,512]{2,1,0:T(8,128)(2,1)S(1)} %slice.120), channel_id=1, source_target_pairs={{0,8},{1,17},{2,10},{3,19},{4,12},{5,21},{6,14},{7,23},{8,0},{9,25... | collective-permute-start | bytes 393224 | tf_op jit(solution)/shard_map/ppermute | solution.py:1032
  17.0 15.8 %collective-permute-start.5 = (bf16[2,144,512]{2,1,0:T(8,128)(2,1)S(1)}, bf16[2,144,512]{2,1,0:T(8,128)(2,1)S(1)}, u32[]{:S(2)}, u32[]{:S(2)}) collective-permute-start(bf16[2,144,512]{2,1,0:T(8,128)(2,1)S(1)} %slice.121), channel_id=1, source_target_pairs={{0,8},{1,17},{2,10},{3,19},{4,12},{5,21},{6,14},{7,23},{8,0},{9,25... | collective-permute-start | bytes 884744 | tf_op jit(solution)/shard_map/ppermute | solution.py:1032
  24.3 8.5 %collective-permute-start.4 = (bf16[4,64,512]{2,1,0:T(8,128)(2,1)S(1)}, bf16[4,64,512]{2,1,0:T(8,128)(2,1)S(1)}, u32[]{:S(2)}, u32[]{:S(2)}) collective-permute-start(bf16[4,64,512]{2,1,0:T(8,128)(2,1)S(1)} %pad_maximum_fusion.3), channel_id=1, source_target_pairs={{0,4},{1,9},{2,6},{3,11},{4,0},{5,13},{6,2},{7,15},{8,12},{9,1},{1... | collective-permute-start | bytes 786440 | tf_op jit(solution)/shard_map/ppermute | solution.py:1032
  32.8 17.5 %copy-start.1 = (bf16[512,512]{1,0:T(8,128)(2,1)S(1)}, bf16[512,512]{1,0:T(8,128)(2,1)}, u32[]{:S(2)}) copy-start(bf16[512,512]{1,0:T(8,128)(2,1)} %tokens.6) | copy-start | bytes 1572868
  32.8 17.5 %copy-start.4 = (s32[10]{0:T(128)S(1)}, s32[10]{0:T(128)}, u32[]{:S(2)}) copy-start(s32[10]{0:T(128)} %get-tuple-element.95.info) | copy-start | bytes 124
  32.9 9.2 %collective-permute-start.6 = (bf16[8,64,512]{2,1,0:T(8,128)(2,1)S(1)}, bf16[8,64,512]{2,1,0:T(8,128)(2,1)S(1)}, u32[]{:S(2)}, u32[]{:S(2)}) collective-permute-start(bf16[8,64,512]{2,1,0:T(8,128)(2,1)S(1)} %pad_maximum_fusion.2.refs_0_), channel_id=1, source_target_pairs={{0,2},{1,5},{2,0},{3,7},{4,6},{5,1},{6,4},{7,3},{8,10},{9,13},{10,... | collective-permute-start | bytes 1572872 | tf_op jit(solution)/shard_map/ppermute | solution.py:1032
  32.9 14.5 %collective-permute-start.9 = (bf16[4,144,512]{2,1,0:T(8,128)(2,1)S(1)}, bf16[4,144,512]{2,1,0:T(8,128)(2,1)S(1)}, u32[]{:S(2)}, u32[]{:S(2)}) collective-permute-start(bf16[4,144,512]{2,1,0:T(8,128)(2,1)S(1)} %pad_maximum_fusion.1), channel_id=1, source_target_pairs={{0,4},{1,9},{2,6},{3,11},{4,0},{5,13},{6,2},{7,15},{8,12},{9,1},{1... | collective-permute-start | bytes 1769480 | tf_op jit(solution)/shard_map/ppermute | solution.py:1032
  33.0 14.6 %collective-permute-start.7 = (bf16[8,64,512]{2,1,0:T(8,128)(2,1)S(1)}, bf16[8,64,512]{2,1,0:T(8,128)(2,1)S(1)}, u32[]{:S(2)}, u32[]{:S(2)}) collective-permute-start(bf16[8,64,512]{2,1,0:T(8,128)(2,1)S(1)} %pad_maximum_fusion.2.refs_0_), channel_id=1, source_target_pairs={{0,1},{1,0},{2,3},{3,2},{4,5},{5,4},{6,7},{7,6},{8,9},{9,8},{10,11... | collective-permute-start | bytes 1572872 | tf_op jit(solution)/shard_map/ppermute | solution.py:1032
  42.1 5.5 %collective-permute-start.8 = (bf16[8,64,512]{2,1,0:T(8,128)(2,1)S(1)}, bf16[8,64,512]{2,1,0:T(8,128)(2,1)S(1)}, u32[]{:S(2)}, u32[]{:S(2)}) collective-permute-start(bf16[8,64,512]{2,1,0:T(8,128)(2,1)S(1)} %collective-permute-done.6.refs_1_), channel_id=1, source_target_pairs={{0,1},{1,0},{2,3},{3,2},{4,5},{5,4},{6,7},{7,6},{8,9},{9,8},{10,11... | collective-permute-start | bytes 1572872 | tf_op jit(solution)/shard_map/ppermute | solution.py:1032
  47.6 16.9 %collective-permute-start.10 = (bf16[8,144,512]{2,1,0:T(8,128)(2,1)S(1)}, bf16[8,144,512]{2,1,0:T(8,128)(2,1)S(1)}, u32[]{:S(2)}, u32[]{:S(2)}) collective-permute-start(bf16[8,144,512]{2,1,0:T(8,128)(2,1)S(1)} %pad_maximum_fusion.refs_0_), channel_id=1, source_target_pairs={{0,2},{1,5},{2,0},{3,7},{4,6},{5,1},{6,4},{7,3},{8,10},{9,13},{10,... | collective-permute-start | bytes 3538952 | tf_op jit(solution)/shard_map/ppermute | solution.py:1032
  50.3 14.2 %collective-permute-start.11 = (bf16[8,144,512]{2,1,0:T(8,128)(2,1)S(1)}, bf16[8,144,512]{2,1,0:T(8,128)(2,1)S(1)}, u32[]{:S(2)}, u32[]{:S(2)}) collective-permute-start(bf16[8,144,512]{2,1,0:T(8,128)(2,1)S(1)} %pad_maximum_fusion.refs_0_), channel_id=1, source_target_pairs={{0,1},{1,0},{2,3},{3,2},{4,5},{5,4},{6,7},{7,6},{8,9},{9,8},{10,11... | collective-permute-start | bytes 3538952 | tf_op jit(solution)/shard_map/ppermute | solution.py:1032
  64.5 2.8 %collective-permute-start.12 = (bf16[8,144,512]{2,1,0:T(8,128)(2,1)S(1)}, bf16[8,144,512]{2,1,0:T(8,128)(2,1)S(1)}, u32[]{:S(2)}, u32[]{:S(2)}) collective-permute-start(bf16[8,144,512]{2,1,0:T(8,128)(2,1)S(1)} %collective-permute-done.10.refs_1_), channel_id=1, source_target_pairs={{0,1},{1,0},{2,3},{3,2},{4,5},{5,4},{6,7},{7,6},{8,9},{9,8},{10,11... | collective-permute-start | bytes 3538952 | tf_op jit(solution)/shard_map/ppermute | solution.py:1032
  77.5 5.4 %collective-permute-start.13 = (bf16[8,128,512]{2,1,0:T(8,128)(2,1)S(1)}, bf16[8,128,512]{2,1,0:T(8,128)(2,1)S(1)}, u32[]{:S(2)}, u32[]{:S(2)}) collective-permute-start(bf16[8,128,512]{2,1,0:T(8,128)(2,1)S(1)} %get-tuple-element.130), channel_id=1, source_target_pairs={{0,1},{1,0},{2,3},{3,2},{4,5},{5,4},{6,7},{7,6},{8,9},{9,8},{10,11... | collective-permute-start | bytes 3145736 | tf_op jit(solution)/shard_map/ppermute | solution.py:1032
  77.7 5.3 %collective-permute-start.18 = (bf16[8,128,512]{2,1,0:T(8,128)(2,1)S(1)}, bf16[8,128,512]{2,1,0:T(8,128)(2,1)S(1)}, u32[]{:S(2)}, u32[]{:S(2)}) collective-permute-start(bf16[8,128,512]{2,1,0:T(8,128)(2,1)S(1)} %get-tuple-element.145), channel_id=1, source_target_pairs={{0,1},{1,0},{2,3},{3,2},{4,5},{5,4},{6,7},{7,6},{8,9},{9,8},{10,11... | collective-permute-start | bytes 3145736 | tf_op jit(solution)/shard_map/ppermute | solution.py:1032
  81.3 1.4 collective-permute-start.14
  81.5 1.4 collective-permute-start.19
  83.7 13.9 %collective-permute-start.17 = (bf16[4,144,512]{2,1,0:T(8,128)(2,1)S(1)}, bf16[4,144,512]{2,1,0:T(8,128)(2,1)S(1)}, u32[]{:S(2)}, u32[]{:S(2)}) collective-permute-start(bf16[4,144,512]{2,1,0:T(8,128)(2,1)S(1)} %get-tuple-element.180), channel_id=1, source_target_pairs={{0,2},{1,5},{2,0},{3,7},{4,6},{5,1},{6,4},{7,3},{8,10},{9,13},{10,... | collective-permute-start | bytes 1769480 | tf_op jit(solution)/shard_map/ppermute | solution.py:1032
  85.8 10.8 %collective-permute-start.15 = (bf16[160,640]{1,0:T(8,128)(2,1)S(1)}, bf16[160,640]{1,0:T(8,128)(2,1)S(1)}, u32[]{:S(2)}, u32[]{:S(2)}) collective-permute-start(bf16[160,640]{1,0:T(8,128)(2,1)S(1)} %get-tuple-element.140), channel_id=1, source_target_pairs={{1,2},{3,4},{5,6},{7,8},{9,10},{11,12},{13,14},{15,16},{17,18},{19... | collective-permute-start | bytes 614408 | tf_op jit(solution)/shard_map/ppermute | solution.py:1141
  86.5 10.1 %collective-permute-start.16 = (bf16[160,640]{1,0:T(8,128)(2,1)S(1)}, bf16[160,640]{1,0:T(8,128)(2,1)S(1)}, u32[]{:S(2)}, u32[]{:S(2)}) collective-permute-start(bf16[160,640]{1,0:T(8,128)(2,1)S(1)} %get-tuple-element.141), channel_id=1, source_target_pairs={{0,1},{1,0},{2,3},{3,2},{4,5},{5,4},{6,7},{7,6},{8,9},{9,8},{10,11... | collective-permute-start | bytes 614408 | tf_op jit(solution)/shard_map/ppermute | solution.py:1141
  97.8 15.6 %collective-permute-start.23 = (bf16[4,144,512]{2,1,0:T(8,128)(2,1)S(1)}, bf16[4,144,512]{2,1,0:T(8,128)(2,1)S(1)}, u32[]{:S(2)}, u32[]{:S(2)}) collective-permute-start(bf16[4,144,512]{2,1,0:T(8,128)(2,1)S(1)} %fusion), channel_id=1, source_target_pairs={{0,4},{1,9},{2,6},{3,11},{4,0},{5,13},{6,2},{7,15},{8,12},{9,1},{1... | collective-permute-start | bytes 1769480 | tf_op jit(solution)/shard_map/ppermute | solution.py:1032
  99.4 14.0 %collective-permute-start.22 = (bf16[4,144,512]{2,1,0:T(8,128)(2,1)S(1)}, bf16[4,144,512]{2,1,0:T(8,128)(2,1)S(1)}, u32[]{:S(2)}, u32[]{:S(2)}) collective-permute-start(bf16[4,144,512]{2,1,0:T(8,128)(2,1)S(1)} %get-tuple-element.144), channel_id=1, source_target_pairs={{0,2},{1,5},{2,0},{3,7},{4,6},{5,1},{6,4},{7,3},{8,10},{9,13},{10,... | collective-permute-start | bytes 1769480 | tf_op jit(solution)/shard_map/ppermute | solution.py:1032
  111.1 2.7 %collective-permute-start.20 = (bf16[8,64,512]{2,1,0:T(8,128)(2,1)S(1)}, bf16[8,64,512]{2,1,0:T(8,128)(2,1)S(1)}, u32[]{:S(2)}, u32[]{:S(2)}) collective-permute-start(bf16[8,64,512]{2,1,0:T(8,128)(2,1)S(1)} %get-tuple-element.154), channel_id=1, source_target_pairs={{0,1},{1,0},{2,3},{3,2},{4,5},{5,4},{6,7},{7,6},{8,9},{9,8},{10,11... | collective-permute-start | bytes 1572872 | tf_op jit(solution)/shard_map/ppermute | solution.py:1032
  111.1 2.7 %collective-permute-start.21 = (bf16[8,64,512]{2,1,0:T(8,128)(2,1)S(1)}, bf16[8,64,512]{2,1,0:T(8,128)(2,1)S(1)}, u32[]{:S(2)}, u32[]{:S(2)}) collective-permute-start(bf16[8,64,512]{2,1,0:T(8,128)(2,1)S(1)} %get-tuple-element.155), channel_id=1, source_target_pairs={{0,1},{1,0},{2,3},{3,2},{4,5},{5,4},{6,7},{7,6},{8,9},{9,8},{10,11... | collective-permute-start | bytes 1572872 | tf_op jit(solution)/shard_map/ppermute | solution.py:1032
  114.1 10.2 %collective-permute-start.24 = (bf16[8,64,512]{2,1,0:T(8,128)(2,1)S(1)}, bf16[8,64,512]{2,1,0:T(8,128)(2,1)S(1)}, u32[]{:S(2)}, u32[]{:S(2)}) collective-permute-start(bf16[8,64,512]{2,1,0:T(8,128)(2,1)S(1)} %get-tuple-element.181), channel_id=1, source_target_pairs={{0,2},{1,5},{2,0},{3,7},{4,6},{5,1},{6,4},{7,3},{8,10},{9,13},{10,... | collective-permute-start | bytes 1572872 | tf_op jit(solution)/shard_map/ppermute | solution.py:1032
  117.2 8.9 %collective-permute-start.26 = (bf16[2,144,512]{2,1,0:T(8,128)(2,1)S(1)}, bf16[2,144,512]{2,1,0:T(8,128)(2,1)S(1)}, u32[]{:S(2)}, u32[]{:S(2)}) collective-permute-start(bf16[2,144,512]{2,1,0:T(8,128)(2,1)S(1)} %get-tuple-element.176), channel_id=1, source_target_pairs={{0,8},{1,17},{2,10},{3,19},{4,12},{5,21},{6,14},{7,23},{8,0},{9,25... | collective-permute-start | bytes 884744 | tf_op jit(solution)/shard_map/ppermute | solution.py:1032
  124.5 6.4 %collective-permute-start.25 = (bf16[4,64,512]{2,1,0:T(8,128)(2,1)S(1)}, bf16[4,64,512]{2,1,0:T(8,128)(2,1)S(1)}, u32[]{:S(2)}, u32[]{:S(2)}) collective-permute-start(bf16[4,64,512]{2,1,0:T(8,128)(2,1)S(1)} %get-tuple-element.177), channel_id=1, source_target_pairs={{0,4},{1,9},{2,6},{3,11},{4,0},{5,13},{6,2},{7,15},{8,12},{9,1},{1... | collective-permute-start | bytes 786440 | tf_op jit(solution)/shard_map/ppermute | solution.py:1032
  131.0 6.5 %collective-permute-start.27 = (bf16[2,64,512]{2,1,0:T(8,128)(2,1)S(1)}, bf16[2,64,512]{2,1,0:T(8,128)(2,1)S(1)}, u32[]{:S(2)}, u32[]{:S(2)}) collective-permute-start(bf16[2,64,512]{2,1,0:T(8,128)(2,1)S(1)} %get-tuple-element.185), channel_id=1, source_target_pairs={{0,8},{1,17},{2,10},{3,19},{4,12},{5,21},{6,14},{7,23},{8,0},{9,25... | collective-permute-start | bytes 393224 | tf_op jit(solution)/shard_map/ppermute | solution.py:1032
  131.9 7.6 %collective-permute-start.29 = (bf16[1,144,512]{2,1,0:T(8,128)(2,1)S(1)}, bf16[1,144,512]{2,1,0:T(8,128)(2,1)S(1)}, u32[]{:S(2)}, u32[]{:S(2)}) collective-permute-start(bf16[1,144,512]{2,1,0:T(8,128)(2,1)S(1)} %get-tuple-element.184), channel_id=1, source_target_pairs={{0,16},{1,3},{2,18},{3,1},{4,20},{5,7},{6,22},{7,5},{8,24},{9,11},... | collective-permute-start | bytes 442376 | tf_op jit(solution)/shard_map/ppermute | solution.py:1032
  138.2 5.2 %collective-permute-start.28 = (bf16[1,64,512]{2,1,0:T(8,128)(2,1)S(1)}, bf16[1,64,512]{2,1,0:T(8,128)(2,1)S(1)}, u32[]{:S(2)}, u32[]{:S(2)}) collective-permute-start(bf16[1,64,512]{2,1,0:T(8,128)(2,1)S(1)} %get-tuple-element.187), channel_id=1, source_target_pairs={{0,16},{1,3},{2,18},{3,1},{4,20},{5,7},{6,22},{7,5},{8,24},{9,11},... | collective-permute-start | bytes 196616 | tf_op jit(solution)/shard_map/ppermute | solution.py:1032
  (7 other events, 48.1 us)

commit v5 on v4

--- a/solution.py
+++ b/solution.py
@@ -158,8 +158,7 @@
     return center, lax.rsqrt(spread + 1e-05)
 
 
-def ln_back(grad, center, rstd, gain):
-    hat = center * rstd
+def ln_back(grad, hat, rstd, gain):
     scaled = grad * gain
     mean_one = jnp.mean(scaled, axis=-1, keepdims=True)
     mean_two = jnp.mean(scaled * hat, axis=-1, keepdims=True)
@@ -197,13 +196,7 @@
         pick = jnp.where(target == first + (source & (each - 1)), 1.0, 0.0).astype(bf16)
         block = lax.broadcasted_iota(jnp.int32, (blocks, length), 0)
         lane = lax.broadcasted_iota(jnp.int32, (blocks, length), 1)
-        spreaded = jnp.where(lane // each == block, row, 0.0)
-        total = jnp.zeros((blocks, lanes), f32)
-        for _ in range(3):
-            part = spreaded.astype(bf16)
-            total = total + dot_nn(part, pick)
-            spreaded = spreaded - part.astype(f32)
-        return total
+        return dot_nn(jnp.where(lane // each == block, row, 0.0).astype(bf16), pick)
 
     total = one(last, 6 * size, 4 * size)
     for k, vector in enumerate(vectors):
@@ -251,13 +244,108 @@
     )(info, tokens)
 
 
+def prepare_kernel(
+    plan,
+    total,
+    info,
+    tokens,
+    standard,
+    spread,
+    pool,
+    allowed,
+    allowed_back,
+    counts,
+    edge_allowed,
+    edge_counts,
+):
+    rows = plan.rows
+    device = info[0]
+    center, rstd = ln_stats(tokens[...].astype(f32))
+    standard[...] = center * rstd
+    spread[...] = jnp.broadcast_to(rstd, spread.shape)
+    pooled_rows = pool.shape[0]
+    row = lax.broadcasted_iota(jnp.int32, (pooled_rows, rows), 0)
+    slot = lax.broadcasted_iota(jnp.int32, (pooled_rows, rows), 1)
+    first = jnp.zeros((pooled_rows, rows), jnp.int32)
+    shift = jnp.zeros((pooled_rows, rows), jnp.int32)
+    for level in range(1, LEVELS):
+        at = plan.query_at[level] - plan.query_at[1]
+        first = jnp.where(row >= at, at, first)
+        shift = jnp.where(row >= at, level, shift)
+    pool[...] = jnp.where((slot >> shift) == row - first, 1.0, 0.0).astype(bf16)
+
+    def block_step(block, carry):
+        level, part = plan.locate(block)
+        first = device * (rows >> level) + BLOCK * part
+        here = pl.ds(pl.multiple_of(BLOCK * block, BLOCK), BLOCK)
+        there = pl.ds(pl.multiple_of(WINDOW * block, WINDOW), WINDOW)
+        row = first + lax.broadcasted_iota(jnp.int32, (BLOCK, WINDOW), 0)
+        column = first - HALO + lax.broadcasted_iota(jnp.int32, (BLOCK, WINDOW), 1)
+        allowed[here, :] = admitted(
+            tile_codes(info, row, level, total, FAR),
+            tile_codes(info, column, level, total, -FAR),
+            level,
+        )
+        key_row = first - HALO + lax.broadcasted_iota(jnp.int32, (WINDOW, 128), 0)
+        lane = lax.broadcasted_iota(jnp.int32, (WINDOW, 128), 1)
+        row = first + (lane & (BLOCK - 1))
+        allowed_back[there, :] = admitted(
+            tile_codes(info, row, level, total, FAR),
+            tile_codes(info, key_row, level, total, -FAR),
+            level,
+        )
+        counts[there, :] = live_counts(info, key_row, level, total).astype(bf16)
+        return carry
+
+    lax.fori_loop(0, len(plan.blocks), block_step, 0, unroll=2)
+    two = 2 * HALO
+    key = lax.broadcasted_iota(jnp.int32, (two, 128), 0)
+    lane = lax.broadcasted_iota(jnp.int32, (two, 128), 1) & (two - 1)
+    facing = jnp.where((key < HALO) == (lane < HALO), 1.0, 0.0)
+    for level in range(LEVELS):
+        count = plan.counts[level]
+        start = device * count
+        key_row = start + jnp.where(key < HALO, key, count - two + key)
+        row = start + jnp.where(lane < HALO, lane - HALO, count - HALO + lane)
+        here = pl.ds(two * level, two)
+        edge_allowed[here, :] = facing * admitted(
+            tile_codes(info, row, level, total, FAR),
+            tile_codes(info, key_row, level, total, -FAR),
+            level,
+        )
+        edge_counts[here, :] = live_counts(info, key_row, level, total).astype(bf16)
+
+
+def prepare(plan, total, info, tokens):
+    rows, width = tokens.shape
+    blocks = len(plan.blocks)
+    return pl.pallas_call(
+        functools.partial(prepare_kernel, plan, total),
+        out_shape=(
+            jax.ShapeDtypeStruct((rows, width), f32),
+            jax.ShapeDtypeStruct((rows, 128), f32),
+            jax.ShapeDtypeStruct((plan.query_rows - plan.query_at[1], rows), bf16),
+            jax.ShapeDtypeStruct((BLOCK * blocks, WINDOW), f32),
+            jax.ShapeDtypeStruct((WINDOW * blocks, 128), f32),
+            jax.ShapeDtypeStruct((WINDOW * blocks, 128), bf16),
+            jax.ShapeDtypeStruct((2 * HALO * LEVELS, 128), f32),
+            jax.ShapeDtypeStruct((2 * HALO * LEVELS, 128), bf16),
+        ),
+        in_specs=[SCALARS] + spec(1),
+        out_specs=tuple(spec(8)),
+        compiler_params=params(8),
+        name="prepare",
+        cost_estimate=cost(4),
+    )(info, tokens)
+
+
 def project_kernel(
-    plan, total, info, inverse, tokens, from_twin, from_other, *refs
+    plan, total, info, inverse, standard, pool, from_twin, from_other, *refs
 ):
     pieces, outs = refs[:PIECES], refs[PIECES:]
     queries, pairs, halo_queries, halo_pairs = (outs[2 * k : 2 * k + 2] for k in range(4))
     weight, vectors, shift_out, table, edges, halos = outs[8:]
-    rows, width = tokens.shape
+    rows, width = standard.shape
     device = info[0]
     each = pieces[0].shape[0]
     block_rows = pieces[0].shape[1] // 4
@@ -273,22 +361,13 @@
     for k, single in enumerate(singles):
         vectors[pl.ds(k, 1), :] = single
     shift_out[...] = wide
-    values = tokens[...].astype(f32)
-    center, rstd = ln_stats(values)
-    low = (center * rstd * singles[0] + singles[1]).astype(bf16)
-    pooled_rows = plan.query_rows - plan.query_at[1]
-    row = lax.broadcasted_iota(jnp.int32, (pooled_rows, rows), 0)
-    slot = lax.broadcasted_iota(jnp.int32, (pooled_rows, rows), 1)
-    first = jnp.zeros((pooled_rows, rows), jnp.int32)
-    shift = jnp.zeros((pooled_rows, rows), jnp.int32)
+    low = (standard[...] * singles[0] + singles[1]).astype(bf16)
+    pooled_rows = pool.shape[0]
     share = jnp.zeros((pooled_rows, 1), f32)
     row_one = lax.broadcasted_iota(jnp.int32, (pooled_rows, 1), 0)
     for level in range(1, LEVELS):
         at = plan.query_at[level] - plan.query_at[1]
-        first = jnp.where(row >= at, at, first)
-        shift = jnp.where(row >= at, level, shift)
         share = jnp.where(row_one >= at, 0.5**level, share)
-    pool = jnp.where((slot >> shift) == row - first, 1.0, 0.0).astype(bf16)
     places = device * rows + lax.broadcasted_iota(jnp.int32, (rows, QUAD_WIDTH), 0)
     live = live_counts(info, places, 0, total)
     place_halos(info, from_twin, from_other, edges)
@@ -314,7 +393,7 @@
         kind, quad = divmod(part, 2)
         if kind == 2:
             block = (block.astype(f32) * live).astype(bf16)
-        pooled = dot_nn(pool, block)
+        pooled = dot_nn(pool[...], block)
         if kind < 2:
             pooled = pooled * share
         side = dot_nn(halos[:, pl.ds(width if kind == 2 else 0, width)], weight[:, columns])
@@ -329,8 +408,8 @@
             halo_pairs[quad][:, there] = side.astype(bf16)
 
 
-def project(plan, total, info, inverse, tokens, from_twin, from_other, pieces):
-    rows, width = tokens.shape
+def project(plan, total, info, inverse, standard, pool, from_twin, from_other, pieces):
+    rows, width = standard.shape
     halo = LEVELS * HALO
     blocks = PIECES * pieces[0].shape[0]
     depth = blocks * pieces[0].shape[1] // 4
@@ -348,7 +427,7 @@
                 jax.ShapeDtypeStruct((1, 4 * depth), f32),
             ]
         ),
-        in_specs=[SCALARS, SCALARS] + spec(3 + PIECES),
+        in_specs=[SCALARS, SCALARS] + spec(4 + PIECES),
         out_specs=spec(11),
         scratch_shapes=[
             pltpu.VMEM((blocks, 2 * LINE), f32),
@@ -358,11 +437,11 @@
         compiler_params=params(18),
         name="project",
         cost_estimate=cost(3.3),
-    )(info, inverse, tokens, from_twin, from_other, *pieces)
+    )(info, inverse, standard, pool, from_twin, from_other, *pieces)
     return [outs[2 * k : 2 * k + 2] for k in range(4)] + list(outs[8:])
 
 
-def attend_kernel(plan, total, info, *refs):
+def attend_kernel(plan, total, info, mask, counts_of, *refs):
     queries, pairs, halos, attended, mixed, scale, extended = (
         refs[2 * k : 2 * k + 2] for k in range(7)
     )
@@ -378,16 +457,8 @@
         level, part = plan.locate(block)
         here = pl.ds(pl.multiple_of(BLOCK * block, BLOCK), BLOCK)
         there = pl.ds(pl.multiple_of(BLOCK * block + 2 * HALO * level, BLOCK), WINDOW)
-        first = device * (rows >> level) + BLOCK * part
-        row = first + lax.broadcasted_iota(jnp.int32, (BLOCK, WINDOW), 0)
-        column = first - HALO + lax.broadcasted_iota(jnp.int32, (BLOCK, WINDOW), 1)
-        allowed = admitted(
-            tile_codes(info, row, level, total, FAR),
-            tile_codes(info, column, level, total, -FAR),
-            level,
-        )
-        key_row = first - HALO + lax.broadcasted_iota(jnp.int32, (WINDOW, 128), 0)
-        counts = live_counts(info, key_row, level, total).astype(bf16)
+        allowed = mask[here, :]
+        counts = counts_of[pl.ds(pl.multiple_of(WINDOW * block, WINDOW), WINDOW), :]
         return here, there, allowed, counts
 
     def block_step(step, carry):
@@ -441,13 +512,13 @@
         attended[quad][:, lanes] = value.astype(bf16)
 
 
-def attend(plan, total, info, queries, pairs, halos):
+def attend(plan, total, info, mask, counts, queries, pairs, halos):
     rows, width = plan.rows, queries[0].shape[1]
     outs = pl.pallas_call(
         functools.partial(attend_kernel, plan, total),
         out_shape=[jax.ShapeDtypeStruct((rows, width), bf16)] * 2
         + [jax.ShapeDtypeStruct((rows, width), f32)] * 4,
-        in_specs=[SCALARS] + spec(6),
+        in_specs=[SCALARS] + spec(8),
         out_specs=spec(6),
         scratch_shapes=[
             pltpu.VMEM((plan.key_rows, 2 * width), bf16),
@@ -458,7 +529,7 @@
         compiler_params=params(20),
         name="attend",
         cost_estimate=cost(8),
-    )(info, *queries, *pairs, *halos)
+    )(info, mask, counts, *queries, *pairs, *halos)
     return outs[:2], outs[2:4], outs[4:]
 
 
@@ -478,7 +549,7 @@
     result, resid_out, grad_normed, w_out, own, low_half, high_half, sum_in = refs[
         parts : parts + 8
     ]
-    w_in, w_back, normed_two, outer, tall, flat = refs[parts + 8 :]
+    w_in, w_back, normed_two, outer, tall, flat, turned, cot_turned = refs[parts + 8 :]
     other = (low_half, high_half)
     width = tokens.shape[1]
     wide = width // 2
@@ -502,6 +573,7 @@
     resid = resid + dot_nn(attended_b[...], w_out[pl.ds(wide, wide), :]) + vectors[pl.ds(2, 1), :]
     center, rstd = ln_stats(resid)
     normed_two[...] = (center * rstd * gain + vectors[pl.ds(4, 1), :]).astype(bf16)
+    turned[...] = normed_two[...].T
     resid_out[...] = resid
     outer[...] = jnp.zeros(outer.shape, f32)
     grad_normed[...] = jnp.zeros(grad_normed.shape, f32)
@@ -518,7 +590,7 @@
         outer[...] += dot_nn(active, back)
         tall[there, :] = dot_tn(active, cotangent[...]).astype(bf16)
         sum_in[:, there] = column_sum(low.astype(f32))
-        flat[...] = dot_tn(normed_two[...], low).astype(bf16)
+        flat[...] = dot_nn(turned[...], low).astype(bf16)
         for p in range(2 * half):
             i = sums_inverse[p]
             rows = flat[pl.ds(pl.multiple_of(i * block, block), block), :]
@@ -530,7 +602,7 @@
         grad_normed[...] += dot_nt(low, w_in[c])
         return carry
 
-    lax.fori_loop(0, chunks, chunk_step, 0)
+    lax.fori_loop(0, chunks, chunk_step, 0, unroll=4)
     result[...] = (resid_out[...] + outer[...] + vectors[pl.ds(5, 1), :]).astype(bf16)
     for p in range(2 * half):
         i = sums_inverse[p]
@@ -570,6 +642,8 @@
             pltpu.VMEM((rows, width), f32),
             pltpu.VMEM((hidden, width), bf16),
             pltpu.VMEM((width, width), bf16),
+            pltpu.VMEM((width, rows), bf16),
+            pltpu.VMEM((width, rows), bf16),
         ],
         compiler_params=params(30),
         name="feed_forward",
@@ -609,7 +683,7 @@
     width = cotangent.shape[1]
     wide = width // 2
     center, rstd = ln_stats(resid[...])
-    grad_in, gain_terms = ln_back(grad_normed[...], center, rstd, vectors[pl.ds(3, 1), :])
+    grad_in, gain_terms = ln_back(grad_normed[...], center * rstd, rstd, vectors[pl.ds(3, 1), :])
     grad_out = cotangent[...].astype(f32)
     total = grad_out + grad_in
     grad_resid[...] = total
@@ -701,11 +775,10 @@
     )(info, sums_inverse, cotangent, *attended, *mixed, *scale, vectors, resid, grad_normed, w_out)
 
 
-def attend_back_kernel(plan, total, info, *refs):
+def attend_back_kernel(plan, total, mask, counts_of, *refs):
     queries, pairs, halos, grads, grad_queries, grad_extended, extended = (
         refs[2 * k : 2 * k + 2] for k in range(7)
     )
-    device = info[0]
     width = QUAD_WIDTH
     for quad in range(2):
         fill_extended(plan, pairs[quad], halos[quad], extended[quad])
@@ -719,17 +792,9 @@
         level, part = plan.locate(block)
         here = pl.ds(pl.multiple_of(BLOCK * block, BLOCK), BLOCK)
         there = pl.ds(pl.multiple_of(BLOCK * block + 2 * HALO * level, BLOCK), WINDOW)
-        first = device * (plan.rows >> level) + BLOCK * part
-        key_row = first - HALO + lax.broadcasted_iota(jnp.int32, (WINDOW, 128), 0)
-        lane = lax.broadcasted_iota(jnp.int32, (WINDOW, 128), 1)
-        row = first + (lane & (BLOCK - 1))
-        allowed = admitted(
-            tile_codes(info, row, level, total, FAR),
-            tile_codes(info, key_row, level, total, -FAR),
-            level,
-        )
-        allowed = jnp.concatenate([allowed] * (QUAD * BLOCK // 128), axis=1) > 0.0
-        counts = live_counts(info, key_row, level, total).astype(bf16)
+        window = pl.ds(pl.multiple_of(WINDOW * block, WINDOW), WINDOW)
+        allowed = jnp.concatenate([mask[window, :]] * (QUAD * BLOCK // 128), axis=1) > 0.0
+        counts = counts_of[window, :]
         return here, there, allowed, counts
 
     def block_step(step, carry):
@@ -775,13 +840,13 @@
     lax.fori_loop(0, len(plan.blocks) // 4, block_step, 0, unroll=1)
 
 
-def attend_back(plan, total, info, queries, pairs, halos, grads):
+def attend_back(plan, total, mask, counts, queries, pairs, halos, grads):
     width = queries[0].shape[1]
     outs = pl.pallas_call(
         functools.partial(attend_back_kernel, plan, total),
         out_shape=[jax.ShapeDtypeStruct((plan.query_rows, width), f32)] * 2
         + [jax.ShapeDtypeStruct((plan.key_rows, 2 * width), f32)] * 2,
-        in_specs=[SCALARS] + spec(8),
+        in_specs=spec(10),
         out_specs=spec(4),
         scratch_shapes=[
             pltpu.VMEM((plan.key_rows, 2 * width), bf16),
@@ -790,14 +855,15 @@
         compiler_params=params(24),
         name="attend_back",
         cost_estimate=cost(12),
-    )(info, *queries, *pairs, *halos, *grads)
+    )(mask, counts, *queries, *pairs, *halos, *grads)
     return outs[:2], outs[2:]
 
 
 def edge_back_kernel(
     plan,
-    total,
     info,
+    mask,
+    counts_of,
     queries_a,
     queries_b,
     pairs_a,
@@ -809,13 +875,10 @@
     grads,
 ):
     width = queries_a.shape[1]
-    device = info[0]
     place_halos(info, from_twin, from_other, grads)
     two = 2 * HALO
     masks = head_masks(two)
     keys = pl.ds(0, width)
-    key = lax.broadcasted_iota(jnp.int32, (two, 128), 0)
-    lane = lax.broadcasted_iota(jnp.int32, (two, 128), 1) & (two - 1)
     heads = 2 * width // HEAD_DIM
     source = lax.broadcasted_iota(jnp.int32, (LINE, width), 0)
     target = lax.broadcasted_iota(jnp.int32, (LINE, width), 1)
@@ -825,61 +888,62 @@
         wanted = jnp.where(target % HEAD_DIM == 0, head, -1)
         wanted = jnp.where(target % HEAD_DIM == 1, head + heads, wanted)
         picks.append(jnp.where(source == wanted, 1.0, 0.0).astype(bf16))
-    facing = jnp.where((key < HALO) == (lane < HALO), 1.0, 0.0)
+    denoms = [dot_nn(grads[:, pl.ds(2 * width, LINE)], pick).astype(bf16) for pick in picks]
+    work = []
     for level in range(LEVELS):
         count, at = plan.counts[level], plan.query_at[level]
-        start = device * count
-        key_row = start + jnp.where(key < HALO, key, count - two + key)
-        row = start + jnp.where(lane < HALO, lane - HALO, count - HALO + lane)
-        allowed = facing * admitted(
-            tile_codes(info, row, level, total, FAR),
-            tile_codes(info, key_row, level, total, -FAR),
-            level,
-        )
-        allowed = jnp.concatenate([allowed] * (QUAD * two // 128), axis=1) > 0.0
-        counts = live_counts(info, key_row, level, total).astype(bf16)
-        ahead = pl.ds(HALO * level, HALO)
-        behind = pl.ds(HALO * (LEVELS + level), HALO)
-
-        def both(source, lanes):
-            return jnp.concatenate([source[ahead, lanes], source[behind, lanes]], axis=0)
-
-        denoms = both(grads, pl.ds(2 * width, LINE))
+        here = pl.ds(two * level, two)
+        allowed = jnp.concatenate([mask[here, :]] * (QUAD * two // 128), axis=1) > 0.0
+        counts = counts_of[here, :]
+        ahead, behind = HALO * level, HALO * (LEVELS + level)
+
+        def both(item, lanes):
+            parts = [item[pl.ds(first, HALO), lanes] for first in (ahead, behind)]
+            return jnp.concatenate(parts, axis=0)
+
         for quad in range(2):
             pairs = (pairs_a, pairs_b)[quad]
             own = jnp.concatenate(
                 [pairs[pl.ds(at, HALO), :], pairs[pl.ds(at + count - HALO, HALO), :]], axis=0
             )
             k, v = own[:, :width], own[:, width:]
+            d = denoms[quad]
+            d = jnp.concatenate([d[ahead : ahead + HALO], d[behind : behind + HALO]], axis=0)
             q = spread_heads(both((queries_a, queries_b)[quad], keys), masks)
             g = spread_heads(both(grads, pl.ds(quad * width, width)), masks)
-            d = spread_heads(dot_nn(denoms, picks[quad]).astype(bf16), masks)
+            d = spread_heads(d, masks)
             value_and_count = jnp.concatenate([v] + [counts] * (width // 128), axis=1)
-            weight = jnp.where(allowed, jnp.exp(dot_nt(k, q)), 0.0)
-            grad_probs = dot_nt(value_and_count, jnp.concatenate([g, d], axis=1))
-            grad_score = (grad_probs * weight).astype(bf16)
             there = pl.ds(HALO * (quad * LEVELS + level), HALO)
-            grad_keys = dot_nn(grad_score, q)
-            grad_values = dot_nn(weight.astype(bf16), g)
-            low[there, keys] = grad_keys[:HALO]
-            high[there, keys] = grad_keys[HALO:]
-            low[there, pl.ds(width, width)] = grad_values[:HALO]
-            high[there, pl.ds(width, width)] = grad_values[HALO:]
-
-
-def edge_back(plan, total, info, queries, pairs, from_twin, from_other):
+            work.append((there, allowed, q, g, d, k, value_and_count))
+    scores = [dot_nt(item[5], item[2]) for item in work]
+    grad_probs = [
+        dot_nt(item[6], jnp.concatenate([item[3], item[4]], axis=1)) for item in work
+    ]
+    weights = [jnp.where(item[1], jnp.exp(score), 0.0) for item, score in zip(work, scores)]
+    grad_scores = [(x * y).astype(bf16) for x, y in zip(grad_probs, weights)]
+    to_keys = [dot_nn(grad_score, item[2]) for grad_score, item in zip(grad_scores, work)]
+    to_values = [dot_nn(weight.astype(bf16), item[3]) for weight, item in zip(weights, work)]
+    for item, to_key, to_value in zip(work, to_keys, to_values):
+        there = item[0]
+        low[there, keys] = to_key[:HALO]
+        high[there, keys] = to_key[HALO:]
+        low[there, pl.ds(width, width)] = to_value[:HALO]
+        high[there, pl.ds(width, width)] = to_value[HALO:]
+
+
+def edge_back(plan, info, mask, counts, queries, pairs, from_twin, from_other):
     width = queries[0].shape[1]
     size = 2 * LEVELS * HALO
     return pl.pallas_call(
-        functools.partial(edge_back_kernel, plan, total),
+        functools.partial(edge_back_kernel, plan),
         out_shape=[jax.ShapeDtypeStruct((size, 2 * width), f32)] * 2,
-        in_specs=[SCALARS] + spec(6),
+        in_specs=[SCALARS] + spec(8),
         out_specs=spec(2),
         scratch_shapes=[pltpu.VMEM((size, 2 * width + LINE), bf16)],
-        compiler_params=params(10),
+        compiler_params=params(12),
         name="edge_back",
         cost_estimate=cost(2.5),
-    )(info, *queries, *pairs, from_twin, from_other)
+    )(info, mask, counts, *queries, *pairs, from_twin, from_other)
 
 
 def finish_kernel(
@@ -887,7 +951,8 @@
     total,
     info,
     inverse,
-    tokens,
+    standard,
+    spread,
     weight,
     vectors,
     grad_resid,
@@ -908,7 +973,7 @@
     flat,
     table,
 ):
-    rows, width = tokens.shape
+    rows, width = standard.shape
     device = info[0]
     half_width = width // 2
     places = device * rows + lax.broadcasted_iota(jnp.int32, (rows, 128), 0)
@@ -939,10 +1004,9 @@
         if chunk * 128 >= 2 * width:
             value = value * live
         joined[:, pl.ds(chunk * 128, 128)] = value.astype(bf16)
-    values = tokens[...].astype(f32)
-    center, rstd = ln_stats(values)
+    hat = standard[...]
     gain = vectors[pl.ds(0, 1), :]
-    normed = (center * rstd * gain + vectors[pl.ds(1, 1), :]).astype(bf16)
+    normed = (hat * gain + vectors[pl.ds(1, 1), :]).astype(bf16)
     half, block = own.shape[0], own.shape[1] // 4
     other = (low_half, high_half)
     for part in range(3):
@@ -957,7 +1021,7 @@
             else:
                 other[(p - half) // 8][(p - half) % 8, there, :] = lines.astype(bf16)
     grad_normed = dot_nt(joined[...], weight[...])
-    grad_in, gain_terms = ln_back(grad_normed, center, rstd, gain)
+    grad_in, gain_terms = ln_back(grad_normed, hat, spread[:, :1], gain)
     grad_tokens[...] = grad_resid[...] + grad_in
     singles = [column_sum(gain_terms), column_sum(grad_normed)]
     singles += [sums[pl.ds(k, 1), :] for k in range(2, 6)]
@@ -975,8 +1039,8 @@
             other[(p - half) // 8][(p - half) % 8, there, :] = lines.astype(bf16)
 
 
-def finish(plan, total, info, inverse, tokens, weight, *rest):
-    rows, width = tokens.shape
+def finish(plan, total, info, inverse, standard, spread, weight, *rest):
+    rows, width = standard.shape
     half = BLOCKS // 2
     block = width // BLOCKS
     return pl.pallas_call(
@@ -987,7 +1051,7 @@
             jax.ShapeDtypeStruct((half // 2, 4 * block, width), bf16),
             jax.ShapeDtypeStruct((half // 2, 4 * block, width), bf16),
         ),
-        in_specs=[SCALARS, SCALARS] + spec(2 + len(rest)),
+        in_specs=[SCALARS, SCALARS] + spec(3 + len(rest)),
         out_specs=tuple(spec(4)),
         scratch_shapes=[
             pltpu.VMEM((3 * width // 128, plan.query_rows, 128), f32),
@@ -998,7 +1062,7 @@
         compiler_params=params(28),
         name="finish",
         cost_estimate=cost(6.2),
-    )(info, inverse, tokens, weight, *rest)
+    )(info, inverse, standard, spread, weight, *rest)
 
 
 class Ring:
@@ -1127,7 +1191,7 @@
         out_shape=[jax.ShapeDtypeStruct(item.shape, f32) for item in like],
         in_specs=spec(4),
         out_specs=spec(len(like)),
-        compiler_params=params(62),
+        compiler_params=params(8),
         name="unpack",
         cost_estimate=cost(1.5),
     )(kept_one, came_one, kept_two, came_two)
@@ -1170,7 +1234,7 @@
     chunks = w_in.shape[1] // width
     small = (ln1_gain, ln1_bias, out_bias, ln2_gain, ln2_bias, back_bias, in_bias)
     direct = devices == BLOCKS
-    ring = Ring(BLOCKS, (16, 8, 4, 2), (2, 16, 8, 4))
+    ring = Ring(BLOCKS, (16, 2, 8, 4), (4, 16, 2, 8))
     sums_ring = Ring(BLOCKS, (16, 8, 4, 2), (2, 16, 8, 4))
     last = ring.stages - 1
     core = ring.stages
@@ -1179,6 +1243,7 @@
             (ring, sums_ring), lengths, w_qkv, w_out, w_in, w_back, small
         )
         from_other, from_twin = exchange(*edge_sums(plan, total, info, order(tokens, payload)))
+        ready = prepare(plan, total, info, order(tokens, payload))
         (payload,) = join([payload], ring.step(0, [payload]))
         a, b = payload[:, : 4 * block], payload[:, 4 * block :]
         a_came, b_came = ring.step(1, [a, b])
@@ -1187,18 +1252,19 @@
         (a_came,) = ring.step(2, [a])
         (a,) = join([a], [a_came])
         (b,) = join([b], [b_came])
-        a = order(a, b)
+        a = order(a, b, ready)
         (b_came,) = ring.step(2, [b])
         (a_came,) = ring.step(3, [a])
         one = [a, a_came] + ring.step(core, [a, a_came])
         (b,) = join([b], [b_came])
-        b = order(b, one)
+        b = order(b, a_came)
     else:
         padded = (lengths + 15) // 16 * 16
         ends = jnp.cumsum(padded, dtype=jnp.int32)
         info = jnp.concatenate([device[None].astype(jnp.int32), lengths, ends - padded, ends])
         inverse = sums_inverse = jnp.arange(BLOCKS, dtype=jnp.int32)
         from_other, from_twin = exchange(*edge_sums(plan, total, info, tokens))
+        ready = prepare(plan, total, info, tokens)
 
         def whole(item):
             return lax.all_gather(item, "seq", axis=0, tiled=True)
@@ -1220,15 +1286,17 @@
             whole(w_back).reshape(BLOCKS, chunks * block, width),
         ]
         two = split(jnp.concatenate(full_two, axis=1), PIECES)
+    standard, spread, pool, allowed, allowed_back, counts, edge_allowed, edge_counts = ready
     queries, pairs, halo_queries, halo_pairs, weight, vectors, shift_in = project(
-        plan, total, info, inverse, tokens, from_twin, from_other, one
+        plan, total, info, inverse, standard, pool, from_twin, from_other, one
     )
-    ready = queries[0]
     if direct:
         (b_came,) = ring.step(last, [b])
         (b_twin,) = ring.step(core, [b])
-        ready = order(ready, b)
-    attended, mixed, scale = attend(plan, total, info, (ready, queries[1]), pairs, halo_pairs)
+        allowed = order(allowed, b)
+    attended, mixed, scale = attend(
+        plan, total, info, allowed, counts, queries, pairs, halo_pairs
+    )
     if direct:
         b_came = order(b_came, attended)
         two = [b, b_came, b_twin] + ring.step(core, [b_came])
@@ -1271,26 +1339,29 @@
             last, with_out(own_two, own_out), with_out(low, low_out), with_out(high, high_out)
         )
         sent_low, sent_high = halves(sent)
-        (high,) = sums_ring.step(last, [sent_high])
-        grads_a = order(grads_a, sent_high)
+        sent_low, sent_high = order((sent_low, sent_high), from_twin)
+        high, low = sums_ring.step(last, [sent_high, sent_low])
+        grads_a = order(grads_a, sent_high, sent_low)
     grad_queries, grad_pairs = attend_back(
-        plan, total, info, queries, pairs, halo_pairs, (grads_a, grads_b)
+        plan, total, allowed_back, counts, queries, pairs, halo_pairs, (grads_a, grads_b)
     )
     from_other, from_twin = order((from_other, from_twin), grad_queries)
     if direct:
-        sent_low, high = order((sent_low, high), grad_queries, from_other, from_twin)
-        (low,) = sums_ring.step(last, [sent_low])
+        high = order(high, grad_queries, from_other, from_twin)
         kept, kept_high = halves(kept)
         sent = (kept_high + high.astype(f32)).astype(bf16)
         (came,) = sums_ring.step(last - 1, [sent])
-        from_other, from_twin = order((from_other, from_twin), sent_low, sent)
-    edges = edge_back(plan, total, info, halo_queries, pairs, from_twin, from_other)
+        from_other, from_twin = order((from_other, from_twin), sent)
+    edges = edge_back(
+        plan, info, edge_allowed, edge_counts, halo_queries, pairs, from_twin, from_other
+    )
     grad_tokens, own_one, low_one, high_one = finish(
         plan,
         total,
         info,
         sums_inverse,
-        tokens,
+        standard,
+        spread,
         weight,
         vectors,
         grad_resid,

time: 146 us -> 131 us (0.90)
  waiting for transfers between devices: 58.8 us -> 46.1 us
  Pallas kernels: 48.5 us -> 45.1 us
  starting transfers between devices: 30.4 us -> 33.7 us
    ppermute x26, waiting for transfers between devices: 58.8 us -> 46.1 us  [step(): return [lax.ppermute(item, 'seq', route) for item in arrays]]
    pallas_call x1 -> x2, Pallas kernels: 4.32 us -> 6.47 us  [the longest x1 4.11 us: prepare(): pl.pallas_call(functools.partial(prepare_kernel, plan, total), out_shape=...]
    ppermute x26, starting transfers between devices: 27.6 us -> 29.1 us  [step(): return [lax.ppermute(item, 'seq', route) for item in arrays]]
    ppermute x2, starting transfers between devices: 1.51 us -> 3.03 us  [exchange(): lax.ppermute(to_twin, 'seq', twin)]
    unnamed x20 -> x16, local copies, waits for them, and re-layouts: 3.48 us -> 2.86 us
  transfers between devices with their start and end apart: 30 -> 30, of which waited for: 17 -> 19; matrix products, arithmetic and copies ran while one was open for 2% -> 2% of each run, Pallas kernels for 24% -> 26%
where the time goes in v5:
time: 131 us
  waiting for transfers between devices  46.1 us (35%)
  Pallas kernels  45.1 us (34%)
  starting transfers between devices  33.7 us (26%)
  local copies, waits for them, and re-layouts  3.02 us (2%)
  other arithmetic  2.12 us (2%)
    ppermute x26, waiting for transfers between devices, step(): return [lax.ppermute(item, 'seq', route) for item in arrays]  46.1 us
    ppermute x26, starting transfers between devices, step(): return [lax.ppermute(item, 'seq', route) for item in arrays]  29.1 us
    pallas_call x1, Pallas kernels, feed_forward(): pl.pallas_call(functools.partial(forward_kernel, parts), out_shape=(jax.S...  8.89 us
    pallas_call x1, Pallas kernels, attend_back(): pl.pallas_call(functools.partial(attend_back_kernel, plan, total), out_sh...  7.67 us
    pallas_call x1, Pallas kernels, finish(): pl.pallas_call(functools.partial(finish_kernel, plan, total), out_shape=(...  5.34 us
    pallas_call x1, Pallas kernels, attend(): pl.pallas_call(functools.partial(attend_kernel, plan, total), out_shape=[...  4.78 us
    pallas_call x1, Pallas kernels, project(): pl.pallas_call(functools.partial(project_kernel, plan, total), out_shape=...  4.64 us
    pallas_call x1, Pallas kernels, prepare(): pl.pallas_call(functools.partial(prepare_kernel, plan, total), out_shape=...  4.11 us
  transfers between devices with their start and end apart: 30, of which 19 were waited for; matrix products, arithmetic and copies ran while one was open for 2% of the time, Pallas kernels for 26%

profile of v5, /device:TPU:0, one launch (start us, length us, event | category | flops | bytes accessed | tf_op | source)
XLA Modules:
  0.0 131.1 jit_solution(360917346631142247)
XLA Ops:
  0.6 1.8 %pack.1 = (s32[10]{0:T(128)}, s32[32]{0:T(128)}, s32[32]{0:T(128)}, bf16[1,208,512]{2,1,0:T(8,128)(2,1)}) custom-call(s32[3]{0:T(128)} %lengths.1, bf16[16,1536]{1,0:T(8,128)(2,1)} %w_qkv.1, bf16[16,512]{1,0:T(8,128)(2,1)} %w_out.1, bf16[16,2048]{1,0:T(8,128)(2,1)} %w_in.1, bf16[64,512]{1,0:T(8,128)(2,1)} %w_back.1, bf16[16]{0:T(256)(128)(2,1)} %refs_0_.1, ...), custom_call_target="tpu_custom_call" | custom-call | flops 1 | bytes 1 | tf_op jit(solution)/shard_map/pack/pallas_call | solution.py:1147
  2.4 4.1 %collective-permute-start = (bf16[1,208,512]{2,1,0:T(8,128)(2,1)}, bf16[1,208,512]{2,1,0:T(8,128)(2,1)S(1)}, u32[]{:S(2)}, u32[]{:S(2)}) collective-permute-start(bf16[1,208,512]{2,1,0:T(8,128)(2,1)} %get-tuple-element.105), channel_id=1, source_target_pairs={{0,16},{1,5},{2,18},{3,7},{4,20},{5,1},{6,22},{7,3},{8,24},{9,13},... | collective-permute-start | bytes 638984 | tf_op jit(solution)/shard_map/ppermute | solution.py:1096
  8.2 1.7 %edge_sums.1 = (bf16[160,1024]{1,0:T(8,128)(2,1)S(1)}, bf16[160,1024]{1,0:T(8,128)(2,1)S(1)}) custom-call(s32[10]{0:T(128)S(1)} %copy-done.3, bf16[512,512]{1,0:T(8,128)(2,1)S(1)} %copy-done), custom_call_target="tpu_custom_call" | custom-call | flops 1 | bytes 1 | tf_op jit(solution)/shard_map/edge_sums/pallas_call | solution.py:235
  10.6 2.9 %collective-permute-start.5 = (bf16[160,1024]{1,0:T(8,128)(2,1)S(1)}, bf16[160,1024]{1,0:T(8,128)(2,1)S(1)}, u32[]{:S(2)}, u32[]{:S(2)}) collective-permute-start(bf16[160,1024]{1,0:T(8,128)(2,1)S(1)} %get-tuple-element.109), channel_id=1, source_target_pairs={{0,1},{1,0},{2,3},{3,2},{4,5},{5,4},{6,7},{7,6},{8,9},{9,8},{10,11... | collective-permute-start | bytes 983048 | tf_op jit(solution)/shard_map/ppermute | solution.py:1205
  14.5 1.6 %collective-permute-start.3 = (bf16[2,64,512]{2,1,0:T(8,128)(2,1)S(1)}, bf16[2,64,512]{2,1,0:T(8,128)(2,1)S(1)}, u32[]{:S(2)}, u32[]{:S(2)}) collective-permute-start(bf16[2,64,512]{2,1,0:T(8,128)(2,1)S(1)} %slice.121), channel_id=1, source_target_pairs={{0,2},{1,17},{2,0},{3,19},{4,6},{5,21},{6,4},{7,23},{8,10},{9,25},... | collective-permute-start | bytes 393224 | tf_op jit(solution)/shard_map/ppermute | solution.py:1096
  16.7 6.6 %collective-permute-done.3 = bf16[2,64,512]{2,1,0:T(8,128)(2,1)S(1)} collective-permute-done((bf16[2,64,512]{2,1,0:T(8,128)(2,1)S(1)}, bf16[2,64,512]{2,1,0:T(8,128)(2,1)S(1)}, u32[]{:S(2)}, u32[]{:S(2)}) %collective-permute-start.3) | collective-permute-done | bytes 131104 | tf_op jit(solution)/shard_map/ppermute | solution.py:1096
  23.3 1.6 %collective-permute-start.6 = (bf16[4,64,512]{2,1,0:T(8,128)(2,1)S(1)}, bf16[4,64,512]{2,1,0:T(8,128)(2,1)S(1)}, u32[]{:S(2)}, u32[]{:S(2)}) collective-permute-start(bf16[4,64,512]{2,1,0:T(8,128)(2,1)S(1)} %pad_maximum_fusion.3), channel_id=1, source_target_pairs={{0,8},{1,3},{2,10},{3,1},{4,12},{5,7},{6,14},{7,5},{8,0},{9,11},{1... | collective-permute-start | bytes 786440 | tf_op jit(solution)/shard_map/ppermute | solution.py:1096
  24.9 1.5 %collective-permute-done.1 = bf16[2,144,512]{2,1,0:T(8,128)(2,1)S(1)} collective-permute-done((bf16[2,144,512]{2,1,0:T(8,128)(2,1)S(1)}, bf16[2,144,512]{2,1,0:T(8,128)(2,1)S(1)}, u32[]{:S(2)}, u32[]{:S(2)}) %collective-permute-start.1) | collective-permute-done | bytes 294944 | tf_op jit(solution)/shard_map/ppermute | solution.py:1096
  26.4 2.1 %collective-permute-start.2 = (bf16[4,144,512]{2,1,0:T(8,128)(2,1)S(1)}, bf16[4,144,512]{2,1,0:T(8,128)(2,1)S(1)}, u32[]{:S(2)}, u32[]{:S(2)}) collective-permute-start(bf16[4,144,512]{2,1,0:T(8,128)(2,1)S(1)} %pad_maximum_fusion.1), channel_id=1, source_target_pairs={{0,8},{1,3},{2,10},{3,1},{4,12},{5,7},{6,14},{7,5},{8,0},{9,11},{1... | collective-permute-start | bytes 1769480 | tf_op jit(solution)/shard_map/ppermute | solution.py:1096
  28.5 4.1 %prepare.1 = (f32[512,512]{1,0:T(8,128)S(1)}, f32[512,128]{1,0:T(8,128)S(1)}, bf16[512,512]{1,0:T(8,128)(2,1)S(1)}, f32[1024,128]{1,0:T(8,128)S(1)}, f32[2048,12...) custom-call(s32[10]{0:T(128)S(1)} %copy-done.4, ...), custom_call_target="tpu_custom_call" | custom-call | flops 1 | bytes 1 | tf_op jit(solution)/shard_map/prepare/pallas_call | solution.py:322
  32.7 2.9 %collective-permute-start.7 = (bf16[8,64,512]{2,1,0:T(8,128)(2,1)S(1)}, bf16[8,64,512]{2,1,0:T(8,128)(2,1)S(1)}, u32[]{:S(2)}, u32[]{:S(2)}) collective-permute-start(bf16[8,64,512]{2,1,0:T(8,128)(2,1)S(1)} %pad_maximum_fusion.2.refs_0_), channel_id=1, source_target_pairs={{0,4},{1,9},{2,6},{3,11},{4,0},{5,13},{6,2},{7,15},{8,12},{9,1},{1... | collective-permute-start | bytes 1572872 | tf_op jit(solution)/shard_map/ppermute | solution.py:1096
  35.7 3.3 %collective-permute-done.2 = bf16[4,144,512]{2,1,0:T(8,128)(2,1)S(1)} collective-permute-done((bf16[4,144,512]{2,1,0:T(8,128)(2,1)S(1)}, bf16[4,144,512]{2,1,0:T(8,128)(2,1)S(1)}, u32[]{:S(2)}, u32[]{:S(2)}) %collective-permute-start.2) | collective-permute-done | bytes 589856 | tf_op jit(solution)/shard_map/ppermute | solution.py:1096
  39.1 3.8 %collective-permute-done.7.refs_1_ = bf16[8,64,512]{2,1,0:T(8,128)(2,1)S(1)} collective-permute-done((bf16[8,64,512]{2,1,0:T(8,128)(2,1)S(1)}, bf16[8,64,512]{2,1,0:T(8,128)(2,1)S(1)}, u32[]{:S(2)}, u32[]{:S(2)}) %collective-permute-start.7) | collective-permute-done | bytes 524320 | tf_op jit(solution)/shard_map/ppermute | solution.py:1096
  42.8 2.0 %collective-permute-start.10 = (bf16[8,144,512]{2,1,0:T(8,128)(2,1)S(1)}, bf16[8,144,512]{2,1,0:T(8,128)(2,1)S(1)}, u32[]{:S(2)}, u32[]{:S(2)}) collective-permute-start(bf16[8,144,512]{2,1,0:T(8,128)(2,1)S(1)} %pad_maximum_fusion.refs_0_), channel_id=1, source_target_pairs={{0,4},{1,9},{2,6},{3,11},{4,0},{5,13},{6,2},{7,15},{8,12},{9,1},{1... | collective-permute-start | bytes 3538952 | tf_op jit(solution)/shard_map/ppermute | solution.py:1096
  45.4 1.4 %collective-permute-done.8.refs_2_ = bf16[8,64,512]{2,1,0:T(8,128)(2,1)S(1)} collective-permute-done((bf16[8,64,512]{2,1,0:T(8,128)(2,1)S(1)}, bf16[8,64,512]{2,1,0:T(8,128)(2,1)S(1)}, u32[]{:S(2)}, u32[]{:S(2)}) %collective-permute-start.8) | collective-permute-done | bytes 524320 | tf_op jit(solution)/shard_map/ppermute | solution.py:1096
  47.5 4.6 %project.1 = (bf16[1024,256]{1,0:T(8,128)(2,1)S(1)}, bf16[1024,256]{1,0:T(8,128)(2,1)S(1)}, bf16[1024,512]{1,0:T(8,128)(2,1)S(1)}, bf16[1024,512]{1,0:T(8,128)(2...) custom-call(s32[10]{0:T(128)S(1)} %copy-done.4, ...), custom_call_target="tpu_custom_call" | custom-call | flops 1 | bytes 1 | tf_op jit(solution)/shard_map/project/pallas_call | solution.py:417
  52.2 4.8 %attend.1 = (bf16[512,256]{1,0:T(8,128)(2,1)S(1)}, bf16[512,256]{1,0:T(8,128)(2,1)S(1)}, f32[512,256]{1,0:T(8,128)S(1)}, f32[512,256]{1,0:T(8,128)S(1)}, f32[512,256]{1,0:T(8,128)S(1)}, /*index=5*/f32[512,256]{1,0:T(8,128)S(1)}) custom-call(s32[10]{0:T(128)S(1)} %copy-done.4, f32[1024,128]{1,0:T(8,128)S(1)} %get-tuple-element.120.mask, ...), custom_call_target="tpu_custom_call" | custom-call | flops 1 | bytes 1 | tf_op jit(solution)/shard_map/attend/pallas_call | solution.py:517
  57.0 2.1 %collective-permute-done.10.refs_1_ = bf16[8,144,512]{2,1,0:T(8,128)(2,1)S(1)} collective-permute-done((bf16[8,144,512]{2,1,0:T(8,128)(2,1)S(1)}, bf16[8,144,512]{2,1,0:T(8,128)(2,1)S(1)}, u32[]{:S(2)}, u32[]{:S(2)}) %collective-permute-start.10) | collective-permute-done | bytes 1179680 | tf_op jit(solution)/shard_map/ppermute | solution.py:1096
  59.0 2.8 %collective-permute-done.12.refs_3_ = bf16[8,144,512]{2,1,0:T(8,128)(2,1)S(1)} collective-permute-done((bf16[8,144,512]{2,1,0:T(8,128)(2,1)S(1)}, bf16[8,144,512]{2,1,0:T(8,128)(2,1)S(1)}, u32[]{:S(2)}, u32[]{:S(2)}) %collective-permute-start.12) | collective-permute-done | bytes 1179680 | tf_op jit(solution)/shard_map/ppermute | solution.py:1096
  61.9 8.9 %feed_forward.1 = (bf16[512,512]{1,0:T(8,128)(2,1)}, f32[512,512]{1,0:T(8,128)S(1)}, f32[512,512]{1,0:T(8,128)S(1)}, bf16[512,512]{1,0:T(8,128)(2,1)S(1)}, bf16[...) custom-call(s32[32]{0:T(128)S(1)} %copy-done.6, ...), custom_call_target="tpu_custom_call" | custom-call | flops 1 | bytes 1 | tf_op jit(solution)/shard_map/feed_forward/pallas_call | solution.py:624
  71.3 3.2 %middle.1 = (f32[512,512]{1,0:T(8,128)S(1)}, bf16[1024,512]{1,0:T(8,128)(2,1)S(1)}, bf16[1024,512]{1,0:T(8,128)(2,1)S(1)}, bf16[160,640]{1,0:T(8,128)(2,1)S(1)},...) custom-call(s32[10]{0:T(128)S(1)} %copy-done.4, ...), custom_call_target="tpu_custom_call" | custom-call | flops 1 | bytes 1 | tf_op jit(solution)/shard_map/middle/pallas_call | solution.py:751
  78.6 4.2 %collective-permute-start.22 = (bf16[4,144,512]{2,1,0:T(8,128)(2,1)S(1)}, bf16[4,144,512]{2,1,0:T(8,128)(2,1)S(1)}, u32[]{:S(2)}, u32[]{:S(2)}) collective-permute-start(bf16[4,144,512]{2,1,0:T(8,128)(2,1)S(1)} %get-tuple-element.151), channel_id=1, source_target_pairs={{0,2},{1,5},{2,0},{3,7},{4,6},{5,1},{6,4},{7,3},{8,10},{9,13},{10,... | collective-permute-start | bytes 1769480 | tf_op jit(solution)/shard_map/ppermute | solution.py:1096
  82.8 7.7 %attend_back.1 = (f32[1024,256]{1,0:T(8,128)S(1)}, f32[1024,256]{1,0:T(8,128)S(1)}, f32[1344,512]{1,0:T(8,128)S(1)}, f32[1344,512]{1,0:T(8,128)S(1)}) custom-call(f32[2048,128]{1,0:T(8,128)S(1)} %get-tuple-element.114.mask, bf16[2048,128]{1,0:T(8,128)(2,1)S(1)} %get-tuple-element.115.counts_of, bf16[1024,256]{1,0:T(8,128)(2,1)S(1)} %get-tuple-element.121.refs_0_, ...), custom_call_target="tpu_custom_call" | custom-call | flops 1 | bytes 1 | tf_op jit(solution)/shard_map/attend_back/pallas_call | solution.py:845
  91.9 2.4 %edge_back.1 = (f32[320,512]{1,0:T(8,128)S(1)}, f32[320,512]{1,0:T(8,128)S(1)}) custom-call(s32[10]{0:T(128)S(1)} %copy-done.4, f32[320,128]{1,0:T(8,128)S(1)} %get-tuple-element.116.mask, bf16[320,128]{1,0:T(8,128)(2,1)S(1)} %get-tuple-element.117.counts_of, bf16[320,256]{1,0:T(8,128)(2,1)S(1)} %get-tuple-element.158.queries_a, ...), custom_call_target="tpu_custom_call" | custom-call | flops 1 | bytes 1 | tf_op jit(solution)/shard_map/edge_back/pallas_call | solution.py:937
  94.2 5.3 %finish.1 = (f32[512,512]{1,0:T(8,128)}, bf16[16,64,512]{2,1,0:T(8,128)(2,1)S(1)}, bf16[8,64,512]{2,1,0:T(8,128)(2,1)S(1)}, bf16[8,64,512]{2,1,0:T(8,128)(2,1)S(1)}) custom-call(s32[10]{0:T(128)S(1)} %copy-done.4, s32[32]{0:T(128)S(1)} %copy-done.5, f32[512,512]{1,0:T(8,128)S(1)} %get-tuple-element.111.standard, f32[512,128]{1,0:T(8,128)S(1)} %get-tuple-element.112.spread, ...), custom_call_target="tpu_custom_call" | custom-call | flops 1 | bytes 1 | tf_op jit(solution)/shard_map/finish/pallas_call | solution.py:1046
  102.5 2.2 %collective-permute-start.24 = (bf16[8,64,512]{2,1,0:T(8,128)(2,1)S(1)}, bf16[8,64,512]{2,1,0:T(8,128)(2,1)S(1)}, u32[]{:S(2)}, u32[]{:S(2)}) collective-permute-start(bf16[8,64,512]{2,1,0:T(8,128)(2,1)S(1)} %get-tuple-element.199), channel_id=1, source_target_pairs={{0,2},{1,5},{2,0},{3,7},{4,6},{5,1},{6,4},{7,3},{8,10},{9,13},{10,... | collective-permute-start | bytes 1572872 | tf_op jit(solution)/shard_map/ppermute | solution.py:1096
  105.8 6.2 %collective-permute-done.24 = bf16[8,64,512]{2,1,0:T(8,128)(2,1)S(1)} collective-permute-done((bf16[8,64,512]{2,1,0:T(8,128)(2,1)S(1)}, bf16[8,64,512]{2,1,0:T(8,128)(2,1)S(1)}, u32[]{:S(2)}, u32[]{:S(2)}) %collective-permute-start.24) | collective-permute-done | bytes 524320 | tf_op jit(solution)/shard_map/ppermute | solution.py:1096
  112.1 1.5 %collective-permute-start.25 = (bf16[4,64,512]{2,1,0:T(8,128)(2,1)S(1)}, bf16[4,64,512]{2,1,0:T(8,128)(2,1)S(1)}, u32[]{:S(2)}, u32[]{:S(2)}) collective-permute-start(bf16[4,64,512]{2,1,0:T(8,128)(2,1)S(1)} %get-tuple-element.195), channel_id=1, source_target_pairs={{0,4},{1,9},{2,6},{3,11},{4,0},{5,13},{6,2},{7,15},{8,12},{9,1},{1... | collective-permute-start | bytes 786440 | tf_op jit(solution)/shard_map/ppermute | solution.py:1096
  114.8 3.8 %collective-permute-done.25 = bf16[4,64,512]{2,1,0:T(8,128)(2,1)S(1)} collective-permute-done((bf16[4,64,512]{2,1,0:T(8,128)(2,1)S(1)}, bf16[4,64,512]{2,1,0:T(8,128)(2,1)S(1)}, u32[]{:S(2)}, u32[]{:S(2)}) %collective-permute-start.25) | collective-permute-done | bytes 262176 | tf_op jit(solution)/shard_map/ppermute | solution.py:1096
  119.7 5.4 %collective-permute-done.27 = bf16[2,64,512]{2,1,0:T(8,128)(2,1)S(1)} collective-permute-done((bf16[2,64,512]{2,1,0:T(8,128)(2,1)S(1)}, bf16[2,64,512]{2,1,0:T(8,128)(2,1)S(1)}, u32[]{:S(2)}, u32[]{:S(2)}) %collective-permute-start.27) | collective-permute-done | bytes 131104 | tf_op jit(solution)/shard_map/ppermute | solution.py:1096
  125.2 2.1 %collective-permute-done.29.came_two = bf16[1,144,512]{2,1,0:T(8,128)(2,1)S(1)} collective-permute-done((bf16[1,144,512]{2,1,0:T(8,128)(2,1)S(1)}, bf16[1,144,512]{2,1,0:T(8,128)(2,1)S(1)}, u32[]{:S(2)}, u32[]{:S(2)}) %collective-permute-start.29) | collective-permute-done | bytes 147488 | tf_op jit(solution)/shard_map/ppermute | solution.py:1096
  127.3 3.0 %collective-permute-done.28.came_one = bf16[1,64,512]{2,1,0:T(8,128)(2,1)S(1)} collective-permute-done((bf16[1,64,512]{2,1,0:T(8,128)(2,1)S(1)}, bf16[1,64,512]{2,1,0:T(8,128)(2,1)S(1)}, u32[]{:S(2)}, u32[]{:S(2)}) %collective-permute-start.28) | collective-permute-done | bytes 65568 | tf_op jit(solution)/shard_map/ppermute | solution.py:1096
  (73 shorter events, 18.7 us)
Async XLA Ops:
  2.4 12.0 %collective-permute-start = (bf16[1,208,512]{2,1,0:T(8,128)(2,1)}, bf16[1,208,512]{2,1,0:T(8,128)(2,1)S(1)}, u32[]{:S(2)}, u32[]{:S(2)}) collective-permute-start(bf16[1,208,512]{2,1,0:T(8,128)(2,1)} %get-tuple-element.105), channel_id=1, source_target_pairs={{0,16},{1,5},{2,18},{3,7},{4,20},{5,1},{6,22},{7,3},{8,24},{9,13},... | collective-permute-start | bytes 638984 | tf_op jit(solution)/shard_map/ppermute | solution.py:1096
  9.9 13.4 %collective-permute-start.4 = (bf16[160,1024]{1,0:T(8,128)(2,1)S(1)}, bf16[160,1024]{1,0:T(8,128)(2,1)S(1)}, u32[]{:S(2)}, u32[]{:S(2)}) collective-permute-start(bf16[160,1024]{1,0:T(8,128)(2,1)S(1)} %get-tuple-element.108), channel_id=1, source_target_pairs={{1,2},{3,4},{5,6},{7,8},{9,10},{11,12},{13,14},{15,16},{17,18},{19... | collective-permute-start | bytes 983048 | tf_op jit(solution)/shard_map/ppermute | solution.py:1205
  10.6 12.7 %collective-permute-start.5 = (bf16[160,1024]{1,0:T(8,128)(2,1)S(1)}, bf16[160,1024]{1,0:T(8,128)(2,1)S(1)}, u32[]{:S(2)}, u32[]{:S(2)}) collective-permute-start(bf16[160,1024]{1,0:T(8,128)(2,1)S(1)} %get-tuple-element.109), channel_id=1, source_target_pairs={{0,1},{1,0},{2,3},{3,2},{4,5},{5,4},{6,7},{7,6},{8,9},{9,8},{10,11... | collective-permute-start | bytes 983048 | tf_op jit(solution)/shard_map/ppermute | solution.py:1205
  14.4 14.1 %copy-start.1 = (bf16[512,512]{1,0:T(8,128)(2,1)S(1)}, bf16[512,512]{1,0:T(8,128)(2,1)}, u32[]{:S(2)}) copy-start(bf16[512,512]{1,0:T(8,128)(2,1)} %tokens.3) | copy-start | bytes 1572868
  14.5 8.7 %collective-permute-start.3 = (bf16[2,64,512]{2,1,0:T(8,128)(2,1)S(1)}, bf16[2,64,512]{2,1,0:T(8,128)(2,1)S(1)}, u32[]{:S(2)}, u32[]{:S(2)}) collective-permute-start(bf16[2,64,512]{2,1,0:T(8,128)(2,1)S(1)} %slice.121), channel_id=1, source_target_pairs={{0,2},{1,17},{2,0},{3,19},{4,6},{5,21},{6,4},{7,23},{8,10},{9,25},... | collective-permute-start | bytes 393224 | tf_op jit(solution)/shard_map/ppermute | solution.py:1096
  16.1 10.3 %collective-permute-start.1 = (bf16[2,144,512]{2,1,0:T(8,128)(2,1)S(1)}, bf16[2,144,512]{2,1,0:T(8,128)(2,1)S(1)}, u32[]{:S(2)}, u32[]{:S(2)}) collective-permute-start(bf16[2,144,512]{2,1,0:T(8,128)(2,1)S(1)} %slice.120), channel_id=1, source_target_pairs={{0,2},{1,17},{2,0},{3,19},{4,6},{5,21},{6,4},{7,23},{8,10},{9,25},... | collective-permute-start | bytes 884744 | tf_op jit(solution)/shard_map/ppermute | solution.py:1096
  23.3 9.4 %collective-permute-start.6 = (bf16[4,64,512]{2,1,0:T(8,128)(2,1)S(1)}, bf16[4,64,512]{2,1,0:T(8,128)(2,1)S(1)}, u32[]{:S(2)}, u32[]{:S(2)}) collective-permute-start(bf16[4,64,512]{2,1,0:T(8,128)(2,1)S(1)} %pad_maximum_fusion.3), channel_id=1, source_target_pairs={{0,8},{1,3},{2,10},{3,1},{4,12},{5,7},{6,14},{7,5},{8,0},{9,11},{1... | collective-permute-start | bytes 786440 | tf_op jit(solution)/shard_map/ppermute | solution.py:1096
  26.4 12.5 %collective-permute-start.2 = (bf16[4,144,512]{2,1,0:T(8,128)(2,1)S(1)}, bf16[4,144,512]{2,1,0:T(8,128)(2,1)S(1)}, u32[]{:S(2)}, u32[]{:S(2)}) collective-permute-start(bf16[4,144,512]{2,1,0:T(8,128)(2,1)S(1)} %pad_maximum_fusion.1), channel_id=1, source_target_pairs={{0,8},{1,3},{2,10},{3,1},{4,12},{5,7},{6,14},{7,5},{8,0},{9,11},{1... | collective-permute-start | bytes 1769480 | tf_op jit(solution)/shard_map/ppermute | solution.py:1096
  32.7 14.8 %copy-start.6 = (s32[32]{0:T(128)S(1)}, s32[32]{0:T(128)}, u32[]{:S(2)}) copy-start(s32[32]{0:T(128)} %get-tuple-element.102.inverse) | copy-start | bytes 388
  32.7 10.1 %collective-permute-start.7 = (bf16[8,64,512]{2,1,0:T(8,128)(2,1)S(1)}, bf16[8,64,512]{2,1,0:T(8,128)(2,1)S(1)}, u32[]{:S(2)}, u32[]{:S(2)}) collective-permute-start(bf16[8,64,512]{2,1,0:T(8,128)(2,1)S(1)} %pad_maximum_fusion.2.refs_0_), channel_id=1, source_target_pairs={{0,4},{1,9},{2,6},{3,11},{4,0},{5,13},{6,2},{7,15},{8,12},{9,1},{1... | collective-permute-start | bytes 1572872 | tf_op jit(solution)/shard_map/ppermute | solution.py:1096
  42.8 16.2 %collective-permute-start.10 = (bf16[8,144,512]{2,1,0:T(8,128)(2,1)S(1)}, bf16[8,144,512]{2,1,0:T(8,128)(2,1)S(1)}, u32[]{:S(2)}, u32[]{:S(2)}) collective-permute-start(bf16[8,144,512]{2,1,0:T(8,128)(2,1)S(1)} %pad_maximum_fusion.refs_0_), channel_id=1, source_target_pairs={{0,4},{1,9},{2,6},{3,11},{4,0},{5,13},{6,2},{7,15},{8,12},{9,1},{1... | collective-permute-start | bytes 3538952 | tf_op jit(solution)/shard_map/ppermute | solution.py:1096
  44.8 1.9 %collective-permute-start.8 = (bf16[8,64,512]{2,1,0:T(8,128)(2,1)S(1)}, bf16[8,64,512]{2,1,0:T(8,128)(2,1)S(1)}, u32[]{:S(2)}, u32[]{:S(2)}) collective-permute-start(bf16[8,64,512]{2,1,0:T(8,128)(2,1)S(1)} %pad_maximum_fusion.2.refs_0_), channel_id=1, source_target_pairs={{0,1},{1,0},{2,3},{3,2},{4,5},{5,4},{6,7},{7,6},{8,9},{9,8},{10,11... | collective-permute-start | bytes 1572872 | tf_op jit(solution)/shard_map/ppermute | solution.py:1096
  44.8 2.7 %collective-permute-start.9 = (bf16[8,64,512]{2,1,0:T(8,128)(2,1)S(1)}, bf16[8,64,512]{2,1,0:T(8,128)(2,1)S(1)}, u32[]{:S(2)}, u32[]{:S(2)}) collective-permute-start(bf16[8,64,512]{2,1,0:T(8,128)(2,1)S(1)} %collective-permute-done.7.refs_1_), channel_id=1, source_target_pairs={{0,1},{1,0},{2,3},{3,2},{4,5},{5,4},{6,7},{7,6},{8,9},{9,8},{10,11... | collective-permute-start | bytes 1572872 | tf_op jit(solution)/shard_map/ppermute | solution.py:1096
  45.4 13.7 %collective-permute-start.11 = (bf16[8,144,512]{2,1,0:T(8,128)(2,1)S(1)}, bf16[8,144,512]{2,1,0:T(8,128)(2,1)S(1)}, u32[]{:S(2)}, u32[]{:S(2)}) collective-permute-start(bf16[8,144,512]{2,1,0:T(8,128)(2,1)S(1)} %pad_maximum_fusion.refs_0_), channel_id=1, source_target_pairs={{0,1},{1,0},{2,3},{3,2},{4,5},{5,4},{6,7},{7,6},{8,9},{9,8},{10,11... | collective-permute-start | bytes 3538952 | tf_op jit(solution)/shard_map/ppermute | solution.py:1096
  59.0 2.8 %collective-permute-start.12 = (bf16[8,144,512]{2,1,0:T(8,128)(2,1)S(1)}, bf16[8,144,512]{2,1,0:T(8,128)(2,1)S(1)}, u32[]{:S(2)}, u32[]{:S(2)}) collective-permute-start(bf16[8,144,512]{2,1,0:T(8,128)(2,1)S(1)} %collective-permute-done.10.refs_1_), channel_id=1, source_target_pairs={{0,1},{1,0},{2,3},{3,2},{4,5},{5,4},{6,7},{7,6},{8,9},{9,8},{10,11... | collective-permute-start | bytes 3538952 | tf_op jit(solution)/shard_map/ppermute | solution.py:1096
  70.8 5.3 %collective-permute-start.13 = (bf16[8,128,512]{2,1,0:T(8,128)(2,1)S(1)}, bf16[8,128,512]{2,1,0:T(8,128)(2,1)S(1)}, u32[]{:S(2)}, u32[]{:S(2)}) collective-permute-start(bf16[8,128,512]{2,1,0:T(8,128)(2,1)S(1)} %get-tuple-element.147), channel_id=1, source_target_pairs={{0,1},{1,0},{2,3},{3,2},{4,5},{5,4},{6,7},{7,6},{8,9},{9,8},{10,11... | collective-permute-start | bytes 3145736 | tf_op jit(solution)/shard_map/ppermute | solution.py:1096
  70.9 5.2 %collective-permute-start.17 = (bf16[8,128,512]{2,1,0:T(8,128)(2,1)S(1)}, bf16[8,128,512]{2,1,0:T(8,128)(2,1)S(1)}, u32[]{:S(2)}, u32[]{:S(2)}) collective-permute-start(bf16[8,128,512]{2,1,0:T(8,128)(2,1)S(1)} %get-tuple-element.163), channel_id=1, source_target_pairs={{0,1},{1,0},{2,3},{3,2},{4,5},{5,4},{6,7},{7,6},{8,9},{9,8},{10,11... | collective-permute-start | bytes 3145736 | tf_op jit(solution)/shard_map/ppermute | solution.py:1096
  74.5 1.4 %collective-permute-start.14 = (bf16[8,16,512]{2,1,0:T(8,128)(2,1)S(1)}, bf16[8,16,512]{2,1,0:T(8,128)(2,1)S(1)}, u32[]{:S(2)}, u32[]{:S(2)}) collective-permute-start(bf16[8,16,512]{2,1,0:T(8,128)(2,1)S(1)} %get-tuple-element.148), channel_id=1, source_target_pairs={{0,1},{1,0},{2,3},{3,2},{4,5},{5,4},{6,7},{7,6},{8,9},{9,8},{10,11... | collective-permute-start | bytes 393224 | tf_op jit(solution)/shard_map/ppermute | solution.py:1096
  74.7 1.4 %collective-permute-start.18 = (bf16[8,16,512]{2,1,0:T(8,128)(2,1)S(1)}, bf16[8,16,512]{2,1,0:T(8,128)(2,1)S(1)}, u32[]{:S(2)}, u32[]{:S(2)}) collective-permute-start(bf16[8,16,512]{2,1,0:T(8,128)(2,1)S(1)} %get-tuple-element.164), channel_id=1, source_target_pairs={{0,1},{1,0},{2,3},{3,2},{4,5},{5,4},{6,7},{7,6},{8,9},{9,8},{10,11... | collective-permute-start | bytes 393224 | tf_op jit(solution)/shard_map/ppermute | solution.py:1096
  75.0 1.8 %collective-permute-start.15 = (bf16[160,640]{1,0:T(8,128)(2,1)S(1)}, bf16[160,640]{1,0:T(8,128)(2,1)S(1)}, u32[]{:S(2)}, u32[]{:S(2)}) collective-permute-start(bf16[160,640]{1,0:T(8,128)(2,1)S(1)} %get-tuple-element.149), channel_id=1, source_target_pairs={{0,1},{1,0},{2,3},{3,2},{4,5},{5,4},{6,7},{7,6},{8,9},{9,8},{10,11... | collective-permute-start | bytes 614408 | tf_op jit(solution)/shard_map/ppermute | solution.py:1205
  76.9 13.6 %collective-permute-start.19 = (bf16[4,144,512]{2,1,0:T(8,128)(2,1)S(1)}, bf16[4,144,512]{2,1,0:T(8,128)(2,1)S(1)}, u32[]{:S(2)}, u32[]{:S(2)}) collective-permute-start(bf16[4,144,512]{2,1,0:T(8,128)(2,1)S(1)} %get-tuple-element.150), channel_id=1, source_target_pairs={{0,2},{1,5},{2,0},{3,7},{4,6},{5,1},{6,4},{7,3},{8,10},{9,13},{10,... | collective-permute-start | bytes 1769480 | tf_op jit(solution)/shard_map/ppermute | solution.py:1096
  77.7 12.8 %collective-permute-start.16 = (bf16[160,640]{1,0:T(8,128)(2,1)S(1)}, bf16[160,640]{1,0:T(8,128)(2,1)S(1)}, u32[]{:S(2)}, u32[]{:S(2)}) collective-permute-start(bf16[160,640]{1,0:T(8,128)(2,1)S(1)} %get-tuple-element.160), channel_id=1, source_target_pairs={{1,2},{3,4},{5,6},{7,8},{9,10},{11,12},{13,14},{15,16},{17,18},{19... | collective-permute-start | bytes 614408 | tf_op jit(solution)/shard_map/ppermute | solution.py:1205
  78.6 21.4 %collective-permute-start.22 = (bf16[4,144,512]{2,1,0:T(8,128)(2,1)S(1)}, bf16[4,144,512]{2,1,0:T(8,128)(2,1)S(1)}, u32[]{:S(2)}, u32[]{:S(2)}) collective-permute-start(bf16[4,144,512]{2,1,0:T(8,128)(2,1)S(1)} %get-tuple-element.151), channel_id=1, source_target_pairs={{0,2},{1,5},{2,0},{3,7},{4,6},{5,1},{6,4},{7,3},{8,10},{9,13},{10,... | collective-permute-start | bytes 1769480 | tf_op jit(solution)/shard_map/ppermute | solution.py:1096
  90.7 9.9 %collective-permute-start.23 = (bf16[4,144,512]{2,1,0:T(8,128)(2,1)S(1)}, bf16[4,144,512]{2,1,0:T(8,128)(2,1)S(1)}, u32[]{:S(2)}, u32[]{:S(2)}) collective-permute-start(bf16[4,144,512]{2,1,0:T(8,128)(2,1)S(1)} %fusion), channel_id=1, source_target_pairs={{0,4},{1,9},{2,6},{3,11},{4,0},{5,13},{6,2},{7,15},{8,12},{9,1},{1... | collective-permute-start | bytes 1769480 | tf_op jit(solution)/shard_map/ppermute | solution.py:1096
  99.6 1.9 %collective-permute-start.20 = (bf16[8,64,512]{2,1,0:T(8,128)(2,1)S(1)}, bf16[8,64,512]{2,1,0:T(8,128)(2,1)S(1)}, u32[]{:S(2)}, u32[]{:S(2)}) collective-permute-start(bf16[8,64,512]{2,1,0:T(8,128)(2,1)S(1)} %get-tuple-element.172), channel_id=1, source_target_pairs={{0,1},{1,0},{2,3},{3,2},{4,5},{5,4},{6,7},{7,6},{8,9},{9,8},{10,11... | collective-permute-start | bytes 1572872 | tf_op jit(solution)/shard_map/ppermute | solution.py:1096
  99.6 2.7 %collective-permute-start.21 = (bf16[8,64,512]{2,1,0:T(8,128)(2,1)S(1)}, bf16[8,64,512]{2,1,0:T(8,128)(2,1)S(1)}, u32[]{:S(2)}, u32[]{:S(2)}) collective-permute-start(bf16[8,64,512]{2,1,0:T(8,128)(2,1)S(1)} %get-tuple-element.173), channel_id=1, source_target_pairs={{0,1},{1,0},{2,3},{3,2},{4,5},{5,4},{6,7},{7,6},{8,9},{9,8},{10,11... | collective-permute-start | bytes 1572872 | tf_op jit(solution)/shard_map/ppermute | solution.py:1096
  102.5 9.4 %collective-permute-start.24 = (bf16[8,64,512]{2,1,0:T(8,128)(2,1)S(1)}, bf16[8,64,512]{2,1,0:T(8,128)(2,1)S(1)}, u32[]{:S(2)}, u32[]{:S(2)}) collective-permute-start(bf16[8,64,512]{2,1,0:T(8,128)(2,1)S(1)} %get-tuple-element.199), channel_id=1, source_target_pairs={{0,2},{1,5},{2,0},{3,7},{4,6},{5,1},{6,4},{7,3},{8,10},{9,13},{10,... | collective-permute-start | bytes 1572872 | tf_op jit(solution)/shard_map/ppermute | solution.py:1096
  104.8 9.9 %collective-permute-start.26 = (bf16[2,144,512]{2,1,0:T(8,128)(2,1)S(1)}, bf16[2,144,512]{2,1,0:T(8,128)(2,1)S(1)}, u32[]{:S(2)}, u32[]{:S(2)}) collective-permute-start(bf16[2,144,512]{2,1,0:T(8,128)(2,1)S(1)} %get-tuple-element.194), channel_id=1, source_target_pairs={{0,8},{1,17},{2,10},{3,19},{4,12},{5,21},{6,14},{7,23},{8,0},{9,25... | collective-permute-start | bytes 884744 | tf_op jit(solution)/shard_map/ppermute | solution.py:1096
  112.1 6.4 %collective-permute-start.25 = (bf16[4,64,512]{2,1,0:T(8,128)(2,1)S(1)}, bf16[4,64,512]{2,1,0:T(8,128)(2,1)S(1)}, u32[]{:S(2)}, u32[]{:S(2)}) collective-permute-start(bf16[4,64,512]{2,1,0:T(8,128)(2,1)S(1)} %get-tuple-element.195), channel_id=1, source_target_pairs={{0,4},{1,9},{2,6},{3,11},{4,0},{5,13},{6,2},{7,15},{8,12},{9,1},{1... | collective-permute-start | bytes 786440 | tf_op jit(solution)/shard_map/ppermute | solution.py:1096
  118.6 6.5 %collective-permute-start.27 = (bf16[2,64,512]{2,1,0:T(8,128)(2,1)S(1)}, bf16[2,64,512]{2,1,0:T(8,128)(2,1)S(1)}, u32[]{:S(2)}, u32[]{:S(2)}) collective-permute-start(bf16[2,64,512]{2,1,0:T(8,128)(2,1)S(1)} %get-tuple-element.203), channel_id=1, source_target_pairs={{0,8},{1,17},{2,10},{3,19},{4,12},{5,21},{6,14},{7,23},{8,0},{9,25... | collective-permute-start | bytes 393224 | tf_op jit(solution)/shard_map/ppermute | solution.py:1096
  119.7 7.6 %collective-permute-start.29 = (bf16[1,144,512]{2,1,0:T(8,128)(2,1)S(1)}, bf16[1,144,512]{2,1,0:T(8,128)(2,1)S(1)}, u32[]{:S(2)}, u32[]{:S(2)}) collective-permute-start(bf16[1,144,512]{2,1,0:T(8,128)(2,1)S(1)} %get-tuple-element.202), channel_id=1, source_target_pairs={{0,16},{1,3},{2,18},{3,1},{4,20},{5,7},{6,22},{7,5},{8,24},{9,11},... | collective-permute-start | bytes 442376 | tf_op jit(solution)/shard_map/ppermute | solution.py:1096
  125.1 5.2 %collective-permute-start.28 = (bf16[1,64,512]{2,1,0:T(8,128)(2,1)S(1)}, bf16[1,64,512]{2,1,0:T(8,128)(2,1)S(1)}, u32[]{:S(2)}, u32[]{:S(2)}) collective-permute-start(bf16[1,64,512]{2,1,0:T(8,128)(2,1)S(1)} %get-tuple-element.205), channel_id=1, source_target_pairs={{0,16},{1,3},{2,18},{3,1},{4,20},{5,7},{6,22},{7,5},{8,24},{9,11},... | collective-permute-start | bytes 196616 | tf_op jit(solution)/shard_map/ppermute | solution.py:1096
  (5 other events, 35.3 us)

commit v6 on v5

--- a/solution.py
+++ b/solution.py
@@ -18,6 +18,8 @@
 PIECES = 4
 BLOCKS = 32
 LINE = 128
+LINE_ROWS = 8
+MIXED = 16
 FAR = 1 << 26
 SEQ_STEP = 1 << 21
 MIB = 1024 * 1024
@@ -140,7 +142,7 @@
 
 def place_halos(info, from_twin, from_other, halos):
     even = is_even(info)
-    size = LEVELS * HALO
+    size = halos.shape[0] // 2
     halos[pl.ds(pl.multiple_of(jnp.where(even, size, 0), size), size), :] = from_twin[...]
     halos[pl.ds(pl.multiple_of(jnp.where(even, 0, size), size), size), :] = from_other[...]
 
@@ -169,21 +171,16 @@
     return jnp.sum(values, axis=0, keepdims=True)
 
 
-def unpack_vectors(table, wide):
+def unpack_vector(table, first, each):
     blocks, lanes = table.shape
-
-    def one(first, each):
-        length = blocks * each
-        source = lax.broadcasted_iota(jnp.int32, (lanes, length), 0)
-        target = lax.broadcasted_iota(jnp.int32, (lanes, length), 1)
-        pick = jnp.where(source == first + (target & (each - 1)), 1.0, 0.0).astype(bf16)
-        spreaded = dot_nn(table, pick)
-        block = lax.broadcasted_iota(jnp.int32, (blocks, length), 0)
-        lane = lax.broadcasted_iota(jnp.int32, (blocks, length), 1)
-        return column_sum(jnp.where(lane // each == block, spreaded, 0.0))
-
-    size = wide // 4
-    return [one(k * size, size) for k in range(6)], one(6 * size, wide)
+    length = blocks * each
+    source = lax.broadcasted_iota(jnp.int32, (lanes, length), 0)
+    target = lax.broadcasted_iota(jnp.int32, (lanes, length), 1)
+    pick = jnp.where(source == first + (target & (each - 1)), 1.0, 0.0).astype(bf16)
+    spreaded = dot_nn(table, pick)
+    block = lax.broadcasted_iota(jnp.int32, (blocks, length), 0)
+    lane = lax.broadcasted_iota(jnp.int32, (blocks, length), 1)
+    return column_sum(jnp.where(lane // each == block, spreaded, 0.0))
 
 
 def pack_vectors(vectors, last, blocks, lanes):
@@ -224,9 +221,24 @@
         shift = jnp.where(row >= at, level, shift)
         share = jnp.where(row_one >= at, 0.5**level, share)
     pool = jnp.where((slot >> shift) == wanted, 1.0, 0.0).astype(bf16)
-    ends[:, pl.ds(0, width)] = (dot_nn(pool, plain) * share).astype(bf16)
-    ends[:, pl.ds(width, width)] = dot_nn(pool, living).astype(bf16)
-    hand_out(info, ends, to_twin, to_other)
+    ends[...] = (dot_nn(pool, plain) * share).astype(bf16)
+    row = lax.broadcasted_iota(jnp.int32, (MIXED, rows), 0)
+    slot = info[0] * rows + lax.broadcasted_iota(jnp.int32, (MIXED, rows), 1)
+    wanted = jnp.full((MIXED, rows), -1, jnp.int32)
+    shift = jnp.zeros((MIXED, rows), jnp.int32)
+    for level in range(1, LEVELS):
+        for k in range(3):
+            here = row == (level - 1) * 3 + k
+            wanted = jnp.where(here, (info[4 + k] + info[1 + k]) >> level, wanted)
+            shift = jnp.where(here, level, shift)
+    pick = jnp.where((slot >> shift) == wanted, 1.0, 0.0).astype(bf16)
+    mixed = dot_nn(pick, living).astype(bf16)
+    even = is_even(info)
+    size = LEVELS * HALO
+    for target, first in ((to_twin, size), (to_other, 0)):
+        at = pl.multiple_of(jnp.where(even, first, size - first), size)
+        target[pl.ds(0, size), :] = ends[pl.ds(at, size), :]
+        target[pl.ds(size, MIXED), :] = mixed
 
 
 def edge_sums(plan, total, info, tokens):
@@ -234,10 +246,10 @@
     size = LEVELS * HALO
     return pl.pallas_call(
         functools.partial(edge_sums_kernel, plan, total),
-        out_shape=[jax.ShapeDtypeStruct((size, 2 * width), bf16)] * 2,
+        out_shape=[jax.ShapeDtypeStruct((size + MIXED, width), bf16)] * 2,
         in_specs=[SCALARS] + spec(1),
         out_specs=spec(2),
-        scratch_shapes=[pltpu.VMEM((2 * size, 2 * width), bf16)],
+        scratch_shapes=[pltpu.VMEM((2 * size, width), bf16)],
         compiler_params=params(10),
         name="edge_sums",
         cost_estimate=cost(1.5),
@@ -344,23 +356,21 @@
 ):
     pieces, outs = refs[:PIECES], refs[PIECES:]
     queries, pairs, halo_queries, halo_pairs = (outs[2 * k : 2 * k + 2] for k in range(4))
-    weight, vectors, shift_out, table, edges, halos = outs[8:]
+    weight, vectors, shift_out, table, edges, halos, mixed = outs[8:]
     rows, width = standard.shape
     device = info[0]
     each = pieces[0].shape[0]
-    block_rows = pieces[0].shape[1] // 4
+    block_rows = pieces[0].shape[1] // 3 // 16 * 16
     for p in range(PIECES * each):
         i = inverse[p]
         there = pl.ds(pl.multiple_of(i * block_rows, block_rows), block_rows)
         piece, q = pieces[p // each], p % each
         for c in range(3):
             weight[there, pl.ds(c * width, width)] = piece[q, pl.ds(block_rows * c, block_rows), :]
-        line = piece[q, pl.ds(block_rows * 3, block_rows), pl.ds(0, 2 * LINE)].astype(f32)
+        line = piece[q, pl.ds(block_rows * 3, LINE_ROWS), pl.ds(0, 2 * LINE)].astype(f32)
         table[pl.ds(i, 1), :] = line[0:1]
-    singles, wide = unpack_vectors(table[...].astype(bf16), 4 * block_rows)
-    for k, single in enumerate(singles):
-        vectors[pl.ds(k, 1), :] = single
-    shift_out[...] = wide
+    packed = table[...].astype(bf16)
+    singles = [unpack_vector(packed, k * block_rows, block_rows) for k in range(2)]
     low = (standard[...] * singles[0] + singles[1]).astype(bf16)
     pooled_rows = pool.shape[0]
     share = jnp.zeros((pooled_rows, 1), f32)
@@ -372,47 +382,70 @@
     live = live_counts(info, places, 0, total)
     place_halos(info, from_twin, from_other, edges)
     size = LEVELS * HALO
-    halos[:, pl.ds(0, width)] = (
-        edges[:, pl.ds(0, width)].astype(f32) * singles[0] + singles[1]
-    ).astype(bf16)
+    for k in range(2):
+        rest = pl.ds(k * (size + MIXED) + size, MIXED)
+        mixed[pl.ds(k * MIXED, MIXED), :] = edges[rest, :].astype(f32)
     for k in range(2 * LEVELS):
         level, here = k % LEVELS, pl.ds(k * HALO, HALO)
+        side, span = k // LEVELS * (size + MIXED), 1 << level
+        mean = edges[pl.ds(side + level * HALO, HALO), :].astype(f32)
+        halos[here, pl.ds(0, width)] = (mean * singles[0] + singles[1]).astype(bf16)
         count = plan.counts[level]
         first = device * count + (-HALO if k < LEVELS else count)
         place = first + lax.broadcasted_iota(jnp.int32, (HALO, 128), 0)
         counts = live_counts(info, place, level, total)
-        counts = jnp.concatenate([counts] * (width // 128), axis=1)
-        halos[here, pl.ds(width, width)] = (
-            edges[here, pl.ds(width, width)].astype(f32) * singles[0] + counts * singles[1]
-        ).astype(bf16)
+        wide = jnp.concatenate([counts] * (width // 128), axis=1)
+        value = jnp.where(wide == span, mean * span, 0.0)
+        if level:
+            number = slot_facts(info, place << level, total)[0]
+            for index in range(3):
+                ends = (counts > 0.0) & (counts < span) & (number == index)
+                ends = jnp.where(ends, 1.0, 0.0)
+                ends = jnp.concatenate([ends] * (width // 128), axis=1)
+                row = k // LEVELS * MIXED + (level - 1) * 3 + index
+                value = value + ends * mixed[pl.ds(row, 1), :]
+        halos[here, pl.ds(width, width)] = (value * singles[0] + wide * singles[1]).astype(bf16)
     lanes = QUAD_WIDTH
     scale = 1.0 / math.sqrt(HEAD_DIM)
-    for part in range(3 * width // lanes):
-        columns = pl.ds(part * lanes, lanes)
-        block = dot_nn(low, weight[:, columns]).astype(bf16)
-        kind, quad = divmod(part, 2)
+    parts = [(divmod(part, 2), pl.ds(part * lanes, lanes)) for part in range(3 * width // lanes)]
+    own = pl.ds(0, rows)
+    above = pl.ds(rows, pooled_rows)
+    blocks = [dot_nn(low, weight[:, columns]).astype(bf16) for _, columns in parts]
+    for index, ((kind, quad), _) in enumerate(parts):
+        if kind == 0:
+            queries[quad][own, :] = (blocks[index].astype(f32) * scale).astype(bf16)
+            continue
         if kind == 2:
-            block = (block.astype(f32) * live).astype(bf16)
-        pooled = dot_nn(pool[...], block)
-        if kind < 2:
-            pooled = pooled * share
-        side = dot_nn(halos[:, pl.ds(width if kind == 2 else 0, width)], weight[:, columns])
+            blocks[index] = (blocks[index].astype(f32) * live).astype(bf16)
+        pairs[quad][own, pl.ds((kind - 1) * lanes, lanes)] = blocks[index]
+    pooled = [dot_nn(pool[...], block) for block in blocks]
+    for ((kind, quad), _), item in zip(parts, pooled):
         if kind == 0:
-            queries[quad][pl.ds(0, rows), :] = (block.astype(f32) * scale).astype(bf16)
-            queries[quad][pl.ds(rows, pooled_rows), :] = (pooled * scale).astype(bf16)
-            halo_queries[quad][...] = (side * scale).astype(bf16)
+            queries[quad][above, :] = (item * (share * scale)).astype(bf16)
+            continue
+        if kind == 1:
+            item = item * share
+        pairs[quad][above, pl.ds((kind - 1) * lanes, lanes)] = item.astype(bf16)
+    sides = [
+        dot_nn(halos[:, pl.ds(width if kind == 2 else 0, width)], weight[:, columns])
+        for (kind, _), columns in parts
+    ]
+    for ((kind, quad), _), item in zip(parts, sides):
+        if kind == 0:
+            halo_queries[quad][...] = (item * scale).astype(bf16)
         else:
-            there = pl.ds((kind - 1) * lanes, lanes)
-            pairs[quad][pl.ds(0, rows), there] = block
-            pairs[quad][pl.ds(rows, pooled_rows), there] = pooled.astype(bf16)
-            halo_pairs[quad][:, there] = side.astype(bf16)
+            halo_pairs[quad][:, pl.ds((kind - 1) * lanes, lanes)] = item.astype(bf16)
+    singles += [unpack_vector(packed, k * block_rows, block_rows) for k in range(2, 6)]
+    for k, single in enumerate(singles):
+        vectors[pl.ds(k, 1), :] = single
+    shift_out[...] = unpack_vector(packed, 6 * block_rows, 4 * block_rows)
 
 
 def project(plan, total, info, inverse, standard, pool, from_twin, from_other, pieces):
     rows, width = standard.shape
     halo = LEVELS * HALO
     blocks = PIECES * pieces[0].shape[0]
-    depth = blocks * pieces[0].shape[1] // 4
+    depth = blocks * (pieces[0].shape[1] - LINE_ROWS) // 3
     half = width // 2
     outs = pl.pallas_call(
         functools.partial(project_kernel, plan, total),
@@ -431,8 +464,9 @@
         out_specs=spec(11),
         scratch_shapes=[
             pltpu.VMEM((blocks, 2 * LINE), f32),
+            pltpu.VMEM((2 * (halo + MIXED), width), bf16),
             pltpu.VMEM((2 * halo, 2 * width), bf16),
-            pltpu.VMEM((2 * halo, 2 * width), bf16),
+            pltpu.VMEM((2 * MIXED, width), f32),
         ],
         compiler_params=params(18),
         name="project",
@@ -978,61 +1012,62 @@
     half_width = width // 2
     places = device * rows + lax.broadcasted_iota(jnp.int32, (rows, 128), 0)
     live = live_counts(info, places, 0, total)
-    for chunk in range(3 * width // 128):
-        part, lane = divmod(chunk * 128, width)
-        quad, lane = divmod(lane, half_width)
-        if part == 0:
-            work[chunk] = (queries_a, queries_b)[quad][:, pl.ds(lane, 128)]
-        else:
-            lanes = pl.ds((part - 1) * half_width + lane, 128)
-            for level in range(LEVELS):
-                at, count = plan.query_at[level], plan.counts[level]
-                own_rows = pl.ds(plan.key_at[level] + HALO, count)
-                work[chunk, pl.ds(at, count), :] = (pairs_a, pairs_b)[quad][own_rows, lanes]
-                halo = pl.ds(HALO * (quad * LEVELS + level), HALO)
-                work[chunk, pl.ds(at, HALO), :] += edge_low[halo, lanes]
-                work[chunk, pl.ds(at + count - HALO, HALO), :] += edge_high[halo, lanes]
-        for level in range(LEVELS - 1, 0, -1):
-            count = plan.counts[level]
-            upper = work[chunk, pl.ds(plan.query_at[level], count), :]
-            if chunk * 128 < 2 * width:
-                upper = upper * 0.5
-            for parity in range(2):
-                there = pl.ds(plan.query_at[level - 1] + parity, count, stride=2)
-                work[chunk, there, :] = work[chunk, there, :] + upper
-        value = work[chunk, pl.ds(0, rows), :]
-        if chunk * 128 >= 2 * width:
-            value = value * live
-        joined[:, pl.ds(chunk * 128, 128)] = value.astype(bf16)
     hat = standard[...]
     gain = vectors[pl.ds(0, 1), :]
     normed = (hat * gain + vectors[pl.ds(1, 1), :]).astype(bf16)
-    half, block = own.shape[0], own.shape[1] // 4
+    half, block = own.shape[0], width // BLOCKS
     other = (low_half, high_half)
+    grad_normed = jnp.zeros((rows, width), f32)
     for part in range(3):
+        for step in range(width // 128):
+            chunk = part * (width // 128) + step
+            quad, lane = divmod(step * 128, half_width)
+            if part == 0:
+                work[chunk] = (queries_a, queries_b)[quad][:, pl.ds(lane, 128)]
+            else:
+                lanes = pl.ds((part - 1) * half_width + lane, 128)
+                for level in range(LEVELS):
+                    at, count = plan.query_at[level], plan.counts[level]
+                    own_rows = pl.ds(plan.key_at[level] + HALO, count)
+                    work[chunk, pl.ds(at, count), :] = (pairs_a, pairs_b)[quad][own_rows, lanes]
+                    halo = pl.ds(HALO * (quad * LEVELS + level), HALO)
+                    work[chunk, pl.ds(at, HALO), :] += edge_low[halo, lanes]
+                    work[chunk, pl.ds(at + count - HALO, HALO), :] += edge_high[halo, lanes]
+            for level in range(LEVELS - 1, 0, -1):
+                count = plan.counts[level]
+                upper = work[chunk, pl.ds(plan.query_at[level], count), :]
+                if chunk * 128 < 2 * width:
+                    upper = upper * 0.5
+                for parity in range(2):
+                    there = pl.ds(plan.query_at[level - 1] + parity, count, stride=2)
+                    work[chunk, there, :] = work[chunk, there, :] + upper
+            value = work[chunk, pl.ds(0, rows), :]
+            if chunk * 128 >= 2 * width:
+                value = value * live
+            joined[:, pl.ds(chunk * 128, 128)] = value.astype(bf16)
         columns = pl.ds(part * width, width)
-        flat[...] = dot_tn(normed, joined[:, columns])
+        flat[part] = dot_tn(normed, joined[:, columns]).astype(bf16)
         for p in range(2 * half):
             i = inverse[p]
-            lines = flat[pl.ds(pl.multiple_of(i * block, block), block), :]
+            lines = flat[part, pl.ds(pl.multiple_of(i * block, block), block), :]
             there = pl.ds(part * block, block)
             if p < half:
-                own[p, there, :] = lines.astype(bf16)
+                own[p, there, :] = lines
             else:
-                other[(p - half) // 8][(p - half) % 8, there, :] = lines.astype(bf16)
-    grad_normed = dot_nt(joined[...], weight[...])
+                other[(p - half) // 8][(p - half) % 8, there, :] = lines
+        grad_normed = grad_normed + dot_nt(joined[:, columns], weight[:, columns])
     grad_in, gain_terms = ln_back(grad_normed, hat, spread[:, :1], gain)
     grad_tokens[...] = grad_resid[...] + grad_in
     singles = [column_sum(gain_terms), column_sum(grad_normed)]
     singles += [sums[pl.ds(k, 1), :] for k in range(2, 6)]
     table[...] = pack_vectors(singles, sum_in[...], 2 * half, table.shape[1])
-    row = lax.broadcasted_iota(jnp.int32, (block, 2 * LINE), 0)
-    there = pl.ds(3 * block, block)
+    row = lax.broadcasted_iota(jnp.int32, (LINE_ROWS, 2 * LINE), 0)
+    there = pl.ds(3 * block, LINE_ROWS)
     for p in range(2 * half):
         i = inverse[p]
         line = table[pl.ds(i, 1), :]
         lines = jnp.where(row == 0, line, 0.0)
-        lines = jnp.concatenate([lines, jnp.zeros((block, width - 2 * LINE), f32)], axis=1)
+        lines = jnp.concatenate([lines, jnp.zeros((LINE_ROWS, width - 2 * LINE), f32)], axis=1)
         if p < half:
             own[p, there, :] = lines.astype(bf16)
         else:
@@ -1047,16 +1082,16 @@
         functools.partial(finish_kernel, plan, total),
         out_shape=(
             jax.ShapeDtypeStruct((rows, width), f32),
-            jax.ShapeDtypeStruct((half, 4 * block, width), bf16),
-            jax.ShapeDtypeStruct((half // 2, 4 * block, width), bf16),
-            jax.ShapeDtypeStruct((half // 2, 4 * block, width), bf16),
+            jax.ShapeDtypeStruct((half, 3 * block + LINE_ROWS, width), bf16),
+            jax.ShapeDtypeStruct((half // 2, 3 * block + LINE_ROWS, width), bf16),
+            jax.ShapeDtypeStruct((half // 2, 3 * block + LINE_ROWS, width), bf16),
         ),
         in_specs=[SCALARS, SCALARS] + spec(3 + len(rest)),
         out_specs=tuple(spec(4)),
         scratch_shapes=[
             pltpu.VMEM((3 * width // 128, plan.query_rows, 128), f32),
             pltpu.VMEM((rows, 3 * width), bf16),
-            pltpu.VMEM((width, width), f32),
+            pltpu.VMEM((3, width, width), bf16),
             pltpu.VMEM((BLOCKS, 2 * LINE), f32),
         ],
         compiler_params=params(28),
@@ -1132,18 +1167,20 @@
         size = vector.shape[0]
         lane = k * block
         staged[pl.ds(0, 1), pl.ds(lane, size)] = vector[...].astype(f32).reshape(1, size)
+    payload[0, pl.ds(0, block), :] = w_out[...]
+    for c in range(chunks):
+        payload[0, pl.ds(block * (c + 1), block), :] = w_in[:, pl.ds(c * width, width)]
+    at = block * (chunks + 1)
+    payload[0, pl.ds(at, block * chunks), :] = w_back[...]
+    at = at + block * chunks
     for c in range(3):
-        payload[0, pl.ds(block * c, block), :] = w_qkv[:, pl.ds(c * width, width)]
-    payload[0, pl.ds(block * 3, block), :] = staged[...].astype(bf16)
-    payload[0, pl.ds(block * 4, block), :] = w_out[...]
-    for c in range(chunks):
-        payload[0, pl.ds(block * (c + 5), block), :] = w_in[:, pl.ds(c * width, width)]
-    payload[0, pl.ds(block * (chunks + 5), block * chunks), :] = w_back[...]
+        payload[0, pl.ds(at + block * c, block), :] = w_qkv[:, pl.ds(c * width, width)]
+    payload[0, pl.ds(at + block * 3, LINE_ROWS), :] = staged[...].astype(bf16)
 
 
 def pack(rings, lengths, w_qkv, w_out, w_in, w_back, vectors):
     block, width = w_out.shape
-    rows = 5 * block + w_in.shape[1] // width * block + w_back.shape[0]
+    rows = 4 * block + w_in.shape[1] // width * block + w_back.shape[0] + LINE_ROWS
     return pl.pallas_call(
         functools.partial(pack_kernel, rings),
         out_shape=(
@@ -1154,7 +1191,7 @@
         ),
         in_specs=[SCALARS] + spec(4 + len(vectors)),
         out_specs=(SCALARS,) * 3 + tuple(spec(1)),
-        scratch_shapes=[pltpu.VMEM((block, width), f32)],
+        scratch_shapes=[pltpu.VMEM((LINE_ROWS, width), f32)],
         compiler_params=params(62),
         name="pack",
         cost_estimate=cost(1.5),
@@ -1162,12 +1199,12 @@
 
 
 def unpack_kernel(kept_one, came_one, kept_two, came_two, *outs):
-    block, width = kept_one.shape[1] // 4, kept_two.shape[2]
+    block, width = (kept_one.shape[1] - LINE_ROWS) // 3, kept_two.shape[2]
     w_qkv, w_out, w_in, w_back = outs[:4]
     for c in range(3):
         rows = pl.ds(block * c, block)
         w_qkv[:, pl.ds(c * width, width)] = kept_one[0, rows, :] + came_one[0, rows, :].astype(f32)
-    rows = pl.ds(block * 3, block)
+    rows = pl.ds(block * 3, LINE_ROWS)
     lines = kept_one[0, rows, :] + came_one[0, rows, :].astype(f32)
     for k, out in enumerate(outs[4:]):
         size = out.shape[0]
@@ -1245,10 +1282,11 @@
         from_other, from_twin = exchange(*edge_sums(plan, total, info, order(tokens, payload)))
         ready = prepare(plan, total, info, order(tokens, payload))
         (payload,) = join([payload], ring.step(0, [payload]))
-        a, b = payload[:, : 4 * block], payload[:, 4 * block :]
+        payload = order(payload, from_other, from_twin)
+        rest = block * (2 * chunks + 1)
+        a, b = payload[:, rest:], payload[:, :rest]
         a_came, b_came = ring.step(1, [a, b])
         (a,) = join([a], [a_came])
-        a = order(a, from_other, from_twin)
         (a_came,) = ring.step(2, [a])
         (a,) = join([a], [a_came])
         (b,) = join([b], [b_came])
@@ -1274,7 +1312,7 @@
             return [item[k * each : (k + 1) * each] for k in range(parts)]
 
         line = jnp.concatenate([whole(item).reshape(BLOCKS, 1, -1) for item in small], axis=2)
-        line = jnp.pad(line, ((0, 0), (0, block - 1), (0, width - line.shape[2])))
+        line = jnp.pad(line, ((0, 0), (0, LINE_ROWS - 1), (0, width - line.shape[2])))
         one = whole(w_qkv).reshape(BLOCKS, block, 3, width).transpose(0, 2, 1, 3)
         one = one.reshape(BLOCKS, 3 * block, width)
         one = split(jnp.concatenate([one, line], axis=1), PIECES)

time: 131 us -> 130 us (level)
  starting transfers between devices: 33.7 us -> 38.7 us
  waiting for transfers between devices: 46.1 us -> 41.4 us
  Pallas kernels: 45.1 us -> 43.5 us
    ppermute x26, waiting for transfers between devices: 46.1 us -> 41.3 us  [step(): return [lax.ppermute(item, 'seq', route) for item in arrays]]
    ppermute x26, starting transfers between devices: 29.1 us -> 33.9 us  [step(): return [lax.ppermute(item, 'seq', route) for item in arrays]]
    unnamed x16 -> x15, local copies, waits for them, and re-layouts: 2.86 us -> 1.92 us
  transfers between devices with their start and end apart: 30 -> 30, of which waited for: 19 -> 20; matrix products, arithmetic and copies ran while one was open for 2% -> 2% of each run, Pallas kernels for 26% -> 25%
where the time goes in v6:
time: 130 us
  Pallas kernels  43.5 us (33%)
  waiting for transfers between devices  41.4 us (32%)
  starting transfers between devices  38.7 us (30%)
  other arithmetic  2.99 us (2%)
  local copies, waits for them, and re-layouts  2.06 us (2%)
    ppermute x26, waiting for transfers between devices, step(): return [lax.ppermute(item, 'seq', route) for item in arrays]  41.3 us
    ppermute x26, starting transfers between devices, step(): return [lax.ppermute(item, 'seq', route) for item in arrays]  33.9 us
    pallas_call x1, Pallas kernels, feed_forward(): pl.pallas_call(functools.partial(forward_kernel, parts), out_shape=(jax.S...  8.88 us
    pallas_call x1, Pallas kernels, attend_back(): pl.pallas_call(functools.partial(attend_back_kernel, plan, total), out_sh...  7.67 us
    pallas_call x1, Pallas kernels, finish(): pl.pallas_call(functools.partial(finish_kernel, plan, total), out_shape=(...  5.15 us
    pallas_call x1, Pallas kernels, attend(): pl.pallas_call(functools.partial(attend_kernel, plan, total), out_shape=[...  4.78 us
    pallas_call x1, Pallas kernels, prepare(): pl.pallas_call(functools.partial(prepare_kernel, plan, total), out_shape=...  4.12 us
    pallas_call x1, Pallas kernels, project(): pl.pallas_call(functools.partial(project_kernel, plan, total), out_shape=...  3.42 us
  transfers between devices with their start and end apart: 30, of which 20 were waited for; matrix products, arithmetic and copies ran while one was open for 2% of the time, Pallas kernels for 25%

profile of v6, /device:TPU:0, one launch (start us, length us, event | category | flops | bytes accessed | tf_op | source)
XLA Modules:
  0.0 129.6 jit_solution(8388244010352767945)
XLA Ops:
  0.6 1.8 %pack.1 = (s32[10]{0:T(128)}, s32[32]{0:T(128)}, s32[32]{0:T(128)}, bf16[1,200,512]{2,1,0:T(8,128)(2,1)}) custom-call(s32[3]{0:T(128)} %lengths.1, bf16[16,1536]{1,0:T(8,128)(2,1)} %w_qkv.1, bf16[16,512]{1,0:T(8,128)(2,1)} %w_out.1, bf16[16,2048]{1,0:T(8,128)(2,1)} %w_in.1, bf16[64,512]{1,0:T(8,128)(2,1)} %w_back.1, bf16[16]{0:T(256)(128)(2,1)} %refs_0_.1, ...), custom_call_target="tpu_custom_call" | custom-call | flops 1 | bytes 1 | tf_op jit(solution)/shard_map/pack/pallas_call | solution.py:1184
  2.4 4.1 %collective-permute-start = (bf16[1,200,512]{2,1,0:T(8,128)(2,1)}, bf16[1,200,512]{2,1,0:T(8,128)(2,1)S(1)}, u32[]{:S(2)}, u32[]{:S(2)}) collective-permute-start(bf16[1,200,512]{2,1,0:T(8,128)(2,1)} %get-tuple-element.105), channel_id=1, source_target_pairs={{0,16},{1,5},{2,18},{3,7},{4,20},{5,1},{6,22},{7,3},{8,24},{9,13},... | collective-permute-start | bytes 614408 | tf_op jit(solution)/shard_map/ppermute | solution.py:1131
  8.2 1.4 %edge_sums.1 = (bf16[176,512]{1,0:T(8,128)(2,1)S(1)}, bf16[176,512]{1,0:T(8,128)(2,1)S(1)}) custom-call(s32[10]{0:T(128)S(1)} %copy-done.3, bf16[512,512]{1,0:T(8,128)(2,1)S(1)} %copy-done), custom_call_target="tpu_custom_call" | custom-call | flops 1 | bytes 1 | tf_op jit(solution)/shard_map/edge_sums/pallas_call | solution.py:247
  10.4 2.9 %collective-permute-start.2 = (bf16[176,512]{1,0:T(8,128)(2,1)S(1)}, bf16[176,512]{1,0:T(8,128)(2,1)S(1)}, u32[]{:S(2)}, u32[]{:S(2)}) collective-permute-start(bf16[176,512]{1,0:T(8,128)(2,1)S(1)} %get-tuple-element.109), channel_id=1, source_target_pairs={{0,1},{1,0},{2,3},{3,2},{4,5},{5,4},{6,7},{7,6},{8,9},{9,8},{10,11... | collective-permute-start | bytes 540680 | tf_op jit(solution)/shard_map/ppermute | solution.py:1242
  14.3 5.6 %collective-permute-start.3 = (bf16[2,144,512]{2,1,0:T(8,128)(2,1)S(1)}, bf16[2,144,512]{2,1,0:T(8,128)(2,1)S(1)}, u32[]{:S(2)}, u32[]{:S(2)}) collective-permute-start(bf16[2,144,512]{2,1,0:T(8,128)(2,1)S(1)} %slice.90), channel_id=1, source_target_pairs={{0,2},{1,17},{2,0},{3,19},{4,6},{5,21},{6,4},{7,23},{8,10},{9,25},... | collective-permute-start | bytes 884744 | tf_op jit(solution)/shard_map/ppermute | solution.py:1131
  20.1 5.8 %collective-permute-done.5 = bf16[2,56,512]{2,1,0:T(8,128)(2,1)S(1)} collective-permute-done((bf16[2,56,512]{2,1,0:T(8,128)(2,1)S(1)}, bf16[2,56,512]{2,1,0:T(8,128)(2,1)S(1)}, u32[]{:S(2)}, u32[]{:S(2)}) %collective-permute-start.5) | collective-permute-done | bytes 114720 | tf_op jit(solution)/shard_map/ppermute | solution.py:1131
  25.9 2.1 %collective-permute-start.6 = (bf16[4,56,512]{2,1,0:T(8,128)(2,1)S(1)}, bf16[4,56,512]{2,1,0:T(8,128)(2,1)S(1)}, u32[]{:S(2)}, u32[]{:S(2)}) collective-permute-start(bf16[4,56,512]{2,1,0:T(8,128)(2,1)S(1)} %pad_maximum_fusion.4), channel_id=1, source_target_pairs={{0,8},{1,3},{2,10},{3,1},{4,12},{5,7},{6,14},{7,5},{8,0},{9,11},{1... | collective-permute-start | bytes 688136 | tf_op jit(solution)/shard_map/ppermute | solution.py:1131
  28.3 4.1 %prepare.1 = (f32[512,512]{1,0:T(8,128)S(1)}, f32[512,128]{1,0:T(8,128)S(1)}, bf16[512,512]{1,0:T(8,128)(2,1)S(1)}, f32[1024,128]{1,0:T(8,128)S(1)}, f32[2048,12...) custom-call(s32[10]{0:T(128)S(1)} %copy-done.4, ...), custom_call_target="tpu_custom_call" | custom-call | flops 1 | bytes 1 | tf_op jit(solution)/shard_map/prepare/pallas_call | solution.py:334
  32.5 2.0 %collective-permute-start.7 = (bf16[8,56,512]{2,1,0:T(8,128)(2,1)S(1)}, bf16[8,56,512]{2,1,0:T(8,128)(2,1)S(1)}, u32[]{:S(2)}, u32[]{:S(2)}) collective-permute-start(bf16[8,56,512]{2,1,0:T(8,128)(2,1)S(1)} %pad_maximum_fusion.2.refs_0_), channel_id=1, source_target_pairs={{0,4},{1,9},{2,6},{3,11},{4,0},{5,13},{6,2},{7,15},{8,12},{9,1},{1... | collective-permute-start | bytes 1376264 | tf_op jit(solution)/shard_map/ppermute | solution.py:1131
  34.5 5.2 %collective-permute-done.4 = bf16[4,144,512]{2,1,0:T(8,128)(2,1)S(1)} collective-permute-done((bf16[4,144,512]{2,1,0:T(8,128)(2,1)S(1)}, bf16[4,144,512]{2,1,0:T(8,128)(2,1)S(1)}, u32[]{:S(2)}, u32[]{:S(2)}) %collective-permute-start.4) | collective-permute-done | bytes 589856 | tf_op jit(solution)/shard_map/ppermute | solution.py:1131
  41.0 2.0 %collective-permute-start.10 = (bf16[8,144,512]{2,1,0:T(8,128)(2,1)S(1)}, bf16[8,144,512]{2,1,0:T(8,128)(2,1)S(1)}, u32[]{:S(2)}, u32[]{:S(2)}) collective-permute-start(bf16[8,144,512]{2,1,0:T(8,128)(2,1)S(1)} %pad_maximum_fusion.refs_0_), channel_id=1, source_target_pairs={{0,4},{1,9},{2,6},{3,11},{4,0},{5,13},{6,2},{7,15},{8,12},{9,1},{1... | collective-permute-start | bytes 3538952 | tf_op jit(solution)/shard_map/ppermute | solution.py:1131
  43.0 1.9 %collective-permute-start.8 = (bf16[8,56,512]{2,1,0:T(8,128)(2,1)S(1)}, bf16[8,56,512]{2,1,0:T(8,128)(2,1)S(1)}, u32[]{:S(2)}, u32[]{:S(2)}) collective-permute-start(bf16[8,56,512]{2,1,0:T(8,128)(2,1)S(1)} %pad_maximum_fusion.2.refs_0_), channel_id=1, source_target_pairs={{0,1},{1,0},{2,3},{3,2},{4,5},{5,4},{6,7},{7,6},{8,9},{9,8},{10,11... | collective-permute-start | bytes 1376264 | tf_op jit(solution)/shard_map/ppermute | solution.py:1131
  47.0 3.4 %project.1 = (bf16[1024,256]{1,0:T(8,128)(2,1)S(1)}, bf16[1024,256]{1,0:T(8,128)(2,1)S(1)}, bf16[1024,512]{1,0:T(8,128)(2,1)S(1)}, bf16[1024,512]{1,0:T(8,128)(2...) custom-call(s32[10]{0:T(128)S(1)} %copy-done.4, ...), custom_call_target="tpu_custom_call" | custom-call | flops 1 | bytes 1 | tf_op jit(solution)/shard_map/project/pallas_call | solution.py:450
  50.4 4.8 %attend.1 = (bf16[512,256]{1,0:T(8,128)(2,1)S(1)}, bf16[512,256]{1,0:T(8,128)(2,1)S(1)}, f32[512,256]{1,0:T(8,128)S(1)}, f32[512,256]{1,0:T(8,128)S(1)}, f32[512,256]{1,0:T(8,128)S(1)}, /*index=5*/f32[512,256]{1,0:T(8,128)S(1)}) custom-call(s32[10]{0:T(128)S(1)} %copy-done.4, f32[1024,128]{1,0:T(8,128)S(1)} %get-tuple-element.120.mask, ...), custom_call_target="tpu_custom_call" | custom-call | flops 1 | bytes 1 | tf_op jit(solution)/shard_map/attend/pallas_call | solution.py:551
  55.2 2.0 %collective-permute-done.10.refs_1_ = bf16[8,144,512]{2,1,0:T(8,128)(2,1)S(1)} collective-permute-done((bf16[8,144,512]{2,1,0:T(8,128)(2,1)S(1)}, bf16[8,144,512]{2,1,0:T(8,128)(2,1)S(1)}, u32[]{:S(2)}, u32[]{:S(2)}) %collective-permute-start.10) | collective-permute-done | bytes 1179680 | tf_op jit(solution)/shard_map/ppermute | solution.py:1131
  58.5 2.5 %collective-permute-done.12.refs_3_ = bf16[8,144,512]{2,1,0:T(8,128)(2,1)S(1)} collective-permute-done((bf16[8,144,512]{2,1,0:T(8,128)(2,1)S(1)}, bf16[8,144,512]{2,1,0:T(8,128)(2,1)S(1)}, u32[]{:S(2)}, u32[]{:S(2)}) %collective-permute-start.12) | collective-permute-done | bytes 1179680 | tf_op jit(solution)/shard_map/ppermute | solution.py:1131
  61.0 8.9 %feed_forward.1 = (bf16[512,512]{1,0:T(8,128)(2,1)}, f32[512,512]{1,0:T(8,128)S(1)}, f32[512,512]{1,0:T(8,128)S(1)}, bf16[512,512]{1,0:T(8,128)(2,1)S(1)}, bf16[...) custom-call(s32[32]{0:T(128)S(1)} %copy-done.6, ...), custom_call_target="tpu_custom_call" | custom-call | flops 1 | bytes 1 | tf_op jit(solution)/shard_map/feed_forward/pallas_call | solution.py:658
  70.4 3.2 %middle.1 = (f32[512,512]{1,0:T(8,128)S(1)}, bf16[1024,512]{1,0:T(8,128)(2,1)S(1)}, bf16[1024,512]{1,0:T(8,128)(2,1)S(1)}, bf16[160,640]{1,0:T(8,128)(2,1)S(1)},...) custom-call(s32[10]{0:T(128)S(1)} %copy-done.4, ...), custom_call_target="tpu_custom_call" | custom-call | flops 1 | bytes 1 | tf_op jit(solution)/shard_map/middle/pallas_call | solution.py:785
  76.1 1.7 %collective-permute-start.19 = (bf16[4,144,512]{2,1,0:T(8,128)(2,1)S(1)}, bf16[4,144,512]{2,1,0:T(8,128)(2,1)S(1)}, u32[]{:S(2)}, u32[]{:S(2)}) collective-permute-start(bf16[4,144,512]{2,1,0:T(8,128)(2,1)S(1)} %get-tuple-element.150), channel_id=1, source_target_pairs={{0,2},{1,5},{2,0},{3,7},{4,6},{5,1},{6,4},{7,3},{8,10},{9,13},{10,... | collective-permute-start | bytes 1769480 | tf_op jit(solution)/shard_map/ppermute | solution.py:1131
  78.8 2.9 %collective-permute-start.22 = (bf16[4,144,512]{2,1,0:T(8,128)(2,1)S(1)}, bf16[4,144,512]{2,1,0:T(8,128)(2,1)S(1)}, u32[]{:S(2)}, u32[]{:S(2)}) collective-permute-start(bf16[4,144,512]{2,1,0:T(8,128)(2,1)S(1)} %get-tuple-element.151), channel_id=1, source_target_pairs={{0,2},{1,5},{2,0},{3,7},{4,6},{5,1},{6,4},{7,3},{8,10},{9,13},{10,... | collective-permute-start | bytes 1769480 | tf_op jit(solution)/shard_map/ppermute | solution.py:1131
  81.6 7.7 %attend_back.1 = (f32[1024,256]{1,0:T(8,128)S(1)}, f32[1024,256]{1,0:T(8,128)S(1)}, f32[1344,512]{1,0:T(8,128)S(1)}, f32[1344,512]{1,0:T(8,128)S(1)}) custom-call(f32[2048,128]{1,0:T(8,128)S(1)} %get-tuple-element.114.mask, bf16[2048,128]{1,0:T(8,128)(2,1)S(1)} %get-tuple-element.115.counts_of, bf16[1024,256]{1,0:T(8,128)(2,1)S(1)} %get-tuple-element.121.refs_0_, ...), custom_call_target="tpu_custom_call" | custom-call | flops 1 | bytes 1 | tf_op jit(solution)/shard_map/attend_back/pallas_call | solution.py:879
  90.6 2.4 %edge_back.1 = (f32[320,512]{1,0:T(8,128)S(1)}, f32[320,512]{1,0:T(8,128)S(1)}) custom-call(s32[10]{0:T(128)S(1)} %copy-done.4, f32[320,128]{1,0:T(8,128)S(1)} %get-tuple-element.116.mask, bf16[320,128]{1,0:T(8,128)(2,1)S(1)} %get-tuple-element.117.counts_of, bf16[320,256]{1,0:T(8,128)(2,1)S(1)} %get-tuple-element.158.queries_a, ...), custom_call_target="tpu_custom_call" | custom-call | flops 1 | bytes 1 | tf_op jit(solution)/shard_map/edge_back/pallas_call | solution.py:971
  93.0 5.1 %finish.1 = (f32[512,512]{1,0:T(8,128)}, bf16[16,56,512]{2,1,0:T(8,128)(2,1)S(1)}, bf16[8,56,512]{2,1,0:T(8,128)(2,1)S(1)}, bf16[8,56,512]{2,1,0:T(8,128)(2,1)S(1)}) custom-call(s32[10]{0:T(128)S(1)} %copy-done.4, s32[32]{0:T(128)S(1)} %copy-done.5, f32[512,512]{1,0:T(8,128)S(1)} %get-tuple-element.111.standard, f32[512,128]{1,0:T(8,128)S(1)} %get-tuple-element.112.spread, ...), custom_call_target="tpu_custom_call" | custom-call | flops 1 | bytes 1 | tf_op jit(solution)/shard_map/finish/pallas_call | solution.py:1081
  98.1 1.4 %collective-permute-start.20 = (bf16[8,56,512]{2,1,0:T(8,128)(2,1)S(1)}, bf16[8,56,512]{2,1,0:T(8,128)(2,1)S(1)}, u32[]{:S(2)}, u32[]{:S(2)}) collective-permute-start(bf16[8,56,512]{2,1,0:T(8,128)(2,1)S(1)} %get-tuple-element.172), channel_id=1, source_target_pairs={{0,1},{1,0},{2,3},{3,2},{4,5},{5,4},{6,7},{7,6},{8,9},{9,8},{10,11... | collective-permute-start | bytes 1376264 | tf_op jit(solution)/shard_map/ppermute | solution.py:1131
  101.9 1.7 %collective-permute-start.24 = (bf16[8,56,512]{2,1,0:T(8,128)(2,1)S(1)}, bf16[8,56,512]{2,1,0:T(8,128)(2,1)S(1)}, u32[]{:S(2)}, u32[]{:S(2)}) collective-permute-start(bf16[8,56,512]{2,1,0:T(8,128)(2,1)S(1)} %get-tuple-element.199), channel_id=1, source_target_pairs={{0,2},{1,5},{2,0},{3,7},{4,6},{5,1},{6,4},{7,3},{8,10},{9,13},{10,... | collective-permute-start | bytes 1376264 | tf_op jit(solution)/shard_map/ppermute | solution.py:1131
  104.1 6.3 %collective-permute-done.24 = bf16[8,56,512]{2,1,0:T(8,128)(2,1)S(1)} collective-permute-done((bf16[8,56,512]{2,1,0:T(8,128)(2,1)S(1)}, bf16[8,56,512]{2,1,0:T(8,128)(2,1)S(1)}, u32[]{:S(2)}, u32[]{:S(2)}) %collective-permute-start.24) | collective-permute-done | bytes 458784 | tf_op jit(solution)/shard_map/ppermute | solution.py:1131
  110.6 1.6 %collective-permute-start.25 = (bf16[4,56,512]{2,1,0:T(8,128)(2,1)S(1)}, bf16[4,56,512]{2,1,0:T(8,128)(2,1)S(1)}, u32[]{:S(2)}, u32[]{:S(2)}) collective-permute-start(bf16[4,56,512]{2,1,0:T(8,128)(2,1)S(1)} %get-tuple-element.195), channel_id=1, source_target_pairs={{0,4},{1,9},{2,6},{3,11},{4,0},{5,13},{6,2},{7,15},{8,12},{9,1},{1... | collective-permute-start | bytes 688136 | tf_op jit(solution)/shard_map/ppermute | solution.py:1131
  112.2 1.5 %collective-permute-done.26 = bf16[2,144,512]{2,1,0:T(8,128)(2,1)S(1)} collective-permute-done((bf16[2,144,512]{2,1,0:T(8,128)(2,1)S(1)}, bf16[2,144,512]{2,1,0:T(8,128)(2,1)S(1)}, u32[]{:S(2)}, u32[]{:S(2)}) %collective-permute-start.26) | collective-permute-done | bytes 294944 | tf_op jit(solution)/shard_map/ppermute | solution.py:1131
  113.8 2.9 %collective-permute-done.25 = bf16[4,56,512]{2,1,0:T(8,128)(2,1)S(1)} collective-permute-done((bf16[4,56,512]{2,1,0:T(8,128)(2,1)S(1)}, bf16[4,56,512]{2,1,0:T(8,128)(2,1)S(1)}, u32[]{:S(2)}, u32[]{:S(2)}) %collective-permute-start.25) | collective-permute-done | bytes 229408 | tf_op jit(solution)/shard_map/ppermute | solution.py:1131
  117.4 1.7 %collective-permute-start.29 = (bf16[1,144,512]{2,1,0:T(8,128)(2,1)S(1)}, bf16[1,144,512]{2,1,0:T(8,128)(2,1)S(1)}, u32[]{:S(2)}, u32[]{:S(2)}) collective-permute-start(bf16[1,144,512]{2,1,0:T(8,128)(2,1)S(1)} %get-tuple-element.202), channel_id=1, source_target_pairs={{0,16},{1,3},{2,18},{3,1},{4,20},{5,7},{6,22},{7,5},{8,24},{9,11},... | collective-permute-start | bytes 442376 | tf_op jit(solution)/shard_map/ppermute | solution.py:1131
  119.1 4.6 %collective-permute-done.27 = bf16[2,56,512]{2,1,0:T(8,128)(2,1)S(1)} collective-permute-done((bf16[2,56,512]{2,1,0:T(8,128)(2,1)S(1)}, bf16[2,56,512]{2,1,0:T(8,128)(2,1)S(1)}, u32[]{:S(2)}, u32[]{:S(2)}) %collective-permute-start.27) | collective-permute-done | bytes 114720 | tf_op jit(solution)/shard_map/ppermute | solution.py:1131
  125.1 3.8 %collective-permute-done.28.came_one = bf16[1,56,512]{2,1,0:T(8,128)(2,1)S(1)} collective-permute-done((bf16[1,56,512]{2,1,0:T(8,128)(2,1)S(1)}, bf16[1,56,512]{2,1,0:T(8,128)(2,1)S(1)}, u32[]{:S(2)}, u32[]{:S(2)}) %collective-permute-start.28) | collective-permute-done | bytes 57376 | tf_op jit(solution)/shard_map/ppermute | solution.py:1131
  (72 shorter events, 19.6 us)
Async XLA Ops:
  2.4 10.9 %collective-permute-start = (bf16[1,200,512]{2,1,0:T(8,128)(2,1)}, bf16[1,200,512]{2,1,0:T(8,128)(2,1)S(1)}, u32[]{:S(2)}, u32[]{:S(2)}) collective-permute-start(bf16[1,200,512]{2,1,0:T(8,128)(2,1)} %get-tuple-element.105), channel_id=1, source_target_pairs={{0,16},{1,5},{2,18},{3,7},{4,20},{5,1},{6,22},{7,3},{8,24},{9,13},... | collective-permute-start | bytes 614408 | tf_op jit(solution)/shard_map/ppermute | solution.py:1131
  9.7 4.6 %collective-permute-start.1 = (bf16[176,512]{1,0:T(8,128)(2,1)S(1)}, bf16[176,512]{1,0:T(8,128)(2,1)S(1)}, u32[]{:S(2)}, u32[]{:S(2)}) collective-permute-start(bf16[176,512]{1,0:T(8,128)(2,1)S(1)} %get-tuple-element.108), channel_id=1, source_target_pairs={{1,2},{3,4},{5,6},{7,8},{9,10},{11,12},{13,14},{15,16},{17,18},{19... | collective-permute-start | bytes 540680 | tf_op jit(solution)/shard_map/ppermute | solution.py:1242
  10.3 17.9 %copy-start.1 = (bf16[512,512]{1,0:T(8,128)(2,1)S(1)}, bf16[512,512]{1,0:T(8,128)(2,1)}, u32[]{:S(2)}) copy-start(bf16[512,512]{1,0:T(8,128)(2,1)} %tokens.3) | copy-start | bytes 1572868
  10.3 17.9 %copy-start.4 = (s32[10]{0:T(128)S(1)}, s32[10]{0:T(128)}, u32[]{:S(2)}) copy-start(s32[10]{0:T(128)} %get-tuple-element.104.info) | copy-start | bytes 124
  10.4 4.0 %collective-permute-start.2 = (bf16[176,512]{1,0:T(8,128)(2,1)S(1)}, bf16[176,512]{1,0:T(8,128)(2,1)S(1)}, u32[]{:S(2)}, u32[]{:S(2)}) collective-permute-start(bf16[176,512]{1,0:T(8,128)(2,1)S(1)} %get-tuple-element.109), channel_id=1, source_target_pairs={{0,1},{1,0},{2,3},{3,2},{4,5},{5,4},{6,7},{7,6},{8,9},{9,8},{10,11... | collective-permute-start | bytes 540680 | tf_op jit(solution)/shard_map/ppermute | solution.py:1242
  14.3 13.8 %collective-permute-start.3 = (bf16[2,144,512]{2,1,0:T(8,128)(2,1)S(1)}, bf16[2,144,512]{2,1,0:T(8,128)(2,1)S(1)}, u32[]{:S(2)}, u32[]{:S(2)}) collective-permute-start(bf16[2,144,512]{2,1,0:T(8,128)(2,1)S(1)} %slice.90), channel_id=1, source_target_pairs={{0,2},{1,17},{2,0},{3,19},{4,6},{5,21},{6,4},{7,23},{8,10},{9,25},... | collective-permute-start | bytes 884744 | tf_op jit(solution)/shard_map/ppermute | solution.py:1131
  20.0 5.9 %collective-permute-start.5 = (bf16[2,56,512]{2,1,0:T(8,128)(2,1)S(1)}, bf16[2,56,512]{2,1,0:T(8,128)(2,1)S(1)}, u32[]{:S(2)}, u32[]{:S(2)}) collective-permute-start(bf16[2,56,512]{2,1,0:T(8,128)(2,1)S(1)} %slice.91), channel_id=1, source_target_pairs={{0,2},{1,17},{2,0},{3,19},{4,6},{5,21},{6,4},{7,23},{8,10},{9,25},... | collective-permute-start | bytes 344072 | tf_op jit(solution)/shard_map/ppermute | solution.py:1131
  25.9 6.4 %collective-permute-start.6 = (bf16[4,56,512]{2,1,0:T(8,128)(2,1)S(1)}, bf16[4,56,512]{2,1,0:T(8,128)(2,1)S(1)}, u32[]{:S(2)}, u32[]{:S(2)}) collective-permute-start(bf16[4,56,512]{2,1,0:T(8,128)(2,1)S(1)} %pad_maximum_fusion.4), channel_id=1, source_target_pairs={{0,8},{1,3},{2,10},{3,1},{4,12},{5,7},{6,14},{7,5},{8,0},{9,11},{1... | collective-permute-start | bytes 688136 | tf_op jit(solution)/shard_map/ppermute | solution.py:1131
  28.2 11.5 %collective-permute-start.4 = (bf16[4,144,512]{2,1,0:T(8,128)(2,1)S(1)}, bf16[4,144,512]{2,1,0:T(8,128)(2,1)S(1)}, u32[]{:S(2)}, u32[]{:S(2)}) collective-permute-start(bf16[4,144,512]{2,1,0:T(8,128)(2,1)S(1)} %pad_maximum_fusion.1), channel_id=1, source_target_pairs={{0,8},{1,3},{2,10},{3,1},{4,12},{5,7},{6,14},{7,5},{8,0},{9,11},{1... | collective-permute-start | bytes 1769480 | tf_op jit(solution)/shard_map/ppermute | solution.py:1131
  32.5 8.5 %collective-permute-start.7 = (bf16[8,56,512]{2,1,0:T(8,128)(2,1)S(1)}, bf16[8,56,512]{2,1,0:T(8,128)(2,1)S(1)}, u32[]{:S(2)}, u32[]{:S(2)}) collective-permute-start(bf16[8,56,512]{2,1,0:T(8,128)(2,1)S(1)} %pad_maximum_fusion.2.refs_0_), channel_id=1, source_target_pairs={{0,4},{1,9},{2,6},{3,11},{4,0},{5,13},{6,2},{7,15},{8,12},{9,1},{1... | collective-permute-start | bytes 1376264 | tf_op jit(solution)/shard_map/ppermute | solution.py:1131
  41.0 16.2 %collective-permute-start.10 = (bf16[8,144,512]{2,1,0:T(8,128)(2,1)S(1)}, bf16[8,144,512]{2,1,0:T(8,128)(2,1)S(1)}, u32[]{:S(2)}, u32[]{:S(2)}) collective-permute-start(bf16[8,144,512]{2,1,0:T(8,128)(2,1)S(1)} %pad_maximum_fusion.refs_0_), channel_id=1, source_target_pairs={{0,4},{1,9},{2,6},{3,11},{4,0},{5,13},{6,2},{7,15},{8,12},{9,1},{1... | collective-permute-start | bytes 3538952 | tf_op jit(solution)/shard_map/ppermute | solution.py:1131
  43.0 3.4 %collective-permute-start.8 = (bf16[8,56,512]{2,1,0:T(8,128)(2,1)S(1)}, bf16[8,56,512]{2,1,0:T(8,128)(2,1)S(1)}, u32[]{:S(2)}, u32[]{:S(2)}) collective-permute-start(bf16[8,56,512]{2,1,0:T(8,128)(2,1)S(1)} %pad_maximum_fusion.2.refs_0_), channel_id=1, source_target_pairs={{0,1},{1,0},{2,3},{3,2},{4,5},{5,4},{6,7},{7,6},{8,9},{9,8},{10,11... | collective-permute-start | bytes 1376264 | tf_op jit(solution)/shard_map/ppermute | solution.py:1131
  44.9 2.1 %collective-permute-start.9 = (bf16[8,56,512]{2,1,0:T(8,128)(2,1)S(1)}, bf16[8,56,512]{2,1,0:T(8,128)(2,1)S(1)}, u32[]{:S(2)}, u32[]{:S(2)}) collective-permute-start(bf16[8,56,512]{2,1,0:T(8,128)(2,1)S(1)} %collective-permute-done.7.refs_1_), channel_id=1, source_target_pairs={{0,1},{1,0},{2,3},{3,2},{4,5},{5,4},{6,7},{7,6},{8,9},{9,8},{10,11... | collective-permute-start | bytes 1376264 | tf_op jit(solution)/shard_map/ppermute | solution.py:1131
  44.9 13.6 %collective-permute-start.11 = (bf16[8,144,512]{2,1,0:T(8,128)(2,1)S(1)}, bf16[8,144,512]{2,1,0:T(8,128)(2,1)S(1)}, u32[]{:S(2)}, u32[]{:S(2)}) collective-permute-start(bf16[8,144,512]{2,1,0:T(8,128)(2,1)S(1)} %pad_maximum_fusion.refs_0_), channel_id=1, source_target_pairs={{0,1},{1,0},{2,3},{3,2},{4,5},{5,4},{6,7},{7,6},{8,9},{9,8},{10,11... | collective-permute-start | bytes 3538952 | tf_op jit(solution)/shard_map/ppermute | solution.py:1131
  57.2 3.8 %collective-permute-start.12 = (bf16[8,144,512]{2,1,0:T(8,128)(2,1)S(1)}, bf16[8,144,512]{2,1,0:T(8,128)(2,1)S(1)}, u32[]{:S(2)}, u32[]{:S(2)}) collective-permute-start(bf16[8,144,512]{2,1,0:T(8,128)(2,1)S(1)} %collective-permute-done.10.refs_1_), channel_id=1, source_target_pairs={{0,1},{1,0},{2,3},{3,2},{4,5},{5,4},{6,7},{7,6},{8,9},{9,8},{10,11... | collective-permute-start | bytes 3538952 | tf_op jit(solution)/shard_map/ppermute | solution.py:1131
  69.8 5.5 %collective-permute-start.13 = (bf16[8,128,512]{2,1,0:T(8,128)(2,1)S(1)}, bf16[8,128,512]{2,1,0:T(8,128)(2,1)S(1)}, u32[]{:S(2)}, u32[]{:S(2)}) collective-permute-start(bf16[8,128,512]{2,1,0:T(8,128)(2,1)S(1)} %get-tuple-element.147), channel_id=1, source_target_pairs={{0,1},{1,0},{2,3},{3,2},{4,5},{5,4},{6,7},{7,6},{8,9},{9,8},{10,11... | collective-permute-start | bytes 3145736 | tf_op jit(solution)/shard_map/ppermute | solution.py:1131
  70.2 5.1 %collective-permute-start.17 = (bf16[8,128,512]{2,1,0:T(8,128)(2,1)S(1)}, bf16[8,128,512]{2,1,0:T(8,128)(2,1)S(1)}, u32[]{:S(2)}, u32[]{:S(2)}) collective-permute-start(bf16[8,128,512]{2,1,0:T(8,128)(2,1)S(1)} %get-tuple-element.163), channel_id=1, source_target_pairs={{0,1},{1,0},{2,3},{3,2},{4,5},{5,4},{6,7},{7,6},{8,9},{9,8},{10,11... | collective-permute-start | bytes 3145736 | tf_op jit(solution)/shard_map/ppermute | solution.py:1131
  73.5 1.4 %collective-permute-start.14 = (bf16[8,16,512]{2,1,0:T(8,128)(2,1)S(1)}, bf16[8,16,512]{2,1,0:T(8,128)(2,1)S(1)}, u32[]{:S(2)}, u32[]{:S(2)}) collective-permute-start(bf16[8,16,512]{2,1,0:T(8,128)(2,1)S(1)} %get-tuple-element.148), channel_id=1, source_target_pairs={{0,1},{1,0},{2,3},{3,2},{4,5},{5,4},{6,7},{7,6},{8,9},{9,8},{10,11... | collective-permute-start | bytes 393224 | tf_op jit(solution)/shard_map/ppermute | solution.py:1131
  74.0 1.3 %collective-permute-start.18 = (bf16[8,16,512]{2,1,0:T(8,128)(2,1)S(1)}, bf16[8,16,512]{2,1,0:T(8,128)(2,1)S(1)}, u32[]{:S(2)}, u32[]{:S(2)}) collective-permute-start(bf16[8,16,512]{2,1,0:T(8,128)(2,1)S(1)} %get-tuple-element.164), channel_id=1, source_target_pairs={{0,1},{1,0},{2,3},{3,2},{4,5},{5,4},{6,7},{7,6},{8,9},{9,8},{10,11... | collective-permute-start | bytes 393224 | tf_op jit(solution)/shard_map/ppermute | solution.py:1131
  74.1 2.0 %collective-permute-start.15 = (bf16[160,640]{1,0:T(8,128)(2,1)S(1)}, bf16[160,640]{1,0:T(8,128)(2,1)S(1)}, u32[]{:S(2)}, u32[]{:S(2)}) collective-permute-start(bf16[160,640]{1,0:T(8,128)(2,1)S(1)} %get-tuple-element.149), channel_id=1, source_target_pairs={{0,1},{1,0},{2,3},{3,2},{4,5},{5,4},{6,7},{7,6},{8,9},{9,8},{10,11... | collective-permute-start | bytes 614408 | tf_op jit(solution)/shard_map/ppermute | solution.py:1242
  76.1 13.5 %collective-permute-start.19 = (bf16[4,144,512]{2,1,0:T(8,128)(2,1)S(1)}, bf16[4,144,512]{2,1,0:T(8,128)(2,1)S(1)}, u32[]{:S(2)}, u32[]{:S(2)}) collective-permute-start(bf16[4,144,512]{2,1,0:T(8,128)(2,1)S(1)} %get-tuple-element.150), channel_id=1, source_target_pairs={{0,2},{1,5},{2,0},{3,7},{4,6},{5,1},{6,4},{7,3},{8,10},{9,13},{10,... | collective-permute-start | bytes 1769480 | tf_op jit(solution)/shard_map/ppermute | solution.py:1131
  77.9 11.4 %collective-permute-start.16 = (bf16[160,640]{1,0:T(8,128)(2,1)S(1)}, bf16[160,640]{1,0:T(8,128)(2,1)S(1)}, u32[]{:S(2)}, u32[]{:S(2)}) collective-permute-start(bf16[160,640]{1,0:T(8,128)(2,1)S(1)} %get-tuple-element.160), channel_id=1, source_target_pairs={{1,2},{3,4},{5,6},{7,8},{9,10},{11,12},{13,14},{15,16},{17,18},{19... | collective-permute-start | bytes 614408 | tf_op jit(solution)/shard_map/ppermute | solution.py:1242
  78.8 20.8 %collective-permute-start.22 = (bf16[4,144,512]{2,1,0:T(8,128)(2,1)S(1)}, bf16[4,144,512]{2,1,0:T(8,128)(2,1)S(1)}, u32[]{:S(2)}, u32[]{:S(2)}) collective-permute-start(bf16[4,144,512]{2,1,0:T(8,128)(2,1)S(1)} %get-tuple-element.151), channel_id=1, source_target_pairs={{0,2},{1,5},{2,0},{3,7},{4,6},{5,1},{6,4},{7,3},{8,10},{9,13},{10,... | collective-permute-start | bytes 1769480 | tf_op jit(solution)/shard_map/ppermute | solution.py:1131
  89.9 9.9 %collective-permute-start.23 = (bf16[4,144,512]{2,1,0:T(8,128)(2,1)S(1)}, bf16[4,144,512]{2,1,0:T(8,128)(2,1)S(1)}, u32[]{:S(2)}, u32[]{:S(2)}) collective-permute-start(bf16[4,144,512]{2,1,0:T(8,128)(2,1)S(1)} %fusion), channel_id=1, source_target_pairs={{0,4},{1,9},{2,6},{3,11},{4,0},{5,13},{6,2},{7,15},{8,12},{9,1},{1... | collective-permute-start | bytes 1769480 | tf_op jit(solution)/shard_map/ppermute | solution.py:1131
  98.1 2.9 %collective-permute-start.20 = (bf16[8,56,512]{2,1,0:T(8,128)(2,1)S(1)}, bf16[8,56,512]{2,1,0:T(8,128)(2,1)S(1)}, u32[]{:S(2)}, u32[]{:S(2)}) collective-permute-start(bf16[8,56,512]{2,1,0:T(8,128)(2,1)S(1)} %get-tuple-element.172), channel_id=1, source_target_pairs={{0,1},{1,0},{2,3},{3,2},{4,5},{5,4},{6,7},{7,6},{8,9},{9,8},{10,11... | collective-permute-start | bytes 1376264 | tf_op jit(solution)/shard_map/ppermute | solution.py:1131
  99.5 2.1 %collective-permute-start.21 = (bf16[8,56,512]{2,1,0:T(8,128)(2,1)S(1)}, bf16[8,56,512]{2,1,0:T(8,128)(2,1)S(1)}, u32[]{:S(2)}, u32[]{:S(2)}) collective-permute-start(bf16[8,56,512]{2,1,0:T(8,128)(2,1)S(1)} %get-tuple-element.173), channel_id=1, source_target_pairs={{0,1},{1,0},{2,3},{3,2},{4,5},{5,4},{6,7},{7,6},{8,9},{9,8},{10,11... | collective-permute-start | bytes 1376264 | tf_op jit(solution)/shard_map/ppermute | solution.py:1131
  101.9 8.5 %collective-permute-start.24 = (bf16[8,56,512]{2,1,0:T(8,128)(2,1)S(1)}, bf16[8,56,512]{2,1,0:T(8,128)(2,1)S(1)}, u32[]{:S(2)}, u32[]{:S(2)}) collective-permute-start(bf16[8,56,512]{2,1,0:T(8,128)(2,1)S(1)} %get-tuple-element.199), channel_id=1, source_target_pairs={{0,2},{1,5},{2,0},{3,7},{4,6},{5,1},{6,4},{7,3},{8,10},{9,13},{10,... | collective-permute-start | bytes 1376264 | tf_op jit(solution)/shard_map/ppermute | solution.py:1131
  103.6 10.1 %collective-permute-start.26 = (bf16[2,144,512]{2,1,0:T(8,128)(2,1)S(1)}, bf16[2,144,512]{2,1,0:T(8,128)(2,1)S(1)}, u32[]{:S(2)}, u32[]{:S(2)}) collective-permute-start(bf16[2,144,512]{2,1,0:T(8,128)(2,1)S(1)} %get-tuple-element.194), channel_id=1, source_target_pairs={{0,8},{1,17},{2,10},{3,19},{4,12},{5,21},{6,14},{7,23},{8,0},{9,25... | collective-permute-start | bytes 884744 | tf_op jit(solution)/shard_map/ppermute | solution.py:1131
  110.6 6.1 %collective-permute-start.25 = (bf16[4,56,512]{2,1,0:T(8,128)(2,1)S(1)}, bf16[4,56,512]{2,1,0:T(8,128)(2,1)S(1)}, u32[]{:S(2)}, u32[]{:S(2)}) collective-permute-start(bf16[4,56,512]{2,1,0:T(8,128)(2,1)S(1)} %get-tuple-element.195), channel_id=1, source_target_pairs={{0,4},{1,9},{2,6},{3,11},{4,0},{5,13},{6,2},{7,15},{8,12},{9,1},{1... | collective-permute-start | bytes 688136 | tf_op jit(solution)/shard_map/ppermute | solution.py:1131
  116.7 6.9 %collective-permute-start.27 = (bf16[2,56,512]{2,1,0:T(8,128)(2,1)S(1)}, bf16[2,56,512]{2,1,0:T(8,128)(2,1)S(1)}, u32[]{:S(2)}, u32[]{:S(2)}) collective-permute-start(bf16[2,56,512]{2,1,0:T(8,128)(2,1)S(1)} %get-tuple-element.203), channel_id=1, source_target_pairs={{0,8},{1,17},{2,10},{3,19},{4,12},{5,21},{6,14},{7,23},{8,0},{9,25... | collective-permute-start | bytes 344072 | tf_op jit(solution)/shard_map/ppermute | solution.py:1131
  117.4 7.6 %collective-permute-start.29 = (bf16[1,144,512]{2,1,0:T(8,128)(2,1)S(1)}, bf16[1,144,512]{2,1,0:T(8,128)(2,1)S(1)}, u32[]{:S(2)}, u32[]{:S(2)}) collective-permute-start(bf16[1,144,512]{2,1,0:T(8,128)(2,1)S(1)} %get-tuple-element.202), channel_id=1, source_target_pairs={{0,16},{1,3},{2,18},{3,1},{4,20},{5,7},{6,22},{7,5},{8,24},{9,11},... | collective-permute-start | bytes 442376 | tf_op jit(solution)/shard_map/ppermute | solution.py:1131
  123.7 5.1 %collective-permute-start.28 = (bf16[1,56,512]{2,1,0:T(8,128)(2,1)S(1)}, bf16[1,56,512]{2,1,0:T(8,128)(2,1)S(1)}, u32[]{:S(2)}, u32[]{:S(2)}) collective-permute-start(bf16[1,56,512]{2,1,0:T(8,128)(2,1)S(1)} %get-tuple-element.205), channel_id=1, source_target_pairs={{0,16},{1,3},{2,18},{3,1},{4,20},{5,7},{6,22},{7,5},{8,24},{9,11},... | collective-permute-start | bytes 172040 | tf_op jit(solution)/shard_map/ppermute | solution.py:1131
  (5 other events, 37.4 us)

commit v7 on v6

--- a/solution.py
+++ b/solution.py
@@ -1146,8 +1146,9 @@
     return [jnp.concatenate(pair) for pair in zip(held, came)]
 
 
-def pack_kernel(rings, lengths, w_qkv, w_out, w_in, w_back, *refs):
-    vectors, (info, *inverses, payload, staged) = refs[:-5], refs[-5:]
+def pack_kernel(rings, plan, total, lengths, tokens, w_qkv, w_out, w_in, w_back, *refs):
+    vectors, refs = refs[:-8], refs[-8:]
+    info, *inverses, payload, to_twin, to_other, staged, ends = refs
     device = lax.axis_index("seq")
     info[0] = device
     start = jnp.int32(0)
@@ -1176,26 +1177,30 @@
     for c in range(3):
         payload[0, pl.ds(at + block * c, block), :] = w_qkv[:, pl.ds(c * width, width)]
     payload[0, pl.ds(at + block * 3, LINE_ROWS), :] = staged[...].astype(bf16)
-
-
-def pack(rings, lengths, w_qkv, w_out, w_in, w_back, vectors):
+    edge_sums_kernel(plan, total, info, tokens, to_twin, to_other, ends)
+
+
+def pack(rings, plan, total, lengths, tokens, w_qkv, w_out, w_in, w_back, vectors):
+    size = LEVELS * HALO
     block, width = w_out.shape
     rows = 4 * block + w_in.shape[1] // width * block + w_back.shape[0] + LINE_ROWS
     return pl.pallas_call(
-        functools.partial(pack_kernel, rings),
+        functools.partial(pack_kernel, rings, plan, total),
         out_shape=(
             jax.ShapeDtypeStruct((10,), jnp.int32),
             jax.ShapeDtypeStruct((BLOCKS,), jnp.int32),
             jax.ShapeDtypeStruct((BLOCKS,), jnp.int32),
             jax.ShapeDtypeStruct((1, rows, width), bf16),
+            jax.ShapeDtypeStruct((size + MIXED, width), bf16),
+            jax.ShapeDtypeStruct((size + MIXED, width), bf16),
         ),
-        in_specs=[SCALARS] + spec(4 + len(vectors)),
-        out_specs=(SCALARS,) * 3 + tuple(spec(1)),
-        scratch_shapes=[pltpu.VMEM((LINE_ROWS, width), f32)],
+        in_specs=[SCALARS] + spec(5 + len(vectors)),
+        out_specs=(SCALARS,) * 3 + tuple(spec(3)),
+        scratch_shapes=[pltpu.VMEM((LINE_ROWS, width), f32), pltpu.VMEM((2 * size, width), bf16)],
         compiler_params=params(62),
         name="pack",
         cost_estimate=cost(1.5),
-    )(lengths, w_qkv, w_out, w_in, w_back, *vectors)
+    )(lengths, tokens, w_qkv, w_out, w_in, w_back, *vectors)
 
 
 def unpack_kernel(kept_one, came_one, kept_two, came_two, *outs):
@@ -1276,10 +1281,10 @@
     last = ring.stages - 1
     core = ring.stages
     if direct:
-        info, inverse, sums_inverse, payload = pack(
-            (ring, sums_ring), lengths, w_qkv, w_out, w_in, w_back, small
+        info, inverse, sums_inverse, payload, to_twin, to_other = pack(
+            (ring, sums_ring), plan, total, lengths, tokens, w_qkv, w_out, w_in, w_back, small
         )
-        from_other, from_twin = exchange(*edge_sums(plan, total, info, order(tokens, payload)))
+        from_other, from_twin = exchange(to_twin, to_other)
         ready = prepare(plan, total, info, order(tokens, payload))
         (payload,) = join([payload], ring.step(0, [payload]))
         payload = order(payload, from_other, from_twin)

time: 130 us -> 128 us (0.985)
  waiting for transfers between devices: 41.4 us -> 36.7 us
  starting transfers between devices: 38.7 us -> 42.7 us
  local copies, waits for them, and re-layouts: 2.06 us -> 0.36 us
    ppermute x26, waiting for transfers between devices: 41.3 us -> 36.7 us  [step(): return [lax.ppermute(item, 'seq', route) for item in arrays]]
    ppermute x26, starting transfers between devices: 33.9 us -> 37.9 us  [step(): return [lax.ppermute(item, 'seq', route) for item in arrays]]
    unnamed x15 -> x11, local copies, waits for them, and re-layouts: 1.92 us -> 0.22 us
    pallas_call x2 -> x1, Pallas kernels: 3.21 us -> 2.97 us  [pack(): pl.pallas_call(functools.partial(pack_kernel, rings, plan, total), out_sh...]
  transfers between devices with their start and end apart: 30 -> 30, of which waited for: 20 -> 20; matrix products, arithmetic and copies ran while one was open for 2% -> 2% of each run, Pallas kernels for 25% -> 24%
where the time goes in v7:
time: 128 us; the launch traced here: 127 us
  Pallas kernels  43.3 us (34%)
  starting transfers between devices  42.7 us (33%)
  waiting for transfers between devices  36.7 us (29%)
  other arithmetic  2.99 us (2%)
    ppermute x26, starting transfers between devices, step(): return [lax.ppermute(item, 'seq', route) for item in arrays]  37.9 us
    ppermute x26, waiting for transfers between devices, step(): return [lax.ppermute(item, 'seq', route) for item in arrays]  36.7 us
    pallas_call x1, Pallas kernels, feed_forward(): pl.pallas_call(functools.partial(forward_kernel, parts), out_shape=(jax.S...  8.88 us
    pallas_call x1, Pallas kernels, attend_back(): pl.pallas_call(functools.partial(attend_back_kernel, plan, total), out_sh...  7.67 us
    pallas_call x1, Pallas kernels, finish(): pl.pallas_call(functools.partial(finish_kernel, plan, total), out_shape=(...  5.15 us
    pallas_call x1, Pallas kernels, attend(): pl.pallas_call(functools.partial(attend_kernel, plan, total), out_shape=[...  4.78 us
    pallas_call x1, Pallas kernels, prepare(): pl.pallas_call(functools.partial(prepare_kernel, plan, total), out_shape=...  4.12 us
    pallas_call x1, Pallas kernels, project(): pl.pallas_call(functools.partial(project_kernel, plan, total), out_shape=...  3.42 us
  transfers between devices with their start and end apart: 30, of which 20 were waited for; matrix products, arithmetic and copies ran while one was open for 2% of the time, Pallas kernels for 24%

profile of v7, /device:TPU:0, one launch (start us, length us, event | category | flops | bytes accessed | tf_op | source)
XLA Modules:
  0.0 126.9 jit_solution(7254817298596004861)
XLA Ops:
  0.6 3.0 %pack.1 = (s32[10]{0:T(128)}, s32[32]{0:T(128)}, s32[32]{0:T(128)}, bf16[1,200,512]{2,1,0:T(8,128)(2,1)}, bf16[176,512]{1,0:T(8,128)(2,1)}, /*index=5*/bf16[176,512]{1,0:T(8,128)(2,1)}) custom-call(s32[3]{0:T(128)} %lengths.1, bf16[512,512]{1,0:T(8,128)(2,1)} %tokens.4, bf16[16,1536]{1,0:T(8,128)(2,1)} %w_qkv.1, bf16[16,512]{1,0:T(8,128)(2,1)} %w_out.1, ...), custom_call_target="tpu_custom_call" | custom-call | flops 1 | bytes 1 | tf_op jit(solution)/shard_map/pack/pallas_call | solution.py:1187
  3.6 4.1 %collective-permute-start = (bf16[1,200,512]{2,1,0:T(8,128)(2,1)}, bf16[1,200,512]{2,1,0:T(8,128)(2,1)S(1)}, u32[]{:S(2)}, u32[]{:S(2)}) collective-permute-start(bf16[1,200,512]{2,1,0:T(8,128)(2,1)} %get-tuple-element.105), channel_id=1, source_target_pairs={{0,16},{1,5},{2,18},{3,7},{4,20},{5,1},{6,22},{7,3},{8,24},{9,13},... | collective-permute-start | bytes 614408 | tf_op jit(solution)/shard_map/ppermute | solution.py:1131
  8.4 2.9 %collective-permute-start.2 = (bf16[176,512]{1,0:T(8,128)(2,1)}, bf16[176,512]{1,0:T(8,128)(2,1)S(1)}, u32[]{:S(2)}, u32[]{:S(2)}) collective-permute-start(bf16[176,512]{1,0:T(8,128)(2,1)} %get-tuple-element.109), channel_id=1, source_target_pairs={{0,1},{1,0},{2,3},{3,2},{4,5},{5,4},{6,7},{7,6},{8,9},{9,8},{10,11... | collective-permute-start | bytes 540680 | tf_op jit(solution)/shard_map/ppermute | solution.py:1247
  11.3 2.6 %collective-permute-done = bf16[1,200,512]{2,1,0:T(8,128)(2,1)S(1)} collective-permute-done((bf16[1,200,512]{2,1,0:T(8,128)(2,1)}, bf16[1,200,512]{2,1,0:T(8,128)(2,1)S(1)}, u32[]{:S(2)}, u32[]{:S(2)}) %collective-permute-start) | collective-permute-done | bytes 204832 | tf_op jit(solution)/shard_map/ppermute | solution.py:1131
  15.0 3.3 %collective-permute-start.3 = (bf16[2,144,512]{2,1,0:T(8,128)(2,1)S(1)}, bf16[2,144,512]{2,1,0:T(8,128)(2,1)S(1)}, u32[]{:S(2)}, u32[]{:S(2)}) collective-permute-start(bf16[2,144,512]{2,1,0:T(8,128)(2,1)S(1)} %slice.90), channel_id=1, source_target_pairs={{0,2},{1,17},{2,0},{3,19},{4,6},{5,21},{6,4},{7,23},{8,10},{9,25},... | collective-permute-start | bytes 884744 | tf_op jit(solution)/shard_map/ppermute | solution.py:1131
  18.4 5.8 %collective-permute-done.5 = bf16[2,56,512]{2,1,0:T(8,128)(2,1)S(1)} collective-permute-done((bf16[2,56,512]{2,1,0:T(8,128)(2,1)S(1)}, bf16[2,56,512]{2,1,0:T(8,128)(2,1)S(1)}, u32[]{:S(2)}, u32[]{:S(2)}) %collective-permute-start.5) | collective-permute-done | bytes 114720 | tf_op jit(solution)/shard_map/ppermute | solution.py:1131
  24.2 2.1 %collective-permute-start.6 = (bf16[4,56,512]{2,1,0:T(8,128)(2,1)S(1)}, bf16[4,56,512]{2,1,0:T(8,128)(2,1)S(1)}, u32[]{:S(2)}, u32[]{:S(2)}) collective-permute-start(bf16[4,56,512]{2,1,0:T(8,128)(2,1)S(1)} %pad_maximum_fusion.4), channel_id=1, source_target_pairs={{0,8},{1,3},{2,10},{3,1},{4,12},{5,7},{6,14},{7,5},{8,0},{9,11},{1... | collective-permute-start | bytes 688136 | tf_op jit(solution)/shard_map/ppermute | solution.py:1131
  26.5 4.1 %prepare.1 = (f32[512,512]{1,0:T(8,128)S(1)}, f32[512,128]{1,0:T(8,128)S(1)}, bf16[512,512]{1,0:T(8,128)(2,1)S(1)}, f32[1024,128]{1,0:T(8,128)S(1)}, f32[2048,12...) custom-call(s32[10]{0:T(128)S(1)} %copy-done.2, ...), custom_call_target="tpu_custom_call" | custom-call | flops 1 | bytes 1 | tf_op jit(solution)/shard_map/prepare/pallas_call | solution.py:334
  30.8 2.0 %collective-permute-start.7 = (bf16[8,56,512]{2,1,0:T(8,128)(2,1)S(1)}, bf16[8,56,512]{2,1,0:T(8,128)(2,1)S(1)}, u32[]{:S(2)}, u32[]{:S(2)}) collective-permute-start(bf16[8,56,512]{2,1,0:T(8,128)(2,1)S(1)} %pad_maximum_fusion.2.refs_0_), channel_id=1, source_target_pairs={{0,4},{1,9},{2,6},{3,11},{4,0},{5,13},{6,2},{7,15},{8,12},{9,1},{1... | collective-permute-start | bytes 1376264 | tf_op jit(solution)/shard_map/ppermute | solution.py:1131
  32.8 5.1 %collective-permute-done.4 = bf16[4,144,512]{2,1,0:T(8,128)(2,1)S(1)} collective-permute-done((bf16[4,144,512]{2,1,0:T(8,128)(2,1)S(1)}, bf16[4,144,512]{2,1,0:T(8,128)(2,1)S(1)}, u32[]{:S(2)}, u32[]{:S(2)}) %collective-permute-start.4) | collective-permute-done | bytes 589856 | tf_op jit(solution)/shard_map/ppermute | solution.py:1131
  38.0 1.3 %collective-permute-done.7.refs_1_ = bf16[8,56,512]{2,1,0:T(8,128)(2,1)S(1)} collective-permute-done((bf16[8,56,512]{2,1,0:T(8,128)(2,1)S(1)}, bf16[8,56,512]{2,1,0:T(8,128)(2,1)S(1)}, u32[]{:S(2)}, u32[]{:S(2)}) %collective-permute-start.7) | collective-permute-done | bytes 458784 | tf_op jit(solution)/shard_map/ppermute | solution.py:1131
  39.3 1.9 %collective-permute-start.10 = (bf16[8,144,512]{2,1,0:T(8,128)(2,1)S(1)}, bf16[8,144,512]{2,1,0:T(8,128)(2,1)S(1)}, u32[]{:S(2)}, u32[]{:S(2)}) collective-permute-start(bf16[8,144,512]{2,1,0:T(8,128)(2,1)S(1)} %pad_maximum_fusion.refs_0_), channel_id=1, source_target_pairs={{0,4},{1,9},{2,6},{3,11},{4,0},{5,13},{6,2},{7,15},{8,12},{9,1},{1... | collective-permute-start | bytes 3538952 | tf_op jit(solution)/shard_map/ppermute | solution.py:1131
  41.2 1.9 %collective-permute-start.8 = (bf16[8,56,512]{2,1,0:T(8,128)(2,1)S(1)}, bf16[8,56,512]{2,1,0:T(8,128)(2,1)S(1)}, u32[]{:S(2)}, u32[]{:S(2)}) collective-permute-start(bf16[8,56,512]{2,1,0:T(8,128)(2,1)S(1)} %pad_maximum_fusion.2.refs_0_), channel_id=1, source_target_pairs={{0,1},{1,0},{2,3},{3,2},{4,5},{5,4},{6,7},{7,6},{8,9},{9,8},{10,11... | collective-permute-start | bytes 1376264 | tf_op jit(solution)/shard_map/ppermute | solution.py:1131
  45.3 3.4 %project.1 = (bf16[1024,256]{1,0:T(8,128)(2,1)S(1)}, bf16[1024,256]{1,0:T(8,128)(2,1)S(1)}, bf16[1024,512]{1,0:T(8,128)(2,1)S(1)}, bf16[1024,512]{1,0:T(8,128)(2...) custom-call(s32[10]{0:T(128)S(1)} %copy-done.2, ...), custom_call_target="tpu_custom_call" | custom-call | flops 1 | bytes 1 | tf_op jit(solution)/shard_map/project/pallas_call | solution.py:450
  48.7 4.8 %attend.1 = (bf16[512,256]{1,0:T(8,128)(2,1)S(1)}, bf16[512,256]{1,0:T(8,128)(2,1)S(1)}, f32[512,256]{1,0:T(8,128)S(1)}, f32[512,256]{1,0:T(8,128)S(1)}, f32[512,256]{1,0:T(8,128)S(1)}, /*index=5*/f32[512,256]{1,0:T(8,128)S(1)}) custom-call(s32[10]{0:T(128)S(1)} %copy-done.2, f32[1024,128]{1,0:T(8,128)S(1)} %get-tuple-element.120.mask, ...), custom_call_target="tpu_custom_call" | custom-call | flops 1 | bytes 1 | tf_op jit(solution)/shard_map/attend/pallas_call | solution.py:551
  53.5 2.0 %collective-permute-done.10.refs_1_ = bf16[8,144,512]{2,1,0:T(8,128)(2,1)S(1)} collective-permute-done((bf16[8,144,512]{2,1,0:T(8,128)(2,1)S(1)}, bf16[8,144,512]{2,1,0:T(8,128)(2,1)S(1)}, u32[]{:S(2)}, u32[]{:S(2)}) %collective-permute-start.10) | collective-permute-done | bytes 1179680 | tf_op jit(solution)/shard_map/ppermute | solution.py:1131
  56.8 2.5 %collective-permute-done.12.refs_3_ = bf16[8,144,512]{2,1,0:T(8,128)(2,1)S(1)} collective-permute-done((bf16[8,144,512]{2,1,0:T(8,128)(2,1)S(1)}, bf16[8,144,512]{2,1,0:T(8,128)(2,1)S(1)}, u32[]{:S(2)}, u32[]{:S(2)}) %collective-permute-start.12) | collective-permute-done | bytes 1179680 | tf_op jit(solution)/shard_map/ppermute | solution.py:1131
  59.3 8.9 %feed_forward.1 = (bf16[512,512]{1,0:T(8,128)(2,1)}, f32[512,512]{1,0:T(8,128)S(1)}, f32[512,512]{1,0:T(8,128)S(1)}, bf16[512,512]{1,0:T(8,128)(2,1)S(1)}, bf16[...) custom-call(s32[32]{0:T(128)S(1)} %copy-done.4, ...), custom_call_target="tpu_custom_call" | custom-call | flops 1 | bytes 1 | tf_op jit(solution)/shard_map/feed_forward/pallas_call | solution.py:658
  68.7 3.2 %middle.1 = (f32[512,512]{1,0:T(8,128)S(1)}, bf16[1024,512]{1,0:T(8,128)(2,1)S(1)}, bf16[1024,512]{1,0:T(8,128)(2,1)S(1)}, bf16[160,640]{1,0:T(8,128)(2,1)S(1)},...) custom-call(s32[10]{0:T(128)S(1)} %copy-done.2, ...), custom_call_target="tpu_custom_call" | custom-call | flops 1 | bytes 1 | tf_op jit(solution)/shard_map/middle/pallas_call | solution.py:785
  74.5 1.7 %collective-permute-start.19 = (bf16[4,144,512]{2,1,0:T(8,128)(2,1)S(1)}, bf16[4,144,512]{2,1,0:T(8,128)(2,1)S(1)}, u32[]{:S(2)}, u32[]{:S(2)}) collective-permute-start(bf16[4,144,512]{2,1,0:T(8,128)(2,1)S(1)} %get-tuple-element.150), channel_id=1, source_target_pairs={{0,2},{1,5},{2,0},{3,7},{4,6},{5,1},{6,4},{7,3},{8,10},{9,13},{10,... | collective-permute-start | bytes 1769480 | tf_op jit(solution)/shard_map/ppermute | solution.py:1131
  77.0 2.9 %collective-permute-start.22 = (bf16[4,144,512]{2,1,0:T(8,128)(2,1)S(1)}, bf16[4,144,512]{2,1,0:T(8,128)(2,1)S(1)}, u32[]{:S(2)}, u32[]{:S(2)}) collective-permute-start(bf16[4,144,512]{2,1,0:T(8,128)(2,1)S(1)} %get-tuple-element.151), channel_id=1, source_target_pairs={{0,2},{1,5},{2,0},{3,7},{4,6},{5,1},{6,4},{7,3},{8,10},{9,13},{10,... | collective-permute-start | bytes 1769480 | tf_op jit(solution)/shard_map/ppermute | solution.py:1131
  79.9 7.7 %attend_back.1 = (f32[1024,256]{1,0:T(8,128)S(1)}, f32[1024,256]{1,0:T(8,128)S(1)}, f32[1344,512]{1,0:T(8,128)S(1)}, f32[1344,512]{1,0:T(8,128)S(1)}) custom-call(f32[2048,128]{1,0:T(8,128)S(1)} %get-tuple-element.114.mask, bf16[2048,128]{1,0:T(8,128)(2,1)S(1)} %get-tuple-element.115.counts_of, bf16[1024,256]{1,0:T(8,128)(2,1)S(1)} %get-tuple-element.121.refs_0_, ...), custom_call_target="tpu_custom_call" | custom-call | flops 1 | bytes 1 | tf_op jit(solution)/shard_map/attend_back/pallas_call | solution.py:879
  89.3 2.4 %edge_back.1 = (f32[320,512]{1,0:T(8,128)S(1)}, f32[320,512]{1,0:T(8,128)S(1)}) custom-call(s32[10]{0:T(128)S(1)} %copy-done.2, f32[320,128]{1,0:T(8,128)S(1)} %get-tuple-element.116.mask, bf16[320,128]{1,0:T(8,128)(2,1)S(1)} %get-tuple-element.117.counts_of, bf16[320,256]{1,0:T(8,128)(2,1)S(1)} %get-tuple-element.158.queries_a, ...), custom_call_target="tpu_custom_call" | custom-call | flops 1 | bytes 1 | tf_op jit(solution)/shard_map/edge_back/pallas_call | solution.py:971
  91.6 5.1 %finish.1 = (f32[512,512]{1,0:T(8,128)}, bf16[16,56,512]{2,1,0:T(8,128)(2,1)S(1)}, bf16[8,56,512]{2,1,0:T(8,128)(2,1)S(1)}, bf16[8,56,512]{2,1,0:T(8,128)(2,1)S(1)}) custom-call(s32[10]{0:T(128)S(1)} %copy-done.2, s32[32]{0:T(128)S(1)} %copy-done.3, f32[512,512]{1,0:T(8,128)S(1)} %get-tuple-element.111.standard, f32[512,128]{1,0:T(8,128)S(1)} %get-tuple-element.112.spread, ...), custom_call_target="tpu_custom_call" | custom-call | flops 1 | bytes 1 | tf_op jit(solution)/shard_map/finish/pallas_call | solution.py:1081
  100.1 2.3 %collective-permute-start.24 = (bf16[8,56,512]{2,1,0:T(8,128)(2,1)S(1)}, bf16[8,56,512]{2,1,0:T(8,128)(2,1)S(1)}, u32[]{:S(2)}, u32[]{:S(2)}) collective-permute-start(bf16[8,56,512]{2,1,0:T(8,128)(2,1)S(1)} %get-tuple-element.199), channel_id=1, source_target_pairs={{0,2},{1,5},{2,0},{3,7},{4,6},{5,1},{6,4},{7,3},{8,10},{9,13},{10,... | collective-permute-start | bytes 1376264 | tf_op jit(solution)/shard_map/ppermute | solution.py:1131
  102.8 6.1 %collective-permute-done.24 = bf16[8,56,512]{2,1,0:T(8,128)(2,1)S(1)} collective-permute-done((bf16[8,56,512]{2,1,0:T(8,128)(2,1)S(1)}, bf16[8,56,512]{2,1,0:T(8,128)(2,1)S(1)}, u32[]{:S(2)}, u32[]{:S(2)}) %collective-permute-start.24) | collective-permute-done | bytes 458784 | tf_op jit(solution)/shard_map/ppermute | solution.py:1131
  109.1 1.4 %collective-permute-start.25 = (bf16[4,56,512]{2,1,0:T(8,128)(2,1)S(1)}, bf16[4,56,512]{2,1,0:T(8,128)(2,1)S(1)}, u32[]{:S(2)}, u32[]{:S(2)}) collective-permute-start(bf16[4,56,512]{2,1,0:T(8,128)(2,1)S(1)} %get-tuple-element.195), channel_id=1, source_target_pairs={{0,4},{1,9},{2,6},{3,11},{4,0},{5,13},{6,2},{7,15},{8,12},{9,1},{1... | collective-permute-start | bytes 688136 | tf_op jit(solution)/shard_map/ppermute | solution.py:1131
  110.4 2.0 %collective-permute-done.26 = bf16[2,144,512]{2,1,0:T(8,128)(2,1)S(1)} collective-permute-done((bf16[2,144,512]{2,1,0:T(8,128)(2,1)S(1)}, bf16[2,144,512]{2,1,0:T(8,128)(2,1)S(1)}, u32[]{:S(2)}, u32[]{:S(2)}) %collective-permute-start.26) | collective-permute-done | bytes 294944 | tf_op jit(solution)/shard_map/ppermute | solution.py:1131
  112.5 2.6 %collective-permute-done.25 = bf16[4,56,512]{2,1,0:T(8,128)(2,1)S(1)} collective-permute-done((bf16[4,56,512]{2,1,0:T(8,128)(2,1)S(1)}, bf16[4,56,512]{2,1,0:T(8,128)(2,1)S(1)}, u32[]{:S(2)}, u32[]{:S(2)}) %collective-permute-start.25) | collective-permute-done | bytes 229408 | tf_op jit(solution)/shard_map/ppermute | solution.py:1131
  116.1 3.9 %collective-permute-start.29 = (bf16[1,144,512]{2,1,0:T(8,128)(2,1)S(1)}, bf16[1,144,512]{2,1,0:T(8,128)(2,1)S(1)}, u32[]{:S(2)}, u32[]{:S(2)}) collective-permute-start(bf16[1,144,512]{2,1,0:T(8,128)(2,1)S(1)} %get-tuple-element.202), channel_id=1, source_target_pairs={{0,16},{1,3},{2,18},{3,1},{4,20},{5,7},{6,22},{7,5},{8,24},{9,11},... | collective-permute-start | bytes 442376 | tf_op jit(solution)/shard_map/ppermute | solution.py:1131
  120.1 3.9 %collective-permute-start.28 = (bf16[1,56,512]{2,1,0:T(8,128)(2,1)S(1)}, bf16[1,56,512]{2,1,0:T(8,128)(2,1)S(1)}, u32[]{:S(2)}, u32[]{:S(2)}) collective-permute-start(bf16[1,56,512]{2,1,0:T(8,128)(2,1)S(1)} %get-tuple-element.205), channel_id=1, source_target_pairs={{0,16},{1,3},{2,18},{3,1},{4,20},{5,7},{6,22},{7,5},{8,24},{9,11},... | collective-permute-start | bytes 172040 | tf_op jit(solution)/shard_map/ppermute | solution.py:1131
  124.0 2.2 %collective-permute-done.28.came_one = bf16[1,56,512]{2,1,0:T(8,128)(2,1)S(1)} collective-permute-done((bf16[1,56,512]{2,1,0:T(8,128)(2,1)S(1)}, bf16[1,56,512]{2,1,0:T(8,128)(2,1)S(1)}, u32[]{:S(2)}, u32[]{:S(2)}) %collective-permute-start.28) | collective-permute-done | bytes 57376 | tf_op jit(solution)/shard_map/ppermute | solution.py:1131
  (67 shorter events, 17.0 us)
Async XLA Ops:
  3.6 10.3 %collective-permute-start = (bf16[1,200,512]{2,1,0:T(8,128)(2,1)}, bf16[1,200,512]{2,1,0:T(8,128)(2,1)S(1)}, u32[]{:S(2)}, u32[]{:S(2)}) collective-permute-start(bf16[1,200,512]{2,1,0:T(8,128)(2,1)} %get-tuple-element.105), channel_id=1, source_target_pairs={{0,16},{1,5},{2,18},{3,7},{4,20},{5,1},{6,22},{7,3},{8,24},{9,13},... | collective-permute-start | bytes 614408 | tf_op jit(solution)/shard_map/ppermute | solution.py:1131
  7.7 7.2 %collective-permute-start.1 = (bf16[176,512]{1,0:T(8,128)(2,1)}, bf16[176,512]{1,0:T(8,128)(2,1)S(1)}, u32[]{:S(2)}, u32[]{:S(2)}) collective-permute-start(bf16[176,512]{1,0:T(8,128)(2,1)} %get-tuple-element.108), channel_id=1, source_target_pairs={{1,2},{3,4},{5,6},{7,8},{9,10},{11,12},{13,14},{15,16},{17,18},{19... | collective-permute-start | bytes 540680 | tf_op jit(solution)/shard_map/ppermute | solution.py:1247
  8.4 18.1 %copy-start = (bf16[512,512]{1,0:T(8,128)(2,1)S(1)}, bf16[512,512]{1,0:T(8,128)(2,1)}, u32[]{:S(2)}) copy-start(bf16[512,512]{1,0:T(8,128)(2,1)} %tokens.4) | copy-start | bytes 1572868
  8.4 18.1 %copy-start.2 = (s32[10]{0:T(128)S(1)}, s32[10]{0:T(128)}, u32[]{:S(2)}) copy-start(s32[10]{0:T(128)} %get-tuple-element.104.info) | copy-start | bytes 124
  8.4 6.5 %collective-permute-start.2 = (bf16[176,512]{1,0:T(8,128)(2,1)}, bf16[176,512]{1,0:T(8,128)(2,1)S(1)}, u32[]{:S(2)}, u32[]{:S(2)}) collective-permute-start(bf16[176,512]{1,0:T(8,128)(2,1)} %get-tuple-element.109), channel_id=1, source_target_pairs={{0,1},{1,0},{2,3},{3,2},{4,5},{5,4},{6,7},{7,6},{8,9},{9,8},{10,11... | collective-permute-start | bytes 540680 | tf_op jit(solution)/shard_map/ppermute | solution.py:1247
  15.0 11.4 %collective-permute-start.3 = (bf16[2,144,512]{2,1,0:T(8,128)(2,1)S(1)}, bf16[2,144,512]{2,1,0:T(8,128)(2,1)S(1)}, u32[]{:S(2)}, u32[]{:S(2)}) collective-permute-start(bf16[2,144,512]{2,1,0:T(8,128)(2,1)S(1)} %slice.90), channel_id=1, source_target_pairs={{0,2},{1,17},{2,0},{3,19},{4,6},{5,21},{6,4},{7,23},{8,10},{9,25},... | collective-permute-start | bytes 884744 | tf_op jit(solution)/shard_map/ppermute | solution.py:1131
  18.3 5.9 %collective-permute-start.5 = (bf16[2,56,512]{2,1,0:T(8,128)(2,1)S(1)}, bf16[2,56,512]{2,1,0:T(8,128)(2,1)S(1)}, u32[]{:S(2)}, u32[]{:S(2)}) collective-permute-start(bf16[2,56,512]{2,1,0:T(8,128)(2,1)S(1)} %slice.91), channel_id=1, source_target_pairs={{0,2},{1,17},{2,0},{3,19},{4,6},{5,21},{6,4},{7,23},{8,10},{9,25},... | collective-permute-start | bytes 344072 | tf_op jit(solution)/shard_map/ppermute | solution.py:1131
  24.2 6.5 %collective-permute-start.6 = (bf16[4,56,512]{2,1,0:T(8,128)(2,1)S(1)}, bf16[4,56,512]{2,1,0:T(8,128)(2,1)S(1)}, u32[]{:S(2)}, u32[]{:S(2)}) collective-permute-start(bf16[4,56,512]{2,1,0:T(8,128)(2,1)S(1)} %pad_maximum_fusion.4), channel_id=1, source_target_pairs={{0,8},{1,3},{2,10},{3,1},{4,12},{5,7},{6,14},{7,5},{8,0},{9,11},{1... | collective-permute-start | bytes 688136 | tf_op jit(solution)/shard_map/ppermute | solution.py:1131
  26.4 11.5 %collective-permute-start.4 = (bf16[4,144,512]{2,1,0:T(8,128)(2,1)S(1)}, bf16[4,144,512]{2,1,0:T(8,128)(2,1)S(1)}, u32[]{:S(2)}, u32[]{:S(2)}) collective-permute-start(bf16[4,144,512]{2,1,0:T(8,128)(2,1)S(1)} %pad_maximum_fusion.1), channel_id=1, source_target_pairs={{0,8},{1,3},{2,10},{3,1},{4,12},{5,7},{6,14},{7,5},{8,0},{9,11},{1... | collective-permute-start | bytes 1769480 | tf_op jit(solution)/shard_map/ppermute | solution.py:1131
  30.8 8.5 %collective-permute-start.7 = (bf16[8,56,512]{2,1,0:T(8,128)(2,1)S(1)}, bf16[8,56,512]{2,1,0:T(8,128)(2,1)S(1)}, u32[]{:S(2)}, u32[]{:S(2)}) collective-permute-start(bf16[8,56,512]{2,1,0:T(8,128)(2,1)S(1)} %pad_maximum_fusion.2.refs_0_), channel_id=1, source_target_pairs={{0,4},{1,9},{2,6},{3,11},{4,0},{5,13},{6,2},{7,15},{8,12},{9,1},{1... | collective-permute-start | bytes 1376264 | tf_op jit(solution)/shard_map/ppermute | solution.py:1131
  39.3 16.2 %collective-permute-start.10 = (bf16[8,144,512]{2,1,0:T(8,128)(2,1)S(1)}, bf16[8,144,512]{2,1,0:T(8,128)(2,1)S(1)}, u32[]{:S(2)}, u32[]{:S(2)}) collective-permute-start(bf16[8,144,512]{2,1,0:T(8,128)(2,1)S(1)} %pad_maximum_fusion.refs_0_), channel_id=1, source_target_pairs={{0,4},{1,9},{2,6},{3,11},{4,0},{5,13},{6,2},{7,15},{8,12},{9,1},{1... | collective-permute-start | bytes 3538952 | tf_op jit(solution)/shard_map/ppermute | solution.py:1131
  41.2 3.4 %collective-permute-start.8 = (bf16[8,56,512]{2,1,0:T(8,128)(2,1)S(1)}, bf16[8,56,512]{2,1,0:T(8,128)(2,1)S(1)}, u32[]{:S(2)}, u32[]{:S(2)}) collective-permute-start(bf16[8,56,512]{2,1,0:T(8,128)(2,1)S(1)} %pad_maximum_fusion.2.refs_0_), channel_id=1, source_target_pairs={{0,1},{1,0},{2,3},{3,2},{4,5},{5,4},{6,7},{7,6},{8,9},{9,8},{10,11... | collective-permute-start | bytes 1376264 | tf_op jit(solution)/shard_map/ppermute | solution.py:1131
  43.2 2.1 %collective-permute-start.9 = (bf16[8,56,512]{2,1,0:T(8,128)(2,1)S(1)}, bf16[8,56,512]{2,1,0:T(8,128)(2,1)S(1)}, u32[]{:S(2)}, u32[]{:S(2)}) collective-permute-start(bf16[8,56,512]{2,1,0:T(8,128)(2,1)S(1)} %collective-permute-done.7.refs_1_), channel_id=1, source_target_pairs={{0,1},{1,0},{2,3},{3,2},{4,5},{5,4},{6,7},{7,6},{8,9},{9,8},{10,11... | collective-permute-start | bytes 1376264 | tf_op jit(solution)/shard_map/ppermute | solution.py:1131
  43.2 13.7 %collective-permute-start.11 = (bf16[8,144,512]{2,1,0:T(8,128)(2,1)S(1)}, bf16[8,144,512]{2,1,0:T(8,128)(2,1)S(1)}, u32[]{:S(2)}, u32[]{:S(2)}) collective-permute-start(bf16[8,144,512]{2,1,0:T(8,128)(2,1)S(1)} %pad_maximum_fusion.refs_0_), channel_id=1, source_target_pairs={{0,1},{1,0},{2,3},{3,2},{4,5},{5,4},{6,7},{7,6},{8,9},{9,8},{10,11... | collective-permute-start | bytes 3538952 | tf_op jit(solution)/shard_map/ppermute | solution.py:1131
  55.5 3.8 %collective-permute-start.12 = (bf16[8,144,512]{2,1,0:T(8,128)(2,1)S(1)}, bf16[8,144,512]{2,1,0:T(8,128)(2,1)S(1)}, u32[]{:S(2)}, u32[]{:S(2)}) collective-permute-start(bf16[8,144,512]{2,1,0:T(8,128)(2,1)S(1)} %collective-permute-done.10.refs_1_), channel_id=1, source_target_pairs={{0,1},{1,0},{2,3},{3,2},{4,5},{5,4},{6,7},{7,6},{8,9},{9,8},{10,11... | collective-permute-start | bytes 3538952 | tf_op jit(solution)/shard_map/ppermute | solution.py:1131
  68.2 5.5 %collective-permute-start.13 = (bf16[8,128,512]{2,1,0:T(8,128)(2,1)S(1)}, bf16[8,128,512]{2,1,0:T(8,128)(2,1)S(1)}, u32[]{:S(2)}, u32[]{:S(2)}) collective-permute-start(bf16[8,128,512]{2,1,0:T(8,128)(2,1)S(1)} %get-tuple-element.147), channel_id=1, source_target_pairs={{0,1},{1,0},{2,3},{3,2},{4,5},{5,4},{6,7},{7,6},{8,9},{9,8},{10,11... | collective-permute-start | bytes 3145736 | tf_op jit(solution)/shard_map/ppermute | solution.py:1131
  68.6 5.1 %collective-permute-start.17 = (bf16[8,128,512]{2,1,0:T(8,128)(2,1)S(1)}, bf16[8,128,512]{2,1,0:T(8,128)(2,1)S(1)}, u32[]{:S(2)}, u32[]{:S(2)}) collective-permute-start(bf16[8,128,512]{2,1,0:T(8,128)(2,1)S(1)} %get-tuple-element.163), channel_id=1, source_target_pairs={{0,1},{1,0},{2,3},{3,2},{4,5},{5,4},{6,7},{7,6},{8,9},{9,8},{10,11... | collective-permute-start | bytes 3145736 | tf_op jit(solution)/shard_map/ppermute | solution.py:1131
  71.9 1.4 %collective-permute-start.14 = (bf16[8,16,512]{2,1,0:T(8,128)(2,1)S(1)}, bf16[8,16,512]{2,1,0:T(8,128)(2,1)S(1)}, u32[]{:S(2)}, u32[]{:S(2)}) collective-permute-start(bf16[8,16,512]{2,1,0:T(8,128)(2,1)S(1)} %get-tuple-element.148), channel_id=1, source_target_pairs={{0,1},{1,0},{2,3},{3,2},{4,5},{5,4},{6,7},{7,6},{8,9},{9,8},{10,11... | collective-permute-start | bytes 393224 | tf_op jit(solution)/shard_map/ppermute | solution.py:1131
  72.3 1.3 %collective-permute-start.18 = (bf16[8,16,512]{2,1,0:T(8,128)(2,1)S(1)}, bf16[8,16,512]{2,1,0:T(8,128)(2,1)S(1)}, u32[]{:S(2)}, u32[]{:S(2)}) collective-permute-start(bf16[8,16,512]{2,1,0:T(8,128)(2,1)S(1)} %get-tuple-element.164), channel_id=1, source_target_pairs={{0,1},{1,0},{2,3},{3,2},{4,5},{5,4},{6,7},{7,6},{8,9},{9,8},{10,11... | collective-permute-start | bytes 393224 | tf_op jit(solution)/shard_map/ppermute | solution.py:1131
  72.5 2.0 %collective-permute-start.15 = (bf16[160,640]{1,0:T(8,128)(2,1)S(1)}, bf16[160,640]{1,0:T(8,128)(2,1)S(1)}, u32[]{:S(2)}, u32[]{:S(2)}) collective-permute-start(bf16[160,640]{1,0:T(8,128)(2,1)S(1)} %get-tuple-element.149), channel_id=1, source_target_pairs={{0,1},{1,0},{2,3},{3,2},{4,5},{5,4},{6,7},{7,6},{8,9},{9,8},{10,11... | collective-permute-start | bytes 614408 | tf_op jit(solution)/shard_map/ppermute | solution.py:1247
  74.5 13.5 %collective-permute-start.19 = (bf16[4,144,512]{2,1,0:T(8,128)(2,1)S(1)}, bf16[4,144,512]{2,1,0:T(8,128)(2,1)S(1)}, u32[]{:S(2)}, u32[]{:S(2)}) collective-permute-start(bf16[4,144,512]{2,1,0:T(8,128)(2,1)S(1)} %get-tuple-element.150), channel_id=1, source_target_pairs={{0,2},{1,5},{2,0},{3,7},{4,6},{5,1},{6,4},{7,3},{8,10},{9,13},{10,... | collective-permute-start | bytes 1769480 | tf_op jit(solution)/shard_map/ppermute | solution.py:1131
  76.1 11.4 %collective-permute-start.16 = (bf16[160,640]{1,0:T(8,128)(2,1)S(1)}, bf16[160,640]{1,0:T(8,128)(2,1)S(1)}, u32[]{:S(2)}, u32[]{:S(2)}) collective-permute-start(bf16[160,640]{1,0:T(8,128)(2,1)S(1)} %get-tuple-element.160), channel_id=1, source_target_pairs={{1,2},{3,4},{5,6},{7,8},{9,10},{11,12},{13,14},{15,16},{17,18},{19... | collective-permute-start | bytes 614408 | tf_op jit(solution)/shard_map/ppermute | solution.py:1247
  77.0 20.7 %collective-permute-start.22 = (bf16[4,144,512]{2,1,0:T(8,128)(2,1)S(1)}, bf16[4,144,512]{2,1,0:T(8,128)(2,1)S(1)}, u32[]{:S(2)}, u32[]{:S(2)}) collective-permute-start(bf16[4,144,512]{2,1,0:T(8,128)(2,1)S(1)} %get-tuple-element.151), channel_id=1, source_target_pairs={{0,2},{1,5},{2,0},{3,7},{4,6},{5,1},{6,4},{7,3},{8,10},{9,13},{10,... | collective-permute-start | bytes 1769480 | tf_op jit(solution)/shard_map/ppermute | solution.py:1131
  88.1 9.9 %collective-permute-start.23 = (bf16[4,144,512]{2,1,0:T(8,128)(2,1)S(1)}, bf16[4,144,512]{2,1,0:T(8,128)(2,1)S(1)}, u32[]{:S(2)}, u32[]{:S(2)}) collective-permute-start(bf16[4,144,512]{2,1,0:T(8,128)(2,1)S(1)} %fusion), channel_id=1, source_target_pairs={{0,4},{1,9},{2,6},{3,11},{4,0},{5,13},{6,2},{7,15},{8,12},{9,1},{1... | collective-permute-start | bytes 1769480 | tf_op jit(solution)/shard_map/ppermute | solution.py:1131
  96.8 2.5 %collective-permute-start.20 = (bf16[8,56,512]{2,1,0:T(8,128)(2,1)S(1)}, bf16[8,56,512]{2,1,0:T(8,128)(2,1)S(1)}, u32[]{:S(2)}, u32[]{:S(2)}) collective-permute-start(bf16[8,56,512]{2,1,0:T(8,128)(2,1)S(1)} %get-tuple-element.172), channel_id=1, source_target_pairs={{0,1},{1,0},{2,3},{3,2},{4,5},{5,4},{6,7},{7,6},{8,9},{9,8},{10,11... | collective-permute-start | bytes 1376264 | tf_op jit(solution)/shard_map/ppermute | solution.py:1131
  97.8 2.1 %collective-permute-start.21 = (bf16[8,56,512]{2,1,0:T(8,128)(2,1)S(1)}, bf16[8,56,512]{2,1,0:T(8,128)(2,1)S(1)}, u32[]{:S(2)}, u32[]{:S(2)}) collective-permute-start(bf16[8,56,512]{2,1,0:T(8,128)(2,1)S(1)} %get-tuple-element.173), channel_id=1, source_target_pairs={{0,1},{1,0},{2,3},{3,2},{4,5},{5,4},{6,7},{7,6},{8,9},{9,8},{10,11... | collective-permute-start | bytes 1376264 | tf_op jit(solution)/shard_map/ppermute | solution.py:1131
  100.1 8.8 %collective-permute-start.24 = (bf16[8,56,512]{2,1,0:T(8,128)(2,1)S(1)}, bf16[8,56,512]{2,1,0:T(8,128)(2,1)S(1)}, u32[]{:S(2)}, u32[]{:S(2)}) collective-permute-start(bf16[8,56,512]{2,1,0:T(8,128)(2,1)S(1)} %get-tuple-element.199), channel_id=1, source_target_pairs={{0,2},{1,5},{2,0},{3,7},{4,6},{5,1},{6,4},{7,3},{8,10},{9,13},{10,... | collective-permute-start | bytes 1376264 | tf_op jit(solution)/shard_map/ppermute | solution.py:1131
  102.4 10.0 %collective-permute-start.26 = (bf16[2,144,512]{2,1,0:T(8,128)(2,1)S(1)}, bf16[2,144,512]{2,1,0:T(8,128)(2,1)S(1)}, u32[]{:S(2)}, u32[]{:S(2)}) collective-permute-start(bf16[2,144,512]{2,1,0:T(8,128)(2,1)S(1)} %get-tuple-element.194), channel_id=1, source_target_pairs={{0,8},{1,17},{2,10},{3,19},{4,12},{5,21},{6,14},{7,23},{8,0},{9,25... | collective-permute-start | bytes 884744 | tf_op jit(solution)/shard_map/ppermute | solution.py:1131
  109.1 6.1 %collective-permute-start.25 = (bf16[4,56,512]{2,1,0:T(8,128)(2,1)S(1)}, bf16[4,56,512]{2,1,0:T(8,128)(2,1)S(1)}, u32[]{:S(2)}, u32[]{:S(2)}) collective-permute-start(bf16[4,56,512]{2,1,0:T(8,128)(2,1)S(1)} %get-tuple-element.195), channel_id=1, source_target_pairs={{0,4},{1,9},{2,6},{3,11},{4,0},{5,13},{6,2},{7,15},{8,12},{9,1},{1... | collective-permute-start | bytes 688136 | tf_op jit(solution)/shard_map/ppermute | solution.py:1131
  115.2 4.9 %collective-permute-start.27 = (bf16[2,56,512]{2,1,0:T(8,128)(2,1)S(1)}, bf16[2,56,512]{2,1,0:T(8,128)(2,1)S(1)}, u32[]{:S(2)}, u32[]{:S(2)}) collective-permute-start(bf16[2,56,512]{2,1,0:T(8,128)(2,1)S(1)} %get-tuple-element.203), channel_id=1, source_target_pairs={{0,8},{1,17},{2,10},{3,19},{4,12},{5,21},{6,14},{7,23},{8,0},{9,25... | collective-permute-start | bytes 344072 | tf_op jit(solution)/shard_map/ppermute | solution.py:1131
  116.1 7.9 %collective-permute-start.29 = (bf16[1,144,512]{2,1,0:T(8,128)(2,1)S(1)}, bf16[1,144,512]{2,1,0:T(8,128)(2,1)S(1)}, u32[]{:S(2)}, u32[]{:S(2)}) collective-permute-start(bf16[1,144,512]{2,1,0:T(8,128)(2,1)S(1)} %get-tuple-element.202), channel_id=1, source_target_pairs={{0,16},{1,3},{2,18},{3,1},{4,20},{5,7},{6,22},{7,5},{8,24},{9,11},... | collective-permute-start | bytes 442376 | tf_op jit(solution)/shard_map/ppermute | solution.py:1131
  120.1 6.1 %collective-permute-start.28 = (bf16[1,56,512]{2,1,0:T(8,128)(2,1)S(1)}, bf16[1,56,512]{2,1,0:T(8,128)(2,1)S(1)}, u32[]{:S(2)}, u32[]{:S(2)}) collective-permute-start(bf16[1,56,512]{2,1,0:T(8,128)(2,1)S(1)} %get-tuple-element.205), channel_id=1, source_target_pairs={{0,16},{1,3},{2,18},{3,1},{4,20},{5,7},{6,22},{7,5},{8,24},{9,11},... | collective-permute-start | bytes 172040 | tf_op jit(solution)/shard_map/ppermute | solution.py:1131
  (3 other events, 35.9 us)

commit v8 on v7

--- a/solution.py
+++ b/solution.py
@@ -728,27 +728,29 @@
     sums[pl.ds(3, 1), :] = column_sum(gain_terms)
     sums[pl.ds(4, 1), :] = column_sum(grad_normed[...])
     sums[pl.ds(5, 1), :] = column_sum(grad_out)
+    mixed_grads = [dot_nt(low, w_out[pl.ds(quad * wide, wide), :]) for quad in range(2)]
     for quad in range(2):
         lines = pl.ds(quad * wide, wide)
         flat[lines, :] = dot_tn((attended_a, attended_b)[quad][...], low).astype(bf16)
-        numer = dot_nt(low, w_out[lines, :]) * (scale_a, scale_b)[quad][...]
+    for quad in range(2):
+        numer = mixed_grads[quad] * (scale_a, scale_b)[quad][...]
         denom = -(numer * (mixed_a, mixed_b)[quad][...])
         for chunk in range(2 * wide // 128):
             source = numer if chunk < wide // 128 else denom
             lane = chunk * 128 % wide
-            levels[chunk, pl.ds(0, plan.rows), :] = source[:, lane : lane + 128]
+            levels[quad * 4 + chunk, pl.ds(0, plan.rows), :] = source[:, lane : lane + 128]
             for level in range(1, LEVELS):
                 count, at = plan.counts[level], plan.query_at[level]
                 below = plan.query_at[level - 1]
-                levels[chunk, pl.ds(at, count), :] = (
-                    levels[chunk, pl.ds(below, count, stride=2), :]
-                    + levels[chunk, pl.ds(below + 1, count, stride=2), :]
+                levels[quad * 4 + chunk, pl.ds(at, count), :] = (
+                    levels[quad * 4 + chunk, pl.ds(below, count, stride=2), :]
+                    + levels[quad * 4 + chunk, pl.ds(below + 1, count, stride=2), :]
                 )
                 rest = plan.padded[level] - count
                 if rest:
-                    levels[chunk, pl.ds(at + count, rest), :] = jnp.zeros((rest, 128), f32)
+                    levels[quad * 4 + chunk, pl.ds(at + count, rest), :] = jnp.zeros((rest, 128), f32)
             grads = (grads_a, grads_b)[quad]
-            grads[:, pl.ds(chunk * 128, 128)] = levels[chunk].astype(bf16)
+            grads[:, pl.ds(chunk * 128, 128)] = levels[quad * 4 + chunk].astype(bf16)
         for k in range(2 * LEVELS):
             level, here = k % LEVELS, pl.ds(k * HALO, HALO)
             at = plan.query_at[level] + (0 if k < LEVELS else plan.counts[level] - HALO)
@@ -756,7 +758,7 @@
             ends[here, pl.ds(quad * wide, wide)] = (grads_a, grads_b)[quad][there, pl.ds(0, wide)]
             for chunk in range(wide // 128):
                 lanes = pl.ds(quad * wide + chunk * 128, 128)
-                denoms[here, lanes] = levels[wide // 128 + chunk, there, :]
+                denoms[here, lanes] = levels[quad * 4 + wide // 128 + chunk, there, :]
     feature = lax.broadcasted_iota(jnp.int32, (width, LINE), 0)
     lane = lax.broadcasted_iota(jnp.int32, (width, LINE), 1)
     pick = jnp.where(lane == feature // HEAD_DIM, 1.0, 0.0).astype(bf16)
@@ -798,7 +800,7 @@
         in_specs=[SCALARS] * 2 + spec(11),
         out_specs=tuple(spec(9)),
         scratch_shapes=[
-            pltpu.VMEM((width // 128, plan.query_rows, 128), f32),
+            pltpu.VMEM((2 * width // 128, plan.query_rows, 128), f32),
             pltpu.VMEM((2 * size, width + LINE), bf16),
             pltpu.VMEM((2 * size, width), f32),
             pltpu.VMEM((width, width), bf16),
@@ -833,8 +835,8 @@
 
     def block_step(step, carry):
         work = []
-        for k in range(4):
-            here, there, allowed, counts = prepare(step * 4 + k)
+        for k in range(8):
+            here, there, allowed, counts = prepare(step * 8 + k)
             for quad in range(2):
                 q = spread_heads(queries[quad][here, :], masks)
                 g = spread_heads(grads[quad][here, keys], masks)
@@ -871,7 +873,7 @@
             grad_extended[quad][there, values] += to_value
         return carry
 
-    lax.fori_loop(0, len(plan.blocks) // 4, block_step, 0, unroll=1)
+    lax.fori_loop(0, len(plan.blocks) // 8, block_step, 0, unroll=1)
 
 
 def attend_back(plan, total, mask, counts, queries, pairs, halos, grads):

time: 128 us -> 128 us (level)
  no operation moved by 1% of the time
where the time goes in v8:
time: 128 us; the launch traced here: 127 us
  Pallas kernels  42.6 us (33%)
  starting transfers between devices  42.5 us (33%)
  waiting for transfers between devices  37.3 us (29%)
  other arithmetic  2.99 us (2%)
    ppermute x26, starting transfers between devices, step(): return [lax.ppermute(item, 'seq', route) for item in arrays]  37.9 us
    ppermute x26, waiting for transfers between devices, step(): return [lax.ppermute(item, 'seq', route) for item in arrays]  37.3 us
    pallas_call x1, Pallas kernels, feed_forward(): pl.pallas_call(functools.partial(forward_kernel, parts), out_shape=(jax.S...  8.88 us
    pallas_call x1, Pallas kernels, attend_back(): pl.pallas_call(functools.partial(attend_back_kernel, plan, total), out_sh...  7.34 us
    pallas_call x1, Pallas kernels, finish(): pl.pallas_call(functools.partial(finish_kernel, plan, total), out_shape=(...  5.15 us
    pallas_call x1, Pallas kernels, attend(): pl.pallas_call(functools.partial(attend_kernel, plan, total), out_shape=[...  4.78 us
    pallas_call x1, Pallas kernels, prepare(): pl.pallas_call(functools.partial(prepare_kernel, plan, total), out_shape=...  4.12 us
    pallas_call x1, Pallas kernels, project(): pl.pallas_call(functools.partial(project_kernel, plan, total), out_shape=...  3.42 us
  transfers between devices with their start and end apart: 30, of which 20 were waited for; matrix products, arithmetic and copies ran while one was open for 2% of the time, Pallas kernels for 24%

profile of v8, /device:TPU:0, one launch (start us, length us, event | category | flops | bytes accessed | tf_op | source)
XLA Modules:
  0.0 126.6 jit_solution(1691222149215446709)
XLA Ops:
  0.6 3.0 %pack.1 = (s32[10]{0:T(128)}, s32[32]{0:T(128)}, s32[32]{0:T(128)}, bf16[1,200,512]{2,1,0:T(8,128)(2,1)}, bf16[176,512]{1,0:T(8,128)(2,1)}, /*index=5*/bf16[176,512]{1,0:T(8,128)(2,1)}) custom-call(s32[3]{0:T(128)} %lengths.1, bf16[512,512]{1,0:T(8,128)(2,1)} %tokens.4, bf16[16,1536]{1,0:T(8,128)(2,1)} %w_qkv.1, bf16[16,512]{1,0:T(8,128)(2,1)} %w_out.1, ...), custom_call_target="tpu_custom_call" | custom-call | flops 1 | bytes 1 | tf_op jit(solution)/shard_map/pack/pallas_call | solution.py:1189
  3.6 4.1 %collective-permute-start = (bf16[1,200,512]{2,1,0:T(8,128)(2,1)}, bf16[1,200,512]{2,1,0:T(8,128)(2,1)S(1)}, u32[]{:S(2)}, u32[]{:S(2)}) collective-permute-start(bf16[1,200,512]{2,1,0:T(8,128)(2,1)} %get-tuple-element.105), channel_id=1, source_target_pairs={{0,16},{1,5},{2,18},{3,7},{4,20},{5,1},{6,22},{7,3},{8,24},{9,13},... | collective-permute-start | bytes 614408 | tf_op jit(solution)/shard_map/ppermute | solution.py:1133
  8.4 2.9 %collective-permute-start.2 = (bf16[176,512]{1,0:T(8,128)(2,1)}, bf16[176,512]{1,0:T(8,128)(2,1)S(1)}, u32[]{:S(2)}, u32[]{:S(2)}) collective-permute-start(bf16[176,512]{1,0:T(8,128)(2,1)} %get-tuple-element.109), channel_id=1, source_target_pairs={{0,1},{1,0},{2,3},{3,2},{4,5},{5,4},{6,7},{7,6},{8,9},{9,8},{10,11... | collective-permute-start | bytes 540680 | tf_op jit(solution)/shard_map/ppermute | solution.py:1249
  11.3 2.6 %collective-permute-done = bf16[1,200,512]{2,1,0:T(8,128)(2,1)S(1)} collective-permute-done((bf16[1,200,512]{2,1,0:T(8,128)(2,1)}, bf16[1,200,512]{2,1,0:T(8,128)(2,1)S(1)}, u32[]{:S(2)}, u32[]{:S(2)}) %collective-permute-start) | collective-permute-done | bytes 204832 | tf_op jit(solution)/shard_map/ppermute | solution.py:1133
  15.0 3.3 %collective-permute-start.3 = (bf16[2,144,512]{2,1,0:T(8,128)(2,1)S(1)}, bf16[2,144,512]{2,1,0:T(8,128)(2,1)S(1)}, u32[]{:S(2)}, u32[]{:S(2)}) collective-permute-start(bf16[2,144,512]{2,1,0:T(8,128)(2,1)S(1)} %slice.90), channel_id=1, source_target_pairs={{0,2},{1,17},{2,0},{3,19},{4,6},{5,21},{6,4},{7,23},{8,10},{9,25},... | collective-permute-start | bytes 884744 | tf_op jit(solution)/shard_map/ppermute | solution.py:1133
  18.4 5.8 %collective-permute-done.5 = bf16[2,56,512]{2,1,0:T(8,128)(2,1)S(1)} collective-permute-done((bf16[2,56,512]{2,1,0:T(8,128)(2,1)S(1)}, bf16[2,56,512]{2,1,0:T(8,128)(2,1)S(1)}, u32[]{:S(2)}, u32[]{:S(2)}) %collective-permute-start.5) | collective-permute-done | bytes 114720 | tf_op jit(solution)/shard_map/ppermute | solution.py:1133
  24.2 2.1 %collective-permute-start.6 = (bf16[4,56,512]{2,1,0:T(8,128)(2,1)S(1)}, bf16[4,56,512]{2,1,0:T(8,128)(2,1)S(1)}, u32[]{:S(2)}, u32[]{:S(2)}) collective-permute-start(bf16[4,56,512]{2,1,0:T(8,128)(2,1)S(1)} %pad_maximum_fusion.4), channel_id=1, source_target_pairs={{0,8},{1,3},{2,10},{3,1},{4,12},{5,7},{6,14},{7,5},{8,0},{9,11},{1... | collective-permute-start | bytes 688136 | tf_op jit(solution)/shard_map/ppermute | solution.py:1133
  26.5 4.1 %prepare.1 = (f32[512,512]{1,0:T(8,128)S(1)}, f32[512,128]{1,0:T(8,128)S(1)}, bf16[512,512]{1,0:T(8,128)(2,1)S(1)}, f32[1024,128]{1,0:T(8,128)S(1)}, f32[2048,12...) custom-call(s32[10]{0:T(128)S(1)} %copy-done.2, ...), custom_call_target="tpu_custom_call" | custom-call | flops 1 | bytes 1 | tf_op jit(solution)/shard_map/prepare/pallas_call | solution.py:334
  30.8 2.0 %collective-permute-start.7 = (bf16[8,56,512]{2,1,0:T(8,128)(2,1)S(1)}, bf16[8,56,512]{2,1,0:T(8,128)(2,1)S(1)}, u32[]{:S(2)}, u32[]{:S(2)}) collective-permute-start(bf16[8,56,512]{2,1,0:T(8,128)(2,1)S(1)} %pad_maximum_fusion.2.refs_0_), channel_id=1, source_target_pairs={{0,4},{1,9},{2,6},{3,11},{4,0},{5,13},{6,2},{7,15},{8,12},{9,1},{1... | collective-permute-start | bytes 1376264 | tf_op jit(solution)/shard_map/ppermute | solution.py:1133
  32.8 5.1 %collective-permute-done.4 = bf16[4,144,512]{2,1,0:T(8,128)(2,1)S(1)} collective-permute-done((bf16[4,144,512]{2,1,0:T(8,128)(2,1)S(1)}, bf16[4,144,512]{2,1,0:T(8,128)(2,1)S(1)}, u32[]{:S(2)}, u32[]{:S(2)}) %collective-permute-start.4) | collective-permute-done | bytes 589856 | tf_op jit(solution)/shard_map/ppermute | solution.py:1133
  38.0 1.3 %collective-permute-done.7.refs_1_ = bf16[8,56,512]{2,1,0:T(8,128)(2,1)S(1)} collective-permute-done((bf16[8,56,512]{2,1,0:T(8,128)(2,1)S(1)}, bf16[8,56,512]{2,1,0:T(8,128)(2,1)S(1)}, u32[]{:S(2)}, u32[]{:S(2)}) %collective-permute-start.7) | collective-permute-done | bytes 458784 | tf_op jit(solution)/shard_map/ppermute | solution.py:1133
  39.3 1.9 %collective-permute-start.10 = (bf16[8,144,512]{2,1,0:T(8,128)(2,1)S(1)}, bf16[8,144,512]{2,1,0:T(8,128)(2,1)S(1)}, u32[]{:S(2)}, u32[]{:S(2)}) collective-permute-start(bf16[8,144,512]{2,1,0:T(8,128)(2,1)S(1)} %pad_maximum_fusion.refs_0_), channel_id=1, source_target_pairs={{0,4},{1,9},{2,6},{3,11},{4,0},{5,13},{6,2},{7,15},{8,12},{9,1},{1... | collective-permute-start | bytes 3538952 | tf_op jit(solution)/shard_map/ppermute | solution.py:1133
  41.2 1.9 %collective-permute-start.8 = (bf16[8,56,512]{2,1,0:T(8,128)(2,1)S(1)}, bf16[8,56,512]{2,1,0:T(8,128)(2,1)S(1)}, u32[]{:S(2)}, u32[]{:S(2)}) collective-permute-start(bf16[8,56,512]{2,1,0:T(8,128)(2,1)S(1)} %pad_maximum_fusion.2.refs_0_), channel_id=1, source_target_pairs={{0,1},{1,0},{2,3},{3,2},{4,5},{5,4},{6,7},{7,6},{8,9},{9,8},{10,11... | collective-permute-start | bytes 1376264 | tf_op jit(solution)/shard_map/ppermute | solution.py:1133
  45.3 3.4 %project.1 = (bf16[1024,256]{1,0:T(8,128)(2,1)S(1)}, bf16[1024,256]{1,0:T(8,128)(2,1)S(1)}, bf16[1024,512]{1,0:T(8,128)(2,1)S(1)}, bf16[1024,512]{1,0:T(8,128)(2...) custom-call(s32[10]{0:T(128)S(1)} %copy-done.2, ...), custom_call_target="tpu_custom_call" | custom-call | flops 1 | bytes 1 | tf_op jit(solution)/shard_map/project/pallas_call | solution.py:450
  48.7 4.8 %attend.1 = (bf16[512,256]{1,0:T(8,128)(2,1)S(1)}, bf16[512,256]{1,0:T(8,128)(2,1)S(1)}, f32[512,256]{1,0:T(8,128)S(1)}, f32[512,256]{1,0:T(8,128)S(1)}, f32[512,256]{1,0:T(8,128)S(1)}, /*index=5*/f32[512,256]{1,0:T(8,128)S(1)}) custom-call(s32[10]{0:T(128)S(1)} %copy-done.2, f32[1024,128]{1,0:T(8,128)S(1)} %get-tuple-element.120.mask, ...), custom_call_target="tpu_custom_call" | custom-call | flops 1 | bytes 1 | tf_op jit(solution)/shard_map/attend/pallas_call | solution.py:551
  53.5 2.0 %collective-permute-done.10.refs_1_ = bf16[8,144,512]{2,1,0:T(8,128)(2,1)S(1)} collective-permute-done((bf16[8,144,512]{2,1,0:T(8,128)(2,1)S(1)}, bf16[8,144,512]{2,1,0:T(8,128)(2,1)S(1)}, u32[]{:S(2)}, u32[]{:S(2)}) %collective-permute-start.10) | collective-permute-done | bytes 1179680 | tf_op jit(solution)/shard_map/ppermute | solution.py:1133
  56.8 2.5 %collective-permute-done.12.refs_3_ = bf16[8,144,512]{2,1,0:T(8,128)(2,1)S(1)} collective-permute-done((bf16[8,144,512]{2,1,0:T(8,128)(2,1)S(1)}, bf16[8,144,512]{2,1,0:T(8,128)(2,1)S(1)}, u32[]{:S(2)}, u32[]{:S(2)}) %collective-permute-start.12) | collective-permute-done | bytes 1179680 | tf_op jit(solution)/shard_map/ppermute | solution.py:1133
  59.3 8.9 %feed_forward.1 = (bf16[512,512]{1,0:T(8,128)(2,1)}, f32[512,512]{1,0:T(8,128)S(1)}, f32[512,512]{1,0:T(8,128)S(1)}, bf16[512,512]{1,0:T(8,128)(2,1)S(1)}, bf16[...) custom-call(s32[32]{0:T(128)S(1)} %copy-done.4, ...), custom_call_target="tpu_custom_call" | custom-call | flops 1 | bytes 1 | tf_op jit(solution)/shard_map/feed_forward/pallas_call | solution.py:658
  68.7 2.8 %middle.1 = (f32[512,512]{1,0:T(8,128)S(1)}, bf16[1024,512]{1,0:T(8,128)(2,1)S(1)}, bf16[1024,512]{1,0:T(8,128)(2,1)S(1)}, bf16[160,640]{1,0:T(8,128)(2,1)S(1)},...) custom-call(s32[10]{0:T(128)S(1)} %copy-done.2, ...), custom_call_target="tpu_custom_call" | custom-call | flops 1 | bytes 1 | tf_op jit(solution)/shard_map/middle/pallas_call | solution.py:787
  74.1 1.7 %collective-permute-start.19 = (bf16[4,144,512]{2,1,0:T(8,128)(2,1)S(1)}, bf16[4,144,512]{2,1,0:T(8,128)(2,1)S(1)}, u32[]{:S(2)}, u32[]{:S(2)}) collective-permute-start(bf16[4,144,512]{2,1,0:T(8,128)(2,1)S(1)} %get-tuple-element.150), channel_id=1, source_target_pairs={{0,2},{1,5},{2,0},{3,7},{4,6},{5,1},{6,4},{7,3},{8,10},{9,13},{10,... | collective-permute-start | bytes 1769480 | tf_op jit(solution)/shard_map/ppermute | solution.py:1133
  76.5 2.9 %collective-permute-start.22 = (bf16[4,144,512]{2,1,0:T(8,128)(2,1)S(1)}, bf16[4,144,512]{2,1,0:T(8,128)(2,1)S(1)}, u32[]{:S(2)}, u32[]{:S(2)}) collective-permute-start(bf16[4,144,512]{2,1,0:T(8,128)(2,1)S(1)} %get-tuple-element.151), channel_id=1, source_target_pairs={{0,2},{1,5},{2,0},{3,7},{4,6},{5,1},{6,4},{7,3},{8,10},{9,13},{10,... | collective-permute-start | bytes 1769480 | tf_op jit(solution)/shard_map/ppermute | solution.py:1133
  79.3 7.3 %attend_back.1 = (f32[1024,256]{1,0:T(8,128)S(1)}, f32[1024,256]{1,0:T(8,128)S(1)}, f32[1344,512]{1,0:T(8,128)S(1)}, f32[1344,512]{1,0:T(8,128)S(1)}) custom-call(f32[2048,128]{1,0:T(8,128)S(1)} %get-tuple-element.114.mask, bf16[2048,128]{1,0:T(8,128)(2,1)S(1)} %get-tuple-element.115.counts_of, bf16[1024,256]{1,0:T(8,128)(2,1)S(1)} %get-tuple-element.121.refs_0_, ...), custom_call_target="tpu_custom_call" | custom-call | flops 1 | bytes 1 | tf_op jit(solution)/shard_map/attend_back/pallas_call | solution.py:881
  88.9 2.4 %edge_back.1 = (f32[320,512]{1,0:T(8,128)S(1)}, f32[320,512]{1,0:T(8,128)S(1)}) custom-call(s32[10]{0:T(128)S(1)} %copy-done.2, f32[320,128]{1,0:T(8,128)S(1)} %get-tuple-element.116.mask, bf16[320,128]{1,0:T(8,128)(2,1)S(1)} %get-tuple-element.117.counts_of, bf16[320,256]{1,0:T(8,128)(2,1)S(1)} %get-tuple-element.158.queries_a, ...), custom_call_target="tpu_custom_call" | custom-call | flops 1 | bytes 1 | tf_op jit(solution)/shard_map/edge_back/pallas_call | solution.py:973
  91.2 5.1 %finish.1 = (f32[512,512]{1,0:T(8,128)}, bf16[16,56,512]{2,1,0:T(8,128)(2,1)S(1)}, bf16[8,56,512]{2,1,0:T(8,128)(2,1)S(1)}, bf16[8,56,512]{2,1,0:T(8,128)(2,1)S(1)}) custom-call(s32[10]{0:T(128)S(1)} %copy-done.2, s32[32]{0:T(128)S(1)} %copy-done.3, f32[512,512]{1,0:T(8,128)S(1)} %get-tuple-element.111.standard, f32[512,128]{1,0:T(8,128)S(1)} %get-tuple-element.112.spread, ...), custom_call_target="tpu_custom_call" | custom-call | flops 1 | bytes 1 | tf_op jit(solution)/shard_map/finish/pallas_call | solution.py:1083
  99.8 2.3 %collective-permute-start.24 = (bf16[8,56,512]{2,1,0:T(8,128)(2,1)S(1)}, bf16[8,56,512]{2,1,0:T(8,128)(2,1)S(1)}, u32[]{:S(2)}, u32[]{:S(2)}) collective-permute-start(bf16[8,56,512]{2,1,0:T(8,128)(2,1)S(1)} %get-tuple-element.199), channel_id=1, source_target_pairs={{0,2},{1,5},{2,0},{3,7},{4,6},{5,1},{6,4},{7,3},{8,10},{9,13},{10,... | collective-permute-start | bytes 1376264 | tf_op jit(solution)/shard_map/ppermute | solution.py:1133
  102.5 6.1 %collective-permute-done.24 = bf16[8,56,512]{2,1,0:T(8,128)(2,1)S(1)} collective-permute-done((bf16[8,56,512]{2,1,0:T(8,128)(2,1)S(1)}, bf16[8,56,512]{2,1,0:T(8,128)(2,1)S(1)}, u32[]{:S(2)}, u32[]{:S(2)}) %collective-permute-start.24) | collective-permute-done | bytes 458784 | tf_op jit(solution)/shard_map/ppermute | solution.py:1133
  108.7 1.4 %collective-permute-start.25 = (bf16[4,56,512]{2,1,0:T(8,128)(2,1)S(1)}, bf16[4,56,512]{2,1,0:T(8,128)(2,1)S(1)}, u32[]{:S(2)}, u32[]{:S(2)}) collective-permute-start(bf16[4,56,512]{2,1,0:T(8,128)(2,1)S(1)} %get-tuple-element.195), channel_id=1, source_target_pairs={{0,4},{1,9},{2,6},{3,11},{4,0},{5,13},{6,2},{7,15},{8,12},{9,1},{1... | collective-permute-start | bytes 688136 | tf_op jit(solution)/shard_map/ppermute | solution.py:1133
  110.1 2.0 %collective-permute-done.26 = bf16[2,144,512]{2,1,0:T(8,128)(2,1)S(1)} collective-permute-done((bf16[2,144,512]{2,1,0:T(8,128)(2,1)S(1)}, bf16[2,144,512]{2,1,0:T(8,128)(2,1)S(1)}, u32[]{:S(2)}, u32[]{:S(2)}) %collective-permute-start.26) | collective-permute-done | bytes 294944 | tf_op jit(solution)/shard_map/ppermute | solution.py:1133
  112.2 2.6 %collective-permute-done.25 = bf16[4,56,512]{2,1,0:T(8,128)(2,1)S(1)} collective-permute-done((bf16[4,56,512]{2,1,0:T(8,128)(2,1)S(1)}, bf16[4,56,512]{2,1,0:T(8,128)(2,1)S(1)}, u32[]{:S(2)}, u32[]{:S(2)}) %collective-permute-start.25) | collective-permute-done | bytes 229408 | tf_op jit(solution)/shard_map/ppermute | solution.py:1133
  115.8 3.9 %collective-permute-start.29 = (bf16[1,144,512]{2,1,0:T(8,128)(2,1)S(1)}, bf16[1,144,512]{2,1,0:T(8,128)(2,1)S(1)}, u32[]{:S(2)}, u32[]{:S(2)}) collective-permute-start(bf16[1,144,512]{2,1,0:T(8,128)(2,1)S(1)} %get-tuple-element.202), channel_id=1, source_target_pairs={{0,16},{1,3},{2,18},{3,1},{4,20},{5,7},{6,22},{7,5},{8,24},{9,11},... | collective-permute-start | bytes 442376 | tf_op jit(solution)/shard_map/ppermute | solution.py:1133
  119.7 3.9 %collective-permute-start.28 = (bf16[1,56,512]{2,1,0:T(8,128)(2,1)S(1)}, bf16[1,56,512]{2,1,0:T(8,128)(2,1)S(1)}, u32[]{:S(2)}, u32[]{:S(2)}) collective-permute-start(bf16[1,56,512]{2,1,0:T(8,128)(2,1)S(1)} %get-tuple-element.205), channel_id=1, source_target_pairs={{0,16},{1,3},{2,18},{3,1},{4,20},{5,7},{6,22},{7,5},{8,24},{9,11},... | collective-permute-start | bytes 172040 | tf_op jit(solution)/shard_map/ppermute | solution.py:1133
  123.7 2.2 %collective-permute-done.28.came_one = bf16[1,56,512]{2,1,0:T(8,128)(2,1)S(1)} collective-permute-done((bf16[1,56,512]{2,1,0:T(8,128)(2,1)S(1)}, bf16[1,56,512]{2,1,0:T(8,128)(2,1)S(1)}, u32[]{:S(2)}, u32[]{:S(2)}) %collective-permute-start.28) | collective-permute-done | bytes 57376 | tf_op jit(solution)/shard_map/ppermute | solution.py:1133
  (67 shorter events, 17.4 us)
Async XLA Ops:
  3.6 10.3 %collective-permute-start = (bf16[1,200,512]{2,1,0:T(8,128)(2,1)}, bf16[1,200,512]{2,1,0:T(8,128)(2,1)S(1)}, u32[]{:S(2)}, u32[]{:S(2)}) collective-permute-start(bf16[1,200,512]{2,1,0:T(8,128)(2,1)} %get-tuple-element.105), channel_id=1, source_target_pairs={{0,16},{1,5},{2,18},{3,7},{4,20},{5,1},{6,22},{7,3},{8,24},{9,13},... | collective-permute-start | bytes 614408 | tf_op jit(solution)/shard_map/ppermute | solution.py:1133
  7.7 7.2 %collective-permute-start.1 = (bf16[176,512]{1,0:T(8,128)(2,1)}, bf16[176,512]{1,0:T(8,128)(2,1)S(1)}, u32[]{:S(2)}, u32[]{:S(2)}) collective-permute-start(bf16[176,512]{1,0:T(8,128)(2,1)} %get-tuple-element.108), channel_id=1, source_target_pairs={{1,2},{3,4},{5,6},{7,8},{9,10},{11,12},{13,14},{15,16},{17,18},{19... | collective-permute-start | bytes 540680 | tf_op jit(solution)/shard_map/ppermute | solution.py:1249
  8.4 18.1 %copy-start = (bf16[512,512]{1,0:T(8,128)(2,1)S(1)}, bf16[512,512]{1,0:T(8,128)(2,1)}, u32[]{:S(2)}) copy-start(bf16[512,512]{1,0:T(8,128)(2,1)} %tokens.4) | copy-start | bytes 1572868
  8.4 18.1 %copy-start.2 = (s32[10]{0:T(128)S(1)}, s32[10]{0:T(128)}, u32[]{:S(2)}) copy-start(s32[10]{0:T(128)} %get-tuple-element.104.info) | copy-start | bytes 124
  8.4 6.5 %collective-permute-start.2 = (bf16[176,512]{1,0:T(8,128)(2,1)}, bf16[176,512]{1,0:T(8,128)(2,1)S(1)}, u32[]{:S(2)}, u32[]{:S(2)}) collective-permute-start(bf16[176,512]{1,0:T(8,128)(2,1)} %get-tuple-element.109), channel_id=1, source_target_pairs={{0,1},{1,0},{2,3},{3,2},{4,5},{5,4},{6,7},{7,6},{8,9},{9,8},{10,11... | collective-permute-start | bytes 540680 | tf_op jit(solution)/shard_map/ppermute | solution.py:1249
  15.0 11.4 %collective-permute-start.3 = (bf16[2,144,512]{2,1,0:T(8,128)(2,1)S(1)}, bf16[2,144,512]{2,1,0:T(8,128)(2,1)S(1)}, u32[]{:S(2)}, u32[]{:S(2)}) collective-permute-start(bf16[2,144,512]{2,1,0:T(8,128)(2,1)S(1)} %slice.90), channel_id=1, source_target_pairs={{0,2},{1,17},{2,0},{3,19},{4,6},{5,21},{6,4},{7,23},{8,10},{9,25},... | collective-permute-start | bytes 884744 | tf_op jit(solution)/shard_map/ppermute | solution.py:1133
  18.3 5.9 %collective-permute-start.5 = (bf16[2,56,512]{2,1,0:T(8,128)(2,1)S(1)}, bf16[2,56,512]{2,1,0:T(8,128)(2,1)S(1)}, u32[]{:S(2)}, u32[]{:S(2)}) collective-permute-start(bf16[2,56,512]{2,1,0:T(8,128)(2,1)S(1)} %slice.91), channel_id=1, source_target_pairs={{0,2},{1,17},{2,0},{3,19},{4,6},{5,21},{6,4},{7,23},{8,10},{9,25},... | collective-permute-start | bytes 344072 | tf_op jit(solution)/shard_map/ppermute | solution.py:1133
  24.2 6.5 %collective-permute-start.6 = (bf16[4,56,512]{2,1,0:T(8,128)(2,1)S(1)}, bf16[4,56,512]{2,1,0:T(8,128)(2,1)S(1)}, u32[]{:S(2)}, u32[]{:S(2)}) collective-permute-start(bf16[4,56,512]{2,1,0:T(8,128)(2,1)S(1)} %pad_maximum_fusion.4), channel_id=1, source_target_pairs={{0,8},{1,3},{2,10},{3,1},{4,12},{5,7},{6,14},{7,5},{8,0},{9,11},{1... | collective-permute-start | bytes 688136 | tf_op jit(solution)/shard_map/ppermute | solution.py:1133
  26.4 11.5 %collective-permute-start.4 = (bf16[4,144,512]{2,1,0:T(8,128)(2,1)S(1)}, bf16[4,144,512]{2,1,0:T(8,128)(2,1)S(1)}, u32[]{:S(2)}, u32[]{:S(2)}) collective-permute-start(bf16[4,144,512]{2,1,0:T(8,128)(2,1)S(1)} %pad_maximum_fusion.1), channel_id=1, source_target_pairs={{0,8},{1,3},{2,10},{3,1},{4,12},{5,7},{6,14},{7,5},{8,0},{9,11},{1... | collective-permute-start | bytes 1769480 | tf_op jit(solution)/shard_map/ppermute | solution.py:1133
  30.8 8.5 %collective-permute-start.7 = (bf16[8,56,512]{2,1,0:T(8,128)(2,1)S(1)}, bf16[8,56,512]{2,1,0:T(8,128)(2,1)S(1)}, u32[]{:S(2)}, u32[]{:S(2)}) collective-permute-start(bf16[8,56,512]{2,1,0:T(8,128)(2,1)S(1)} %pad_maximum_fusion.2.refs_0_), channel_id=1, source_target_pairs={{0,4},{1,9},{2,6},{3,11},{4,0},{5,13},{6,2},{7,15},{8,12},{9,1},{1... | collective-permute-start | bytes 1376264 | tf_op jit(solution)/shard_map/ppermute | solution.py:1133
  39.3 16.2 %collective-permute-start.10 = (bf16[8,144,512]{2,1,0:T(8,128)(2,1)S(1)}, bf16[8,144,512]{2,1,0:T(8,128)(2,1)S(1)}, u32[]{:S(2)}, u32[]{:S(2)}) collective-permute-start(bf16[8,144,512]{2,1,0:T(8,128)(2,1)S(1)} %pad_maximum_fusion.refs_0_), channel_id=1, source_target_pairs={{0,4},{1,9},{2,6},{3,11},{4,0},{5,13},{6,2},{7,15},{8,12},{9,1},{1... | collective-permute-start | bytes 3538952 | tf_op jit(solution)/shard_map/ppermute | solution.py:1133
  41.2 3.4 %collective-permute-start.8 = (bf16[8,56,512]{2,1,0:T(8,128)(2,1)S(1)}, bf16[8,56,512]{2,1,0:T(8,128)(2,1)S(1)}, u32[]{:S(2)}, u32[]{:S(2)}) collective-permute-start(bf16[8,56,512]{2,1,0:T(8,128)(2,1)S(1)} %pad_maximum_fusion.2.refs_0_), channel_id=1, source_target_pairs={{0,1},{1,0},{2,3},{3,2},{4,5},{5,4},{6,7},{7,6},{8,9},{9,8},{10,11... | collective-permute-start | bytes 1376264 | tf_op jit(solution)/shard_map/ppermute | solution.py:1133
  43.2 2.1 %collective-permute-start.9 = (bf16[8,56,512]{2,1,0:T(8,128)(2,1)S(1)}, bf16[8,56,512]{2,1,0:T(8,128)(2,1)S(1)}, u32[]{:S(2)}, u32[]{:S(2)}) collective-permute-start(bf16[8,56,512]{2,1,0:T(8,128)(2,1)S(1)} %collective-permute-done.7.refs_1_), channel_id=1, source_target_pairs={{0,1},{1,0},{2,3},{3,2},{4,5},{5,4},{6,7},{7,6},{8,9},{9,8},{10,11... | collective-permute-start | bytes 1376264 | tf_op jit(solution)/shard_map/ppermute | solution.py:1133
  43.2 13.7 %collective-permute-start.11 = (bf16[8,144,512]{2,1,0:T(8,128)(2,1)S(1)}, bf16[8,144,512]{2,1,0:T(8,128)(2,1)S(1)}, u32[]{:S(2)}, u32[]{:S(2)}) collective-permute-start(bf16[8,144,512]{2,1,0:T(8,128)(2,1)S(1)} %pad_maximum_fusion.refs_0_), channel_id=1, source_target_pairs={{0,1},{1,0},{2,3},{3,2},{4,5},{5,4},{6,7},{7,6},{8,9},{9,8},{10,11... | collective-permute-start | bytes 3538952 | tf_op jit(solution)/shard_map/ppermute | solution.py:1133
  55.5 3.8 %collective-permute-start.12 = (bf16[8,144,512]{2,1,0:T(8,128)(2,1)S(1)}, bf16[8,144,512]{2,1,0:T(8,128)(2,1)S(1)}, u32[]{:S(2)}, u32[]{:S(2)}) collective-permute-start(bf16[8,144,512]{2,1,0:T(8,128)(2,1)S(1)} %collective-permute-done.10.refs_1_), channel_id=1, source_target_pairs={{0,1},{1,0},{2,3},{3,2},{4,5},{5,4},{6,7},{7,6},{8,9},{9,8},{10,11... | collective-permute-start | bytes 3538952 | tf_op jit(solution)/shard_map/ppermute | solution.py:1133
  68.2 5.1 %collective-permute-start.13 = (bf16[8,128,512]{2,1,0:T(8,128)(2,1)S(1)}, bf16[8,128,512]{2,1,0:T(8,128)(2,1)S(1)}, u32[]{:S(2)}, u32[]{:S(2)}) collective-permute-start(bf16[8,128,512]{2,1,0:T(8,128)(2,1)S(1)} %get-tuple-element.147), channel_id=1, source_target_pairs={{0,1},{1,0},{2,3},{3,2},{4,5},{5,4},{6,7},{7,6},{8,9},{9,8},{10,11... | collective-permute-start | bytes 3145736 | tf_op jit(solution)/shard_map/ppermute | solution.py:1133
  68.6 4.7 %collective-permute-start.17 = (bf16[8,128,512]{2,1,0:T(8,128)(2,1)S(1)}, bf16[8,128,512]{2,1,0:T(8,128)(2,1)S(1)}, u32[]{:S(2)}, u32[]{:S(2)}) collective-permute-start(bf16[8,128,512]{2,1,0:T(8,128)(2,1)S(1)} %get-tuple-element.163), channel_id=1, source_target_pairs={{0,1},{1,0},{2,3},{3,2},{4,5},{5,4},{6,7},{7,6},{8,9},{9,8},{10,11... | collective-permute-start | bytes 3145736 | tf_op jit(solution)/shard_map/ppermute | solution.py:1133
  71.5 1.4 %collective-permute-start.14 = (bf16[8,16,512]{2,1,0:T(8,128)(2,1)S(1)}, bf16[8,16,512]{2,1,0:T(8,128)(2,1)S(1)}, u32[]{:S(2)}, u32[]{:S(2)}) collective-permute-start(bf16[8,16,512]{2,1,0:T(8,128)(2,1)S(1)} %get-tuple-element.148), channel_id=1, source_target_pairs={{0,1},{1,0},{2,3},{3,2},{4,5},{5,4},{6,7},{7,6},{8,9},{9,8},{10,11... | collective-permute-start | bytes 393224 | tf_op jit(solution)/shard_map/ppermute | solution.py:1133
  72.0 1.3 %collective-permute-start.18 = (bf16[8,16,512]{2,1,0:T(8,128)(2,1)S(1)}, bf16[8,16,512]{2,1,0:T(8,128)(2,1)S(1)}, u32[]{:S(2)}, u32[]{:S(2)}) collective-permute-start(bf16[8,16,512]{2,1,0:T(8,128)(2,1)S(1)} %get-tuple-element.164), channel_id=1, source_target_pairs={{0,1},{1,0},{2,3},{3,2},{4,5},{5,4},{6,7},{7,6},{8,9},{9,8},{10,11... | collective-permute-start | bytes 393224 | tf_op jit(solution)/shard_map/ppermute | solution.py:1133
  72.1 2.0 %collective-permute-start.15 = (bf16[160,640]{1,0:T(8,128)(2,1)S(1)}, bf16[160,640]{1,0:T(8,128)(2,1)S(1)}, u32[]{:S(2)}, u32[]{:S(2)}) collective-permute-start(bf16[160,640]{1,0:T(8,128)(2,1)S(1)} %get-tuple-element.149), channel_id=1, source_target_pairs={{0,1},{1,0},{2,3},{3,2},{4,5},{5,4},{6,7},{7,6},{8,9},{9,8},{10,11... | collective-permute-start | bytes 614408 | tf_op jit(solution)/shard_map/ppermute | solution.py:1249
  74.1 13.5 %collective-permute-start.19 = (bf16[4,144,512]{2,1,0:T(8,128)(2,1)S(1)}, bf16[4,144,512]{2,1,0:T(8,128)(2,1)S(1)}, u32[]{:S(2)}, u32[]{:S(2)}) collective-permute-start(bf16[4,144,512]{2,1,0:T(8,128)(2,1)S(1)} %get-tuple-element.150), channel_id=1, source_target_pairs={{0,2},{1,5},{2,0},{3,7},{4,6},{5,1},{6,4},{7,3},{8,10},{9,13},{10,... | collective-permute-start | bytes 1769480 | tf_op jit(solution)/shard_map/ppermute | solution.py:1133
  75.8 10.9 %collective-permute-start.16 = (bf16[160,640]{1,0:T(8,128)(2,1)S(1)}, bf16[160,640]{1,0:T(8,128)(2,1)S(1)}, u32[]{:S(2)}, u32[]{:S(2)}) collective-permute-start(bf16[160,640]{1,0:T(8,128)(2,1)S(1)} %get-tuple-element.160), channel_id=1, source_target_pairs={{1,2},{3,4},{5,6},{7,8},{9,10},{11,12},{13,14},{15,16},{17,18},{19... | collective-permute-start | bytes 614408 | tf_op jit(solution)/shard_map/ppermute | solution.py:1249
  76.5 21.0 %collective-permute-start.22 = (bf16[4,144,512]{2,1,0:T(8,128)(2,1)S(1)}, bf16[4,144,512]{2,1,0:T(8,128)(2,1)S(1)}, u32[]{:S(2)}, u32[]{:S(2)}) collective-permute-start(bf16[4,144,512]{2,1,0:T(8,128)(2,1)S(1)} %get-tuple-element.151), channel_id=1, source_target_pairs={{0,2},{1,5},{2,0},{3,7},{4,6},{5,1},{6,4},{7,3},{8,10},{9,13},{10,... | collective-permute-start | bytes 1769480 | tf_op jit(solution)/shard_map/ppermute | solution.py:1133
  87.8 9.9 %collective-permute-start.23 = (bf16[4,144,512]{2,1,0:T(8,128)(2,1)S(1)}, bf16[4,144,512]{2,1,0:T(8,128)(2,1)S(1)}, u32[]{:S(2)}, u32[]{:S(2)}) collective-permute-start(bf16[4,144,512]{2,1,0:T(8,128)(2,1)S(1)} %fusion), channel_id=1, source_target_pairs={{0,4},{1,9},{2,6},{3,11},{4,0},{5,13},{6,2},{7,15},{8,12},{9,1},{1... | collective-permute-start | bytes 1769480 | tf_op jit(solution)/shard_map/ppermute | solution.py:1133
  96.4 2.5 %collective-permute-start.20 = (bf16[8,56,512]{2,1,0:T(8,128)(2,1)S(1)}, bf16[8,56,512]{2,1,0:T(8,128)(2,1)S(1)}, u32[]{:S(2)}, u32[]{:S(2)}) collective-permute-start(bf16[8,56,512]{2,1,0:T(8,128)(2,1)S(1)} %get-tuple-element.172), channel_id=1, source_target_pairs={{0,1},{1,0},{2,3},{3,2},{4,5},{5,4},{6,7},{7,6},{8,9},{9,8},{10,11... | collective-permute-start | bytes 1376264 | tf_op jit(solution)/shard_map/ppermute | solution.py:1133
  97.4 2.1 %collective-permute-start.21 = (bf16[8,56,512]{2,1,0:T(8,128)(2,1)S(1)}, bf16[8,56,512]{2,1,0:T(8,128)(2,1)S(1)}, u32[]{:S(2)}, u32[]{:S(2)}) collective-permute-start(bf16[8,56,512]{2,1,0:T(8,128)(2,1)S(1)} %get-tuple-element.173), channel_id=1, source_target_pairs={{0,1},{1,0},{2,3},{3,2},{4,5},{5,4},{6,7},{7,6},{8,9},{9,8},{10,11... | collective-permute-start | bytes 1376264 | tf_op jit(solution)/shard_map/ppermute | solution.py:1133
  99.8 8.8 %collective-permute-start.24 = (bf16[8,56,512]{2,1,0:T(8,128)(2,1)S(1)}, bf16[8,56,512]{2,1,0:T(8,128)(2,1)S(1)}, u32[]{:S(2)}, u32[]{:S(2)}) collective-permute-start(bf16[8,56,512]{2,1,0:T(8,128)(2,1)S(1)} %get-tuple-element.199), channel_id=1, source_target_pairs={{0,2},{1,5},{2,0},{3,7},{4,6},{5,1},{6,4},{7,3},{8,10},{9,13},{10,... | collective-permute-start | bytes 1376264 | tf_op jit(solution)/shard_map/ppermute | solution.py:1133
  102.1 10.0 %collective-permute-start.26 = (bf16[2,144,512]{2,1,0:T(8,128)(2,1)S(1)}, bf16[2,144,512]{2,1,0:T(8,128)(2,1)S(1)}, u32[]{:S(2)}, u32[]{:S(2)}) collective-permute-start(bf16[2,144,512]{2,1,0:T(8,128)(2,1)S(1)} %get-tuple-element.194), channel_id=1, source_target_pairs={{0,8},{1,17},{2,10},{3,19},{4,12},{5,21},{6,14},{7,23},{8,0},{9,25... | collective-permute-start | bytes 884744 | tf_op jit(solution)/shard_map/ppermute | solution.py:1133
  108.7 6.1 %collective-permute-start.25 = (bf16[4,56,512]{2,1,0:T(8,128)(2,1)S(1)}, bf16[4,56,512]{2,1,0:T(8,128)(2,1)S(1)}, u32[]{:S(2)}, u32[]{:S(2)}) collective-permute-start(bf16[4,56,512]{2,1,0:T(8,128)(2,1)S(1)} %get-tuple-element.195), channel_id=1, source_target_pairs={{0,4},{1,9},{2,6},{3,11},{4,0},{5,13},{6,2},{7,15},{8,12},{9,1},{1... | collective-permute-start | bytes 688136 | tf_op jit(solution)/shard_map/ppermute | solution.py:1133
  114.8 4.9 %collective-permute-start.27 = (bf16[2,56,512]{2,1,0:T(8,128)(2,1)S(1)}, bf16[2,56,512]{2,1,0:T(8,128)(2,1)S(1)}, u32[]{:S(2)}, u32[]{:S(2)}) collective-permute-start(bf16[2,56,512]{2,1,0:T(8,128)(2,1)S(1)} %get-tuple-element.203), channel_id=1, source_target_pairs={{0,8},{1,17},{2,10},{3,19},{4,12},{5,21},{6,14},{7,23},{8,0},{9,25... | collective-permute-start | bytes 344072 | tf_op jit(solution)/shard_map/ppermute | solution.py:1133
  115.8 7.9 %collective-permute-start.29 = (bf16[1,144,512]{2,1,0:T(8,128)(2,1)S(1)}, bf16[1,144,512]{2,1,0:T(8,128)(2,1)S(1)}, u32[]{:S(2)}, u32[]{:S(2)}) collective-permute-start(bf16[1,144,512]{2,1,0:T(8,128)(2,1)S(1)} %get-tuple-element.202), channel_id=1, source_target_pairs={{0,16},{1,3},{2,18},{3,1},{4,20},{5,7},{6,22},{7,5},{8,24},{9,11},... | collective-permute-start | bytes 442376 | tf_op jit(solution)/shard_map/ppermute | solution.py:1133
  119.7 6.1 %collective-permute-start.28 = (bf16[1,56,512]{2,1,0:T(8,128)(2,1)S(1)}, bf16[1,56,512]{2,1,0:T(8,128)(2,1)S(1)}, u32[]{:S(2)}, u32[]{:S(2)}) collective-permute-start(bf16[1,56,512]{2,1,0:T(8,128)(2,1)S(1)} %get-tuple-element.205), channel_id=1, source_target_pairs={{0,16},{1,3},{2,18},{3,1},{4,20},{5,7},{6,22},{7,5},{8,24},{9,11},... | collective-permute-start | bytes 172040 | tf_op jit(solution)/shard_map/ppermute | solution.py:1133
  (3 other events, 35.9 us)
